TPU v7x, 32 devices: a whole 2x2x4 slice. The times are simulated.
32 devices in a mesh: dp: 4 (over y, x), head: 8 (over z, core).
Axes of the slice: x: 2, y: 2, z: 4, core: 2. Of those that a mesh axis runs over, the one named last changes fastest.
Arguments:
- tokens: bfloat16 [8192, 2048], P(('dp', 'head')), may hold values from -6 to 6
- keep_mask: int32 [8192], P('dp'), may hold values 0 or 1
- seq_lengths: int32 [4, 3], P('dp'), may hold values from 32 to 1984, as said below
- attn_gain: float32 [2048], replicated, may hold values from 0.5 to 1.5
- in_weight: bfloat16 [2048, 2560], P(None, 'head'), may hold values from -0.125 to 0.125
- out_weight: bfloat16 [2048, 2048], P('head'), may hold values from -2 to 2
- ffn_gain: float32 [2048], replicated, may hold values from 0.5 to 1.5
- gate_weight: bfloat16 [2048, 5632], P('dp', 'head'), may hold values from -0.125 to 0.125
- up_weight: bfloat16 [2048, 5632], P('dp', 'head'), may hold values from -0.125 to 0.125
- down_weight: bfloat16 [5632, 2048], P('head', 'dp'), may hold values from -0.078125 to 0.078125
- out_grad: bfloat16 [8192, 2048], P(('dp', 'head')), may hold values from -6 to 6
Outputs:
- output: bfloat16 [8192, 2048], P(('dp', 'head'))
- in_grad: float32 [8192, 2048], P(('dp', 'head'))
- attn_gain_grad: float32 [2048], replicated
- in_weight_grad: float32 [2048, 2560], P(None, 'head')
- out_weight_grad: float32 [2048, 2048], P('head')
- ffn_gain_grad: float32 [2048], replicated
- gate_grad: float32 [2048, 5632], P('dp', 'head')
- up_grad: float32 [2048, 5632], P('dp', 'head')
- down_grad: float32 [5632, 2048], P('head', 'dp')
Inputs may be any that keep to these rules, and one draw needn't show every extreme that they name: `seq_lengths`: each row sums to 2048; one sequence of each group, at a slot drawn from the seed, holds all but at most 255 of the group's tokens.
All inputs are finite; a program needn't handle non-finite values. No bound on the sum of `keep_mask` on one device may be relied on, other than what follows from the above.
Results may differ from a plain program's by a relative error of at most 0.023.
Values may be sent and summed in bfloat16 or wider, within the bound.
No kernel may reach another device: no remote copies, remote signals or barrier semaphores. Data moves between devices by JAX's collectives and lax.ppermute only.
A program may use at most 256 MiB of HBM per device.

v0:
```python
import jax
import jax.numpy as jnp
from jax import lax
from jax.sharding import PartitionSpec as P

FD = 16
VD = 128


highest = lax.Precision.HIGHEST
epsilon = 1e-05
inv_root_two = 0.7071067811865476


def taylor_features(scaled):
    head_count = scaled.shape[0]
    block_len = scaled.shape[1]
    feat_width = scaled.shape[2]
    products = (scaled[:, :, :, None] * scaled[:, :, None, :]).reshape(
        head_count, block_len, feat_width * feat_width
    )
    return jnp.concatenate(
        [jnp.ones((head_count, block_len, 1), jnp.float32), scaled, products * inv_root_two], axis=2
    )


def blockwise_attention(queries, key_in, value_in, segment, keep_row):
    head_count = queries.shape[0]
    total_rows = queries.shape[1]
    value_width = value_in.shape[2]
    feature_count = 1 + queries.shape[2] + queries.shape[2] * queries.shape[2]
    block_rows = min(512, total_rows)
    blocks = total_rows // block_rows

    def split_blocks(stacked):
        return stacked.reshape(head_count, blocks, block_rows, stacked.shape[2]).transpose(
            1, 0, 2, 3
        )

    local_pos = jnp.arange(block_rows, dtype=jnp.int32)
    causal = local_pos[:, None] >= local_pos[None, :]

    def block_step(state_carry, inputs):
        kv_state, norm_vec, state_seg = state_carry
        query_block, key_block, value_block, seg_block, keep_block = inputs
        inner_prod = jnp.einsum("hbf,hcf->hbc", query_block, key_block, precision=highest) * 0.25
        kernel = 1.0 + inner_prod + 0.5 * inner_prod * inner_prod
        allowed = causal & (seg_block[:, None] == seg_block[None, :])
        weights = jnp.where(allowed[None], kernel * keep_block[None, None, :], 0.0)
        numerator = jnp.einsum("hbc,hcv->hbv", weights, value_block, precision=highest)
        denominator = jnp.sum(weights, axis=2)
        query_feats = taylor_features(query_block * 0.5)
        carried = (seg_block == state_seg).astype(jnp.float32)
        numerator = numerator + carried[None, :, None] * jnp.einsum(
            "hbf,hfv->hbv", query_feats, kv_state, precision=highest
        )
        denominator = denominator + carried[None, :] * jnp.einsum(
            "hbf,hf->hb", query_feats, norm_vec, precision=highest
        )
        block_out = (
            keep_block[None, :, None]
            * numerator
            / (denominator + 1.0 - keep_block[None, :])[:, :, None]
        )
        last_seg = seg_block[block_rows - 1]
        adding = (seg_block == last_seg).astype(jnp.float32) * keep_block
        key_feats = taylor_features(key_block * 0.5) * adding[None, :, None]
        same_seg = (state_seg == last_seg).astype(jnp.float32)
        kv_state = same_seg * kv_state + jnp.einsum(
            "hbf,hbv->hfv", key_feats, value_block, precision=highest
        )
        norm_vec = same_seg * norm_vec + jnp.sum(key_feats, axis=1)
        return ((kv_state, norm_vec, last_seg), block_out)

    start_carry = (
        jnp.zeros((head_count, feature_count, value_width), jnp.float32),
        jnp.zeros((head_count, feature_count), jnp.float32),
        jnp.array(-1, jnp.int32),
    )
    final_carry, outputs = lax.scan(
        jax.checkpoint(block_step),
        start_carry,
        (
            split_blocks(queries),
            split_blocks(key_in),
            split_blocks(value_in),
            segment.reshape(blocks, block_rows),
            keep_row.reshape(blocks, block_rows),
        ),
    )
    return outputs.transpose(1, 0, 2, 3).reshape(head_count, total_rows, value_width)


def inv_root_mean(values):
    return lax.rsqrt(jnp.mean(values * values, axis=1, keepdims=True) + epsilon)


def per_device(
    tokens,
    keep_mask,
    seq_lengths,
    attn_gain,
    in_weight,
    out_weight,
    ffn_gain,
    gate_weight,
    up_weight,
    down_weight,
    out_grad,
):
    group = lax.all_gather(tokens, "head", axis=0, tiled=True)
    total_rows = group.shape[0]
    group_wide = group.astype(jnp.float32)
    normed = (group_wide * inv_root_mean(group_wide) * attn_gain).astype(jnp.bfloat16)
    head_width = 2 * FD + VD
    heads_here = in_weight.shape[1] // head_width
    projected = jnp.dot(normed, in_weight, preferred_element_type=jnp.float32).astype(jnp.bfloat16)
    per_head = (
        projected.reshape(total_rows, heads_here, head_width).transpose(1, 0, 2).astype(jnp.float32)
    )
    ends = jnp.cumsum(seq_lengths[0])
    positions = jnp.arange(total_rows, dtype=jnp.int32)
    segment = jnp.sum((positions[:, None] >= ends[None, :]).astype(jnp.int32), axis=1)
    keep_row = keep_mask.astype(jnp.float32)

    def attend(queries, key_in, value_in):
        return blockwise_attention(queries, key_in, value_in, segment, keep_row)

    attended_wide, attend_back = jax.vjp(
        attend, per_head[:, :, :FD], per_head[:, :, FD : 2 * FD], per_head[:, :, 2 * FD :]
    )
    attended = (
        attended_wide.transpose(1, 0, 2).reshape(total_rows, heads_here * VD).astype(jnp.bfloat16)
    )
    tokens_wide = tokens.astype(jnp.float32)
    middle = tokens_wide + lax.psum_scatter(
        jnp.dot(attended, out_weight, preferred_element_type=jnp.float32).astype(jnp.bfloat16),
        "head",
        scatter_dimension=0,
        tiled=True,
    ).astype(jnp.float32)
    inv_two = inv_root_mean(middle)
    normed_two = lax.all_gather(
        (middle * inv_two * ffn_gain).astype(jnp.bfloat16), "head", axis=0, tiled=True
    )
    gate_all, up_all, down_all = (
        lax.all_gather(gate_weight, "dp", axis=0, tiled=True),
        lax.all_gather(up_weight, "dp", axis=0, tiled=True),
        lax.all_gather(down_weight, "dp", axis=1, tiled=True),
    )
    gate_pre = jnp.dot(normed_two, gate_all, preferred_element_type=jnp.float32)
    up_pre = jnp.dot(normed_two, up_all, preferred_element_type=jnp.float32)
    sigmoid_gate = jax.nn.sigmoid(gate_pre)
    silu_gate = gate_pre * sigmoid_gate
    hidden = (silu_gate * up_pre).astype(jnp.bfloat16)
    output = (
        middle
        + lax.psum_scatter(
            jnp.dot(hidden, down_all, preferred_element_type=jnp.float32).astype(jnp.bfloat16),
            "head",
            scatter_dimension=0,
            tiled=True,
        ).astype(jnp.float32)
    ).astype(jnp.bfloat16)
    grad_group = lax.all_gather(out_grad, "head", axis=0, tiled=True)
    d_hidden = jnp.dot(grad_group, down_all.T, preferred_element_type=jnp.float32)
    d_gate = (d_hidden * up_pre * sigmoid_gate * (1.0 + gate_pre * (1.0 - sigmoid_gate))).astype(
        jnp.bfloat16
    )
    d_up = (d_hidden * silu_gate).astype(jnp.bfloat16)
    down_grad = jnp.dot(hidden.T, grad_group, preferred_element_type=jnp.float32)
    gate_grad = jnp.dot(normed_two.T, d_gate, preferred_element_type=jnp.float32)
    up_grad = jnp.dot(normed_two.T, d_up, preferred_element_type=jnp.float32)
    d_normed_two = lax.psum_scatter(
        (
            jnp.dot(d_gate, gate_all.T, preferred_element_type=jnp.float32)
            + jnp.dot(d_up, up_all.T, preferred_element_type=jnp.float32)
        ).astype(jnp.bfloat16),
        "head",
        scatter_dimension=0,
        tiled=True,
    ).astype(jnp.float32)
    scaled_two = middle * inv_two
    error_two = d_normed_two * ffn_gain
    d_middle = out_grad.astype(jnp.float32) + inv_two * (
        error_two - scaled_two * jnp.mean(error_two * scaled_two, axis=1, keepdims=True)
    )
    ffn_gain_part = jnp.sum(d_normed_two * scaled_two, axis=0)
    d_mixed = lax.all_gather(d_middle.astype(jnp.bfloat16), "head", axis=0, tiled=True)
    d_attended = jnp.dot(d_mixed, out_weight.T, preferred_element_type=jnp.float32)
    d_attended = d_attended.reshape(total_rows, heads_here, VD).transpose(1, 0, 2)
    out_weight_grad = jnp.dot(attended.T, d_mixed, preferred_element_type=jnp.float32)
    d_query, d_key, d_value = attend_back(d_attended)
    d_projected = jnp.concatenate([d_query, d_key, d_value], axis=2).transpose(1, 0, 2)
    d_projected = d_projected.reshape(total_rows, heads_here * head_width).astype(jnp.bfloat16)
    in_weight_grad = jnp.dot(normed.T, d_projected, preferred_element_type=jnp.float32)
    d_normed = lax.psum_scatter(
        jnp.dot(d_projected, in_weight.T, preferred_element_type=jnp.float32).astype(jnp.bfloat16),
        "head",
        scatter_dimension=0,
        tiled=True,
    ).astype(jnp.float32)
    inv_one = inv_root_mean(tokens_wide)
    scaled_one = tokens_wide * inv_one
    error_one = d_normed * attn_gain
    in_grad = d_middle + inv_one * (
        error_one - scaled_one * jnp.mean(error_one * scaled_one, axis=1, keepdims=True)
    )
    attn_gain_part = jnp.sum(d_normed * scaled_one, axis=0)
    attn_gain_grad, ffn_gain_grad = lax.psum((attn_gain_part, ffn_gain_part), ("dp", "head"))
    in_weight_grad, out_weight_grad = (
        lax.psum(in_weight_grad.astype(jnp.bfloat16), "dp").astype(jnp.float32),
        lax.psum(out_weight_grad.astype(jnp.bfloat16), "dp").astype(jnp.float32),
    )
    gate_grad, up_grad, down_grad = (
        lax.psum_scatter(
            gate_grad.astype(jnp.bfloat16), "dp", scatter_dimension=0, tiled=True
        ).astype(jnp.float32),
        lax.psum_scatter(
            up_grad.astype(jnp.bfloat16), "dp", scatter_dimension=0, tiled=True
        ).astype(jnp.float32),
        lax.psum_scatter(
            down_grad.astype(jnp.bfloat16), "dp", scatter_dimension=1, tiled=True
        ).astype(jnp.float32),
    )
    return (
        output,
        in_grad,
        attn_gain_grad,
        in_weight_grad,
        out_weight_grad,
        ffn_gain_grad,
        gate_grad,
        up_grad,
        down_grad,
    )


def solution(mesh):
    return jax.shard_map(
        per_device,
        mesh=mesh,
        in_specs=(
            P(("dp", "head"), None),
            P("dp"),
            P("dp", None),
            P(),
            P(None, "head"),
            P("head", None),
            P(),
            P("dp", "head"),
            P("dp", "head"),
            P("head", "dp"),
            P(("dp", "head"), None),
        ),
        out_specs=(
            P(("dp", "head"), None),
            P(("dp", "head"), None),
            P(),
            P(None, "head"),
            P("head", None),
            P(),
            P("dp", "head"),
            P("dp", "head"),
            P("head", "dp"),
        ),
        check_vma=False,
    )
```

profile of v0, /device:TPU:0, one launch (start us, length us, event | category | flops | bytes accessed | tf_op | source)
XLA Modules:
  0.0 1202.2 jit_solution(16503500288799568464)
XLA Ops:
  10.5 84.7 %all-gather.8.cloned.1.call-done = bf16[2048,2048]{1,0:T(8,128)(2,1)} async-done(((bf16[256,2048]{1,0:T(8,128)(2,1)}), bf16[2048,2048]{1,0:T(8,128)(2,1)}) %all-gather.8.cloned.1.call-update) | async-done | bytes 8388624 | tf_op jit(solution)/shard_map/all_gather | solution.py:111
  123.6 73.3 %while.49 = (s32[]{:T(128)}, f32[2,273,128]{2,1,0:T(8,128)}, f32[2,273]{1,0:T(2,128)S(1)}, s32[]{:T(128)}, bf16[4,2,512,128]{3,2,0,1:T(8,128)(2,1)}, /*index=5*/...) while((s32[]{:T(128)}, f32[2,273,128]{2,1,0:T(8,128)}, ...), condition=%wide.region_6.7_spmd.clone, body=%wide.region_3.6_spmd.clone.sunk | while | flops 1778126592 | bytes 26551704 | solution.py:80
  207.9 87.6 %reduce-scatter.8.cloned.1.call-done = bf16[256,2048]{1,0:T(8,128)(2,1)} async-done(((bf16[2048,2048]{1,0:T(8,128)(2,1)}), bf16[256,2048]{1,0:T(8,128)(2,1)}) %reduce-scatter.8.cloned.1.call-update) | async-done | bytes 1048592 | tf_op jit(solution)/shard_map/reduce_scatter | solution.py:136
  301.0 78.2 %all-gather.10.cloned.1.call-done = bf16[2048,2048]{1,0:T(8,128)(2,1)} async-done(((bf16[256,2048]{1,0:T(8,128)(2,1)}), bf16[2048,2048]{1,0:T(8,128)(2,1)}) %all-gather.10.cloned.1.call-update) | async-done | bytes 8388624 | tf_op jit(solution)/shard_map/all_gather | solution.py:143
  379.2 11.0 fusion.105
  390.2 30.8 %all-gather.12.cloned.1.call-done = bf16[2048,704]{0,1:T(8,128)(2,1)} async-done(((bf16[512,704]{0,1:T(8,128)(2,1)}), bf16[2048,704]{0,1:T(8,128)(2,1)}) %all-gather.12.cloned.1.call-update) | async-done | bytes 2883600 | tf_op jit(solution)/shard_map/all_gather | solution.py:147
  420.9 11.0 fusion.104
  431.9 32.3 %all-gather.16.cloned.1.call-done = bf16[704,2048]{1,0:T(8,128)(2,1)} async-done(((bf16[704,512]{1,0:T(8,128)(2,1)}), bf16[704,2048]{1,0:T(8,128)(2,1)}) %all-gather.16.cloned.1.call-update) | async-done | bytes 2883600 | tf_op jit(solution)/shard_map/all_gather | solution.py:149
  464.3 83.6 %all-gather.18.cloned.1.call-done = bf16[2048,2048]{1,0:T(8,128)(2,1)} async-done(((bf16[256,2048]{1,0:T(8,128)(2,1)}), bf16[2048,2048]{1,0:T(8,128)(2,1)}) %all-gather.18.cloned.1.call-update) | async-done | bytes 8388624 | tf_op jit(solution)/shard_map/all_gather | solution.py:165
  547.8 15.3 %multiply_convert_fusion = (bf16[2048,704]{0,1:T(8,128)(2,1)S(1)}, bf16[2048,704]{0,1:T(8,128)(2,1)S(1)}, bf16[2048,704]{0,1:T(8,128)(2,1)}) fusion(f32[2048,704]{0,1:T(8,128)} %fusion.104, f32[2048,704]{0,1:T(8,128)} %fusion.105, bf16[2048,2048]{1,0:T(8,128)(2,1)} %all-gather.18.cloned.1.call-done, bf16[704,2048]{1,0:T(8,128)(2,1)} %all-gather.16.cloned.1.call-done), kind=kOutput, calls=%fused_computation.146 | convolution fusion | flops 5927206912 | bytes 31457280 | tf_op jit(solution)/shard_map/dot_general | solution.py:166
  563.2 10.5 fusion.106
  573.7 12.5 %add_convert_fusion = bf16[2048,2048]{1,0:T(8,128)(2,1)} fusion(f32[2048,2048]{1,0:T(8,128)} %fusion.106, bf16[2048,704]{0,1:T(8,128)(2,1)S(1)} %get-tuple-element.814, bf16[2048,704]{0,1:T(8,128)(2,1)S(1)} %copy-done.34), kind=kOutput, calls=%fused_computation.142 | convolution fusion | flops 5913968640 | bytes 30932992 | tf_op jit(solution)/shard_map/dot_general | solution.py:177
  586.3 88.3 %reduce-scatter.12.cloned.1.call-done = bf16[256,2048]{1,0:T(8,128)(2,1)} async-done(((bf16[2048,2048]{1,0:T(8,128)(2,1)}), bf16[256,2048]{1,0:T(8,128)(2,1)}) %reduce-scatter.12.cloned.1.call-update) | async-done | bytes 1048592 | tf_op jit(solution)/shard_map/reduce_scatter | solution.py:174
  679.8 10.6 convolution_convert_fusion.5
  690.4 11.1 convolution_convert_fusion.3
  701.6 10.6 convolution_convert_fusion.4
  712.3 47.8 %all-gather.20.cloned.1.call-done = bf16[2048,2048]{1,0:T(8,128)(2,1)} async-done(((bf16[256,2048]{1,0:T(8,128)(2,1)}), bf16[2048,2048]{1,0:T(8,128)(2,1)}) %all-gather.20.cloned.1.call-update) | async-done | bytes 8388624 | tf_op jit(solution)/shard_map/all_gather | solution.py:189
  772.2 138.0 %while.50 = (s32[]{:T(128)}, f32[2,273,128]{2,1,0:T(8,128)S(1)}, f32[2,273]{1,0:T(2,128)S(1)}, bf16[4,2,512,16]{2,3,1,0:T(8,128)(2,1)}, bf16[4,2,512,16]{2,3,1,0...) while((s32[]{:T(128)}, f32[2,273,128]{2,1,0:T(8,128)S(1)}, ...), condition=%wide.region_20.21_spmd.clone, body=%wide.region_13.20_spmd.clone.sunk | while | flops 4900599296 | bytes 60184812 | solution.py:80
  926.7 7.5 convolution_convert_fusion.6
  941.2 11.4 convolution_convert_fusion.1
  960.0 46.4 %all-reduce.4.cloned.1.call-done = (bf16[2048,320]{0,1:T(8,128)(2,1)}, bf16[256,2048]{1,0:T(8,128)(2,1)}) async-done(((bf16[2048,320]{0,1:T(8,128)(2,1)}, bf16[256,2048]{1,0:T(8,128)(2,1)}), (bf16[2048,320]{0,1:T(8,128)(2,1)}, bf16[256,2048]{1,0:T(8,128)(2,1)})) %all-reduce.4.cloned.1.call-update) | async-done | bytes 2359312 | tf_op jit(solution)/shard_map/psum | solution.py:212
  1011.1 86.9 %reduce-scatter.14.cloned.1.call-done = bf16[256,2048]{1,0:T(8,128)(2,1)} async-done(((bf16[2048,2048]{1,0:T(8,128)(2,1)}), bf16[256,2048]{1,0:T(8,128)(2,1)}) %reduce-scatter.14.cloned.1.call-update) | async-done | bytes 1048592 | tf_op jit(solution)/shard_map/reduce_scatter | solution.py:197
  1100.1 39.6 %all-reduce = (f32[2048]{0:T(1024)}, f32[2048]{0:T(1024)}) all-reduce(f32[2048]{0:T(1024)S(1)} %get-tuple-element.734, f32[2048]{0:T(1024)S(1)} %copy-done.24), channel_id=1, replica_groups=mesh['dp'=4,'head'=8] {'dp','head'}, use_global_device_ids=true, to_apply=%region_24.25 | all-reduce | flops 4096 | bytes 32768 | tf_op jit(solution)/shard_map/psum | solution.py:210
  1139.7 49.6 %reduce-scatter.10.cloned.1.call-done = bf16[256,2048]{1,0:T(8,128)(2,1)} async-done(((bf16[2048,2048]{1,0:T(8,128)(2,1)}), bf16[256,2048]{1,0:T(8,128)(2,1)}) %reduce-scatter.10.cloned.1.call-update) | async-done | bytes 1048592 | tf_op jit(solution)/shard_map/reduce_scatter | solution.py:158
  (460 shorter events, 306.3 us)
Async XLA Ops:
  8.0 92.5 %copy-start = (bf16[2048,320]{0,1:T(8,128)(2,1)S(1)}, bf16[2048,320]{0,1:T(8,128)(2,1)}, u32[]{:S(2)}) copy-start(bf16[2048,320]{0,1:T(8,128)(2,1)} %param.19) | copy-start | bytes 3932164
  8.0 87.2 %all-gather.8.cloned.1.call-start = ((), (), s32[]{:S(2)}) async-start(), calls=%async_computation.7 | async-start | bytes 9437184 | tf_op jit(solution)/shard_map/all_gather | solution.py:111
  8.8 286.8 %reduce-scatter.8.cloned.1.call-start = ((), (), s32[]{:S(2)}) async-start(), calls=%async_computation.8 | async-start | bytes 9437184 | tf_op jit(solution)/shard_map/reduce_scatter | solution.py:136
  10.5 90.0 %copy-start.25 = (f32[2048]{0:T(1024)S(1)}, f32[2048]{0:T(1024)}, u32[]{:S(2)}) copy-start(f32[2048]{0:T(1024)} %param.18) | copy-start | bytes 24580
  207.2 90.0 %copy-start.22 = (f32[2048]{0:T(1024)S(1)}, f32[2048]{0:T(1024)}, u32[]{:S(2)}) copy-start(f32[2048]{0:T(1024)} %param.21) | copy-start | bytes 24580
  207.3 93.7 %all-gather.14.cloned.1.call-start = ((), (), s32[]{:S(2)}) async-start(), calls=%async_computation.11 | async-start | bytes 3604480 | tf_op jit(solution)/shard_map/all_gather | solution.py:148
  207.8 171.3 %all-gather.10.cloned.1.call-start = ((), (), s32[]{:S(2)}) async-start(), calls=%async_computation.9 | async-start | bytes 9437184 | tf_op jit(solution)/shard_map/all_gather | solution.py:143
  297.3 380.4 %copy-start.27 = (f32[256]{0:T(256)}, f32[256]{0:T(256)S(1)}, u32[]{:S(2)}) copy-start(f32[256]{0:T(256)S(1)} %add_rsqrt_fusion.2) | copy-start | bytes 3076
  298.8 122.1 %all-gather.12.cloned.1.call-start = ((), (), s32[]{:S(2)}) async-start(), calls=%async_computation.10 | async-start | bytes 3604480 | tf_op jit(solution)/shard_map/all_gather | solution.py:147
  299.4 164.9 %all-gather.16.cloned.1.call-start = ((), (), s32[]{:S(2)}) async-start(), calls=%async_computation.12 | async-start | bytes 3604480 | tf_op jit(solution)/shard_map/all_gather | solution.py:149
  300.1 247.7 %all-gather.18.cloned.1.call-start = ((), (), s32[]{:S(2)}) async-start(), calls=%async_computation.14 | async-start | bytes 9437184 | tf_op jit(solution)/shard_map/all_gather | solution.py:165
  300.9 373.7 %reduce-scatter.12.cloned.1.call-start = ((), (), s32[]{:S(2)}) async-start(), calls=%async_computation.15 | async-start | bytes 9437184 | tf_op jit(solution)/shard_map/reduce_scatter | solution.py:174
  586.3 173.8 %all-gather.20.cloned.1.call-start = ((), (), s32[]{:S(2)}) async-start(), calls=%async_computation.16 | async-start | bytes 9437184 | tf_op jit(solution)/shard_map/all_gather | solution.py:189
  679.7 273.0 %reduce-scatter.20.cloned.1.call-start = ((), (), s32[]{:S(2)}) async-start(), calls=%async_computation.20 | async-start | bytes 3604480 | tf_op jit(solution)/shard_map/reduce_scatter | solution.py:222
  690.4 264.8 %reduce-scatter.18.cloned.1.call-start = ((), (), s32[]{:S(2)}) async-start(), calls=%async_computation.19 | async-start | bytes 3604480 | tf_op jit(solution)/shard_map/reduce_scatter | solution.py:219
  701.5 256.0 %reduce-scatter.16.cloned.1.call-start = ((), (), s32[]{:S(2)}) async-start(), calls=%async_computation.18 | async-start | bytes 3604480 | tf_op jit(solution)/shard_map/reduce_scatter | solution.py:216
  712.3 294.0 %all-reduce.4.cloned.1.call-start = ((), (), s32[]{:S(2)}) async-start(), calls=%async_computation.21 | async-start | bytes 4718592 | tf_op jit(solution)/shard_map/psum | solution.py:212
  934.2 163.8 %reduce-scatter.14.cloned.1.call-start = ((), (), s32[]{:S(2)}) async-start(), calls=%async_computation.17 | async-start | bytes 9437184 | tf_op jit(solution)/shard_map/reduce_scatter | solution.py:197
  941.2 248.2 %reduce-scatter.10.cloned.1.call-start = ((), (), s32[]{:S(2)}) async-start(), calls=%async_computation.13 | async-start | bytes 9437184 | tf_op jit(solution)/shard_map/reduce_scatter | solution.py:158
  1009.5 90.6 %copy-start.24 = (f32[2048]{0:T(1024)S(1)}, f32[2048]{0:T(1024)}, u32[]{:S(2)}) copy-start(f32[2048]{0:T(1024)} %get-tuple-element.732) | copy-start | bytes 24580
  1009.5 179.8 %copy-start.7 = (bf16[256,2048]{1,0:T(8,128)(2,1)S(1)}, bf16[256,2048]{1,0:T(8,128)(2,1)}, u32[]{:S(2)}) copy-start(bf16[256,2048]{1,0:T(8,128)(2,1)} %reduce-scatter.8.cloned.1.call-done) | copy-start | bytes 3145732
  1009.5 179.8 %copy-start.23 = (f32[2048]{0:T(1024)S(1)}, f32[2048]{0:T(1024)}, u32[]{:S(2)}) copy-start(f32[2048]{0:T(1024)} %param.21) | copy-start | bytes 24580
  1009.5 179.8 %copy-start.28 = (f32[256]{0:T(256)S(1)}, f32[256]{0:T(256)}, u32[]{:S(2)}) copy-start(f32[256]{0:T(256)} %copy-done.27) | copy-start | bytes 3076
  1009.6 179.8 %copy-start.30 = (f32[256]{0:T(256)S(1)}, f32[256]{0:T(256)}, u32[]{:S(2)}) copy-start(f32[256]{0:T(256)} %copy-done.29) | copy-start | bytes 3076
  (56 other events, 398.1 us)
Sparse Core Ops, SparseCore 0:
  10.5 84.7 all-gather.7
  207.4 88.1 reduce-scatter.7
  586.4 88.1 reduce-scatter.11
Sparse Core Ops, SparseCore 1:
  209.6 40.0 all-gather.13
  298.9 80.2 all-gather.9
  380.9 40.0 all-gather.11
  422.8 41.5 all-gather.15
  465.9 81.9 all-gather.17
  679.8 80.2 all-gather.19
  763.0 40.1 reduce-scatter.19
  806.1 41.6 reduce-scatter.17
  850.7 41.6 reduce-scatter.15
  934.3 71.9 all-reduce.3
  1008.6 89.4 reduce-scatter.13
  1100.4 88.9 reduce-scatter.9
where the time goes:
time: 1210 us; the launch traced here: 1200 us
  waiting for transfers between devices  719 us (59%)
  matrix products  285 us (24%)
  local copies, waits for them, and re-layouts  65.2 us (5%)
  other arithmetic  63.3 us (5%)
  blocking collectives  39.6 us (3%)
  between operations  15.9 us (1%)
  loops' own time  12.7 us (1%)
    reduce_scatter x1, waiting for transfers between devices, per_device(): lax.psum_scatter((jnp.dot(d_gate, gate_all.T, preferred_element_type=jnp....  88.3 us
    reduce_scatter x1, waiting for transfers between devices, per_device(): lax.psum_scatter(jnp.dot(attended, out_weight, preferred_element_type=jnp...  87.6 us
    reduce_scatter x1, waiting for transfers between devices, per_device(): lax.psum_scatter(jnp.dot(d_projected, in_weight.T, preferred_element_type...  86.9 us
    all_gather x1, waiting for transfers between devices, per_device(): group = lax.all_gather(tokens, 'head', axis=0, tiled=True)  84.7 us
    all_gather x1, waiting for transfers between devices, per_device(): grad_group = lax.all_gather(out_grad, 'head', axis=0, tiled=True)  83.6 us
    all_gather x1, waiting for transfers between devices, per_device(): lax.all_gather((middle * inv_two * ffn_gain).astype(jnp.bfloat16), 'head'...  78.2 us
    reduce_scatter x1, waiting for transfers between devices, per_device(): lax.psum_scatter(jnp.dot(hidden, down_all, preferred_element_type=jnp.flo...  49.6 us
    all_gather x1, waiting for transfers between devices, per_device(): lax.all_gather(d_middle.astype(jnp.bfloat16), 'head', axis=0, tiled=True)  47.8 us
  transfers between devices with their start and end apart: 15, of which 11 were waited for; matrix products, arithmetic and copies ran while one was open for 21% of the time, Pallas kernels for 0%

commit v1 on v0

v1 whole, which is shorter than its diff:
```python
import functools
import jax
import jax.numpy as jnp
from jax import lax
from jax.experimental import pallas as pl
from jax.experimental.pallas import tpu as pltpu
from jax.sharding import PartitionSpec as P

FD = 16
VD = 128
LANES = 128
epsilon = 1e-05
NT = (((1,), (1,)), ((), ()))
TN = (((0,), (0,)), ((), ()))


def head_lanes(block, rows, head, offset):
    lane = lax.broadcasted_iota(jnp.int32, (rows, LANES), 1)
    low = offset + head * FD
    return jnp.where((lane >= low) & (lane < low + FD), block, 0.0)


def segment_start(ends_ref, positions):
    start = jnp.zeros_like(positions)
    for slot in range(ends_ref.shape[0]):
        end = ends_ref[slot]
        start = jnp.where(positions >= end, jnp.maximum(start, end), start)
    return start


def attend_kernel(heads, rows, ends_ref, projected_ref, keep_ref, y_ref, inv_ref, att_ref, key_s, value_s):
    step = pl.program_id(0)
    own = pl.ds(step * rows, rows)
    keep = keep_ref[own, :]
    packed = projected_ref[own, heads * VD :].astype(jnp.float32)
    key_s[own, :] = pltpu.roll(packed, LANES - heads * FD, 1).astype(jnp.bfloat16)
    lane = lax.broadcasted_iota(jnp.int32, (rows, LANES), 1)
    ones = jnp.where(lane < 2, keep, 0.0).astype(jnp.bfloat16)
    for head in range(heads):
        value_s[head, own, :VD] = (
            projected_ref[own, head * VD : (head + 1) * VD].astype(jnp.float32) * keep
        ).astype(jnp.bfloat16)
        value_s[head, own, VD:] = ones
    queries = [(head_lanes(packed, rows, head, 0) * 0.25).astype(jnp.bfloat16) for head in range(heads)]
    row = step * rows + lax.broadcasted_iota(jnp.int32, (rows, 1), 0)
    start = segment_start(ends_ref, row)
    column = lax.broadcasted_iota(jnp.int32, (rows, rows), 1)

    def tile(block, totals, diagonal):
        at = pl.ds(pl.multiple_of(block * rows, rows), rows)
        allowed = column >= start - block * rows
        if diagonal:
            allowed &= column <= lax.broadcasted_iota(jnp.int32, (rows, rows), 0)
        keys = key_s[at, :]
        added = []
        for head in range(heads):
            inner = lax.dot_general(queries[head], keys, NT, preferred_element_type=jnp.float32)
            weights = jnp.where(allowed, (inner * 0.5 + 1.0) * inner + 1.0, 0.0).astype(jnp.bfloat16)
            added.append(
                totals[head]
                + jnp.dot(weights, value_s[head, at, :], preferred_element_type=jnp.float32)
            )
        return tuple(added)

    totals = tuple(jnp.zeros((rows, 2 * VD), jnp.float32) for _ in range(heads))
    totals = lax.fori_loop(0, step, lambda block, held: tile(block, held, False), totals)
    totals = tile(step, totals, True)
    inverses = jnp.zeros((rows, LANES), jnp.float32)
    for head in range(heads):
        inverse = 1.0 / (totals[head][:, VD : VD + 1] + 1.0 - keep)
        y = totals[head][:, :VD] * (keep * inverse)
        y_ref[:, head * VD : (head + 1) * VD] = y
        att_ref[:, head * VD : (head + 1) * VD] = y.astype(jnp.bfloat16)
        inverses = jnp.where(lane == head, inverse, inverses)
    inv_ref[...] = inverses


def attend(projected, keep, ends, heads):
    total = projected.shape[0]
    rows = min(512, total)
    width = projected.shape[1]
    pairs = total * (total + rows) // 2 * heads
    return pl.pallas_call(
        functools.partial(attend_kernel, heads, rows),
        grid_spec=pltpu.PrefetchScalarGridSpec(
            num_scalar_prefetch=1,
            grid=(total // rows,),
            in_specs=[
                pl.BlockSpec((total, width), lambda i, e: (0, 0)),
                pl.BlockSpec((total, 1), lambda i, e: (0, 0)),
            ],
            out_specs=[
                pl.BlockSpec((rows, heads * VD), lambda i, e: (i, 0)),
                pl.BlockSpec((rows, LANES), lambda i, e: (i, 0)),
                pl.BlockSpec((rows, heads * VD), lambda i, e: (i, 0)),
            ],
            scratch_shapes=[
                pltpu.VMEM((total, LANES), jnp.bfloat16),
                pltpu.VMEM((heads, total, 2 * VD), jnp.bfloat16),
            ],
        ),
        out_shape=[
            jax.ShapeDtypeStruct((total, heads * VD), jnp.float32),
            jax.ShapeDtypeStruct((total, LANES), jnp.float32),
            jax.ShapeDtypeStruct((total, heads * VD), jnp.bfloat16),
        ],
        compiler_params=pltpu.CompilerParams(
            dimension_semantics=("arbitrary",), vmem_limit_bytes=48 * 1024 * 1024
        ),
        cost_estimate=pl.CostEstimate(flops=pairs * 1024, bytes_accessed=8 << 20, transcendentals=0),
    )(ends, projected, keep)


def attend_back_kernel(
    heads, rows, ends_ref, projected_ref, keep_ref, y_ref, inv_ref, grad_ref, out_ref,
    key_s, query_s, value_s, error_s, dquery_s,
):
    step = pl.program_id(0)
    blocks = pl.num_programs(0)
    lane = lax.broadcasted_iota(jnp.int32, (rows, LANES), 1)

    @pl.when(step == 0)
    def _():
        dquery_s[...] = jnp.zeros_like(dquery_s)

        def fill(block, nothing):
            at = pl.ds(pl.multiple_of(block * rows, rows), rows)
            keep = keep_ref[at, :]
            packed = projected_ref[at, heads * VD :].astype(jnp.float32)
            rolled = pltpu.roll(packed, LANES - heads * FD, 1)
            ones = jnp.where(lane < 2, keep, 0.0).astype(jnp.bfloat16)
            inverses = inv_ref[at, :]
            for head in range(heads):
                columns = slice(head * VD, (head + 1) * VD)
                key_s[head, at, :] = head_lanes(rolled, rows, head, 0).astype(jnp.bfloat16)
                query_s[head, at, :] = (head_lanes(packed, rows, head, 0) * 0.25).astype(jnp.bfloat16)
                value_s[head, at, :VD] = (projected_ref[at, columns].astype(jnp.float32) * keep).astype(jnp.bfloat16)
                value_s[head, at, VD:] = ones
                inverse = inverses[:, head : head + 1]
                grad = grad_ref[at, columns].astype(jnp.float32)
                error_s[head, at, :VD] = (grad * (keep * inverse)).astype(jnp.bfloat16)
                offset = -jnp.sum(grad * y_ref[at, columns], axis=1, keepdims=True) * inverse
                high = offset.astype(jnp.bfloat16).astype(jnp.float32)
                error_s[head, at, VD:] = jnp.where(
                    lane == 0, high, jnp.where(lane == 1, offset - high, 0.0)
                ).astype(jnp.bfloat16)
            return nothing

        lax.fori_loop(0, blocks, fill, 0)

    own = pl.ds(pl.multiple_of(step * rows, rows), rows)
    row = lax.broadcasted_iota(jnp.int32, (rows, rows), 0)

    def tile(block, totals, diagonal):
        at = pl.ds(pl.multiple_of(block * rows, rows), rows)
        column = block * rows + lax.broadcasted_iota(jnp.int32, (1, rows), 1)
        allowed = row >= segment_start(ends_ref, column) - step * rows
        if diagonal:
            allowed &= row <= lax.broadcasted_iota(jnp.int32, (rows, rows), 1)
        dkey, dvalues = totals
        added = []
        for head in range(heads):
            query = query_s[head, at, :]
            error = error_s[head, at, :]
            keys = key_s[head, own, :]
            inner = lax.dot_general(keys, query, NT, preferred_element_type=jnp.float32)
            dweight = lax.dot_general(value_s[head, own, :], error, NT, preferred_element_type=jnp.float32)
            slope = inner + 1.0
            weights = jnp.where(allowed, (slope * slope + 1.0) * 0.5, 0.0).astype(jnp.bfloat16)
            dinner = jnp.where(allowed, slope * dweight, 0.0).astype(jnp.bfloat16)
            added.append(
                dvalues[head] + jnp.dot(weights, error[:, :VD], preferred_element_type=jnp.float32)
            )
            dkey = dkey + jnp.dot(dinner, query, preferred_element_type=jnp.float32)
            dquery_s[at, :] += lax.dot_general(dinner, keys, TN, preferred_element_type=jnp.float32)
        return dkey, tuple(added)

    totals = (
        jnp.zeros((rows, LANES), jnp.float32),
        tuple(jnp.zeros((rows, VD), jnp.float32) for _ in range(heads)),
    )
    totals = tile(step, totals, True)
    dkey, dvalues = lax.fori_loop(step + 1, blocks, lambda block, held: tile(block, held, False), totals)
    keep = keep_ref[own, :]
    for head in range(heads):
        out_ref[:, head * VD : (head + 1) * VD] = (dvalues[head] * keep).astype(jnp.bfloat16)
    out_ref[:, heads * VD :] = (
        dquery_s[own, :] * 0.25 + pltpu.roll(dkey, heads * FD, 1)
    ).astype(jnp.bfloat16)


def attend_back(projected, keep, ends, y, inverses, grad, heads):
    total = projected.shape[0]
    rows = min(512, total)
    width = projected.shape[1]
    pairs = total * (total + rows) // 2 * heads
    whole = lambda columns: pl.BlockSpec((total, columns), lambda i, e: (0, 0))
    return pl.pallas_call(
        functools.partial(attend_back_kernel, heads, rows),
        grid_spec=pltpu.PrefetchScalarGridSpec(
            num_scalar_prefetch=1,
            grid=(total // rows,),
            in_specs=[whole(width), whole(1), whole(heads * VD), whole(LANES), whole(heads * VD)],
            out_specs=pl.BlockSpec((rows, width), lambda i, e: (i, 0)),
            scratch_shapes=[
                pltpu.VMEM((heads, total, LANES), jnp.bfloat16),
                pltpu.VMEM((heads, total, LANES), jnp.bfloat16),
                pltpu.VMEM((heads, total, 2 * VD), jnp.bfloat16),
                pltpu.VMEM((heads, total, 2 * VD), jnp.bfloat16),
                pltpu.VMEM((total, LANES), jnp.float32),
            ],
        ),
        out_shape=jax.ShapeDtypeStruct((total, width), jnp.bfloat16),
        compiler_params=pltpu.CompilerParams(
            dimension_semantics=("arbitrary",), vmem_limit_bytes=56 * 1024 * 1024
        ),
        cost_estimate=pl.CostEstimate(flops=pairs * 2560, bytes_accessed=12 << 20, transcendentals=0),
    )(ends, projected, keep, y, inverses, grad)


def pack_columns(weight, heads):
    depth = weight.shape[0]
    per_head = weight.reshape(depth, heads, 2 * FD + VD)
    return jnp.concatenate(
        [
            per_head[:, :, 2 * FD :].reshape(depth, heads * VD),
            per_head[:, :, :FD].reshape(depth, heads * FD),
            per_head[:, :, FD : 2 * FD].reshape(depth, heads * FD),
            jnp.zeros((depth, LANES - 2 * heads * FD), weight.dtype),
        ],
        axis=1,
    )


def unpack_columns(packed, heads):
    depth = packed.shape[0]
    wide, narrow = heads * VD, heads * FD
    return jnp.concatenate(
        [
            packed[:, wide : wide + narrow].reshape(depth, heads, FD),
            packed[:, wide + narrow : wide + 2 * narrow].reshape(depth, heads, FD),
            packed[:, :wide].reshape(depth, heads, VD),
        ],
        axis=2,
    ).reshape(depth, heads * (2 * FD + VD))


def inv_root_mean(values):
    return lax.rsqrt(jnp.mean(values * values, axis=1, keepdims=True) + epsilon)


def per_device(
    tokens,
    keep_mask,
    seq_lengths,
    attn_gain,
    in_weight,
    out_weight,
    ffn_gain,
    gate_weight,
    up_weight,
    down_weight,
    out_grad,
):
    group = lax.all_gather(tokens, "head", axis=0, tiled=True)
    group_wide = group.astype(jnp.float32)
    normed = (group_wide * inv_root_mean(group_wide) * attn_gain).astype(jnp.bfloat16)
    heads_here = in_weight.shape[1] // (2 * FD + VD)
    in_packed = pack_columns(in_weight, heads_here)
    projected = jnp.dot(normed, in_packed, preferred_element_type=jnp.float32).astype(jnp.bfloat16)
    ends = jnp.cumsum(seq_lengths[0])
    keep_column = keep_mask.astype(jnp.float32)[:, None]
    attended_wide, inverses, attended = attend(projected, keep_column, ends, heads_here)
    tokens_wide = tokens.astype(jnp.float32)
    middle = tokens_wide + lax.psum_scatter(
        jnp.dot(attended, out_weight, preferred_element_type=jnp.float32).astype(jnp.bfloat16),
        "head",
        scatter_dimension=0,
        tiled=True,
    ).astype(jnp.float32)
    inv_two = inv_root_mean(middle)
    normed_two = lax.all_gather(
        (middle * inv_two * ffn_gain).astype(jnp.bfloat16), "head", axis=0, tiled=True
    )
    gate_all, up_all, down_all = (
        lax.all_gather(gate_weight, "dp", axis=0, tiled=True),
        lax.all_gather(up_weight, "dp", axis=0, tiled=True),
        lax.all_gather(down_weight, "dp", axis=1, tiled=True),
    )
    gate_pre = jnp.dot(normed_two, gate_all, preferred_element_type=jnp.float32)
    up_pre = jnp.dot(normed_two, up_all, preferred_element_type=jnp.float32)
    sigmoid_gate = jax.nn.sigmoid(gate_pre)
    silu_gate = gate_pre * sigmoid_gate
    hidden = (silu_gate * up_pre).astype(jnp.bfloat16)
    output = (
        middle
        + lax.psum_scatter(
            jnp.dot(hidden, down_all, preferred_element_type=jnp.float32).astype(jnp.bfloat16),
            "head",
            scatter_dimension=0,
            tiled=True,
        ).astype(jnp.float32)
    ).astype(jnp.bfloat16)
    grad_group = lax.all_gather(out_grad, "head", axis=0, tiled=True)
    d_hidden = jnp.dot(grad_group, down_all.T, preferred_element_type=jnp.float32)
    d_gate = (d_hidden * up_pre * sigmoid_gate * (1.0 + gate_pre * (1.0 - sigmoid_gate))).astype(
        jnp.bfloat16
    )
    d_up = (d_hidden * silu_gate).astype(jnp.bfloat16)
    down_grad = jnp.dot(hidden.T, grad_group, preferred_element_type=jnp.float32)
    gate_grad = jnp.dot(normed_two.T, d_gate, preferred_element_type=jnp.float32)
    up_grad = jnp.dot(normed_two.T, d_up, preferred_element_type=jnp.float32)
    d_normed_two = lax.psum_scatter(
        (
            jnp.dot(d_gate, gate_all.T, preferred_element_type=jnp.float32)
            + jnp.dot(d_up, up_all.T, preferred_element_type=jnp.float32)
        ).astype(jnp.bfloat16),
        "head",
        scatter_dimension=0,
        tiled=True,
    ).astype(jnp.float32)
    scaled_two = middle * inv_two
    error_two = d_normed_two * ffn_gain
    d_middle = out_grad.astype(jnp.float32) + inv_two * (
        error_two - scaled_two * jnp.mean(error_two * scaled_two, axis=1, keepdims=True)
    )
    ffn_gain_part = jnp.sum(d_normed_two * scaled_two, axis=0)
    d_mixed = lax.all_gather(d_middle.astype(jnp.bfloat16), "head", axis=0, tiled=True)
    d_attended = jnp.dot(d_mixed, out_weight.T, preferred_element_type=jnp.float32)
    out_weight_grad = jnp.dot(attended.T, d_mixed, preferred_element_type=jnp.float32)
    d_projected = attend_back(
        projected, keep_column, ends, attended_wide, inverses, d_attended, heads_here
    )
    in_weight_grad = jnp.dot(normed.T, d_projected, preferred_element_type=jnp.float32)
    d_normed = lax.psum_scatter(
        jnp.dot(d_projected, in_packed.T, preferred_element_type=jnp.float32).astype(jnp.bfloat16),
        "head",
        scatter_dimension=0,
        tiled=True,
    ).astype(jnp.float32)
    inv_one = inv_root_mean(tokens_wide)
    scaled_one = tokens_wide * inv_one
    error_one = d_normed * attn_gain
    in_grad = d_middle + inv_one * (
        error_one - scaled_one * jnp.mean(error_one * scaled_one, axis=1, keepdims=True)
    )
    attn_gain_part = jnp.sum(d_normed * scaled_one, axis=0)
    attn_gain_grad, ffn_gain_grad = lax.psum((attn_gain_part, ffn_gain_part), ("dp", "head"))
    in_weight_grad, out_weight_grad = (
        unpack_columns(
            lax.psum(in_weight_grad[:, : in_weight.shape[1]].astype(jnp.bfloat16), "dp"), heads_here
        ).astype(jnp.float32),
        lax.psum(out_weight_grad.astype(jnp.bfloat16), "dp").astype(jnp.float32),
    )
    gate_grad, up_grad, down_grad = (
        lax.psum_scatter(
            gate_grad.astype(jnp.bfloat16), "dp", scatter_dimension=0, tiled=True
        ).astype(jnp.float32),
        lax.psum_scatter(
            up_grad.astype(jnp.bfloat16), "dp", scatter_dimension=0, tiled=True
        ).astype(jnp.float32),
        lax.psum_scatter(
            down_grad.astype(jnp.bfloat16), "dp", scatter_dimension=1, tiled=True
        ).astype(jnp.float32),
    )
    return (
        output,
        in_grad,
        attn_gain_grad,
        in_weight_grad,
        out_weight_grad,
        ffn_gain_grad,
        gate_grad,
        up_grad,
        down_grad,
    )


def solution(mesh):
    return jax.shard_map(
        per_device,
        mesh=mesh,
        in_specs=(
            P(("dp", "head"), None),
            P("dp"),
            P("dp", None),
            P(),
            P(None, "head"),
            P("head", None),
            P(),
            P("dp", "head"),
            P("dp", "head"),
            P("head", "dp"),
            P(("dp", "head"), None),
        ),
        out_specs=(
            P(("dp", "head"), None),
            P(("dp", "head"), None),
            P(),
            P(None, "head"),
            P("head", None),
            P(),
            P("dp", "head"),
            P("dp", "head"),
            P("head", "dp"),
        ),
        check_vma=False,
    )
```

time: 1210 us -> 1100 us (0.909)
  matrix products: 285 us -> 143 us
  waiting for transfers between devices: 719 us -> 799 us
  local copies, waits for them, and re-layouts: 65.2 us -> 10.6 us
  Pallas kernels: 0 us -> 42.4 us
  other arithmetic: 63.3 us -> 34.4 us
  loops' own time: 12.7 us -> 0 us
    dot_general x74 -> x2, matrix products: 152 us -> 15.5 us  [the longest x1 9.59 us: per_device(): jnp.dot(d_projected, in_packed.T, preferred_element_type=jnp.float32)]
    pallas_call x0 -> x2, Pallas kernels: none -> 42.4 us  [the longest x1 29.8 us: attend_back(): pl.pallas_call(functools.partial(attend_back_kernel, heads, rows), grid_s...]
    reduce_scatter x1, waiting for transfers between devices: 0.01 us -> 42.2 us  [per_device(): lax.psum_scatter(gate_grad.astype(jnp.bfloat16), 'dp', scatter_dimension=...]
    psum x1, waiting for transfers between devices: 46.4 us -> 75.3 us  [per_device(): lax.psum(in_weight_grad[:, :in_weight.shape[1]].astype(jnp.bfloat16), 'dp')]
    reduce_scatter x1, waiting for transfers between devices: 0.01 us -> 13.8 us  [per_device(): lax.psum_scatter(up_grad.astype(jnp.bfloat16), 'dp', scatter_dimension=0,...]
    another operation x2 -> x0, loops' own time: 12.7 us -> none  [blockwise_attention(): lax.scan(jax.checkpoint(block_step), start_carry, (split_blocks(queries),...]
    reshape x7 -> x0, local copies, waits for them, and re-layouts: 12.6 us -> none  [the longest x4 9.28 us: split_blocks(): stacked.reshape(head_count, blocks, block_rows, stacked.shape[2])]
  transfers between devices with their start and end apart: 15 -> 15, of which waited for: 11 -> 13; matrix products, arithmetic and copies ran while one was open for 21% -> 11% of each run, Pallas kernels for 0% -> 3%
where the time goes in v1:
time: 1100 us; the launch traced here: 1090 us
  waiting for transfers between devices  799 us (73%)
  matrix products  143 us (13%)
  Pallas kernels  42.4 us (4%)
  blocking collectives  39.6 us (4%)
  other arithmetic  34.4 us (3%)
  between operations  16.1 us (1%)
    reduce_scatter x1, waiting for transfers between devices, per_device(): lax.psum_scatter((jnp.dot(d_gate, gate_all.T, preferred_element_type=jnp....  88.3 us
    reduce_scatter x1, waiting for transfers between devices, per_device(): lax.psum_scatter(jnp.dot(attended, out_weight, preferred_element_type=jnp...  87.5 us
    reduce_scatter x1, waiting for transfers between devices, per_device(): lax.psum_scatter(jnp.dot(d_projected, in_packed.T, preferred_element_type...  84.6 us
    all_gather x1, waiting for transfers between devices, per_device(): grad_group = lax.all_gather(out_grad, 'head', axis=0, tiled=True)  83.6 us
    all_gather x1, waiting for transfers between devices, per_device(): group = lax.all_gather(tokens, 'head', axis=0, tiled=True)  81.4 us
    all_gather x1, waiting for transfers between devices, per_device(): lax.all_gather((middle * inv_two * ffn_gain).astype(jnp.bfloat16), 'head'...  78.2 us
    psum x1, waiting for transfers between devices, per_device(): lax.psum(in_weight_grad[:, :in_weight.shape[1]].astype(jnp.bfloat16), 'dp')  75.3 us
    reduce_scatter x1, waiting for transfers between devices, per_device(): lax.psum_scatter(jnp.dot(hidden, down_all, preferred_element_type=jnp.flo...  49.7 us
  transfers between devices with their start and end apart: 15, of which 13 were waited for; matrix products, arithmetic and copies ran while one was open for 11% of the time, Pallas kernels for 3%

profile of v1, /device:TPU:0, one launch (start us, length us, event | category | flops | bytes accessed | tf_op | source)
XLA Modules:
  0.0 1086.6 jit_solution(17729208084702851702)
XLA Ops:
  13.9 81.4 %all-gather.8.cloned.1.call-done = bf16[2048,2048]{1,0:T(8,128)(2,1)} async-done(((bf16[256,2048]{1,0:T(8,128)(2,1)}), bf16[2048,2048]{1,0:T(8,128)(2,1)}) %all-gather.8.cloned.1.call-update) | async-done | bytes 8388624 | tf_op jit(solution)/shard_map/all_gather | solution.py:265
  107.0 12.5 %shard_map.178 = (f32[2048,256]{1,0:T(8,128)}, f32[2048,128]{1,0:T(8,128)S(1)}, bf16[2048,256]{1,0:T(8,128)(2,1)S(1)}) custom-call(s32[3]{0:T(128)S(1)} %bitcast.39, bf16[2048,384]{1,0:T(8,128)(2,1)S(1)} %convolution_convert_fusion.6.projected_ref, f32[2048,1]{1,0:T(8,128)S(1)} %copy.20.keep_ref), custom_call_target="tpu_custom_call" | custom-call | flops 5368709120 | bytes 8388608 | tf_op jit(solution)/shard_map/pallas_call | solution.py:83
  128.0 87.5 %reduce-scatter.8.cloned.1.call-done = bf16[256,2048]{1,0:T(8,128)(2,1)} async-done(((bf16[2048,2048]{1,0:T(8,128)(2,1)}), bf16[256,2048]{1,0:T(8,128)(2,1)}) %reduce-scatter.8.cloned.1.call-update) | async-done | bytes 1048592 | tf_op jit(solution)/shard_map/reduce_scatter | solution.py:275
  221.9 78.2 %all-gather.10.cloned.1.call-done = bf16[2048,2048]{1,0:T(8,128)(2,1)} async-done(((bf16[256,2048]{1,0:T(8,128)(2,1)}), bf16[2048,2048]{1,0:T(8,128)(2,1)}) %all-gather.10.cloned.1.call-update) | async-done | bytes 8388624 | tf_op jit(solution)/shard_map/all_gather | solution.py:282
  300.1 11.0 %fusion.27 = f32[2048,704]{0,1:T(8,128)} fusion(bf16[2048,2048]{1,0:T(8,128)(2,1)} %all-gather.10.cloned.1.call-done, bf16[2048,704]{0,1:T(8,128)(2,1)} %all-gather.14.cloned.1.call-done), kind=kOutput, calls=%fused_computation.58 | convolution fusion | flops 5905580032 | bytes 17039360 | tf_op jit(solution)/shard_map/dot_general | solution.py:291
  311.1 30.8 %all-gather.12.cloned.1.call-done = bf16[2048,704]{0,1:T(8,128)(2,1)} async-done(((bf16[512,704]{0,1:T(8,128)(2,1)}), bf16[2048,704]{0,1:T(8,128)(2,1)}) %all-gather.12.cloned.1.call-update) | async-done | bytes 2883600 | tf_op jit(solution)/shard_map/all_gather | solution.py:286
  341.8 11.0 %fusion.26 = f32[2048,704]{0,1:T(8,128)} fusion(bf16[2048,2048]{1,0:T(8,128)(2,1)} %all-gather.10.cloned.1.call-done, bf16[2048,704]{0,1:T(8,128)(2,1)} %all-gather.12.cloned.1.call-done), kind=kOutput, calls=%fused_computation.57 | convolution fusion | flops 5905580032 | bytes 17039360 | tf_op jit(solution)/shard_map/dot_general | solution.py:290
  352.9 32.4 %all-gather.16.cloned.1.call-done = bf16[704,2048]{1,0:T(8,128)(2,1)} async-done(((bf16[704,512]{1,0:T(8,128)(2,1)}), bf16[704,2048]{1,0:T(8,128)(2,1)}) %all-gather.16.cloned.1.call-update) | async-done | bytes 2883600 | tf_op jit(solution)/shard_map/all_gather | solution.py:288
  385.2 83.6 %all-gather.18.cloned.1.call-done = bf16[2048,2048]{1,0:T(8,128)(2,1)} async-done(((bf16[256,2048]{1,0:T(8,128)(2,1)}), bf16[2048,2048]{1,0:T(8,128)(2,1)}) %all-gather.18.cloned.1.call-update) | async-done | bytes 8388624 | tf_op jit(solution)/shard_map/all_gather | solution.py:304
  468.8 15.3 %multiply_convert_fusion = (bf16[2048,704]{0,1:T(8,128)(2,1)S(1)}, bf16[2048,704]{0,1:T(8,128)(2,1)S(1)}, bf16[2048,704]{0,1:T(8,128)(2,1)}) fusion(f32[2048,704]{0,1:T(8,128)} %fusion.26, f32[2048,704]{0,1:T(8,128)} %fusion.27, bf16[2048,2048]{1,0:T(8,128)(2,1)} %all-gather.18.cloned.1.call-done, bf16[704,2048]{1,0:T(8,128)(2,1)} %all-gather.16.cloned.1.call-done), kind=kOutput, calls=%fused_computation.9 | convolution fusion | flops 5927206912 | bytes 31457280 | tf_op jit(solution)/shard_map/dot_general | solution.py:305
  484.1 10.7 fusion.28
  494.8 12.5 %add_convert_fusion = bf16[2048,2048]{1,0:T(8,128)(2,1)} fusion(f32[2048,2048]{1,0:T(8,128)} %fusion.28, bf16[2048,704]{0,1:T(8,128)(2,1)S(1)} %get-tuple-element.24, bf16[2048,704]{0,1:T(8,128)(2,1)S(1)} %copy-done.24), kind=kOutput, calls=%fused_computation.5 | convolution fusion | flops 5913968640 | bytes 30932992 | tf_op jit(solution)/shard_map/dot_general | solution.py:316
  507.5 88.3 %reduce-scatter.12.cloned.1.call-done = bf16[256,2048]{1,0:T(8,128)(2,1)} async-done(((bf16[2048,2048]{1,0:T(8,128)(2,1)}), bf16[256,2048]{1,0:T(8,128)(2,1)}) %reduce-scatter.12.cloned.1.call-update) | async-done | bytes 1048592 | tf_op jit(solution)/shard_map/reduce_scatter | solution.py:313
  611.0 10.8 convolution_convert_fusion.3
  621.8 10.6 convolution_convert_fusion.4
  632.5 48.1 %all-gather.20.cloned.1.call-done = bf16[2048,2048]{1,0:T(8,128)(2,1)} async-done(((bf16[256,2048]{1,0:T(8,128)(2,1)}), bf16[2048,2048]{1,0:T(8,128)(2,1)}) %all-gather.20.cloned.1.call-update) | async-done | bytes 8388624 | tf_op jit(solution)/shard_map/all_gather | solution.py:328
  687.7 29.8 %shard_map.179 = bf16[2048,384]{1,0:T(8,128)(2,1)} custom-call(s32[3]{0:T(128)} %bitcast.40, bf16[2048,384]{1,0:T(8,128)(2,1)} %copy-done.5, f32[2048,1]{1,0:T(8,128)} %copy-done.3, f32[2048,256]{1,0:T(8,128)} %get-tuple-element.13.y_ref, f32[2048,128]{1,0:T(8,128)} %copy-done.6, f32[2048,256]{1,0:T(8,128)} %fusion.29.grad_ref), custom_call_target="tpu_custom_call" | custom-call | flops 13421772800 | bytes 12582912 | tf_op jit(solution)/shard_map/pallas_call | solution.py:198
  740.7 11.3 %convolution_convert_fusion.1 = bf16[2048,2048]{1,0:T(8,128)(2,1)} fusion(bf16[2048,704]{0,1:T(8,128)(2,1)} %get-tuple-element.26, bf16[704,2048]{1,0:T(8,128)(2,1)} %all-gather.16.cloned.1.call-done), kind=kOutput, calls=%fused_computation.7 | convolution fusion | flops 5909774336 | bytes 14155776 | tf_op jit(solution)/shard_map/dot_general | solution.py:298
  754.4 13.8 %reduce-scatter.18.cloned.1.call-done = bf16[512,704]{0,1:T(8,128)(2,1)} async-done(((bf16[2048,704]{0,1:T(8,128)(2,1)}), bf16[512,704]{0,1:T(8,128)(2,1)}) %reduce-scatter.18.cloned.1.call-update) | async-done | bytes 720912 | tf_op jit(solution)/shard_map/reduce_scatter | solution.py:359
  770.7 42.2 %reduce-scatter.16.cloned.1.call-done = bf16[512,704]{0,1:T(8,128)(2,1)} async-done(((bf16[2048,704]{0,1:T(8,128)(2,1)}), bf16[512,704]{0,1:T(8,128)(2,1)}) %reduce-scatter.16.cloned.1.call-update) | async-done | bytes 720912 | tf_op jit(solution)/shard_map/reduce_scatter | solution.py:356
  815.2 75.3 %all-reduce.4.cloned.1.call-done = (bf16[2048,320]{0,1:T(8,128)(2,1)}, bf16[256,2048]{1,0:T(8,128)(2,1)}) async-done(((bf16[2048,320]{0,1:T(8,128)(2,1)}, bf16[256,2048]{1,0:T(8,128)(2,1)}), (bf16[2048,320]{0,1:T(8,128)(2,1)}, bf16[256,2048]{1,0:T(8,128)(2,1)})) %all-reduce.4.cloned.1.call-update) | async-done | bytes 2359312 | tf_op jit(solution)/shard_map/psum | solution.py:351
  897.6 84.6 %reduce-scatter.14.cloned.1.call-done = bf16[256,2048]{1,0:T(8,128)(2,1)} async-done(((bf16[2048,2048]{1,0:T(8,128)(2,1)}), bf16[256,2048]{1,0:T(8,128)(2,1)}) %reduce-scatter.14.cloned.1.call-update) | async-done | bytes 1048592 | tf_op jit(solution)/shard_map/reduce_scatter | solution.py:335
  984.3 39.6 %all-reduce = (f32[2048]{0:T(1024)}, f32[2048]{0:T(1024)}) all-reduce(f32[2048]{0:T(1024)S(1)} %get-tuple-element.17, f32[2048]{0:T(1024)S(1)} %get-tuple-element.15), channel_id=1, replica_groups=mesh['dp'=4,'head'=8] {'dp','head'}, use_global_device_ids=true, to_apply=%region_11.12 | all-reduce | flops 4096 | bytes 32768 | tf_op jit(solution)/shard_map/psum | solution.py:348
  1023.9 49.7 %reduce-scatter.10.cloned.1.call-done = bf16[256,2048]{1,0:T(8,128)(2,1)} async-done(((bf16[2048,2048]{1,0:T(8,128)(2,1)}), bf16[256,2048]{1,0:T(8,128)(2,1)}) %reduce-scatter.10.cloned.1.call-update) | async-done | bytes 1048592 | tf_op jit(solution)/shard_map/reduce_scatter | solution.py:297
  (125 shorter events, 99.6 us)
Async XLA Ops:
  8.0 113.5 %copy-start = (bf16[256,2048]{1,0:T(8,128)(2,1)S(1)}, bf16[256,2048]{1,0:T(8,128)(2,1)}, u32[]{:S(2)}) copy-start(bf16[256,2048]{1,0:T(8,128)(2,1)} %param.16) | copy-start | bytes 3145732
  8.0 87.2 %all-gather.8.cloned.1.call-start = ((), (), s32[]{:S(2)}) async-start(), calls=%async_computation.7 | async-start | bytes 9437184 | tf_op jit(solution)/shard_map/all_gather | solution.py:265
  8.8 206.7 %reduce-scatter.8.cloned.1.call-start = ((), (), s32[]{:S(2)}) async-start(), calls=%async_computation.8 | async-start | bytes 9437184 | tf_op jit(solution)/shard_map/reduce_scatter | solution.py:275
  9.9 97.1 %copy-start.3 = (f32[2048,1]{1,0:T(8,128)}, f32[2048,1]{1,0:T(8,128)S(1)}, u32[]{:S(2)}) copy-start(f32[2048,1]{1,0:T(8,128)S(1)} %copy.20.keep_ref) | copy-start | bytes 24580
  12.8 94.2 %copy-start.4 = (s32[3,1]{0,1:T(1,128)}, s32[3,1]{0,1:T(1,128)S(1)}, u32[]{:S(2)}) copy-start(s32[3,1]{0,1:T(1,128)S(1)} %reduce-window.9) | copy-start | bytes 40
  12.9 87.7 %copy-start.22 = (bf16[384]{0:T(512)(128)(2,1)}, bf16[384]{0:T(512)(128)(2,1)S(1)}, u32[]{:S(2)}) copy-start(bf16[384]{0:T(512)(128)(2,1)S(1)} %pad.6.clone) | copy-start | bytes 2308
  13.8 86.7 %copy-start.13 = (bf16[2048,2,16]{0,2,1:T(8,128)(2,1)}, bf16[2048,2,16]{0,2,1:T(8,128)(2,1)S(1)}, u32[]{:S(2)}) copy-start(bf16[2048,2,16]{0,2,1:T(8,128)(2,1)S(1)} %get-tuple-element.31) | copy-start | bytes 393220
  13.9 86.7 %copy-start.15 = (bf16[2048,2,16]{0,2,1:T(8,128)(2,1)}, bf16[2048,2,16]{0,2,1:T(8,128)(2,1)S(1)}, u32[]{:S(2)}) copy-start(bf16[2048,2,16]{0,2,1:T(8,128)(2,1)S(1)} %get-tuple-element.32) | copy-start | bytes 393220
  127.1 88.3 %copy-start.7 = (bf16[256,2048]{1,0:T(8,128)(2,1)S(1)}, bf16[256,2048]{1,0:T(8,128)(2,1)}, u32[]{:S(2)}) copy-start(bf16[256,2048]{1,0:T(8,128)(2,1)} %param.11) | copy-start | bytes 3145732
  127.1 90.0 %copy-start.17 = (f32[2048]{0:T(1024)S(1)}, f32[2048]{0:T(1024)}, u32[]{:S(2)}) copy-start(f32[2048]{0:T(1024)} %param.17) | copy-start | bytes 24580
  127.1 94.7 %all-gather.14.cloned.1.call-start = ((), (), s32[]{:S(2)}) async-start(), calls=%async_computation.11 | async-start | bytes 3604480 | tf_op jit(solution)/shard_map/all_gather | solution.py:287
  127.7 172.4 %all-gather.10.cloned.1.call-start = ((), (), s32[]{:S(2)}) async-start(), calls=%async_computation.9 | async-start | bytes 9437184 | tf_op jit(solution)/shard_map/all_gather | solution.py:282
  219.7 122.1 %all-gather.12.cloned.1.call-start = ((), (), s32[]{:S(2)}) async-start(), calls=%async_computation.10 | async-start | bytes 3604480 | tf_op jit(solution)/shard_map/all_gather | solution.py:286
  220.3 164.9 %all-gather.16.cloned.1.call-start = ((), (), s32[]{:S(2)}) async-start(), calls=%async_computation.12 | async-start | bytes 3604480 | tf_op jit(solution)/shard_map/all_gather | solution.py:288
  221.0 247.7 %all-gather.18.cloned.1.call-start = ((), (), s32[]{:S(2)}) async-start(), calls=%async_computation.14 | async-start | bytes 9437184 | tf_op jit(solution)/shard_map/all_gather | solution.py:304
  221.8 373.9 %reduce-scatter.12.cloned.1.call-start = ((), (), s32[]{:S(2)}) async-start(), calls=%async_computation.15 | async-start | bytes 9437184 | tf_op jit(solution)/shard_map/reduce_scatter | solution.py:313
  507.4 88.3 %copy-start.8 = (bf16[256,2048]{1,0:T(8,128)(2,1)S(1)}, bf16[256,2048]{1,0:T(8,128)(2,1)}, u32[]{:S(2)}) copy-start(bf16[256,2048]{1,0:T(8,128)(2,1)} %reduce-scatter.8.cloned.1.call-done) | copy-start | bytes 3145732
  507.4 173.2 %all-gather.20.cloned.1.call-start = ((), (), s32[]{:S(2)}) async-start(), calls=%async_computation.16 | async-start | bytes 9437184 | tf_op jit(solution)/shard_map/all_gather | solution.py:328
  600.3 151.7 %reduce-scatter.20.cloned.1.call-start = ((), (), s32[]{:S(2)}) async-start(), calls=%async_computation.20 | async-start | bytes 3604480 | tf_op jit(solution)/shard_map/reduce_scatter | solution.py:362
  610.9 157.4 %reduce-scatter.18.cloned.1.call-start = ((), (), s32[]{:S(2)}) async-start(), calls=%async_computation.19 | async-start | bytes 3604480 | tf_op jit(solution)/shard_map/reduce_scatter | solution.py:359
  621.8 191.1 %reduce-scatter.16.cloned.1.call-start = ((), (), s32[]{:S(2)}) async-start(), calls=%async_computation.18 | async-start | bytes 3604480 | tf_op jit(solution)/shard_map/reduce_scatter | solution.py:356
  632.5 258.0 %all-reduce.4.cloned.1.call-start = ((), (), s32[]{:S(2)}) async-start(), calls=%async_computation.21 | async-start | bytes 4718592 | tf_op jit(solution)/shard_map/psum | solution.py:351
  730.7 251.5 %reduce-scatter.14.cloned.1.call-start = ((), (), s32[]{:S(2)}) async-start(), calls=%async_computation.17 | async-start | bytes 9437184 | tf_op jit(solution)/shard_map/reduce_scatter | solution.py:335
  740.6 332.9 %reduce-scatter.10.cloned.1.call-start = ((), (), s32[]{:S(2)}) async-start(), calls=%async_computation.13 | async-start | bytes 9437184 | tf_op jit(solution)/shard_map/reduce_scatter | solution.py:297
  (20 other events, 252.0 us)
Sparse Core Ops, SparseCore 0:
  10.5 84.7 all-gather.7
  127.3 88.1 reduce-scatter.7
  507.5 88.1 reduce-scatter.11
Sparse Core Ops, SparseCore 1:
  129.4 40.0 all-gather.13
  219.8 80.2 all-gather.9
  301.8 40.0 all-gather.11
  343.7 41.5 all-gather.15
  386.8 81.9 all-gather.17
  600.4 80.2 all-gather.19
  683.5 40.1 reduce-scatter.19
  726.6 41.6 reduce-scatter.17
  771.2 41.6 reduce-scatter.15
  816.6 73.8 all-reduce.3
  892.8 89.4 reduce-scatter.13
  984.6 88.9 reduce-scatter.9

commit v2 on v1

--- a/solution.py
+++ b/solution.py
@@ -226,7 +226,6 @@
             per_head[:, :, 2 * FD :].reshape(depth, heads * VD),
             per_head[:, :, :FD].reshape(depth, heads * FD),
             per_head[:, :, FD : 2 * FD].reshape(depth, heads * FD),
-            jnp.zeros((depth, LANES - 2 * heads * FD), weight.dtype),
         ],
         axis=1,
     )
@@ -249,7 +248,406 @@
     return lax.rsqrt(jnp.mean(values * values, axis=1, keepdims=True) + epsilon)
 
 
+def wide(values):
+    return values.astype(jnp.float32)
+
+
+def low(values):
+    return values.astype(jnp.bfloat16)
+
+
+def pick(values, index, count, axis):
+    size = values.shape[axis] // count
+    if count == 2:
+        first = lax.slice_in_dim(values, 0, size, axis=axis)
+        second = lax.slice_in_dim(values, size, 2 * size, axis=axis)
+        return jnp.where(index == 0, first, second)
+    return lax.dynamic_slice_in_dim(values, index * size, size, axis)
+
+
+def in_order(pieces, index, axis):
+    count = len(pieces)
+    if count == 1:
+        return pieces[0]
+    if count == 2:
+        first = jnp.where(index == 0, pieces[0], pieces[1])
+        second = jnp.where(index == 0, pieces[1], pieces[0])
+        return jnp.concatenate([first, second], axis=axis)
+    stacked = jnp.stack(pieces)
+    placed = [
+        lax.dynamic_index_in_dim(stacked, (index - place) % count, 0, keepdims=False)
+        for place in range(count)
+    ]
+    return jnp.concatenate(placed, axis=axis)
+
+
+class Wires:
+    def __init__(self, mesh):
+        self.dp, self.head = mesh.shape["dp"], mesh.shape["head"]
+        self.ny, self.nz, self.nzh = self.dp // 2, self.head // 2, self.head // 4
+
+    def place(self):
+        p, h = lax.axis_index("dp"), lax.axis_index("head")
+        self.p, self.h = p, h
+        self.y, self.x, self.z, self.c = p // 2, p % 2, h // 2, h % 2
+        self.zl, self.zh = self.z % 2, self.z // 2
+
+    def over_x(self, values):
+        return lax.ppermute(values, "dp", [(i, i ^ 1) for i in range(self.dp)])
+
+    def over_y(self, values, shift):
+        return lax.ppermute(
+            values, "dp", [(i, ((i // 2 + shift) % self.ny) * 2 + i % 2) for i in range(self.dp)]
+        )
+
+    def over_core(self, values):
+        return lax.ppermute(values, "head", [(i, i ^ 1) for i in range(self.head)])
+
+    def over_zl(self, values):
+        return lax.ppermute(values, "head", [(i, i ^ 2) for i in range(self.head)])
+
+    def over_zh(self, values, shift):
+        return lax.ppermute(
+            values, "head", [(i, ((i // 4 + shift) % self.nzh) * 4 + i % 4) for i in range(self.head)]
+        )
+
+    def right(self, values, first, last):
+        return lax.ppermute(
+            values, "head", [(i, i + 2) for i in range(self.head) if first <= i // 2 <= last]
+        )
+
+    def left(self, values, first, last):
+        return lax.ppermute(
+            values, "head", [(i, i - 2) for i in range(self.head) if first <= i // 2 <= last]
+        )
+
+    def line_gather(self, block):
+        n = self.nz
+        rights, lefts = [block], [block]
+        for step in range(1, n):
+            rights.append(self.right(rights[-1], step - 1, n - 2))
+            lefts.append(self.left(lefts[-1], 1, n - step))
+        return [block] + [
+            jnp.where(self.z >= s, rights[s], lefts[n - s]) for s in range(1, n)
+        ]
+
+    def line_reduce(self, parts):
+        n = self.nz
+        held = {s: wide(parts[s]) for s in range(n)}
+        leftward, rightward = [None] * n, [None] * n
+        to_left = jnp.zeros_like(held[0])
+        to_right = jnp.zeros_like(held[0])
+        for s in range(n - 1, 0, -1):
+            to_left = wide(self.left(low(held[s] + to_left), s, n - 1))
+            to_right = wide(self.right(low(held[n - s] + to_right), 0, n - 1 - s))
+        return held[0] + to_left + to_right
+
+    def square_gather(self, block):
+        half = block.shape[0] // 2
+        by_x, by_z = self.over_x(block), self.over_zl(block)
+        corner = jnp.concatenate([self.over_zl(by_x[:half]), self.over_x(by_z[half:])], axis=0)
+        mine = [block, by_x, by_z, corner]
+        return [(own, self.over_core(own)) for own in mine]
+
+    def square_reduce(self, pairs):
+        sums = [low(wide(own) + wide(self.over_core(other))) for own, other in pairs]
+        half = sums[0].shape[0] // 2
+        to_z = self.over_x(sums[3][:half])
+        to_x = self.over_zl(sums[3][half:])
+        by_x = jnp.concatenate([sums[1][:half], low(wide(sums[1][half:]) + wide(to_x))], axis=0)
+        by_z = jnp.concatenate([low(wide(sums[2][:half]) + wide(to_z)), sums[2][half:]], axis=0)
+        return sums[0], self.over_x(by_x), self.over_zl(by_z)
+
+    def whole_weight(self, shard):
+        rows = shard.shape[0]
+        part = lax.dynamic_slice_in_dim(
+            shard, self.p * (shard.shape[1] // self.dp), shard.shape[1] // self.dp, 1
+        )
+        line = in_order([slot[None] for slot in self.line_gather(part)], self.z, 0)[None]
+        line = jnp.where(
+            self.x == 0,
+            jnp.concatenate([line, self.over_x(line)], 0),
+            jnp.concatenate([self.over_x(line), line], 0),
+        )
+        line = in_order([line] + [self.over_y(line, s) for s in range(1, self.ny)], self.y, 0)
+        other = self.over_core(line)
+        both = jnp.stack(
+            [jnp.where(self.c == 0, line, other), jnp.where(self.c == 0, other, line)], axis=2
+        )
+        return both.reshape(self.dp, self.head * rows, shard.shape[1] // self.dp)
+
+    def ffn_weights(self, stacked):
+        own = pick(stacked, self.x, 2, 1)
+        other = self.over_x(pick(stacked, 1 - self.x, 2, 1))
+        pair = in_order([own, other], self.x, 2)
+        pair = jnp.concatenate([pair] + [self.over_zh(pair, s) for s in range(1, self.nzh)], axis=1)
+        return in_order([pair] + [self.over_y(pair, s) for s in range(1, self.ny)], self.y, 2)
+
+    def ffn_grads(self, grad):
+        total = wide(pick(grad, self.y, self.ny, 1))
+        for s in range(1, self.ny):
+            total = total + wide(self.over_y(low(pick(grad, (self.y + s) % self.ny, self.ny, 1)), s))
+        rows = grad.shape[0] // self.nzh
+        kept = total[:rows]
+        for s in range(1, self.nzh):
+            kept = kept + wide(self.over_zh(low(total[s * rows : (s + 1) * rows]), -s))
+        own = pick(kept, self.x, 2, 1)
+        other = wide(self.over_x(low(pick(kept, 1 - self.x, 2, 1))))
+        return in_order([own, other], self.x, 0)
+
+    def sum_y(self, values):
+        total = wide(values)
+        for s in range(1, self.ny):
+            total = total + wide(self.over_y(values, s))
+        return low(total)
+
+    def sum_x(self, values):
+        return low(wide(values) + wide(self.over_x(values)))
+
+    def sum_dp(self, values):
+        half = values.shape[0] // 2
+        return jnp.concatenate(
+            [self.sum_y(self.sum_x(values[:half])), self.sum_x(self.sum_y(values[half:]))], axis=0
+        )
+
+    def out_grads(self, grad):
+        by_core = grad.reshape(self.nz, 2, *grad.shape[1:])
+        other = self.over_core(pick(by_core, 1 - self.c, 2, 1)[:, 0])
+        total = low(wide(pick(by_core, self.c, 2, 1)[:, 0]) + wide(other))
+        mine = wide(pick(total, self.y, self.ny, 2))
+        for s in range(1, self.ny):
+            mine = mine + wide(self.over_y(pick(total, (self.y + s) % self.ny, self.ny, 2), s))
+        mine = low(mine)
+        sent = self.over_x(pick(mine, 1 - self.x, 2, 2))
+        mine = low(wide(pick(mine, self.x, 2, 2)) + wide(sent))
+        parts = [
+            lax.dynamic_index_in_dim(mine, (self.z - s) % self.nz, 0, keepdims=False)
+            for s in range(self.nz)
+        ]
+        part = low(self.line_reduce(parts))
+        part = in_order([part, self.over_x(part)], self.x, 1)
+        return in_order([part] + [self.over_y(part, s) for s in range(1, self.ny)], self.y, 1)
+
+    def sum_all(self, values):
+        values = values + self.over_core(values)
+        values = values + self.over_zl(values)
+        values = values + sum(self.over_zh(values, s) for s in range(1, self.nzh))
+        values = values + self.over_x(values)
+        return values + sum(self.over_y(values, s) for s in range(1, self.ny))
+
+
+def mix_kernel(heads, attended_ref, weight_ref, tokens_ref, gain_ref, middle_ref, normed_ref):
+    step = pl.program_id(0)
+    width = weight_ref.shape[2]
+    rows = attended_ref.shape[2]
+    total = jnp.zeros((tokens_ref.shape[0], width), jnp.float32)
+    for head in range(heads):
+        total += jnp.dot(
+            attended_ref[head],
+            weight_ref[0, head * rows : (head + 1) * rows, :],
+            preferred_element_type=jnp.float32,
+        )
+    at = pl.ds(pl.multiple_of(step * width, width), width)
+    middle_ref[:, at] = total + tokens_ref[:, at].astype(jnp.float32)
+
+    @pl.when(step == pl.num_programs(0) - 1)
+    def _():
+        middle = middle_ref[...]
+        normed_ref[...] = (middle * inv_root_mean(middle) * gain_ref[...]).astype(jnp.bfloat16)
+
+
+def mix(attended, weight, tokens, gain):
+    heads, count, rows = attended.shape
+    blocks, depth, width = weight.shape
+    full = lambda *shape: pl.BlockSpec(shape, lambda i: (0,) * len(shape))
+    return pl.pallas_call(
+        functools.partial(mix_kernel, heads),
+        grid=(blocks,),
+        in_specs=[
+            full(heads, count, rows),
+            pl.BlockSpec((1, depth, width), lambda i: (i, 0, 0)),
+            full(*tokens.shape),
+            full(1, tokens.shape[1]),
+        ],
+        out_specs=[full(*tokens.shape), full(*tokens.shape)],
+        out_shape=[
+            jax.ShapeDtypeStruct(tokens.shape, jnp.float32),
+            jax.ShapeDtypeStruct(tokens.shape, jnp.bfloat16),
+        ],
+        compiler_params=pltpu.CompilerParams(
+            dimension_semantics=("arbitrary",), vmem_limit_bytes=40 * 1024 * 1024
+        ),
+        cost_estimate=pl.CostEstimate(
+            flops=2 * count * heads * rows * tokens.shape[1], bytes_accessed=14 << 20, transcendentals=0
+        ),
+    )(attended, weight, tokens, gain)
+
+
+def unmix_kernel(
+    heads, a_ref, b_ref, c_ref, middle_ref, grad_ref, gain_ref, weight_ref,
+    dmiddle_ref, dmixed_ref, part_ref, out_ref, total_s,
+):
+    step = pl.program_id(0)
+    width = weight_ref.shape[2]
+    rows = weight_ref.shape[1] // heads
+
+    @pl.when(step == 0)
+    def _():
+        total_s[...] = jnp.zeros_like(total_s)
+        middle = middle_ref[...]
+        inv_two = inv_root_mean(middle)
+        dnormed = wide(a_ref[...]) + wide(b_ref[...]) + wide(c_ref[...])
+        scaled = middle * inv_two
+        error = dnormed * gain_ref[...]
+        dmiddle = wide(grad_ref[...]) + inv_two * (
+            error - scaled * jnp.mean(error * scaled, axis=1, keepdims=True)
+        )
+        part_ref[...] = jnp.sum(dnormed * scaled, axis=0, keepdims=True)
+        dmiddle_ref[...] = dmiddle
+        dmixed_ref[...] = dmiddle.astype(jnp.bfloat16)
+
+    at = pl.ds(pl.multiple_of(step * width, width), width)
+    total_s[...] += lax.dot_general(
+        dmixed_ref[:, at], weight_ref[0], NT, preferred_element_type=jnp.float32
+    )
+
+    @pl.when(step == pl.num_programs(0) - 1)
+    def _():
+        for head in range(heads):
+            out_ref[head] = total_s[:, head * rows : (head + 1) * rows].astype(jnp.bfloat16)
+
+
+def unmix(parts, middle, grad, gain, weight, heads):
+    blocks, depth, width = weight.shape
+    count, size = middle.shape
+    rows = depth // heads
+    full = lambda *shape: pl.BlockSpec(shape, lambda i: (0,) * len(shape))
+    same = full(count, size)
+    return pl.pallas_call(
+        functools.partial(unmix_kernel, heads),
+        grid=(blocks,),
+        in_specs=[same] * 5 + [full(1, size), pl.BlockSpec((1, depth, width), lambda i: (i, 0, 0))],
+        out_specs=[same, same, full(1, size), full(heads, count, rows)],
+        out_shape=[
+            jax.ShapeDtypeStruct((count, size), jnp.float32),
+            jax.ShapeDtypeStruct((count, size), jnp.bfloat16),
+            jax.ShapeDtypeStruct((1, size), jnp.float32),
+            jax.ShapeDtypeStruct((heads, count, rows), jnp.bfloat16),
+        ],
+        scratch_shapes=[pltpu.VMEM((count, depth), jnp.float32)],
+        compiler_params=pltpu.CompilerParams(
+            dimension_semantics=("arbitrary",), vmem_limit_bytes=48 * 1024 * 1024
+        ),
+        cost_estimate=pl.CostEstimate(
+            flops=2 * count * depth * size, bytes_accessed=18 << 20, transcendentals=0
+        ),
+    )(*parts, middle, grad, gain, weight)
+
+
+def last_kernel(heads, proj_ref, weight_ref, tokens_ref, dmiddle_ref, gain_ref, grad_ref, part_ref):
+    step = pl.program_id(0)
+    width = weight_ref.shape[2]
+    rows = proj_ref.shape[2]
+    total = jnp.zeros((tokens_ref.shape[0], width), jnp.float32)
+    for head in range(heads):
+        total += jnp.dot(
+            proj_ref[head],
+            weight_ref[0, head * rows : (head + 1) * rows, :],
+            preferred_element_type=jnp.float32,
+        )
+    grad_ref[:, pl.ds(pl.multiple_of(step * width, width), width)] = total
+
+    @pl.when(step == pl.num_programs(0) - 1)
+    def _():
+        dnormed = grad_ref[...]
+        tokens = wide(tokens_ref[...])
+        inv_one = inv_root_mean(tokens)
+        scaled = tokens * inv_one
+        error = dnormed * gain_ref[...]
+        part_ref[...] = jnp.sum(dnormed * scaled, axis=0, keepdims=True)
+        grad_ref[...] = dmiddle_ref[...] + inv_one * (
+            error - scaled * jnp.mean(error * scaled, axis=1, keepdims=True)
+        )
+
+
+def last(proj, weight, tokens, dmiddle, gain):
+    heads, count, rows = proj.shape
+    blocks, depth, width = weight.shape
+    size = tokens.shape[1]
+    full = lambda *shape: pl.BlockSpec(shape, lambda i: (0,) * len(shape))
+    return pl.pallas_call(
+        functools.partial(last_kernel, heads),
+        grid=(blocks,),
+        in_specs=[
+            full(heads, count, rows),
+            pl.BlockSpec((1, depth, width), lambda i: (i, 0, 0)),
+            full(count, size),
+            full(count, size),
+            full(1, size),
+        ],
+        out_specs=[full(count, size), full(1, size)],
+        out_shape=[
+            jax.ShapeDtypeStruct((count, size), jnp.float32),
+            jax.ShapeDtypeStruct((1, size), jnp.float32),
+        ],
+        compiler_params=pltpu.CompilerParams(
+            dimension_semantics=("arbitrary",), vmem_limit_bytes=48 * 1024 * 1024
+        ),
+        cost_estimate=pl.CostEstimate(
+            flops=2 * count * depth * size, bytes_accessed=18 << 20, transcendentals=0
+        ),
+    )(proj, weight, tokens, dmiddle, gain)
+
+
+def ffn_kernel(count, *refs):
+    normed, grads, weight_ref = refs[:count], refs[count : 2 * count], refs[2 * count]
+    hidden_ref, dgate_ref, dup_ref = refs[2 * count + 1 : 2 * count + 4]
+    branches, dnormed = refs[2 * count + 4 : 3 * count + 4], refs[3 * count + 4 :]
+    rows = normed[0].shape[0]
+    dot = functools.partial(jnp.dot, preferred_element_type=jnp.float32)
+    across = functools.partial(
+        lax.dot_general, dimension_numbers=NT, preferred_element_type=jnp.float32
+    )
+    for block in range(count):
+        at = slice(block * rows, (block + 1) * rows)
+        gate = across(normed[block][...], weight_ref[0])
+        up = across(normed[block][...], weight_ref[1])
+        dhidden = across(grads[block][...], weight_ref[2])
+        sigmoid = jax.nn.sigmoid(gate)
+        silu = gate * sigmoid
+        hidden = (silu * up).astype(jnp.bfloat16)
+        dgate = (dhidden * up * sigmoid * (1.0 + gate * (1.0 - sigmoid))).astype(jnp.bfloat16)
+        dup = (dhidden * silu).astype(jnp.bfloat16)
+        hidden_ref[at, :] = hidden
+        dgate_ref[at, :] = dgate
+        dup_ref[at, :] = dup
+        dnormed[block][...] = (dot(dgate, weight_ref[0]) + dot(dup, weight_ref[1])).astype(jnp.bfloat16)
+        branches[block][...] = dot(hidden, weight_ref[2]).astype(jnp.bfloat16)
+
+
+def ffn(normed, grads, weights):
+    count = len(normed)
+    rows, depth = normed[0].shape
+    units = weights.shape[1]
+    wide_out = jax.ShapeDtypeStruct((rows, depth), jnp.bfloat16)
+    unit_out = jax.ShapeDtypeStruct((count * rows, units), jnp.bfloat16)
+    outs = pl.pallas_call(
+        functools.partial(ffn_kernel, count),
+        in_specs=[pl.BlockSpec(memory_space=pltpu.VMEM)] * (2 * count + 1),
+        out_specs=[pl.BlockSpec(memory_space=pltpu.VMEM)] * (2 * count + 3),
+        out_shape=[unit_out] * 3 + [wide_out] * (2 * count),
+        compiler_params=pltpu.CompilerParams(vmem_limit_bytes=56 * 1024 * 1024),
+        cost_estimate=pl.CostEstimate(
+            flops=12 * count * rows * depth * units,
+            bytes_accessed=20 << 20,
+            transcendentals=count * rows * units,
+        ),
+    )(*normed, *grads, weights)
+    return outs[:3], outs[3 : 3 + count], outs[3 + count :]
+
+
 def per_device(
+    wires,
     tokens,
     keep_mask,
     seq_lengths,
@@ -262,114 +660,86 @@
     down_weight,
     out_grad,
 ):
-    group = lax.all_gather(tokens, "head", axis=0, tiled=True)
-    group_wide = group.astype(jnp.float32)
-    normed = (group_wide * inv_root_mean(group_wide) * attn_gain).astype(jnp.bfloat16)
+    wires.place()
     heads_here = in_weight.shape[1] // (2 * FD + VD)
+    rows, depth = tokens.shape
+    group_rows = rows * wires.head
+    tokens_wide = wide(tokens)
+    own_normed = low(tokens_wide * inv_root_mean(tokens_wide) * attn_gain)
+    slots = wires.line_gather(own_normed)
+    normed = jnp.zeros((group_rows, depth), jnp.bfloat16)
+    for s, slot in enumerate(slots):
+        chip = (wires.z - s) % wires.nz
+        normed = lax.dynamic_update_slice(normed, slot, ((chip * 2 + wires.c) * rows, 0))
+        normed = lax.dynamic_update_slice(
+            normed, wires.over_core(slot), ((chip * 2 + 1 - wires.c) * rows, 0)
+        )
     in_packed = pack_columns(in_weight, heads_here)
-    projected = jnp.dot(normed, in_packed, preferred_element_type=jnp.float32).astype(jnp.bfloat16)
+    packed_width = in_packed.shape[1]
+    in_padded = jnp.pad(in_packed, ((0, 0), (0, heads_here * VD + LANES - packed_width)))
+    projected = low(jnp.dot(normed, in_padded, preferred_element_type=jnp.float32))
+
+    out_whole = wires.whole_weight(out_weight)
+    ffn_whole = wires.ffn_weights(jnp.stack([gate_weight.T, up_weight.T, down_weight]))
+    grads = wires.square_gather(out_grad)
+    in_whole = wires.whole_weight(in_packed.T)
+
     ends = jnp.cumsum(seq_lengths[0])
     keep_column = keep_mask.astype(jnp.float32)[:, None]
     attended_wide, inverses, attended = attend(projected, keep_column, ends, heads_here)
-    tokens_wide = tokens.astype(jnp.float32)
-    middle = tokens_wide + lax.psum_scatter(
-        jnp.dot(attended, out_weight, preferred_element_type=jnp.float32).astype(jnp.bfloat16),
-        "head",
-        scatter_dimension=0,
-        tiled=True,
-    ).astype(jnp.float32)
-    inv_two = inv_root_mean(middle)
-    normed_two = lax.all_gather(
-        (middle * inv_two * ffn_gain).astype(jnp.bfloat16), "head", axis=0, tiled=True
-    )
-    gate_all, up_all, down_all = (
-        lax.all_gather(gate_weight, "dp", axis=0, tiled=True),
-        lax.all_gather(up_weight, "dp", axis=0, tiled=True),
-        lax.all_gather(down_weight, "dp", axis=1, tiled=True),
-    )
-    gate_pre = jnp.dot(normed_two, gate_all, preferred_element_type=jnp.float32)
-    up_pre = jnp.dot(normed_two, up_all, preferred_element_type=jnp.float32)
-    sigmoid_gate = jax.nn.sigmoid(gate_pre)
-    silu_gate = gate_pre * sigmoid_gate
-    hidden = (silu_gate * up_pre).astype(jnp.bfloat16)
-    output = (
-        middle
-        + lax.psum_scatter(
-            jnp.dot(hidden, down_all, preferred_element_type=jnp.float32).astype(jnp.bfloat16),
-            "head",
-            scatter_dimension=0,
-            tiled=True,
-        ).astype(jnp.float32)
-    ).astype(jnp.bfloat16)
-    grad_group = lax.all_gather(out_grad, "head", axis=0, tiled=True)
-    d_hidden = jnp.dot(grad_group, down_all.T, preferred_element_type=jnp.float32)
-    d_gate = (d_hidden * up_pre * sigmoid_gate * (1.0 + gate_pre * (1.0 - sigmoid_gate))).astype(
-        jnp.bfloat16
-    )
-    d_up = (d_hidden * silu_gate).astype(jnp.bfloat16)
-    down_grad = jnp.dot(hidden.T, grad_group, preferred_element_type=jnp.float32)
-    gate_grad = jnp.dot(normed_two.T, d_gate, preferred_element_type=jnp.float32)
-    up_grad = jnp.dot(normed_two.T, d_up, preferred_element_type=jnp.float32)
-    d_normed_two = lax.psum_scatter(
-        (
-            jnp.dot(d_gate, gate_all.T, preferred_element_type=jnp.float32)
-            + jnp.dot(d_up, up_all.T, preferred_element_type=jnp.float32)
-        ).astype(jnp.bfloat16),
-        "head",
-        scatter_dimension=0,
-        tiled=True,
-    ).astype(jnp.float32)
-    scaled_two = middle * inv_two
-    error_two = d_normed_two * ffn_gain
-    d_middle = out_grad.astype(jnp.float32) + inv_two * (
-        error_two - scaled_two * jnp.mean(error_two * scaled_two, axis=1, keepdims=True)
-    )
-    ffn_gain_part = jnp.sum(d_normed_two * scaled_two, axis=0)
-    d_mixed = lax.all_gather(d_middle.astype(jnp.bfloat16), "head", axis=0, tiled=True)
-    d_attended = jnp.dot(d_mixed, out_weight.T, preferred_element_type=jnp.float32)
-    out_weight_grad = jnp.dot(attended.T, d_mixed, preferred_element_type=jnp.float32)
+
+    def swap(values):
+        return lax.all_to_all(values, "head", split_axis=0, concat_axis=0, tiled=True)
+
+    attended_here = swap(attended).reshape(wires.head, rows, heads_here * VD)
+    middle, normed_two = mix(attended_here, out_whole, tokens, ffn_gain[None])
+    pairs = wires.square_gather(normed_two)
+    units, branch_pairs, dnormed_pairs = [], [], []
+    for (own, other), (own_grad, other_grad) in zip(pairs, grads):
+        unit, branch, dnormed = ffn([own, other], [own_grad, other_grad], ffn_whole)
+        units.append(unit)
+        branch_pairs.append(branch)
+        dnormed_pairs.append(dnormed)
+    dnormed_parts = wires.square_reduce(dnormed_pairs)
+    d_middle, d_mixed, ffn_gain_part, d_attended = unmix(
+        dnormed_parts, middle, out_grad, ffn_gain[None], out_whole, wires.head
+    )
+    d_attended = swap(d_attended).reshape(group_rows, heads_here * VD)
     d_projected = attend_back(
         projected, keep_column, ends, attended_wide, inverses, d_attended, heads_here
     )
-    in_weight_grad = jnp.dot(normed.T, d_projected, preferred_element_type=jnp.float32)
-    d_normed = lax.psum_scatter(
-        jnp.dot(d_projected, in_packed.T, preferred_element_type=jnp.float32).astype(jnp.bfloat16),
-        "head",
-        scatter_dimension=0,
-        tiled=True,
-    ).astype(jnp.float32)
-    inv_one = inv_root_mean(tokens_wide)
-    scaled_one = tokens_wide * inv_one
-    error_one = d_normed * attn_gain
-    in_grad = d_middle + inv_one * (
-        error_one - scaled_one * jnp.mean(error_one * scaled_one, axis=1, keepdims=True)
-    )
-    attn_gain_part = jnp.sum(d_normed * scaled_one, axis=0)
-    attn_gain_grad, ffn_gain_grad = lax.psum((attn_gain_part, ffn_gain_part), ("dp", "head"))
-    in_weight_grad, out_weight_grad = (
-        unpack_columns(
-            lax.psum(in_weight_grad[:, : in_weight.shape[1]].astype(jnp.bfloat16), "dp"), heads_here
-        ).astype(jnp.float32),
-        lax.psum(out_weight_grad.astype(jnp.bfloat16), "dp").astype(jnp.float32),
-    )
-    gate_grad, up_grad, down_grad = (
-        lax.psum_scatter(
-            gate_grad.astype(jnp.bfloat16), "dp", scatter_dimension=0, tiled=True
-        ).astype(jnp.float32),
-        lax.psum_scatter(
-            up_grad.astype(jnp.bfloat16), "dp", scatter_dimension=0, tiled=True
-        ).astype(jnp.float32),
-        lax.psum_scatter(
-            down_grad.astype(jnp.bfloat16), "dp", scatter_dimension=1, tiled=True
-        ).astype(jnp.float32),
-    )
+    d_here = swap(d_projected[:, :packed_width]).reshape(wires.head, rows, packed_width)
+    in_grad, attn_gain_part = last(d_here, in_whole, tokens, d_middle, attn_gain[None])
+
+    a, b, c = wires.square_reduce(branch_pairs)
+    output = low(middle + wide(a) + wide(b) + wide(c))
+
+    normed_all = jnp.concatenate([block for pair in pairs for block in pair], axis=0)
+    grad_all = jnp.concatenate([block for pair in grads for block in pair], axis=0)
+    hidden, d_gate, d_up = (jnp.concatenate([unit[i] for unit in units], axis=0) for i in range(3))
+
+    def weight_grad(left, right):
+        return low(lax.dot_general(left, right, TN, preferred_element_type=jnp.float32))
+
+    gate_grad = wires.ffn_grads(weight_grad(d_gate, normed_all)).T
+    up_grad = wires.ffn_grads(weight_grad(d_up, normed_all)).T
+    down_grad = wires.ffn_grads(weight_grad(hidden, grad_all))
+    out_weight_grad = wide(
+        wires.out_grads(
+            low(jnp.einsum("htv,td->hvd", attended_here, d_mixed, preferred_element_type=jnp.float32))
+        )
+    )
+    in_weight_grad = unpack_columns(
+        wide(wires.sum_dp(weight_grad(normed, d_projected)[:, :packed_width])), heads_here
+    )
+    gains = wires.sum_all(jnp.concatenate([attn_gain_part, ffn_gain_part], axis=0))
     return (
         output,
         in_grad,
-        attn_gain_grad,
+        gains[0],
         in_weight_grad,
         out_weight_grad,
-        ffn_gain_grad,
+        gains[1],
         gate_grad,
         up_grad,
         down_grad,
@@ -378,7 +748,7 @@
 
 def solution(mesh):
     return jax.shard_map(
-        per_device,
+        functools.partial(per_device, Wires(mesh)),
         mesh=mesh,
         in_specs=(
             P(("dp", "head"), None),

time: 1100 us -> 956 us (0.87)
  waiting for transfers between devices: 799 us -> 450 us
  starting transfers between devices: 1.1 us -> 125 us
  matrix products: 143 us -> 39.5 us
  Pallas kernels: 42.4 us -> 133 us
  other arithmetic: 34.4 us -> 120 us
  local copies, waits for them, and re-layouts: 10.6 us -> 75.6 us
  blocking collectives: 39.6 us -> 0 us
  between operations: 16.1 us -> 2.96 us
    ppermute x0 -> x92, waiting for transfers between devices: none -> 439 us  [the longest x5 128 us: over_zh(): lax.ppermute(values, 'head', [(i, (i // 4 + shift) % self.nzh * 4 + i % 4...]
    reduce_scatter x7 -> x0, waiting for transfers between devices: 366 us -> none  [the longest x1 88.3 us: per_device(): lax.psum_scatter((jnp.dot(d_gate, gate_all.T, preferred_element_type=jnp....]
    all_gather x7 -> x0, waiting for transfers between devices: 354 us -> none  [the longest x1 83.6 us: per_device(): grad_group = lax.all_gather(out_grad, 'head', axis=0, tiled=True)]
    ppermute x0 -> x92, starting transfers between devices: none -> 112 us  [the longest x12 43.6 us: right(): lax.ppermute(values, 'head', [(i, i + 2) for i in range(self.head) if fir...]
    dot_general x15 -> x6, matrix products: 143 us -> 39.5 us  [the longest x4 32.4 us: weight_grad(): lax.dot_general(left, right, TN, preferred_element_type=jnp.float32)]
    pallas_call x0 -> x7, Pallas kernels: none -> 91.6 us  [the longest x4 67.8 us: ffn(): pl.pallas_call(functools.partial(ffn_kernel, count), in_specs=[pl.BlockSp...]
    psum x1 -> x0, waiting for transfers between devices: 75.3 us -> none  [per_device(): lax.psum(in_weight_grad[:, :in_weight.shape[1]].astype(jnp.bfloat16), 'dp')]
    unnamed x58 -> x184, local copies, waits for them, and re-layouts: 3.09 us -> 48.9 us
  transfers between devices with their start and end apart: 15 -> 95, of which waited for: 13 -> 30; matrix products, arithmetic and copies ran while one was open for 11% -> 22% of each run, Pallas kernels for 3% -> 14%
where the time goes in v2:
time: 956 us; the launch traced here: 947 us
  waiting for transfers between devices  450 us (47%)
  Pallas kernels  133 us (14%)
  starting transfers between devices  125 us (13%)
  other arithmetic  120 us (13%)
  local copies, waits for them, and re-layouts  75.6 us (8%)
  matrix products  39.5 us (4%)
    ppermute x5, waiting for transfers between devices, over_zh(): lax.ppermute(values, 'head', [(i, (i // 4 + shift) % self.nzh * 4 + i % 4...  128 us
    ppermute x19, waiting for transfers between devices, over_x(): return lax.ppermute(values, 'dp', [(i, i ^ 1) for i in range(self.dp)])  106 us
    ppermute x11, waiting for transfers between devices, over_y(): lax.ppermute(values, 'dp', [(i, (i // 2 + shift) % self.ny * 2 + i % 2) f...  90.5 us
    ppermute x12, waiting for transfers between devices, left(): lax.ppermute(values, 'head', [(i, i - 2) for i in range(self.head) if fir...  74.5 us
    pallas_call x4, Pallas kernels, ffn(): pl.pallas_call(functools.partial(ffn_kernel, count), in_specs=[pl.BlockSp...  67.8 us
    unnamed x184, local copies, waits for them, and re-layouts  48.9 us
    ppermute x12, starting transfers between devices, right(): lax.ppermute(values, 'head', [(i, i + 2) for i in range(self.head) if fir...  43.6 us
    dot_general x4, matrix products, weight_grad(): lax.dot_general(left, right, TN, preferred_element_type=jnp.float32)  32.4 us
  transfers between devices with their start and end apart: 95, of which 30 were waited for; matrix products, arithmetic and copies ran while one was open for 22% of the time, Pallas kernels for 14%

profile of v2, /device:TPU:0, one launch (start us, length us, event | category | flops | bytes accessed | tf_op | source)
XLA Modules:
  0.0 946.5 jit_solution(16598705372096116153)
XLA Ops:
  56.0 24.3 %collective-permute-done.13 = bf16[256,512]{1,0:T(8,128)(2,1)S(1)} collective-permute-done((bf16[256,512]{1,0:T(8,128)(2,1)S(1)}, bf16[256,512]{1,0:T(8,128)(2,1)S(1)}, u32[]{:S(2)}, u32[]{:S(2)}) %collective-permute-start.13) | collective-permute-done | bytes 262176 | tf_op jit(solution)/shard_map/ppermute | solution.py:320
  97.7 17.6 %collective-permute-done.3 = bf16[256,2048]{1,0:T(8,128)(2,1)S(1)} collective-permute-done((bf16[256,2048]{1,0:T(8,128)(2,1)S(1)}, bf16[256,2048]{1,0:T(8,128)(2,1)S(1)}, u32[]{:S(2)}, u32[]{:S(2)}) %collective-permute-start.3) | collective-permute-done | bytes 1048608 | tf_op jit(solution)/shard_map/ppermute | solution.py:320
  117.9 19.8 %collective-permute-done.35.refs_2_ = bf16[256,2048]{1,0:T(8,128)(2,1)S(1)} collective-permute-done((bf16[256,2048]{1,0:T(8,128)(2,1)}, bf16[256,2048]{1,0:T(8,128)(2,1)S(1)}, u32[]{:S(2)}, u32[]{:S(2)}) %collective-permute-start.35) | collective-permute-done | bytes 1048608 | tf_op jit(solution)/shard_map/ppermute | solution.py:307
  143.7 14.8 %collective-permute-done.4 = bf16[256,2048]{1,0:T(8,128)(2,1)S(1)} collective-permute-done((bf16[256,2048]{1,0:T(8,128)(2,1)S(1)}, bf16[256,2048]{1,0:T(8,128)(2,1)S(1)}, u32[]{:S(2)}, u32[]{:S(2)}) %collective-permute-start.4) | collective-permute-done | bytes 1048608 | tf_op jit(solution)/shard_map/ppermute | solution.py:320
  169.1 20.1 %collective-permute-done.60 = bf16[1,4,320,512]{3,2,1,0:T(8,128)(2,1)S(1)} collective-permute-done((bf16[1,4,320,512]{3,2,1,0:T(8,128)(2,1)S(1)}, bf16[1,4,320,512]{3,2,1,0:T(8,128)(2,1)S(1)}, u32[]{:S(2)}, u32[]{:S(2)}) %collective-permute-start.60) | collective-permute-done | bytes 1310752 | tf_op jit(solution)/shard_map/ppermute | solution.py:296
  198.9 11.9 %collective-permute-start.8 = (bf16[256,2048]{1,0:T(8,128)(2,1)}, bf16[256,2048]{1,0:T(8,128)(2,1)}, u32[]{:S(2)}, u32[]{:S(2)}) collective-permute-start(bf16[256,2048]{1,0:T(8,128)(2,1)} %collective-permute-done.6), channel_id=1, source_target_pairs={{4,6},{5,7},{12,14},{13,15},{20,22},{21,23},{28,30},{29,31}} | collective-permute-start | bytes 3145736 | tf_op jit(solution)/shard_map/ppermute | solution.py:315
  220.0 61.7 %collective-permute-done.22 = bf16[3,352,1024]{2,1,0:T(8,128)(2,1)S(1)} collective-permute-done((bf16[3,352,1024]{2,1,0:T(8,128)(2,1)S(1)}, bf16[3,352,1024]{2,1,0:T(8,128)(2,1)S(1)}, u32[]{:S(2)}, u32[]{:S(2)}) %collective-permute-start.22) | collective-permute-done | bytes 2162720 | tf_op jit(solution)/shard_map/ppermute | solution.py:310
  298.4 12.5 %shard_map.178 = (f32[2048,256]{1,0:T(8,128)}, f32[2048,128]{1,0:T(8,128)S(1)}, bf16[2048,256]{1,0:T(8,128)(2,1)S(1)}) custom-call(s32[3]{0:T(128)S(1)} %bitcast.131, bf16[2048,384]{1,0:T(8,128)(2,1)S(1)} %convolution_convert_fusion.5.projected_ref, f32[2048,1]{1,0:T(8,128)S(1)} %copy.32.keep_ref), custom_call_target="tpu_custom_call" | custom-call | flops 5368709120 | bytes 8388608 | tf_op jit(solution)/shard_map/pallas_call | solution.py:83
  332.0 11.1 %all-to-all-done.attended_ref = bf16[8,256,256]{2,1,0:T(8,128)(2,1)S(1)} async-done(((bf16[8,256,256]{2,1,0:T(8,128)(2,1)}), bf16[8,256,256]{2,1,0:T(8,128)(2,1)S(1)}, u32[]{:S(2)}, u32[]{:S(2)}) %all-to-all-start) | async-done | bytes 1048608 | tf_op jit(solution)/shard_map/all_to_all | solution.py:692
  350.4 31.2 %collective-permute-done.23 = bf16[3,704,1024]{2,1,0:T(8,128)(2,1)} collective-permute-done((bf16[3,704,1024]{2,1,0:T(8,128)(2,1)}, bf16[3,704,1024]{2,1,0:T(8,128)(2,1)}, u32[]{:S(2)}, u32[]{:S(2)}) %collective-permute-start.23) | collective-permute-done | bytes 4325408 | tf_op jit(solution)/shard_map/ppermute | solution.py:299
  402.9 16.9 %shard_map.180 = (bf16[512,704]{1,0:T(8,128)(2,1)}, bf16[512,704]{1,0:T(8,128)(2,1)}, bf16[512,704]{1,0:T(8,128)(2,1)}, bf16[256,2048]{1,0:T(8,128)(2,1)}, bf16[...) custom-call(bf16[256,2048]{1,0:T(8,128)(2,1)} %copy-done.10, ...), custom_call_target="tpu_custom_call" | custom-call | flops 8858370048 | bytes 20971520 | tf_op jit(solution)/shard_map/pallas_call | solution.py:634
  441.5 16.7 %shard_map.183 = (bf16[512,704]{1,0:T(8,128)(2,1)}, bf16[512,704]{1,0:T(8,128)(2,1)}, bf16[512,704]{1,0:T(8,128)(2,1)}, bf16[256,2048]{1,0:T(8,128)(2,1)}, bf16[...) custom-call(bf16[256,2048]{1,0:T(8,128)(2,1)} %collective-permute-done.31.refs_0_, ...), custom_call_target="tpu_custom_call" | custom-call | flops 8858370048 | bytes 20971520 | tf_op jit(solution)/shard_map/pallas_call | solution.py:634
  468.7 17.0 %shard_map.181 = (bf16[512,704]{1,0:T(8,128)(2,1)}, bf16[512,704]{1,0:T(8,128)(2,1)}, bf16[512,704]{1,0:T(8,128)(2,1)}, bf16[256,2048]{1,0:T(8,128)(2,1)}, bf16[...) custom-call(bf16[256,2048]{1,0:T(8,128)(2,1)} %collective-permute-done.25.refs_0_, ...), custom_call_target="tpu_custom_call" | custom-call | flops 8858370048 | bytes 20971520 | tf_op jit(solution)/shard_map/pallas_call | solution.py:634
  487.6 17.2 %shard_map.182 = (bf16[512,704]{1,0:T(8,128)(2,1)}, bf16[512,704]{1,0:T(8,128)(2,1)}, bf16[512,704]{1,0:T(8,128)(2,1)}, bf16[256,2048]{1,0:T(8,128)(2,1)}, bf16[...) custom-call(bf16[256,2048]{1,0:T(8,128)(2,1)} %get-tuple-element.144.refs_0_, ...), custom_call_target="tpu_custom_call" | custom-call | flops 8858370048 | bytes 20971520 | tf_op jit(solution)/shard_map/pallas_call | solution.py:634
  560.8 10.8 %collective-permute-done.52 = bf16[128,2048]{1,0:T(8,128)(2,1)S(1)} collective-permute-done((bf16[128,2048]{1,0:T(8,128)(2,1)S(1)}, bf16[128,2048]{1,0:T(8,128)(2,1)S(1)}, u32[]{:S(2)}, u32[]{:S(2)}) %collective-permute-start.52) | collective-permute-done | bytes 524320 | tf_op jit(solution)/shard_map/ppermute | solution.py:296
  576.7 24.4 %collective-permute-done.86 = bf16[704,1024]{1,0:T(8,128)(2,1)S(1)} collective-permute-done((bf16[704,1024]{1,0:T(8,128)(2,1)S(1)}, bf16[704,1024]{1,0:T(8,128)(2,1)S(1)}, u32[]{:S(2)}, u32[]{:S(2)}) %collective-permute-start.86) | collective-permute-done | bytes 1441824 | tf_op jit(solution)/shard_map/ppermute | solution.py:299
  604.4 26.8 %collective-permute-done.89 = bf16[704,1024]{1,0:T(8,128)(2,1)S(1)} collective-permute-done((bf16[704,1024]{1,0:T(8,128)(2,1)S(1)}, bf16[704,1024]{1,0:T(8,128)(2,1)S(1)}, u32[]{:S(2)}, u32[]{:S(2)}) %collective-permute-start.89) | collective-permute-done | bytes 1441824 | tf_op jit(solution)/shard_map/ppermute | solution.py:299
  659.3 42.7 %collective-permute-done.84 = bf16[352,1024]{1,0:T(8,128)(2,1)} collective-permute-done((bf16[352,1024]{1,0:T(8,128)(2,1)}, bf16[352,1024]{1,0:T(8,128)(2,1)}, u32[]{:S(2)}, u32[]{:S(2)}) %collective-permute-start.84) | collective-permute-done | bytes 720928 | tf_op jit(solution)/shard_map/ppermute | solution.py:310
  703.3 14.1 %collective-permute-done.87 = bf16[352,1024]{1,0:T(8,128)(2,1)} collective-permute-done((bf16[352,1024]{1,0:T(8,128)(2,1)}, bf16[352,1024]{1,0:T(8,128)(2,1)}, u32[]{:S(2)}, u32[]{:S(2)}) %collective-permute-start.87) | collective-permute-done | bytes 720928 | tf_op jit(solution)/shard_map/ppermute | solution.py:310
  748.1 21.7 %collective-permute-done.91 = bf16[352,512]{1,0:T(8,128)(2,1)S(1)} collective-permute-done((bf16[352,512]{1,0:T(8,128)(2,1)}, bf16[352,512]{1,0:T(8,128)(2,1)S(1)}, u32[]{:S(2)}, u32[]{:S(2)}) %collective-permute-start.91) | collective-permute-done | bytes 360480 | tf_op jit(solution)/shard_map/ppermute | solution.py:296
  780.9 29.3 %shard_map.185 = bf16[2048,384]{1,0:T(8,128)(2,1)} custom-call(s32[3]{0:T(128)} %bitcast.132, bf16[2048,384]{1,0:T(8,128)(2,1)} %copy-done.15, f32[2048,1]{1,0:T(8,128)} %copy-done.8, f32[2048,256]{1,0:T(8,128)} %get-tuple-element.59.y_ref, f32[2048,128]{1,0:T(8,128)} %copy-done.16, bf16[2048,256]{1,0:T(8,128)(2,1)} %bitcast.27.grad_ref), custom_call_target="tpu_custom_call" | custom-call | flops 13421772800 | bytes 12582912 | tf_op jit(solution)/shard_map/pallas_call | solution.py:198
  830.0 11.8 %collective-permute-done.68 = bf16[1024,320]{0,1:T(8,128)(2,1)S(1)} collective-permute-done((bf16[1024,320]{0,1:T(8,128)(2,1)S(1)}, bf16[1024,320]{0,1:T(8,128)(2,1)S(1)}, u32[]{:S(2)}, u32[]{:S(2)}) %collective-permute-start.68) | collective-permute-done | bytes 655392 | tf_op jit(solution)/shard_map/ppermute | solution.py:296
  850.6 17.4 %collective-permute-done.74 = bf16[4,256,512]{2,1,0:T(8,128)(2,1)S(1)} collective-permute-done((bf16[4,256,512]{2,1,0:T(8,128)(2,1)S(1)}, bf16[4,256,512]{2,1,0:T(8,128)(2,1)S(1)}, u32[]{:S(2)}, u32[]{:S(2)}) %collective-permute-start.74) | collective-permute-done | bytes 1048608 | tf_op jit(solution)/shard_map/ppermute | solution.py:296
  869.2 11.5 %collective-permute-done.71 = bf16[1024,320]{0,1:T(8,128)(2,1)S(1)} collective-permute-done((bf16[1024,320]{0,1:T(8,128)(2,1)S(1)}, bf16[1024,320]{0,1:T(8,128)(2,1)S(1)}, u32[]{:S(2)}, u32[]{:S(2)}) %collective-permute-start.71) | collective-permute-done | bytes 655392 | tf_op jit(solution)/shard_map/ppermute | solution.py:296
  (497 shorter events, 440.3 us)
Async XLA Ops:
  20.5 72.4 %collective-permute-start.20 = (bf16[256,2048]{1,0:T(8,128)(2,1)}, bf16[256,2048]{1,0:T(8,128)(2,1)}, u32[]{:S(2)}, u32[]{:S(2)}) collective-permute-start(bf16[256,2048]{1,0:T(8,128)(2,1)} %grad_ref.1), channel_id=1, source_target_pairs={{0,1},{1,0},{2,3},{3,2},{4,5},{5,4},{6,7},{7,6},{8,9},{9,8},{10,11... | collective-permute-start | bytes 3145736 | tf_op jit(solution)/shard_map/ppermute | solution.py:304
  192.4 89.3 %collective-permute-start.22 = (bf16[3,352,1024]{2,1,0:T(8,128)(2,1)S(1)}, bf16[3,352,1024]{2,1,0:T(8,128)(2,1)S(1)}, u32[]{:S(2)}, u32[]{:S(2)}) collective-permute-start(bf16[3,352,1024]{2,1,0:T(8,128)(2,1)S(1)} %pad_maximum_fusion.8), channel_id=1, source_target_pairs={{0,4},{1,5},{2,6},{3,7},{4,0},{5,1},{6,2},{7,3},{8,12},{9,13},{10,... | collective-permute-start | bytes 6488072 | tf_op jit(solution)/shard_map/ppermute | solution.py:310
  192.5 95.1 %collective-permute-start.61 = (bf16[2,4,320,512]{3,2,1,0:T(8,128)(2,1)}, bf16[2,4,320,512]{3,2,1,0:T(8,128)(2,1)}, u32[]{:S(2)}, u32[]{:S(2)}) collective-permute-start(bf16[2,4,320,512]{3,2,1,0:T(8,128)(2,1)} %maximum_select_fusion), channel_id=1, source_target_pairs={{0,16},{8,24},{16,0},{24,8},{1,17},{9,25},{17,1},{25,9},{2,18},{10... | collective-permute-start | bytes 7864328 | tf_op jit(solution)/shard_map/ppermute | solution.py:299
  212.7 103.9 %collective-permute-start.37 = (bf16[256,2048]{1,0:T(8,128)(2,1)}, bf16[256,2048]{1,0:T(8,128)(2,1)}, u32[]{:S(2)}, u32[]{:S(2)}) collective-permute-start(bf16[256,2048]{1,0:T(8,128)(2,1)} %get-tuple-element.140.refs_2_), channel_id=1, source_target_pairs={{0,1},{1,0},{2,3},{3,2},{4,5},{5,4},{6,7},{7,6},{8,9},{9,8},{10,11... | collective-permute-start | bytes 3145736 | tf_op jit(solution)/shard_map/ppermute | solution.py:304
  216.6 102.5 %collective-permute-start.18 = (bf16[4,4,256,512]{3,2,1,0:T(8,128)(2,1)}, bf16[4,4,256,512]{3,2,1,0:T(8,128)(2,1)}, u32[]{:S(2)}, u32[]{:S(2)}) collective-permute-start(bf16[4,4,256,512]{3,2,1,0:T(8,128)(2,1)} %pad_maximum_fusion.5), channel_id=1, source_target_pairs={{0,1},{1,0},{2,3},{3,2},{4,5},{5,4},{6,7},{7,6},{8,9},{9,8},{10,11... | collective-permute-start | bytes 12582920 | tf_op jit(solution)/shard_map/ppermute | solution.py:304
  219.8 73.7 %collective-permute-start.9 = (bf16[256,2048]{1,0:T(8,128)(2,1)}, bf16[256,2048]{1,0:T(8,128)(2,1)S(1)}, u32[]{:S(2)}, u32[]{:S(2)}) collective-permute-start(bf16[256,2048]{1,0:T(8,128)(2,1)} %get-tuple-element.90), channel_id=1, source_target_pairs={{0,1},{1,0},{2,3},{3,2},{4,5},{5,4},{6,7},{7,6},{8,9},{9,8},{10,11... | collective-permute-start | bytes 3145736 | tf_op jit(solution)/shard_map/ppermute | solution.py:304
  286.1 95.6 %collective-permute-start.23 = (bf16[3,704,1024]{2,1,0:T(8,128)(2,1)}, bf16[3,704,1024]{2,1,0:T(8,128)(2,1)}, u32[]{:S(2)}, u32[]{:S(2)}) collective-permute-start(bf16[3,704,1024]{2,1,0:T(8,128)(2,1)} %pad_maximum_fusion.4), channel_id=1, source_target_pairs={{0,16},{8,24},{16,0},{24,8},{1,17},{9,25},{17,1},{25,9},{2,18},{10... | collective-permute-start | bytes 12976136 | tf_op jit(solution)/shard_map/ppermute | solution.py:299
  293.6 131.7 %collective-permute-start.62 = (bf16[4,4,320,512]{3,2,1,0:T(8,128)(2,1)}, bf16[4,4,320,512]{3,2,1,0:T(8,128)(2,1)}, u32[]{:S(2)}, u32[]{:S(2)}) collective-permute-start(bf16[4,4,320,512]{3,2,1,0:T(8,128)(2,1)} %pad_maximum_fusion.3), channel_id=1, source_target_pairs={{0,1},{1,0},{2,3},{3,2},{4,5},{5,4},{6,7},{7,6},{8,9},{9,8},{10,11... | collective-permute-start | bytes 15728648 | tf_op jit(solution)/shard_map/ppermute | solution.py:304
  400.5 63.6 %collective-permute-start.30 = (bf16[128,2048]{1,0:T(8,128)(2,1)}, bf16[128,2048]{1,0:T(8,128)(2,1)}, u32[]{:S(2)}, u32[]{:S(2)}) collective-permute-start(bf16[128,2048]{1,0:T(8,128)(2,1)} %slice.245), channel_id=1, source_target_pairs={{0,2},{1,3},{2,0},{3,1},{4,6},{5,7},{6,4},{7,5},{8,10},{9,11},{10,... | collective-permute-start | bytes 1572872 | tf_op jit(solution)/shard_map/ppermute | solution.py:307
  402.3 63.9 %collective-permute-start.32 = (bf16[128,2048]{1,0:T(8,128)(2,1)}, bf16[128,2048]{1,0:T(8,128)(2,1)}, u32[]{:S(2)}, u32[]{:S(2)}) collective-permute-start(bf16[128,2048]{1,0:T(8,128)(2,1)} %slice.246), channel_id=1, source_target_pairs={{0,8},{8,0},{16,24},{24,16},{1,9},{9,1},{17,25},{25,17},{2,10},{10... | collective-permute-start | bytes 1572872 | tf_op jit(solution)/shard_map/ppermute | solution.py:296
  419.8 426.0 %collective-permute-start.24 = (bf16[256,2048]{1,0:T(8,128)(2,1)}, bf16[256,2048]{1,0:T(8,128)(2,1)}, u32[]{:S(2)}, u32[]{:S(2)}) collective-permute-start(bf16[256,2048]{1,0:T(8,128)(2,1)} %get-tuple-element.52), channel_id=1, source_target_pairs={{0,1},{1,0},{2,3},{3,2},{4,5},{5,4},{6,7},{7,6},{8,9},{9,8},{10,11... | collective-permute-start | bytes 3145736 | tf_op jit(solution)/shard_map/ppermute | solution.py:304
  458.2 74.1 %collective-permute-start.43 = (bf16[256,2048]{1,0:T(8,128)(2,1)}, bf16[256,2048]{1,0:T(8,128)(2,1)S(1)}, u32[]{:S(2)}, u32[]{:S(2)}) collective-permute-start(bf16[256,2048]{1,0:T(8,128)(2,1)} %get-tuple-element.58), channel_id=1, source_target_pairs={{0,1},{1,0},{2,3},{3,2},{4,5},{5,4},{6,7},{7,6},{8,9},{9,8},{10,11... | collective-permute-start | bytes 3145736 | tf_op jit(solution)/shard_map/ppermute | solution.py:304
  542.9 58.2 %collective-permute-start.86 = (bf16[704,1024]{1,0:T(8,128)(2,1)S(1)}, bf16[704,1024]{1,0:T(8,128)(2,1)S(1)}, u32[]{:S(2)}, u32[]{:S(2)}) collective-permute-start(bf16[704,1024]{1,0:T(8,128)(2,1)S(1)} %broadcast_select_fusion.8), channel_id=1, source_target_pairs={{0,16},{8,24},{16,0},{24,8},{1,17},{9,25},{17,1},{25,9},{2,18},{10... | collective-permute-start | bytes 4325384 | tf_op jit(solution)/shard_map/ppermute | solution.py:299
  544.0 87.3 %collective-permute-start.89 = (bf16[704,1024]{1,0:T(8,128)(2,1)S(1)}, bf16[704,1024]{1,0:T(8,128)(2,1)S(1)}, u32[]{:S(2)}, u32[]{:S(2)}) collective-permute-start(bf16[704,1024]{1,0:T(8,128)(2,1)S(1)} %broadcast_select_fusion.7), channel_id=1, source_target_pairs={{0,16},{8,24},{16,0},{24,8},{1,17},{9,25},{17,1},{25,9},{2,18},{10... | collective-permute-start | bytes 4325384 | tf_op jit(solution)/shard_map/ppermute | solution.py:299
  571.6 63.6 %collective-permute-start.50 = (bf16[256,2048]{1,0:T(8,128)(2,1)S(1)}, bf16[256,2048]{1,0:T(8,128)(2,1)S(1)}, u32[]{:S(2)}, u32[]{:S(2)}) collective-permute-start(bf16[256,2048]{1,0:T(8,128)(2,1)S(1)} %pad_maximum_fusion.16), channel_id=1, source_target_pairs={{0,8},{8,0},{16,24},{24,16},{1,9},{9,1},{17,25},{25,17},{2,10},{10... | collective-permute-start | bytes 3145736 | tf_op jit(solution)/shard_map/ppermute | solution.py:296
  573.4 61.9 %collective-permute-start.53 = (bf16[256,2048]{1,0:T(8,128)(2,1)S(1)}, bf16[256,2048]{1,0:T(8,128)(2,1)S(1)}, u32[]{:S(2)}, u32[]{:S(2)}) collective-permute-start(bf16[256,2048]{1,0:T(8,128)(2,1)S(1)} %pad_maximum_fusion.17), channel_id=1, source_target_pairs={{0,2},{1,3},{2,0},{3,1},{4,6},{5,7},{6,4},{7,5},{8,10},{9,11},{10,... | collective-permute-start | bytes 3145736 | tf_op jit(solution)/shard_map/ppermute | solution.py:307
  601.1 54.5 %collective-permute-start.44 = (bf16[128,2048]{1,0:T(8,128)(2,1)}, bf16[128,2048]{1,0:T(8,128)(2,1)}, u32[]{:S(2)}, u32[]{:S(2)}) collective-permute-start(bf16[128,2048]{1,0:T(8,128)(2,1)} %get-tuple-element.134), channel_id=1, source_target_pairs={{0,8},{8,0},{16,24},{24,16},{1,9},{9,1},{17,25},{25,17},{2,10},{10... | collective-permute-start | bytes 1572872 | tf_op jit(solution)/shard_map/ppermute | solution.py:296
  635.2 66.7 %collective-permute-start.84 = (bf16[352,1024]{1,0:T(8,128)(2,1)}, bf16[352,1024]{1,0:T(8,128)(2,1)}, u32[]{:S(2)}, u32[]{:S(2)}) collective-permute-start(bf16[352,1024]{1,0:T(8,128)(2,1)} %slice.380), channel_id=1, source_target_pairs={{0,4},{1,5},{2,6},{3,7},{4,0},{5,1},{6,2},{7,3},{8,12},{9,13},{10,... | collective-permute-start | bytes 2162696 | tf_op jit(solution)/shard_map/ppermute | solution.py:310
  635.2 82.2 %collective-permute-start.87 = (bf16[352,1024]{1,0:T(8,128)(2,1)}, bf16[352,1024]{1,0:T(8,128)(2,1)}, u32[]{:S(2)}, u32[]{:S(2)}) collective-permute-start(bf16[352,1024]{1,0:T(8,128)(2,1)} %slice.379), channel_id=1, source_target_pairs={{0,4},{1,5},{2,6},{3,7},{4,0},{5,1},{6,2},{7,3},{8,12},{9,13},{10,... | collective-permute-start | bytes 2162696 | tf_op jit(solution)/shard_map/ppermute | solution.py:310
  655.6 115.3 %collective-permute-start.72 = (bf16[4,256,2048]{2,1,0:T(8,128)(2,1)}, bf16[4,256,2048]{2,1,0:T(8,128)(2,1)}, u32[]{:S(2)}, u32[]{:S(2)}) collective-permute-start(bf16[4,256,2048]{2,1,0:T(8,128)(2,1)} %select_bitcast_fusion.2), channel_id=1, source_target_pairs={{0,1},{1,0},{2,3},{3,2},{4,5},{5,4},{6,7},{7,6},{8,9},{9,8},{10,11... | collective-permute-start | bytes 12582920 | tf_op jit(solution)/shard_map/ppermute | solution.py:304
  657.9 72.9 %collective-permute-start.90 = (bf16[352,1024]{1,0:T(8,128)(2,1)S(1)}, bf16[352,1024]{1,0:T(8,128)(2,1)S(1)}, u32[]{:S(2)}, u32[]{:S(2)}) collective-permute-start(bf16[352,1024]{1,0:T(8,128)(2,1)S(1)} %copy-done.65), channel_id=1, source_target_pairs={{0,4},{1,5},{2,6},{3,7},{4,0},{5,1},{6,2},{7,3},{8,12},{9,13},{10,... | collective-permute-start | bytes 2162696 | tf_op jit(solution)/shard_map/ppermute | solution.py:310
  702.0 143.8 %collective-permute-start.45 = (bf16[256,2048]{1,0:T(8,128)(2,1)}, bf16[256,2048]{1,0:T(8,128)(2,1)}, u32[]{:S(2)}, u32[]{:S(2)}) collective-permute-start(bf16[256,2048]{1,0:T(8,128)(2,1)} %pad_maximum_fusion.15), channel_id=1, source_target_pairs={{0,2},{1,3},{2,0},{3,1},{4,6},{5,7},{6,4},{7,5},{8,10},{9,11},{10,... | collective-permute-start | bytes 3145736 | tf_op jit(solution)/shard_map/ppermute | solution.py:307
  733.4 112.3 %collective-permute-start.40 = (bf16[256,2048]{1,0:T(8,128)(2,1)}, bf16[256,2048]{1,0:T(8,128)(2,1)}, u32[]{:S(2)}, u32[]{:S(2)}) collective-permute-start(bf16[256,2048]{1,0:T(8,128)(2,1)} %pad_maximum_fusion.14), channel_id=1, source_target_pairs={{0,8},{8,0},{16,24},{24,16},{1,9},{9,1},{17,25},{25,17},{2,10},{10... | collective-permute-start | bytes 3145736 | tf_op jit(solution)/shard_map/ppermute | solution.py:296
  812.7 70.9 %all-to-all-start.2 = ((bf16[8,256,320]{1,2,0:T(8,128)(2,1)}), bf16[8,256,320]{1,2,0:T(8,128)(2,1)}, u32[]{:S(2)}, u32[]{:S(2)}) async-start(bf16[8,256,320]{1,2,0:T(8,128)(2,1)} %copy.35), calls=%async_computation.2 | async-start | bytes 2621440 | tf_op jit(solution)/shard_map/all_to_all | solution.py:692
  (155 other events, 3572.8 us)

commit v3 on v1

v3 whole, which is shorter than its diff:
```python
import functools
import jax
import jax.numpy as jnp
from jax import lax
from jax.experimental import pallas as pl
from jax.experimental.pallas import tpu as pltpu
from jax.sharding import PartitionSpec as P

FD = 16
VD = 128
LANES = 128
VMEM = 60 * 1024 * 1024
epsilon = 1e-05
NT = (((1,), (1,)), ((), ()))
TN = (((0,), (0,)), ((), ()))


def head_lanes(block, rows, head, offset):
    lane = lax.broadcasted_iota(jnp.int32, (rows, LANES), 1)
    low = offset + head * FD
    return jnp.where((lane >= low) & (lane < low + FD), block, 0.0)


def segment_start(ends_ref, positions):
    start = jnp.zeros_like(positions)
    for slot in range(ends_ref.shape[0]):
        end = ends_ref[slot]
        start = jnp.where(positions >= end, jnp.maximum(start, end), start)
    return start


def attend_kernel(heads, rows, pieces, ends_ref, at_ref, *refs):
    sources = refs[:pieces]
    weight_ref, keep_ref, projected_ref, normed_ref, y_ref, inv_ref, att_ref = refs[pieces : pieces + 7]
    normed_s, key_s, value_s, sems = refs[pieces + 7 :]
    step = pl.program_id(0)
    own = pl.ds(pl.multiple_of(step * rows, rows), rows)

    @pl.when(step == 0)
    def _():
        size = sources[0].shape[0]
        copies = [
            pltpu.make_async_copy(
                sources[i].at[:, pl.ds(0, normed_s.shape[1])], normed_s.at[pl.ds(pl.multiple_of(at_ref[i], size), size), :], sems.at[i]
            )
            for i in range(pieces)
        ]
        for copy in copies:
            copy.start()
        for copy in copies:
            copy.wait()

    keep = keep_ref[own, :]
    normed = normed_s[own, :]
    normed_ref[...] = normed
    projected = jnp.dot(normed, weight_ref[...], preferred_element_type=jnp.float32).astype(jnp.bfloat16)
    projected_ref[...] = projected
    packed = projected[:, heads * VD :].astype(jnp.float32)
    key_s[own, :] = pltpu.roll(packed, LANES - heads * FD, 1).astype(jnp.bfloat16)
    lane = lax.broadcasted_iota(jnp.int32, (rows, LANES), 1)
    ones = jnp.where(lane < 2, keep, 0.0).astype(jnp.bfloat16)
    for head in range(heads):
        value_s[head, own, :VD] = (
            projected[:, head * VD : (head + 1) * VD].astype(jnp.float32) * keep
        ).astype(jnp.bfloat16)
        value_s[head, own, VD:] = ones
    queries = [(head_lanes(packed, rows, head, 0) * 0.25).astype(jnp.bfloat16) for head in range(heads)]
    row = step * rows + lax.broadcasted_iota(jnp.int32, (rows, 1), 0)
    start = segment_start(ends_ref, row)
    column = lax.broadcasted_iota(jnp.int32, (rows, rows), 1)

    def tile(block, totals, diagonal):
        at = pl.ds(pl.multiple_of(block * rows, rows), rows)
        allowed = column >= start - block * rows
        if diagonal:
            allowed &= column <= lax.broadcasted_iota(jnp.int32, (rows, rows), 0)
        keys = key_s[at, :]
        added = []
        for head in range(heads):
            inner = lax.dot_general(queries[head], keys, NT, preferred_element_type=jnp.float32)
            weights = jnp.where(allowed, (inner * 0.5 + 1.0) * inner + 1.0, 0.0).astype(jnp.bfloat16)
            added.append(
                totals[head]
                + jnp.dot(weights, value_s[head, at, :], preferred_element_type=jnp.float32)
            )
        return tuple(added)

    totals = tuple(jnp.zeros((rows, 2 * VD), jnp.float32) for _ in range(heads))
    totals = lax.fori_loop(0, step, lambda block, held: tile(block, held, False), totals)
    totals = tile(step, totals, True)
    inverses = jnp.zeros((rows, LANES), jnp.float32)
    for head in range(heads):
        inverse = 1.0 / (totals[head][:, VD : VD + 1] + 1.0 - keep)
        y = totals[head][:, :VD] * (keep * inverse)
        y_ref[:, head * VD : (head + 1) * VD] = y
        att_ref[:, head * VD : (head + 1) * VD] = y.astype(jnp.bfloat16)
        inverses = jnp.where(lane == head, inverse, inverses)
    inv_ref[...] = inverses


def attend(pieces, places, weight, keep, ends, heads):
    size, depth = pieces[0].shape[0], weight.shape[0]
    total = size * len(pieces)
    rows = min(512, total)
    width = weight.shape[1]
    pairs = total * (total + rows) // 2 * heads
    blocked = lambda columns: pl.BlockSpec((rows, columns), lambda i, e, a: (i, 0))
    return pl.pallas_call(
        functools.partial(attend_kernel, heads, rows, len(pieces)),
        grid_spec=pltpu.PrefetchScalarGridSpec(
            num_scalar_prefetch=2,
            grid=(total // rows,),
            in_specs=[pl.BlockSpec(memory_space=pl.ANY)] * len(pieces)
            + [
                pl.BlockSpec((depth, width), lambda i, e, a: (0, 0)),
                pl.BlockSpec((total, 1), lambda i, e, a: (0, 0)),
            ],
            out_specs=[
                blocked(width), blocked(depth), blocked(heads * VD), blocked(LANES), blocked(heads * VD)
            ],
            scratch_shapes=[
                pltpu.VMEM((total, depth), jnp.bfloat16),
                pltpu.VMEM((total, LANES), jnp.bfloat16),
                pltpu.VMEM((heads, total, 2 * VD), jnp.bfloat16),
                pltpu.SemaphoreType.DMA((len(pieces),)),
            ],
        ),
        out_shape=[
            jax.ShapeDtypeStruct((total, width), jnp.bfloat16),
            jax.ShapeDtypeStruct((total, depth), jnp.bfloat16),
            jax.ShapeDtypeStruct((total, heads * VD), jnp.float32),
            jax.ShapeDtypeStruct((total, LANES), jnp.float32),
            jax.ShapeDtypeStruct((total, heads * VD), jnp.bfloat16),
        ],
        compiler_params=pltpu.CompilerParams(
            dimension_semantics=("arbitrary",), vmem_limit_bytes=VMEM
        ),
        cost_estimate=pl.CostEstimate(
            flops=pairs * 1024 + 2 * total * depth * width, bytes_accessed=28 << 20, transcendentals=0
        ),
    )(ends, places, *pieces, weight, keep)


def attend_back_kernel(
    heads, rows, ends_ref, projected_ref, keep_ref, y_ref, inv_ref, grad_ref, out_ref,
    key_s, query_s, value_s, error_s, dquery_s,
):
    step = pl.program_id(0)
    blocks = pl.num_programs(0)
    lane = lax.broadcasted_iota(jnp.int32, (rows, LANES), 1)

    @pl.when(step == 0)
    def _():
        dquery_s[...] = jnp.zeros_like(dquery_s)

        def fill(block, nothing):
            at = pl.ds(pl.multiple_of(block * rows, rows), rows)
            keep = keep_ref[at, :]
            packed = projected_ref[at, heads * VD :].astype(jnp.float32)
            rolled = pltpu.roll(packed, LANES - heads * FD, 1)
            ones = jnp.where(lane < 2, keep, 0.0).astype(jnp.bfloat16)
            inverses = inv_ref[at, :]
            for head in range(heads):
                columns = slice(head * VD, (head + 1) * VD)
                key_s[head, at, :] = head_lanes(rolled, rows, head, 0).astype(jnp.bfloat16)
                query_s[head, at, :] = (head_lanes(packed, rows, head, 0) * 0.25).astype(jnp.bfloat16)
                value_s[head, at, :VD] = (projected_ref[at, columns].astype(jnp.float32) * keep).astype(jnp.bfloat16)
                value_s[head, at, VD:] = ones
                inverse = inverses[:, head : head + 1]
                grad = grad_ref[at, columns].astype(jnp.float32)
                error_s[head, at, :VD] = (grad * (keep * inverse)).astype(jnp.bfloat16)
                offset = -jnp.sum(grad * y_ref[at, columns], axis=1, keepdims=True) * inverse
                high = offset.astype(jnp.bfloat16).astype(jnp.float32)
                error_s[head, at, VD:] = jnp.where(
                    lane == 0, high, jnp.where(lane == 1, offset - high, 0.0)
                ).astype(jnp.bfloat16)
            return nothing

        lax.fori_loop(0, blocks, fill, 0)

    own = pl.ds(pl.multiple_of(step * rows, rows), rows)
    row = lax.broadcasted_iota(jnp.int32, (rows, rows), 0)

    def tile(block, totals, diagonal):
        at = pl.ds(pl.multiple_of(block * rows, rows), rows)
        column = block * rows + lax.broadcasted_iota(jnp.int32, (1, rows), 1)
        allowed = row >= segment_start(ends_ref, column) - step * rows
        if diagonal:
            allowed &= row <= lax.broadcasted_iota(jnp.int32, (rows, rows), 1)
        dkey, dvalues = totals
        added = []
        for head in range(heads):
            query = query_s[head, at, :]
            error = error_s[head, at, :]
            keys = key_s[head, own, :]
            inner = lax.dot_general(keys, query, NT, preferred_element_type=jnp.float32)
            dweight = lax.dot_general(value_s[head, own, :], error, NT, preferred_element_type=jnp.float32)
            slope = inner + 1.0
            weights = jnp.where(allowed, (slope * slope + 1.0) * 0.5, 0.0).astype(jnp.bfloat16)
            dinner = jnp.where(allowed, slope * dweight, 0.0).astype(jnp.bfloat16)
            added.append(
                dvalues[head] + jnp.dot(weights, error[:, :VD], preferred_element_type=jnp.float32)
            )
            dkey = dkey + jnp.dot(dinner, query, preferred_element_type=jnp.float32)
            dquery_s[at, :] += lax.dot_general(dinner, keys, TN, preferred_element_type=jnp.float32)
        return dkey, tuple(added)

    totals = (
        jnp.zeros((rows, LANES), jnp.float32),
        tuple(jnp.zeros((rows, VD), jnp.float32) for _ in range(heads)),
    )
    totals = tile(step, totals, True)
    dkey, dvalues = lax.fori_loop(step + 1, blocks, lambda block, held: tile(block, held, False), totals)
    keep = keep_ref[own, :]
    for head in range(heads):
        out_ref[:, head * VD : (head + 1) * VD] = (dvalues[head] * keep).astype(jnp.bfloat16)
    packed = (dquery_s[own, :] * 0.25 + pltpu.roll(dkey, heads * FD, 1)).astype(jnp.bfloat16)
    out_ref[:, heads * VD :] = packed[:, : 2 * heads * FD]


def attend_back(projected, keep, ends, y, inverses, grad, heads):
    total = projected.shape[0]
    rows = min(512, total)
    width = projected.shape[1]
    pairs = total * (total + rows) // 2 * heads
    packed = heads * (2 * FD + VD)
    whole = lambda columns: pl.BlockSpec((total, columns), lambda i, e: (0, 0))
    return pl.pallas_call(
        functools.partial(attend_back_kernel, heads, rows),
        grid_spec=pltpu.PrefetchScalarGridSpec(
            num_scalar_prefetch=1,
            grid=(total // rows,),
            in_specs=[whole(width), whole(1), whole(heads * VD), whole(LANES), whole(heads * VD)],
            out_specs=pl.BlockSpec((rows, packed), lambda i, e: (i, 0)),
            scratch_shapes=[
                pltpu.VMEM((heads, total, LANES), jnp.bfloat16),
                pltpu.VMEM((heads, total, LANES), jnp.bfloat16),
                pltpu.VMEM((heads, total, 2 * VD), jnp.bfloat16),
                pltpu.VMEM((heads, total, 2 * VD), jnp.bfloat16),
                pltpu.VMEM((total, LANES), jnp.float32),
            ],
        ),
        out_shape=jax.ShapeDtypeStruct((total, packed), jnp.bfloat16),
        compiler_params=pltpu.CompilerParams(
            dimension_semantics=("arbitrary",), vmem_limit_bytes=VMEM
        ),
        cost_estimate=pl.CostEstimate(flops=pairs * 2560, bytes_accessed=12 << 20, transcendentals=0),
    )(ends, projected, keep, y, inverses, grad)


def pack_columns(weight, heads):
    depth = weight.shape[0]
    per_head = weight.reshape(depth, heads, 2 * FD + VD)
    return jnp.concatenate(
        [
            per_head[:, :, 2 * FD :].reshape(depth, heads * VD),
            per_head[:, :, :FD].reshape(depth, heads * FD),
            per_head[:, :, FD : 2 * FD].reshape(depth, heads * FD),
        ],
        axis=1,
    )


def unpack_columns(packed, heads):
    depth = packed.shape[0]
    wide, narrow = heads * VD, heads * FD
    return jnp.concatenate(
        [
            packed[:, wide : wide + narrow].reshape(depth, heads, FD),
            packed[:, wide + narrow : wide + 2 * narrow].reshape(depth, heads, FD),
            packed[:, :wide].reshape(depth, heads, VD),
        ],
        axis=2,
    ).reshape(depth, heads * (2 * FD + VD))


def inv_root_mean(values):
    return lax.rsqrt(jnp.mean(values * values, axis=1, keepdims=True) + epsilon)


def wide(values):
    return values.astype(jnp.float32)


def low(values):
    return values.astype(jnp.bfloat16)


def pick(values, index, count, axis):
    size = values.shape[axis] // count
    if count == 2:
        first = lax.slice_in_dim(values, 0, size, axis=axis)
        second = lax.slice_in_dim(values, size, 2 * size, axis=axis)
        return jnp.where(index == 0, first, second)
    return lax.dynamic_slice_in_dim(values, index * size, size, axis)


def in_order(pieces, index, axis):
    count = len(pieces)
    if count == 1:
        return pieces[0]
    if count == 2:
        first = jnp.where(index == 0, pieces[0], pieces[1])
        second = jnp.where(index == 0, pieces[1], pieces[0])
        return jnp.concatenate([first, second], axis=axis)
    stacked = jnp.stack(pieces)
    placed = [
        lax.dynamic_index_in_dim(stacked, (index - place) % count, 0, keepdims=False)
        for place in range(count)
    ]
    return jnp.concatenate(placed, axis=axis)


class Wires:
    def __init__(self, mesh):
        self.dp, self.head = mesh.shape["dp"], mesh.shape["head"]
        self.ny, self.nz, self.nzh = self.dp // 2, self.head // 2, self.head // 4

    def place(self):
        p, h = lax.axis_index("dp"), lax.axis_index("head")
        self.p, self.h = p, h
        self.y, self.x, self.z, self.c = p // 2, p % 2, h // 2, h % 2
        self.zh = self.z // 2

    def over_x(self, values):
        return lax.ppermute(values, "dp", [(i, i ^ 1) for i in range(self.dp)])

    def over_y(self, values, shift):
        return lax.ppermute(
            values, "dp", [(i, ((i // 2 + shift) % self.ny) * 2 + i % 2) for i in range(self.dp)]
        )

    def over_core(self, values):
        return lax.ppermute(values, "head", [(i, i ^ 1) for i in range(self.head)])

    def over_zl(self, values):
        return lax.ppermute(values, "head", [(i, i ^ 2) for i in range(self.head)])

    def over_zh(self, values, shift):
        return lax.ppermute(
            values, "head", [(i, ((i // 4 + shift) % self.nzh) * 4 + i % 4) for i in range(self.head)]
        )

    def over_z(self, values, shift):
        return lax.ppermute(
            values, "head", [(i, ((i // 2 + shift) % self.nz) * 2 + i % 2) for i in range(self.head)]
        )

    def right(self, values, first, last):
        return lax.ppermute(
            values, "head", [(i, i + 2) for i in range(self.head) if first <= i // 2 <= last]
        )

    def left(self, values, first, last):
        return lax.ppermute(
            values, "head", [(i, i - 2) for i in range(self.head) if first <= i // 2 <= last]
        )

    def spread(self, line):
        return self.over_x(line), [self.over_y(line, s) for s in range(1, self.ny)]

    def ends(self, values):
        pairs = [(i, i + 2 if i // 2 == self.nz - 2 else i - 2) for i in range(self.head)]
        return lax.ppermute(
            values, "head", [pair for pair in pairs if pair[0] // 2 in (1, self.nz - 2)]
        )

    def arrivals(self):
        orders = []
        for z in range(self.nz):
            order = []
            for step in range(1, self.nz):
                order += [(0, step)] if z >= step else []
                order += [(1, step)] if z + step < self.nz else []
            orders.append(order)
        return orders

    def by_place(self, values):
        chosen, taken = values[0], [values[0]]
        for value in values[1:]:
            if any(value is other for other in taken):
                continue
            taken.append(value)
            here = [z for z in range(self.nz) if values[z] is value]
            chosen = jnp.where(sum((self.z == z).astype(jnp.int32) for z in here) > 0, value, chosen)
        return chosen

    def sum_y(self, values):
        total = wide(values)
        for s in range(1, self.ny):
            total = total + wide(self.over_y(values, s))
        return low(total)

    def sum_x(self, values):
        return low(wide(values) + wide(self.over_x(values)))

    def sum_all(self, values):
        values = values + self.over_core(values)
        values = values + self.over_zl(values)
        values = values + sum(self.over_zh(values, s) for s in range(1, self.nzh))
        values = values + self.over_x(values)
        return values + sum(self.over_y(values, s) for s in range(1, self.ny))

    def quarter(self, shard):
        size = shard.shape[1] // self.dp
        return lax.dynamic_slice_in_dim(shard, self.p * size, size, 1)

    def line_of(self, part):
        return [part] + [self.over_z(part, s) for s in range(1, self.nz)]

    def whole_places(self, chips, rows, size):
        at_rows = [(chip * 2 + (self.c ^ r)) * rows for r in range(2) for chip in chips]
        at_columns = [
            (((self.y - s) % self.ny) * 2 + (self.x ^ t)) * size
            for s in range(self.ny)
            for t in range(2)
        ]
        return jnp.stack(at_rows + at_columns).astype(jnp.int32)

    def line(self, block, during):
        steps = self.nz
        right = left = block
        rights, lefts = {}, {}
        orders = self.arrivals()
        chunks, chips = [block], [self.z]
        for step in range(1, steps):
            if step < steps - 1:
                right = self.right(right, step - 1, steps - 2)
                left = self.left(left, 1, steps - step)
                right, left = during(step, (right, left))
            else:
                both = jnp.where(self.z == steps - 2, right, left)
                (right, both) = during(step, (self.ends(both), both))
                left = right
            rights[step], lefts[step] = right, left
            arrived = {(0, s): rights[s] for s in rights} | {(1, s): lefts[s] for s in lefts}
            while len(chunks) < steps and all(
                orders[z][len(chunks) - 1] in arrived for z in range(steps)
            ):
                order = [orders[z][len(chunks) - 1] for z in range(steps)]
                values = [arrived[key] for key in order]
                if step == steps - 1 and values[1] is lefts[steps - 2] and values[-2] is rights[steps - 2]:
                    values[1] = values[-2] = both
                chunks.append(self.by_place(values))
                chips.append(
                    self.by_place([z - key[1] * (1 - 2 * key[0]) for z, key in enumerate(order)])
                )
        return chunks, chips


class Whole:
    def __init__(self, wires, pieces, places, rows, size):
        self.layout = [(s, t, 0, wires.nz) for s in range(wires.ny) for t in range(2)]
        self.nz = wires.nz
        self.pieces, self.rows, self.size = pieces, rows, size
        self.places = places
        self.copies = 2 * sum(count for _, _, _, count in self.layout)
        self.shape = (wires.head * rows, wires.dp * size)

    def fill(self, places_ref, refs, scratch, sems):
        copies = []
        for core in range(2):
            for piece, (s, t, first, count) in enumerate(self.layout):
                column = pl.multiple_of(places_ref[2 * self.nz + 2 * s + t], self.size)
                for slot in range(count):
                    row = pl.multiple_of(places_ref[core * self.nz + first + slot], self.rows)
                    copies.append(
                        pltpu.make_async_copy(
                            refs[core * len(self.layout) + piece].at[slot],
                            scratch.at[pl.ds(row, self.rows), pl.ds(column, self.size)],
                            sems.at[len(copies)],
                        )
                    )
        for copy in copies:
            copy.start()
        return copies


def swapped(wires, pieces):
    return [*pieces, *[wires.over_core(piece) for piece in pieces]]


def side_by_side(blocks_ref):
    return jnp.concatenate([blocks_ref[i] for i in range(blocks_ref.shape[0])], axis=1)


def mix_kernel(whole, places_ref, *refs):
    count = len(whole.pieces)
    attended_ref, tokens_ref, gain_ref, middle_ref, normed_ref, weight_s, sems = refs[count:]
    for copy in whole.fill(places_ref, refs[:count], weight_s, sems):
        copy.wait()
    middle = jnp.dot(
        side_by_side(attended_ref), weight_s[...], preferred_element_type=jnp.float32
    ) + wide(tokens_ref[...])
    middle_ref[...] = middle
    normed_ref[...] = (middle * inv_root_mean(middle) * gain_ref[...]).astype(jnp.bfloat16)


def with_whole(kernel, whole, args, outs, flops):
    in_vmem = pl.BlockSpec(memory_space=pltpu.VMEM)
    return pl.pallas_call(
        functools.partial(kernel, whole),
        grid_spec=pltpu.PrefetchScalarGridSpec(
            num_scalar_prefetch=1,
            grid=(),
            in_specs=[pl.BlockSpec(memory_space=pl.ANY)] * len(whole.pieces) + [in_vmem] * len(args),
            out_specs=[in_vmem] * len(outs),
            scratch_shapes=[
                pltpu.VMEM(whole.shape, jnp.bfloat16),
                pltpu.SemaphoreType.DMA((whole.copies,)),
            ],
        ),
        out_shape=[jax.ShapeDtypeStruct(shape, kind) for shape, kind in outs],
        compiler_params=pltpu.CompilerParams(vmem_limit_bytes=VMEM),
        cost_estimate=pl.CostEstimate(flops=flops, bytes_accessed=16 << 20, transcendentals=0),
    )(whole.places, *whole.pieces, *args)


def mix(attended, whole, tokens, gain):
    return with_whole(
        mix_kernel,
        whole,
        (attended, tokens, gain),
        ((tokens.shape, jnp.float32), (tokens.shape, jnp.bfloat16)),
        2 * tokens.shape[0] * whole.shape[0] * whole.shape[1],
    )


def unmix_kernel(whole, places_ref, *refs):
    count = len(whole.pieces)
    a_ref, b_ref, c_ref, middle_ref, grad_ref, gain_ref = refs[count : count + 6]
    dmiddle_ref, dmixed_ref, part_ref, out_ref, weight_s, sems = refs[count + 6 :]
    copies = whole.fill(places_ref, refs[:count], weight_s, sems)
    middle = middle_ref[...]
    inv_two = inv_root_mean(middle)
    dnormed = wide(a_ref[...]) + wide(b_ref[...]) + wide(c_ref[...])
    scaled = middle * inv_two
    error = dnormed * gain_ref[...]
    dmiddle = wide(grad_ref[...]) + inv_two * (
        error - scaled * jnp.mean(error * scaled, axis=1, keepdims=True)
    )
    part_ref[...] = jnp.sum(dnormed * scaled, axis=0, keepdims=True)
    dmiddle_ref[...] = dmiddle
    dmixed = dmiddle.astype(jnp.bfloat16)
    dmixed_ref[...] = dmixed
    for copy in copies:
        copy.wait()
    width = out_ref.shape[2]
    for head in range(out_ref.shape[0]):
        out_ref[head] = lax.dot_general(
            dmixed, weight_s[head * width : (head + 1) * width, :], NT, preferred_element_type=jnp.float32
        ).astype(jnp.bfloat16)


def unmix(parts, middle, grad, gain, whole, heads):
    rows, depth = middle.shape
    return with_whole(
        unmix_kernel,
        whole,
        (*parts, middle, grad, gain),
        (
            (middle.shape, jnp.float32),
            (middle.shape, jnp.bfloat16),
            ((1, depth), jnp.float32),
            ((heads, rows, whole.shape[0] // heads), jnp.bfloat16),
        ),
        2 * rows * whole.shape[0] * whole.shape[1],
    )


def last_kernel(whole, places_ref, *refs):
    count = len(whole.pieces)
    proj_ref, tokens_ref, dmiddle_ref, gain_ref, grad_ref, weight_s, sems = refs[count:]
    for copy in whole.fill(places_ref, refs[:count], weight_s, sems):
        copy.wait()
    width = proj_ref.shape[2]
    dnormed = jnp.zeros(grad_ref.shape, jnp.float32)
    for head in range(proj_ref.shape[0]):
        dnormed += jnp.dot(
            proj_ref[head],
            weight_s[head * width : (head + 1) * width, :],
            preferred_element_type=jnp.float32,
        )
    tokens = wide(tokens_ref[...])
    inv_one = inv_root_mean(tokens)
    scaled = tokens * inv_one
    error = dnormed * gain_ref[...]
    grad_ref[...] = dmiddle_ref[...] + inv_one * (
        error - scaled * jnp.mean(error * scaled, axis=1, keepdims=True)
    )


def last(proj, whole, tokens, dmiddle, gain):
    return with_whole(
        last_kernel,
        whole,
        (proj, tokens, dmiddle, gain),
        ((tokens.shape, jnp.float32),),
        2 * tokens.shape[0] * whole.shape[0] * whole.shape[1],
    )[0]


class Units:
    def __init__(self, wires, pieces, matrices, rows, columns):
        self.matrices = matrices
        self.layout = [piece[1:] for piece in pieces]
        self.pieces = [piece[0] for piece in pieces]
        self.rows, self.columns = rows, columns
        self.places = jnp.stack([((wires.y - s) % wires.ny) * columns for s in range(wires.ny)]).astype(
            jnp.int32
        )
        self.shape = (matrices, wires.nzh * rows, wires.ny * columns)

    def fill(self, places_ref, refs, scratch, sems):
        copies = []
        for matrix in range(self.matrices):
            for ref, (first, count, zh, y) in zip(refs, self.layout):
                if not first <= matrix < first + count:
                    continue
                column = pl.multiple_of(places_ref[y], self.columns)
                copies.append(
                    pltpu.make_async_copy(
                        ref.at[matrix - first],
                        scratch.at[
                            matrix, pl.ds(zh * self.rows, self.rows), pl.ds(column, self.columns)
                        ],
                        sems.at[len(copies)],
                    )
                )
        for copy in copies:
            copy.start()
        return copies


def gate_kernel(units, places_ref, *refs):
    pieces, refs = refs[: len(units.pieces)], refs[len(units.pieces) :]
    blocks, (gate_ref, up_ref, normed_ref, weight_s, sems, in_sems) = refs[:2], refs[2:]
    rows = blocks[0].shape[0]
    copies = [
        pltpu.make_async_copy(blocks[i], normed_ref.at[pl.ds(i * rows, rows)], in_sems.at[i])
        for i in range(2)
    ]
    for copy in copies:
        copy.start()
    weights = units.fill(places_ref, pieces, weight_s, sems)
    each = len(weights) // units.matrices
    for copy in copies + weights[:each]:
        copy.wait()
    normed = normed_ref[...]
    gate_ref[...] = lax.dot_general(normed, weight_s[0], NT, preferred_element_type=jnp.float32)
    for copy in weights[each:]:
        copy.wait()
    up_ref[...] = lax.dot_general(normed, weight_s[1], NT, preferred_element_type=jnp.float32)


def with_units(kernel, units, blocks, values, outs, flops, transcendentals):
    in_vmem, anywhere = pl.BlockSpec(memory_space=pltpu.VMEM), pl.BlockSpec(memory_space=pl.ANY)
    copies = sum(count for _, count, _, _ in units.layout)
    return pl.pallas_call(
        functools.partial(kernel, units),
        grid_spec=pltpu.PrefetchScalarGridSpec(
            num_scalar_prefetch=1,
            grid=(),
            in_specs=[anywhere] * (len(units.pieces) + len(blocks)) + [in_vmem] * len(values),
            out_specs=[in_vmem] * len(outs),
            scratch_shapes=[
                pltpu.VMEM(units.shape, jnp.bfloat16),
                pltpu.SemaphoreType.DMA((copies,)),
                pltpu.SemaphoreType.DMA((len(blocks),)),
            ],
        ),
        out_shape=[jax.ShapeDtypeStruct(shape, kind) for shape, kind in outs],
        compiler_params=pltpu.CompilerParams(vmem_limit_bytes=VMEM),
        cost_estimate=pl.CostEstimate(
            flops=flops, bytes_accessed=20 << 20, transcendentals=transcendentals
        ),
    )(units.places, *units.pieces, *blocks, *values)


def gate_up(pair, units):
    rows, depth = pair[0].shape
    out = ((2 * rows, units.shape[1]), jnp.float32)
    return with_units(
        gate_kernel,
        units,
        pair,
        (),
        (out, out, ((2 * rows, depth), jnp.bfloat16)),
        8 * rows * depth * units.shape[1],
        0,
    )


def down_kernel(units, places_ref, *refs):
    pieces, refs = refs[: len(units.pieces)], refs[len(units.pieces) :]
    grads, (gate_ref, up_ref) = refs[:2], refs[2:4]
    hidden_ref, dgate_ref, dup_ref, grad_ref = refs[4:8]
    dnormed, branches = refs[8:10], refs[10:12]
    weight_s, sems, in_sems = refs[12:]
    rows = grads[0].shape[0]
    both = [slice(0, rows), slice(rows, 2 * rows)]
    copies = [
        pltpu.make_async_copy(grads[i], grad_ref.at[both[i]], in_sems.at[i]) for i in range(2)
    ]
    for copy in copies:
        copy.start()
    weights = units.fill(places_ref, pieces, weight_s, sems)
    each = len(weights) // units.matrices
    gate, up = gate_ref[...], up_ref[...]
    sigmoid = jax.nn.sigmoid(gate)
    silu = gate * sigmoid
    hidden = (silu * up).astype(jnp.bfloat16)
    hidden_ref[...] = hidden
    dot = functools.partial(jnp.dot, preferred_element_type=jnp.float32)
    for copy in copies + weights[:each]:
        copy.wait()
    dhidden = lax.dot_general(grad_ref[...], weight_s[0], NT, preferred_element_type=jnp.float32)
    branch = dot(hidden, weight_s[0]).astype(jnp.bfloat16)
    dgate = (dhidden * up * sigmoid * (1.0 + gate * (1.0 - sigmoid))).astype(jnp.bfloat16)
    dup = (dhidden * silu).astype(jnp.bfloat16)
    dgate_ref[...] = dgate
    dup_ref[...] = dup
    for copy in weights[each:]:
        copy.wait()
    back = (dot(dgate, weight_s[1]) + dot(dup, weight_s[2])).astype(jnp.bfloat16)
    for i in range(2):
        branches[i][...] = branch[both[i]]
        dnormed[i][...] = back[both[i]]


def down(grads, gate, up, units):
    rows, depth = grads[0].shape
    unit = (gate.shape, jnp.bfloat16)
    part = ((rows, depth), jnp.bfloat16)
    outs = with_units(
        down_kernel,
        units,
        grads,
        (gate, up),
        (unit, unit, unit, ((2 * rows, depth), jnp.bfloat16), part, part, part, part),
        16 * rows * depth * units.shape[1],
        2 * rows * units.shape[1],
    )
    return outs[:4], outs[4:6], outs[6:]


def unit_grad_kernel(count, ny, nzh, places_ref, *refs):
    lefts, rights = refs[:count], refs[count : 2 * count]
    mine_ref, sent_ref, total_s = refs[2 * count :]
    for i in range(count):
        added = lax.dot_general(lefts[i][...], rights[i][...], TN, preferred_element_type=jnp.float32)
        if i == 0:
            total_s[...] = added
        else:
            total_s[...] += added
    units, columns = mine_ref.shape[1:]
    for y in range(ny):
        for zh in range(nzh):
            block = total_s[
                pl.ds(pl.multiple_of(places_ref[ny + zh], units), units),
                pl.ds(pl.multiple_of(places_ref[y], columns), columns),
            ].astype(jnp.bfloat16)
            if y == 0:
                mine_ref[zh] = block
            else:
                sent_ref[y - 1, zh] = block


def unit_grad(wires, lefts, rights):
    ny, nzh = wires.ny, wires.nzh
    units, depth = lefts[0].shape[1], rights[0].shape[1]
    rows, columns = units // nzh, depth // ny
    places = jnp.stack(
        [((wires.y + s) % ny) * columns for s in range(ny)]
        + [s * rows for s in range(nzh)]
    ).astype(jnp.int32)
    in_vmem = pl.BlockSpec(memory_space=pltpu.VMEM)
    tokens = sum(left.shape[0] for left in lefts)
    return pl.pallas_call(
        functools.partial(unit_grad_kernel, len(lefts), ny, nzh),
        grid_spec=pltpu.PrefetchScalarGridSpec(
            num_scalar_prefetch=1,
            grid=(),
            in_specs=[in_vmem] * (2 * len(lefts)),
            out_specs=[in_vmem] * 2,
            scratch_shapes=[pltpu.VMEM((units, depth), jnp.float32)],
        ),
        out_shape=[
            jax.ShapeDtypeStruct((nzh, rows, columns), jnp.bfloat16),
            jax.ShapeDtypeStruct((ny - 1, nzh, rows, columns), jnp.bfloat16),
        ],
        compiler_params=pltpu.CompilerParams(vmem_limit_bytes=VMEM),
        cost_estimate=pl.CostEstimate(
            flops=2 * tokens * depth * units, bytes_accessed=14 << 20, transcendentals=0
        ),
    )(places, *lefts, *rights)


def out_grad_kernel(nz, ny, places_ref, left_ref, right_ref, mine_ref, sent_ref):
    step = pl.program_id(0)
    width = mine_ref.shape[4]
    for core, out_ref in ((0, mine_ref), (1, sent_ref)):
        left = left_ref[places_ref[core * nz + step]]
        total = lax.dot_general(left, right_ref[...], TN, preferred_element_type=jnp.float32)
        for x in range(2):
            for y in range(ny):
                out_ref[x, y, 0] = total[:, (x * ny + y) * width : (x * ny + y + 1) * width].astype(
                    jnp.bfloat16
                )


def out_grad_parts(wires, attended, d_mixed):
    heads, tokens, rows = attended.shape
    depth = d_mixed.shape[1]
    nz, ny, width = wires.nz, wires.ny, depth // wires.dp
    places = jnp.stack(
        [((wires.z - s) % nz) * 2 + (wires.c ^ r) for r in range(2) for s in range(nz)]
    ).astype(jnp.int32)
    columns = [((wires.y + s) % ny) * 2 + (wires.x ^ t) for t in range(2) for s in range(ny)]
    ordered = jnp.concatenate(
        [lax.dynamic_slice_in_dim(d_mixed, column * width, width, 1) for column in columns], axis=1
    )
    out = jax.ShapeDtypeStruct((2, ny, nz, rows, width), jnp.bfloat16)
    block = pl.BlockSpec((2, ny, 1, rows, width), lambda i, p: (0, 0, i, 0, 0))
    return pl.pallas_call(
        functools.partial(out_grad_kernel, nz, ny),
        grid_spec=pltpu.PrefetchScalarGridSpec(
            num_scalar_prefetch=1,
            grid=(nz,),
            in_specs=[
                pl.BlockSpec((heads, tokens, rows), lambda i, p: (0, 0, 0)),
                pl.BlockSpec((tokens, depth), lambda i, p: (0, 0)),
            ],
            out_specs=[block, block],
        ),
        out_shape=[out, out],
        compiler_params=pltpu.CompilerParams(
            dimension_semantics=("arbitrary",), vmem_limit_bytes=VMEM
        ),
        cost_estimate=pl.CostEstimate(
            flops=2 * tokens * depth * heads * rows, bytes_accessed=10 << 20, transcendentals=0
        ),
    )(places, attended, ordered)


def tie(*values):
    return lax.optimization_barrier(values)


def per_device(
    wires,
    tokens,
    keep_mask,
    seq_lengths,
    attn_gain,
    in_weight,
    out_weight,
    ffn_gain,
    gate_weight,
    up_weight,
    down_weight,
    out_grad,
):
    wires.place()
    heads_here = in_weight.shape[1] // (2 * FD + VD)
    rows, depth = tokens.shape
    group_rows = rows * wires.head
    half = rows // 2
    out_rows = heads_here * VD
    size = depth // wires.dp
    tokens_wide = wide(tokens)
    own = low(tokens_wide * inv_root_mean(tokens_wide) * attn_gain)
    across_y = range(1, wires.ny)

    def on_y(pieces):
        return [[wires.over_y(piece, s) for s in across_y] for piece in pieces]

    def swap(values):
        return lax.all_to_all(values, "head", split_axis=0, concat_axis=0, tiled=True)

    def add(*values):
        return low(sum(wide(value) for value in values))

    in_packed = pack_columns(in_weight, heads_here)
    packed_width = in_packed.shape[1]
    in_padded = jnp.pad(in_packed, ((0, 0), (0, heads_here * VD + LANES - packed_width)))
    in_part = wires.quarter(in_packed.T)
    keep_column = keep_mask.astype(jnp.float32)[:, None]
    ends = jnp.cumsum(seq_lengths[0])
    stacked = jnp.stack([gate_weight.T, up_weight.T, down_weight])
    unit_own = pick(stacked, wires.x, 2, 1)
    unit_other = pick(stacked, 1 - wires.x, 2, 1)
    share = out_rows * size // rows
    block = jnp.concatenate([own, wires.quarter(out_weight).reshape(rows, share)], axis=1)

    flying = {}

    def beside_line(step, values):
        if step == 1:
            by_x = wires.over_x(unit_other)
            values, flying["by_x"], flying["own"], flying["in_part"], flying["out_grad"], flying["swap"] = tie(
                values, by_x, unit_own, in_part, out_grad, wires.over_core(block)
            )
        elif step == 2:
            pair = in_order([flying["own"], flying["by_x"]], wires.x, 2)
            by_x = wires.over_x(flying["out_grad"])
            values, flying["grad_x"], flying["pair"], flying["out_grad"] = tie(
                values, by_x, pair, flying["out_grad"]
            )
        elif step == wires.nz - 1:
            by_y = [wires.over_y(flying["pair"][:2], s) for s in across_y]
            values, flying["by_y"], flying["pair"], flying["grad_x"] = tie(
                values, by_y, flying["pair"], flying["grad_x"]
            )
        else:
            (values,) = tie(values)
        return values

    chunks, chips = wires.line(block, beside_line)
    others = [flying["swap"]] + [wires.over_core(chunk) for chunk in chunks[1:]]
    pieces = [piece for pair in zip(chunks, others) for piece in pair]
    places = jnp.stack(
        [(chip * 2 + (wires.c ^ r)) * rows for chip in chips for r in range(2)]
    ).astype(jnp.int32)
    pieces, unit_pair, out_grad, grad_x = tie(
        pieces, flying["pair"], flying["out_grad"], flying["grad_x"]
    )

    def shares(blocks):
        return jnp.stack([piece[:, depth:].reshape(out_rows, size) for piece in blocks])

    by_zh_g = [wires.over_zh(unit_pair[:1], s) for s in range(1, wires.nzh)]
    out_line = shares(pieces[::2])
    out_x, out_y = wires.over_x(out_line), [wires.over_y(out_line, s) for s in across_y]
    projected, normed, attended_wide, inverses, attended = attend(
        pieces, places, in_padded, keep_column, ends, heads_here
    )
    attended, out_x, out_y, by_zh_g, unit_pair, out_grad = tie(
        attended, out_x, out_y, by_zh_g, unit_pair, out_grad
    )
    attended_here = swap(attended).reshape(wires.head, rows, out_rows)
    grad_z = wires.over_zl(out_grad)
    out_across = [wires.over_x(piece) for piece in out_y]
    by_zh_gy = on_y(by_zh_g)
    out_line_swap = shares(pieces[1::2])
    out_x_swap, out_y_swap = wires.over_core(out_x), [wires.over_core(piece) for piece in out_y]
    attended_here, out_across, grad_z, out_x_swap, out_y_swap, unit_pair, by_zh_gy = tie(
        attended_here, out_across, grad_z, out_x_swap, out_y_swap, unit_pair, by_zh_gy
    )
    out_across_swap = [wires.over_core(piece) for piece in out_across]

    def in_layout(line, by_x, by_y, across):
        pieces = [line, by_x]
        for piece in zip(by_y, across):
            pieces += piece
        return pieces

    out_pieces = in_layout(out_line, out_x, out_y, out_across)
    out_pieces += in_layout(out_line_swap, out_x_swap, out_y_swap, out_across_swap)
    out_whole = Whole(wires, out_pieces, wires.whole_places(chips, out_rows, size), out_rows, size)
    middle, normed_two = mix(attended_here, out_whole, tokens, ffn_gain[None])

    normed_two, unit_pair, grad_x, grad_z, out_grad = tie(normed_two, unit_pair, grad_x, grad_z, out_grad)
    two_x, two_z = wires.over_x(normed_two), wires.over_zl(normed_two)
    by_zh_u = [wires.over_zh(unit_pair[1:2], s) for s in range(1, wires.nzh)]
    by_y_d = [wires.over_y(unit_pair[2:], s) for s in across_y]
    two_swap = wires.over_core(normed_two)
    two_x, two_z, by_zh_u, two_swap, by_y_d, unit_pair = tie(
        two_x, two_z, by_zh_u, two_swap, by_y_d, unit_pair
    )
    two_corner = (wires.over_zl(two_x[:half]), wires.over_x(two_z[half:]))
    by_zh_uy = on_y(by_zh_u)
    two_swaps = [two_swap] + [wires.over_core(piece) for piece in (two_x, two_z)]
    two_corner, by_zh_uy, two_swaps, two_x, two_z, unit_pair = tie(
        two_corner, by_zh_uy, two_swaps, two_x, two_z, unit_pair
    )
    two_corner = jnp.concatenate(two_corner, axis=0)

    def spots(matrix, place, by_y, piece, on):
        units = [(unit_pair[matrix : matrix + 1], place, 1, 0, 0)]
        units += [(by_y[s - 1], place, 1, 0, s) for s in across_y]
        for zh in range(1, wires.nzh):
            units.append((piece[zh - 1], place, 1, zh, 0))
            units += [(on[zh - 1][s - 1], place, 1, zh, s) for s in across_y]
        return units

    spot = unit_pair.shape[1], unit_pair.shape[2]
    gu_pair = unit_pair[:2]
    gates = [(gu_pair, 0, 2, 0, 0)] + [(flying["by_y"][s - 1], 0, 2, 0, s) for s in across_y]
    for zh in range(1, wires.nzh):
        for place, piece, on in ((0, by_zh_g, by_zh_gy), (1, by_zh_u, by_zh_uy)):
            gates.append((piece[zh - 1], place, 1, zh, 0))
            gates += [(on[zh - 1][s - 1], place, 1, zh, s) for s in across_y]
    units = Units(wires, gates, 2, *spot)

    by_zh_d = [wires.over_zh(unit_pair[2:], s) for s in range(1, wires.nzh)]
    grad_corner = wires.over_x(grad_z)
    two_corner_swap = wires.over_core(two_corner)
    first = [gate_up(pair, units) for pair in zip([normed_two, two_x, two_z], two_swaps)]
    first, by_zh_d, grad_corner, two_corner, two_corner_swap, grad_z = tie(
        first, by_zh_d, grad_corner, two_corner, two_corner_swap, grad_z
    )
    by_zh_dy = on_y(by_zh_d)
    grad_all = [out_grad, grad_x, grad_z, grad_corner]
    grad_pairs = [(grad, wires.over_core(grad)) for grad in grad_all]
    first.append(gate_up((two_corner, two_corner_swap), units))
    first, by_zh_dy, grad_pairs = tie(first, by_zh_dy, grad_pairs)
    downs = [(unit_pair[2:], 0, 1, 0, 0)] + [(by_y_d[s - 1], 0, 1, 0, s) for s in across_y]
    for zh in range(1, wires.nzh):
        downs.append((by_zh_d[zh - 1], 0, 1, zh, 0))
        downs += [(by_zh_dy[zh - 1][s - 1], 0, 1, zh, s) for s in across_y]
    units = Units(
        wires, downs + [(array, at + 1, count, zh, s) for array, at, count, zh, s in gates], 3, *spot
    )

    def feed(place, *after):
        given, grads, *_ = tie(first[place], grad_pairs[place], *after)
        gate, up, normed = given
        outs, dnormed, branches = down(grads, gate, up, units)
        return (*outs[:3], normed, outs[3]), dnormed, branches

    in_part, grad_corner = tie(flying["in_part"], grad_corner)
    in_line = [in_part] + [wires.over_z(in_part, s) for s in range(1, wires.nz)]
    unit_c, dnormed_c, branch_c = feed(3)
    swap_c = wires.over_core(dnormed_c[1])
    unit_o, dnormed_o, branch_o = feed(0, unit_c)
    unit_o, swap_c, in_line = tie(unit_o, swap_c, in_line)
    sum_c = add(dnormed_c[0], swap_c)
    to_z, to_x = wires.over_x(sum_c[:half]), wires.over_zl(sum_c[half:])
    in_line = jnp.stack(in_line)
    in_y = [wires.over_y(in_line, s) for s in across_y]
    swap_o = wires.over_core(dnormed_o[1])
    unit_x, dnormed_x, branch_x = feed(1, unit_o, sum_c, in_line)
    unit_x, to_x, to_z, swap_o = tie(unit_x, to_x, to_z, swap_o)
    swap_x = wires.over_core(dnormed_x[1])
    in_x = wires.over_x(in_line)
    unit_z, dnormed_z, branch_z = feed(2, unit_x)
    swap_z = wires.over_core(dnormed_z[1])
    unit_z, swap_x, swap_z, in_x, in_y = tie(unit_z, swap_x, swap_z, in_x, in_y)
    sum_x = jnp.concatenate(
        [add(dnormed_x[0][:half], swap_x[:half]), add(dnormed_x[0][half:], swap_x[half:], to_x)], axis=0
    )
    final_x = wires.over_x(sum_x)
    sum_z = jnp.concatenate(
        [add(dnormed_z[0][:half], swap_z[:half], to_z), add(dnormed_z[0][half:], swap_z[half:])], axis=0
    )
    final_z = wires.over_zl(sum_z)
    sum_o = add(dnormed_o[0], swap_o)
    in_across = [wires.over_y(in_x, s) for s in across_y]

    every = [unit_o, unit_x, unit_z, unit_c]

    def grad_of(every, unit, token):
        return unit_grad(wires, [outs[unit] for outs in every], [outs[token] for outs in every])

    def grad_y(mine, sent):
        return mine, [wires.over_y(sent[s - 1], s) for s in across_y]

    def grad_zh(mine, sent):
        total = add(mine, *sent)
        return total[0], [wires.over_zh(total[s], -s) for s in range(1, wires.nzh)]

    def grad_x_swap(mine, sent):
        total = add(mine, *sent)
        return pick(total, wires.x, 2, 1), wires.over_x(pick(total, 1 - wires.x, 2, 1))

    def grad_last(mine, sent):
        return wide(in_order([mine, sent], wires.x, 0))

    every, sum_x, sum_z = tie(every, sum_x, sum_z)
    gate_mine, gate_sent = grad_of(every, 1, 3)
    in_swaps = [wires.over_core(piece) for piece in (in_line, in_x, *in_y)]
    final_x, final_z, gate_mine, gate_sent, in_swaps, in_across = tie(
        final_x, final_z, gate_mine, gate_sent, in_swaps, in_across
    )
    gate_back = grad_y(gate_mine, gate_sent)
    d_middle, d_mixed, ffn_gain_part, d_attended = unmix(
        (sum_o, final_x, final_z), middle, out_grad, ffn_gain[None], out_whole, wires.head
    )
    every, d_attended, d_mixed, branches = tie(
        every, d_attended, d_mixed, (branch_o, branch_x, branch_z, branch_c)
    )
    d_attended = swap(d_attended).reshape(group_rows, out_rows)
    out_mine, out_sent = out_grad_parts(wires, attended_here, d_mixed)
    up_parts = grad_of(every, 2, 3)
    down_parts = grad_of(every, 0, 4)
    out_sent = wires.over_core(out_sent)
    in_across_swap = [wires.over_core(piece) for piece in in_across]
    d_attended, out_mine, out_sent, up_parts, down_parts, gate_back, in_across_swap = tie(
        d_attended, out_mine, out_sent, up_parts, down_parts, gate_back, in_across_swap
    )
    up_back = grad_y(*up_parts)
    gate_back = grad_zh(*gate_back)
    out_total = add(out_mine, out_sent)
    out_sent = wires.over_x(out_total[1])
    d_attended, out_total = tie(d_attended, out_total)
    d_projected = attend_back(
        projected, keep_column, ends, attended_wide, inverses, d_attended, heads_here
    )
    swaps = [wires.over_core(branch[1]) for branch in branches]
    d_projected, gate_back, up_back, branches, swaps = tie(
        d_projected, gate_back, up_back, branches, swaps
    )
    d_here = swap(d_projected).reshape(wires.head, rows, packed_width)
    up_back = grad_zh(*up_back)
    down_back = grad_y(*down_parts)
    gate_back = grad_x_swap(*gate_back)
    sums = [add(branch[0], swap_) for branch, swap_ in zip(branches, swaps)]
    in_back = lax.dot_general(normed, d_projected, TN, preferred_element_type=jnp.float32)
    attn_gain_part = jnp.sum(in_back * wide(in_packed), axis=1) / attn_gain
    in_back = low(in_back)
    gains = jnp.stack([attn_gain_part, ffn_gain_part[0]])
    d_here, up_back, in_back, down_back, out_sent, sums, gate_back, gains = tie(
        d_here, up_back, in_back, down_back, out_sent, sums, gate_back, gains
    )
    in_pieces = in_layout(in_line, in_x, in_y, in_across)
    in_pieces += in_layout(in_swaps[0], in_swaps[1], in_swaps[2:], in_across_swap)
    in_chips = [(wires.z - s) % wires.nz for s in range(wires.nz)]
    in_whole = Whole(
        wires, in_pieces, wires.whole_places(in_chips, packed_width, size), packed_width, size
    )
    down_back = grad_zh(*down_back)
    up_back = grad_x_swap(*up_back)
    to_z, to_x = wires.over_x(sums[3][:half]), wires.over_zl(sums[3][half:])
    out_total = add(out_total[0], out_sent)
    out_y = [wires.over_y(out_total[s], s) for s in across_y]
    in_grad = last(d_here, in_whole, tokens, d_middle, attn_gain[None])
    gains = gains + wires.over_core(gains)
    in_grad, out_y, down_back, to_x, to_z, up_back, in_back, gains, sums = tie(
        in_grad, out_y, down_back, to_x, to_z, up_back, in_back, gains, sums
    )
    cut = depth // 2
    out_parts = add(out_total[0], *out_y)
    out_turns = [wires.over_z(out_parts[s], -s) for s in range(1, wires.nz)]
    in_halves = (wires.sum_x(in_back[:cut]), wires.sum_y(in_back[cut:]))
    out_parts, out_turns, in_halves, by_x, by_z = tie(
        out_parts, out_turns, in_halves, (sums[1], to_x), (sums[2], to_z)
    )
    out_part = add(out_parts[0], *out_turns)
    by_x = jnp.concatenate([by_x[0][:half], add(by_x[0][half:], by_x[1])], axis=0)
    by_z = jnp.concatenate([add(by_z[0][:half], by_z[1]), by_z[0][half:]], axis=0)
    final_x, final_z = wires.over_x(by_x), wires.over_zl(by_z)
    in_halves = (wires.sum_y(in_halves[0]), wires.sum_x(in_halves[1]))
    gains = gains + wires.over_zl(gains)
    final_x, final_z, in_halves, out_part, gains, down_back = tie(
        final_x, final_z, in_halves, out_part, gains, down_back
    )
    down_back = grad_x_swap(*down_back)
    out_x = wires.over_x(out_part)
    out_by_y = [wires.over_y(out_part, s) for s in across_y]
    gains = gains + sum(wires.over_zh(gains, s) for s in range(1, wires.nzh))
    out_x, out_by_y, gains, down_back = tie(out_x, out_by_y, gains, down_back)
    out_by_yx = [wires.over_y(out_x, s) for s in across_y]
    gains = gains + wires.over_x(gains)
    out_by_yx, gains = tie(out_by_yx, gains)
    gains = gains + sum(wires.over_y(gains, s) for s in across_y)
    out_weight_grad = wide(
        in_order(
            [
                in_order([a, b], wires.x, 1)
                for a, b in zip([out_part, *out_by_y], [out_x, *out_by_yx])
            ],
            wires.y,
            1,
        )
    )
    output = low(middle + wide(sums[0]) + wide(final_x) + wide(final_z))
    gate_grad = grad_last(*gate_back).T
    up_grad = grad_last(*up_back).T
    down_grad = grad_last(*down_back)
    in_weight_grad = unpack_columns(wide(jnp.concatenate(in_halves, axis=0)), heads_here)
    return (
        output,
        in_grad,
        gains[0],
        in_weight_grad,
        out_weight_grad,
        gains[1],
        gate_grad,
        up_grad,
        down_grad,
    )


def solution(mesh):
    return jax.shard_map(
        functools.partial(per_device, Wires(mesh)),
        mesh=mesh,
        in_specs=(
            P(("dp", "head"), None),
            P("dp"),
            P("dp", None),
            P(),
            P(None, "head"),
            P("head", None),
            P(),
            P("dp", "head"),
            P("dp", "head"),
            P("head", "dp"),
            P(("dp", "head"), None),
        ),
        out_specs=(
            P(("dp", "head"), None),
            P(("dp", "head"), None),
            P(),
            P(None, "head"),
            P("head", None),
            P(),
            P("dp", "head"),
            P("dp", "head"),
            P("head", "dp"),
        ),
        check_vma=False,
    )
```

time: 1100 us -> 797 us (0.72)
  waiting for transfers between devices: 799 us -> 323 us
  Pallas kernels: 42.4 us -> 231 us
  matrix products: 143 us -> 7.63 us
  starting transfers between devices: 1.1 us -> 112 us
  blocking collectives: 39.6 us -> 0 us
  other arithmetic: 34.4 us -> 67.6 us
  local copies, waits for them, and re-layouts: 10.6 us -> 42.2 us
  between operations: 16.1 us -> 2.77 us
    reduce_scatter x7 -> x0, waiting for transfers between devices: 366 us -> none  [the longest x1 88.3 us: per_device(): lax.psum_scatter((jnp.dot(d_gate, gate_all.T, preferred_element_type=jnp....]
    all_gather x7 -> x0, waiting for transfers between devices: 354 us -> none  [the longest x1 83.6 us: per_device(): grad_group = lax.all_gather(out_grad, 'head', axis=0, tiled=True)]
    ppermute x0 -> x92, waiting for transfers between devices: none -> 311 us  [the longest x20 121 us: over_x(): return lax.ppermute(values, 'dp', [(i, i ^ 1) for i in range(self.dp)])]
    pallas_call x1 -> x16, Pallas kernels: 12.5 us -> 202 us  [the longest x8 98.6 us: with_units(): pl.pallas_call(functools.partial(kernel, units), grid_spec=pltpu.Prefetch...]
    dot_general x15 -> x1, matrix products: 143 us -> 7.63 us  [per_device(): lax.dot_general(normed, d_projected, TN, preferred_element_type=jnp.float32)]
    ppermute x0 -> x92, starting transfers between devices: none -> 99.2 us  [the longest x20 22.9 us: over_x(): return lax.ppermute(values, 'dp', [(i, i ^ 1) for i in range(self.dp)])]
    psum x1 -> x0, waiting for transfers between devices: 75.3 us -> none  [per_device(): lax.psum(in_weight_grad[:, :in_weight.shape[1]].astype(jnp.bfloat16), 'dp')]
    psum x1 -> x0, blocking collectives: 39.6 us -> none  [per_device(): lax.psum((attn_gain_part, ffn_gain_part), ('dp', 'head'))]
  transfers between devices with their start and end apart: 15 -> 95, of which waited for: 13 -> 40; matrix products, arithmetic and copies ran while one was open for 11% -> 13% of each run, Pallas kernels for 3% -> 24%
where the time goes in v3:
time: 797 us; the launch traced here: 787 us
  waiting for transfers between devices  323 us (41%)
  Pallas kernels  231 us (29%)
  starting transfers between devices  112 us (14%)
  other arithmetic  67.6 us (8%)
  local copies, waits for them, and re-layouts  42.2 us (5%)
    ppermute x20, waiting for transfers between devices, over_x(): return lax.ppermute(values, 'dp', [(i, i ^ 1) for i in range(self.dp)])  121 us
    pallas_call x8, Pallas kernels, with_units(): pl.pallas_call(functools.partial(kernel, units), grid_spec=pltpu.Prefetch...  98.6 us
    ppermute x7, waiting for transfers between devices, over_zh(): lax.ppermute(values, 'head', [(i, (i // 4 + shift) % self.nzh * 4 + i % 4...  46.5 us
    ppermute x8, waiting for transfers between devices, over_zl(): return lax.ppermute(values, 'head', [(i, i ^ 2) for i in range(self.head)])  41.5 us
    convert_element_type x25, other arithmetic, low(): return values.astype(jnp.bfloat16)  41.1 us
    pallas_call x3, Pallas kernels, unit_grad(): pl.pallas_call(functools.partial(unit_grad_kernel, len(lefts), ny, nzh),...  39.2 us
    ppermute x17, waiting for transfers between devices, over_y(): lax.ppermute(values, 'dp', [(i, (i // 2 + shift) % self.ny * 2 + i % 2) f...  38.1 us
    pallas_call x3, Pallas kernels, with_whole(): pl.pallas_call(functools.partial(kernel, whole), grid_spec=pltpu.Prefetch...  34 us
  transfers between devices with their start and end apart: 95, of which 40 were waited for; matrix products, arithmetic and copies ran while one was open for 13% of the time, Pallas kernels for 24%

profile of v3, /device:TPU:0, one launch (start us, length us, event | category | flops | bytes accessed | tf_op | source)
XLA Modules:
  0.0 786.9 jit_solution(8048611142925309752)
XLA Ops:
  16.4 22.9 %collective-permute-done.2 = bf16[3,352,512]{2,1,0:T(8,128)(2,1)} collective-permute-done((bf16[3,352,512]{2,1,0:T(8,128)(2,1)S(1)}, bf16[3,352,512]{2,1,0:T(8,128)(2,1)}, u32[]{:S(2)}, u32[]{:S(2)}) %collective-permute-start.2) | collective-permute-done | bytes 1081376 | tf_op jit(solution)/shard_map/ppermute | solution.py:326
  48.7 20.9 %collective-permute-done.7.refs_10_ = bf16[256,2048]{1,0:T(8,128)(2,1)} collective-permute-done((bf16[256,2048]{1,0:T(8,128)(2,1)}, bf16[256,2048]{1,0:T(8,128)(2,1)}, u32[]{:S(2)}, u32[]{:S(2)}) %collective-permute-start.7) | collective-permute-done | bytes 1048608 | tf_op jit(solution)/shard_map/ppermute | solution.py:326
  83.0 28.1 %collective-permute-done.9 = bf16[256,2560]{1,0:T(8,128)(2,1)S(1)} collective-permute-done((bf16[256,2560]{1,0:T(8,128)(2,1)S(1)}, bf16[256,2560]{1,0:T(8,128)(2,1)S(1)}, u32[]{:S(2)}, u32[]{:S(2)}) %collective-permute-start.9) | collective-permute-done | bytes 1310752 | tf_op jit(solution)/shard_map/ppermute | solution.py:364
  126.8 23.1 %shard_map.178 = (bf16[2048,384]{1,0:T(8,128)(2,1)}, bf16[2048,2048]{1,0:T(8,128)(2,1)}, f32[2048,256]{1,0:T(8,128)}, f32[2048,128]{1,0:T(8,128)}, bf16[2048,256]{1,0:T(8,128)(2,1)}) custom-call(s32[3]{0:T(128)} %bitcast.151, s32[8]{0:T(128)} %stack.218.at_ref, bf16[256,2560]{1,0:T(8,128)(2,1)} %pad_maximum_fusion.3.refs_0_, ...), custom_call_target="tpu_custom_call" | custom-call | flops 8589934592 | bytes 29360128 | tf_op jit(solution)/shard_map/pallas_call | solution.py:108
  168.4 16.9 %collective-permute-done.19.refs_3_.refs_7_ = bf16[1,352,1024]{2,1,0:T(8,128)(2,1)S(1)} collective-permute-done((bf16[1,352,1024]{2,1,0:T(8,128)(2,1)}, bf16[1,352,1024]{2,1,0:T(8,128)(2,1)S(1)}, u32[]{:S(2)}, u32[]{:S(2)}) %collective-permute-start.19) | collective-permute-done | bytes 720928 | tf_op jit(solution)/shard_map/ppermute | solution.py:329
  189.8 16.6 %collective-permute-done.16.refs_10_ = bf16[256,2048]{1,0:T(8,128)(2,1)} collective-permute-done((bf16[256,2048]{1,0:T(8,128)(2,1)}, bf16[256,2048]{1,0:T(8,128)(2,1)}, u32[]{:S(2)}, u32[]{:S(2)}) %collective-permute-start.16) | collective-permute-done | bytes 1048608 | tf_op jit(solution)/shard_map/ppermute | solution.py:337
  226.4 34.3 %collective-permute-done.23.refs_4_.refs_8_ = bf16[1,352,1024]{2,1,0:T(8,128)(2,1)S(1)} collective-permute-done((bf16[1,352,1024]{2,1,0:T(8,128)(2,1)S(1)}, bf16[1,352,1024]{2,1,0:T(8,128)(2,1)S(1)}, u32[]{:S(2)}, u32[]{:S(2)}) %collective-permute-start.23) | collective-permute-done | bytes 720928 | tf_op jit(solution)/shard_map/ppermute | solution.py:340
  308.1 10.7 %shard_map.181 = (f32[512,704]{1,0:T(8,128)}, f32[512,704]{1,0:T(8,128)}, bf16[512,2048]{1,0:T(8,128)(2,1)}) custom-call(s32[2]{0:T(128)} %pad_add_fusion.places_ref, bf16[2,352,1024]{2,1,0:T(8,128)(2,1)} %slice.221.refs_0_.refs_4_, bf16[2,352,1024]{2,1,0:T(8,128)(2,1)} %copy-done.63, bf16[1,352,1024]{2,1,0:T(8,128)(2,1)} %collective-permute-done.14.refs_2_.refs_6_, ...), custom_call_target="tpu_custom_call" | custom-call | flops 2952790016 | bytes 20971520 | tf_op jit(solution)/shard_map/pallas_call | solution.py:659
  323.5 10.5 %shard_map.183 = (f32[512,704]{1,0:T(8,128)}, f32[512,704]{1,0:T(8,128)}, bf16[512,2048]{1,0:T(8,128)(2,1)}) custom-call(s32[2]{0:T(128)} %pad_add_fusion.places_ref, bf16[2,352,1024]{2,1,0:T(8,128)(2,1)} %slice.221.refs_0_.refs_4_, bf16[2,352,1024]{2,1,0:T(8,128)(2,1)} %copy-done.63, bf16[1,352,1024]{2,1,0:T(8,128)(2,1)} %collective-permute-done.14.refs_2_.refs_6_, ...), custom_call_target="tpu_custom_call" | custom-call | flops 2952790016 | bytes 20971520 | tf_op jit(solution)/shard_map/pallas_call | solution.py:659
  341.6 14.2 %shard_map.184 = (bf16[512,704]{1,0:T(8,128)(2,1)}, bf16[512,704]{1,0:T(8,128)(2,1)}, bf16[512,704]{1,0:T(8,128)(2,1)}, bf16[512,2048]{1,0:T(8,128)(2,1)}, bf16[...) custom-call(s32[2]{0:T(128)} %pad_add_fusion.places_ref, ...), custom_call_target="tpu_custom_call" | custom-call | flops 5905580032 | bytes 20971520 | tf_op jit(solution)/shard_map/pallas_call | solution.py:659
  359.9 14.0 %shard_map.185 = (bf16[512,704]{1,0:T(8,128)(2,1)}, bf16[512,704]{1,0:T(8,128)(2,1)}, bf16[512,704]{1,0:T(8,128)(2,1)}, bf16[512,2048]{1,0:T(8,128)(2,1)}, bf16[...) custom-call(s32[2]{0:T(128)} %pad_add_fusion.places_ref, ...), custom_call_target="tpu_custom_call" | custom-call | flops 5905580032 | bytes 20971520 | tf_op jit(solution)/shard_map/pallas_call | solution.py:659
  394.7 14.3 %shard_map.186 = (bf16[512,704]{1,0:T(8,128)(2,1)}, bf16[512,704]{1,0:T(8,128)(2,1)}, bf16[512,704]{1,0:T(8,128)(2,1)}, bf16[512,2048]{1,0:T(8,128)(2,1)}, bf16[...) custom-call(s32[2]{0:T(128)} %pad_add_fusion.places_ref, ...), custom_call_target="tpu_custom_call" | custom-call | flops 5905580032 | bytes 20971520 | tf_op jit(solution)/shard_map/pallas_call | solution.py:659
  409.0 14.7 %collective-permute-done.44 = bf16[128,2048]{1,0:T(8,128)(2,1)S(1)} collective-permute-done((bf16[128,2048]{1,0:T(8,128)(2,1)}, bf16[128,2048]{1,0:T(8,128)(2,1)S(1)}, u32[]{:S(2)}, u32[]{:S(2)}) %collective-permute-start.44) | collective-permute-done | bytes 524320 | tf_op jit(solution)/shard_map/ppermute | solution.py:326
  423.7 14.1 %shard_map.187 = (bf16[512,704]{1,0:T(8,128)(2,1)}, bf16[512,704]{1,0:T(8,128)(2,1)}, bf16[512,704]{1,0:T(8,128)(2,1)}, bf16[512,2048]{1,0:T(8,128)(2,1)}, bf16[...) custom-call(s32[2]{0:T(128)} %pad_add_fusion.places_ref, ...), custom_call_target="tpu_custom_call" | custom-call | flops 5905580032 | bytes 20971520 | tf_op jit(solution)/shard_map/pallas_call | solution.py:659
  461.1 13.4 %shard_map.188 = (bf16[2,352,1024]{2,1,0:T(8,128)(2,1)}, bf16[1,2,352,1024]{3,2,1,0:T(8,128)(2,1)}) custom-call(s32[4]{0:T(128)} %pad_add_fusion.1.places_ref, bf16[512,704]{1,0:T(8,128)(2,1)} %get-tuple-element.528.refs_0_, bf16[512,704]{1,0:T(8,128)(2,1)} %get-tuple-element.529.refs_1_, bf16[512,704]{1,0:T(8,128)(2,1)} %get-tuple-element.530.refs_2_, ...), custom_call_target="tpu_custom_call" | custom-call | flops 5905580032 | bytes 14680064 | tf_op jit(solution)/shard_map/pallas_call | solution.py:779
  483.8 10.5 %shard_map.189 = (f32[256,2048]{1,0:T(8,128)}, bf16[256,2048]{1,0:T(8,128)(2,1)}, f32[1,2048]{1,0:T(1,128)}, bf16[8,256,256]{2,1,0:T(8,128)(2,1)}) custom-call(s32[12]{0:T(128)} %stack.208.places_ref, bf16[4,256,512]{2,1,0:T(8,128)(2,1)} %copy-done.4, bf16[4,256,512]{2,1,0:T(8,128)(2,1)} %collective-permute-done.12.refs_1_, ...), custom_call_target="tpu_custom_call" | custom-call | flops 2147483648 | bytes 16777216 | tf_op jit(solution)/shard_map/pallas_call | solution.py:501
  510.3 12.9 %shard_map.192 = (bf16[2,352,1024]{2,1,0:T(8,128)(2,1)}, bf16[1,2,352,1024]{3,2,1,0:T(8,128)(2,1)}) custom-call(s32[4]{0:T(128)} %pad_add_fusion.1.places_ref, bf16[512,704]{1,0:T(8,128)(2,1)} %get-tuple-element.582.refs_0_, bf16[512,704]{1,0:T(8,128)(2,1)} %get-tuple-element.583.refs_1_, bf16[512,704]{1,0:T(8,128)(2,1)} %get-tuple-element.584.refs_2_, ...), custom_call_target="tpu_custom_call" | custom-call | flops 5905580032 | bytes 14680064 | tf_op jit(solution)/shard_map/pallas_call | solution.py:779
  523.2 12.9 %shard_map.191 = (bf16[2,352,1024]{2,1,0:T(8,128)(2,1)}, bf16[1,2,352,1024]{3,2,1,0:T(8,128)(2,1)}) custom-call(s32[4]{0:T(128)} %pad_add_fusion.1.places_ref, bf16[512,704]{1,0:T(8,128)(2,1)} %get-tuple-element.572.refs_0_, bf16[512,704]{1,0:T(8,128)(2,1)} %get-tuple-element.573.refs_1_, bf16[512,704]{1,0:T(8,128)(2,1)} %get-tuple-element.574.refs_2_, ...), custom_call_target="tpu_custom_call" | custom-call | flops 5905580032 | bytes 14680064 | tf_op jit(solution)/shard_map/pallas_call | solution.py:779
  556.1 29.3 %shard_map.193 = bf16[2048,320]{1,0:T(8,128)(2,1)} custom-call(s32[3]{0:T(128)} %bitcast.152, bf16[2048,384]{1,0:T(8,128)(2,1)} %get-tuple-element.595.projected_ref, f32[2048,1]{1,0:T(8,128)} %copy.25.refs_9_.keep_ref, f32[2048,256]{1,0:T(8,128)} %get-tuple-element.596.y_ref, f32[2048,128]{1,0:T(8,128)} %get-tuple-element.597.inv_ref, ...), custom_call_target="tpu_custom_call" | custom-call | flops 13421772800 | bytes 12582912 | tf_op jit(solution)/shard_map/pallas_call | solution.py:228
  622.4 20.6 %collective-permute-done.68 = bf16[352,512]{1,0:T(8,128)(2,1)} collective-permute-done((bf16[352,512]{1,0:T(8,128)(2,1)}, bf16[352,512]{1,0:T(8,128)(2,1)}, u32[]{:S(2)}, u32[]{:S(2)}) %collective-permute-start.68) | collective-permute-done | bytes 360480 | tf_op jit(solution)/shard_map/ppermute | solution.py:326
  643.0 12.9 %all-to-all-done.2 = bf16[8,256,320]{1,2,0:T(8,128)(2,1)S(1)} async-done(((bf16[8,256,320]{1,2,0:T(8,128)(2,1)}), bf16[8,256,320]{1,2,0:T(8,128)(2,1)S(1)}, u32[]{:S(2)}, u32[]{:S(2)}) %all-to-all-start.2) | async-done | bytes 1310752 | tf_op jit(solution)/shard_map/all_to_all | solution.py:879
  672.4 13.7 %shard_map.194 = f32[256,2048]{1,0:T(8,128)} custom-call(s32[12]{0:T(128)} %stack.232.places_ref, bf16[4,320,512]{2,1,0:T(8,128)(2,1)} %copy-done.7, bf16[4,320,512]{2,1,0:T(8,128)(2,1)} %copy-done.30, bf16[4,320,512]{2,1,0:T(8,128)(2,1)} %collective-permute-done.49.refs_2_, bf16[4,320,512]{2,1,0:T(8,128)(2,1)} %collective-permute-done.55.refs_3_, ...), custom_call_target="tpu_custom_call" | custom-call | flops 2684354560 | bytes 16777216 | tf_op jit(solution)/shard_map/pallas_call | solution.py:501
  712.5 12.7 %collective-permute-done.76 = bf16[256,512]{1,0:T(8,128)(2,1)S(1)} collective-permute-done((bf16[256,512]{1,0:T(8,128)(2,1)S(1)}, bf16[256,512]{1,0:T(8,128)(2,1)S(1)}, u32[]{:S(2)}, u32[]{:S(2)}) %collective-permute-start.76) | collective-permute-done | bytes 262176 | tf_op jit(solution)/shard_map/ppermute | solution.py:345
  750.5 12.1 %collective-permute-done.80 = bf16[256,2048]{1,0:T(8,128)(2,1)S(1)} collective-permute-done((bf16[256,2048]{1,0:T(8,128)(2,1)S(1)}, bf16[256,2048]{1,0:T(8,128)(2,1)S(1)}, u32[]{:S(2)}, u32[]{:S(2)}) %collective-permute-start.80) | collective-permute-done | bytes 1048608 | tf_op jit(solution)/shard_map/ppermute | solution.py:326
  (449 shorter events, 377.9 us)
Async XLA Ops:
  115.8 44.4 %collective-permute-start.12 = (bf16[4,256,512]{2,1,0:T(8,128)(2,1)S(1)}, bf16[4,256,512]{2,1,0:T(8,128)(2,1)}, u32[]{:S(2)}, u32[]{:S(2)}) collective-permute-start(bf16[4,256,512]{2,1,0:T(8,128)(2,1)S(1)} %pad_maximum_fusion.7.refs_0_), channel_id=1, source_target_pairs={{0,8},{8,0},{16,24},{24,16},{1,9},{9,1},{17,25},{25,17},{2,10},{10... | collective-permute-start | bytes 3145736 | tf_op jit(solution)/shard_map/ppermute | solution.py:326
  117.4 42.9 %collective-permute-start.13 = (bf16[4,256,512]{2,1,0:T(8,128)(2,1)S(1)}, bf16[4,256,512]{2,1,0:T(8,128)(2,1)}, u32[]{:S(2)}, u32[]{:S(2)}) collective-permute-start(bf16[4,256,512]{2,1,0:T(8,128)(2,1)S(1)} %pad_maximum_fusion.7.refs_0_), channel_id=1, source_target_pairs={{0,16},{8,24},{16,0},{24,8},{1,17},{9,25},{17,1},{25,9},{2,18},{10... | collective-permute-start | bytes 3145736 | tf_op jit(solution)/shard_map/ppermute | solution.py:329
  160.3 47.1 %all-to-all-start = ((bf16[8,256,256]{2,1,0:T(8,128)(2,1)}), bf16[8,256,256]{2,1,0:T(8,128)(2,1)S(1)}, u32[]{:S(2)}, u32[]{:S(2)}) async-start(bf16[8,256,256]{2,1,0:T(8,128)(2,1)} %bitcast.131), calls=%async_computation | async-start | bytes 2097152 | tf_op jit(solution)/shard_map/all_to_all | solution.py:879
  164.7 41.7 %collective-permute-start.16 = (bf16[256,2048]{1,0:T(8,128)(2,1)}, bf16[256,2048]{1,0:T(8,128)(2,1)}, u32[]{:S(2)}, u32[]{:S(2)}) collective-permute-start(bf16[256,2048]{1,0:T(8,128)(2,1)} %refs_12_), channel_id=1, source_target_pairs={{0,2},{1,3},{2,0},{3,1},{4,6},{5,7},{6,4},{7,5},{8,10},{9,11},{10,... | collective-permute-start | bytes 3145736 | tf_op jit(solution)/shard_map/ppermute | solution.py:337
  166.5 39.8 %collective-permute-start.17 = (bf16[4,256,512]{2,1,0:T(8,128)(2,1)}, bf16[4,256,512]{2,1,0:T(8,128)(2,1)S(1)}, u32[]{:S(2)}, u32[]{:S(2)}) collective-permute-start(bf16[4,256,512]{2,1,0:T(8,128)(2,1)} %collective-permute-done.12.refs_1_), channel_id=1, source_target_pairs={{0,1},{1,0},{2,3},{3,2},{4,5},{5,4},{6,7},{7,6},{8,9},{9,8},{10,11... | collective-permute-start | bytes 3145736 | tf_op jit(solution)/shard_map/ppermute | solution.py:334
  166.6 40.8 %collective-permute-start.18 = (bf16[4,256,512]{2,1,0:T(8,128)(2,1)}, bf16[4,256,512]{2,1,0:T(8,128)(2,1)}, u32[]{:S(2)}, u32[]{:S(2)}) collective-permute-start(bf16[4,256,512]{2,1,0:T(8,128)(2,1)} %collective-permute-done.13.refs_2_), channel_id=1, source_target_pairs={{0,1},{1,0},{2,3},{3,2},{4,5},{5,4},{6,7},{7,6},{8,9},{9,8},{10,11... | collective-permute-start | bytes 3145736 | tf_op jit(solution)/shard_map/ppermute | solution.py:334
  221.9 40.8 %collective-permute-start.22 = (bf16[256,2048]{1,0:T(8,128)(2,1)}, bf16[256,2048]{1,0:T(8,128)(2,1)S(1)}, u32[]{:S(2)}, u32[]{:S(2)}) collective-permute-start(bf16[256,2048]{1,0:T(8,128)(2,1)} %get-tuple-element.388.refs_6_), channel_id=1, source_target_pairs={{0,2},{1,3},{2,0},{3,1},{4,6},{5,7},{6,4},{7,5},{8,10},{9,11},{10,... | collective-permute-start | bytes 3145736 | tf_op jit(solution)/shard_map/ppermute | solution.py:337
  222.4 40.3 %collective-permute-start.24 = (bf16[256,2048]{1,0:T(8,128)(2,1)}, bf16[256,2048]{1,0:T(8,128)(2,1)S(1)}, u32[]{:S(2)}, u32[]{:S(2)}) collective-permute-start(bf16[256,2048]{1,0:T(8,128)(2,1)} %get-tuple-element.388.refs_6_), channel_id=1, source_target_pairs={{0,1},{1,0},{2,3},{3,2},{4,5},{5,4},{6,7},{7,6},{8,9},{9,8},{10,11... | collective-permute-start | bytes 3145736 | tf_op jit(solution)/shard_map/ppermute | solution.py:334
  279.2 39.7 %collective-permute-start.32 = (bf16[256,2048]{1,0:T(8,128)(2,1)}, bf16[256,2048]{1,0:T(8,128)(2,1)}, u32[]{:S(2)}, u32[]{:S(2)}) collective-permute-start(bf16[256,2048]{1,0:T(8,128)(2,1)} %collective-permute-done.16.refs_10_), channel_id=1, source_target_pairs={{0,8},{8,0},{16,24},{24,16},{1,9},{9,1},{17,25},{25,17},{2,10},{10... | collective-permute-start | bytes 3145736 | tf_op jit(solution)/shard_map/ppermute | solution.py:326
  284.0 50.0 %collective-permute-start.35 = (bf16[256,2048]{1,0:T(8,128)(2,1)}, bf16[256,2048]{1,0:T(8,128)(2,1)}, u32[]{:S(2)}, u32[]{:S(2)}) collective-permute-start(bf16[256,2048]{1,0:T(8,128)(2,1)} %refs_12_), channel_id=1, source_target_pairs={{0,1},{1,0},{2,3},{3,2},{4,5},{5,4},{6,7},{7,6},{8,9},{9,8},{10,11... | collective-permute-start | bytes 3145736 | tf_op jit(solution)/shard_map/ppermute | solution.py:334
  284.5 49.5 %collective-permute-start.36 = (bf16[256,2048]{1,0:T(8,128)(2,1)}, bf16[256,2048]{1,0:T(8,128)(2,1)S(1)}, u32[]{:S(2)}, u32[]{:S(2)}) collective-permute-start(bf16[256,2048]{1,0:T(8,128)(2,1)} %collective-permute-done.7.refs_10_), channel_id=1, source_target_pairs={{0,1},{1,0},{2,3},{3,2},{4,5},{5,4},{6,7},{7,6},{8,9},{9,8},{10,11... | collective-permute-start | bytes 3145736 | tf_op jit(solution)/shard_map/ppermute | solution.py:334
  382.7 56.9 %collective-permute-start.48 = (bf16[4,320,512]{2,1,0:T(8,128)(2,1)S(1)}, bf16[4,320,512]{2,1,0:T(8,128)(2,1)S(1)}, u32[]{:S(2)}, u32[]{:S(2)}) collective-permute-start(bf16[4,320,512]{2,1,0:T(8,128)(2,1)S(1)} %pad_maximum_fusion.5.refs_0_), channel_id=1, source_target_pairs={{0,8},{8,0},{16,24},{24,16},{1,9},{9,1},{17,25},{25,17},{2,10},{10... | collective-permute-start | bytes 3932168 | tf_op jit(solution)/shard_map/ppermute | solution.py:326
  384.3 55.3 %collective-permute-start.49 = (bf16[4,320,512]{2,1,0:T(8,128)(2,1)S(1)}, bf16[4,320,512]{2,1,0:T(8,128)(2,1)}, u32[]{:S(2)}, u32[]{:S(2)}) collective-permute-start(bf16[4,320,512]{2,1,0:T(8,128)(2,1)S(1)} %pad_maximum_fusion.5.refs_0_), channel_id=1, source_target_pairs={{0,16},{8,24},{16,0},{24,8},{1,17},{9,25},{17,1},{25,9},{2,18},{10... | collective-permute-start | bytes 3932168 | tf_op jit(solution)/shard_map/ppermute | solution.py:329
  440.9 41.9 %collective-permute-start.53 = (bf16[4,320,512]{2,1,0:T(8,128)(2,1)S(1)}, bf16[4,320,512]{2,1,0:T(8,128)(2,1)}, u32[]{:S(2)}, u32[]{:S(2)}) collective-permute-start(bf16[4,320,512]{2,1,0:T(8,128)(2,1)S(1)} %collective-permute-done.48.refs_1_), channel_id=1, source_target_pairs={{0,1},{1,0},{2,3},{3,2},{4,5},{5,4},{6,7},{7,6},{8,9},{9,8},{10,11... | collective-permute-start | bytes 3932168 | tf_op jit(solution)/shard_map/ppermute | solution.py:334
  441.0 41.8 %collective-permute-start.55 = (bf16[4,320,512]{2,1,0:T(8,128)(2,1)S(1)}, bf16[4,320,512]{2,1,0:T(8,128)(2,1)}, u32[]{:S(2)}, u32[]{:S(2)}) collective-permute-start(bf16[4,320,512]{2,1,0:T(8,128)(2,1)S(1)} %collective-permute-done.48.refs_1_), channel_id=1, source_target_pairs={{0,16},{8,24},{16,0},{24,8},{1,17},{9,25},{17,1},{25,9},{2,18},{10... | collective-permute-start | bytes 3932168 | tf_op jit(solution)/shard_map/ppermute | solution.py:329
  509.8 45.6 %collective-permute-start.61 = (bf16[256,2048]{1,0:T(8,128)(2,1)}, bf16[256,2048]{1,0:T(8,128)(2,1)}, u32[]{:S(2)}, u32[]{:S(2)}) collective-permute-start(bf16[256,2048]{1,0:T(8,128)(2,1)} %get-tuple-element.607), channel_id=1, source_target_pairs={{0,1},{1,0},{2,3},{3,2},{4,5},{5,4},{6,7},{7,6},{8,9},{9,8},{10,11... | collective-permute-start | bytes 3145736 | tf_op jit(solution)/shard_map/ppermute | solution.py:334
  510.2 78.3 %collective-permute-start.62 = (bf16[256,2048]{1,0:T(8,128)(2,1)}, bf16[256,2048]{1,0:T(8,128)(2,1)}, u32[]{:S(2)}, u32[]{:S(2)}) collective-permute-start(bf16[256,2048]{1,0:T(8,128)(2,1)} %get-tuple-element.609), channel_id=1, source_target_pairs={{0,1},{1,0},{2,3},{3,2},{4,5},{5,4},{6,7},{7,6},{8,9},{9,8},{10,11... | collective-permute-start | bytes 3145736 | tf_op jit(solution)/shard_map/ppermute | solution.py:334
  536.1 53.8 %collective-permute-start.63 = (bf16[256,2048]{1,0:T(8,128)(2,1)}, bf16[256,2048]{1,0:T(8,128)(2,1)}, u32[]{:S(2)}, u32[]{:S(2)}) collective-permute-start(bf16[256,2048]{1,0:T(8,128)(2,1)} %get-tuple-element.611), channel_id=1, source_target_pairs={{0,1},{1,0},{2,3},{3,2},{4,5},{5,4},{6,7},{7,6},{8,9},{9,8},{10,11... | collective-permute-start | bytes 3145736 | tf_op jit(solution)/shard_map/ppermute | solution.py:334
  542.6 48.7 %collective-permute-start.64 = (bf16[256,2048]{1,0:T(8,128)(2,1)}, bf16[256,2048]{1,0:T(8,128)(2,1)}, u32[]{:S(2)}, u32[]{:S(2)}) collective-permute-start(bf16[256,2048]{1,0:T(8,128)(2,1)} %get-tuple-element.613), channel_id=1, source_target_pairs={{0,1},{1,0},{2,3},{3,2},{4,5},{5,4},{6,7},{7,6},{8,9},{9,8},{10,11... | collective-permute-start | bytes 3145736 | tf_op jit(solution)/shard_map/ppermute | solution.py:334
  547.2 44.1 %collective-permute-start.59 = (bf16[352,1024]{1,0:T(8,128)(2,1)}, bf16[352,1024]{1,0:T(8,128)(2,1)S(1)}, u32[]{:S(2)}, u32[]{:S(2)}) collective-permute-start(bf16[352,1024]{1,0:T(8,128)(2,1)} %get-tuple-element.703), channel_id=1, source_target_pairs={{0,4},{1,5},{2,6},{3,7},{4,0},{5,1},{6,2},{7,3},{8,12},{9,13},{10,... | collective-permute-start | bytes 2162696 | tf_op jit(solution)/shard_map/ppermute | solution.py:340
  588.5 54.5 %collective-permute-start.67 = (bf16[2,4,256,512]{3,2,1,0:T(8,128)(2,1)}, bf16[2,4,256,512]{3,2,1,0:T(8,128)(2,1)}, u32[]{:S(2)}, u32[]{:S(2)}) collective-permute-start(bf16[2,4,256,512]{3,2,1,0:T(8,128)(2,1)} %slice_bitcast_fusion), channel_id=1, source_target_pairs={{0,8},{8,0},{16,24},{24,16},{1,9},{9,1},{17,25},{25,17},{2,10},{10... | collective-permute-start | bytes 6291464 | tf_op jit(solution)/shard_map/ppermute | solution.py:326
  592.5 50.4 %collective-permute-start.68 = (bf16[352,512]{1,0:T(8,128)(2,1)}, bf16[352,512]{1,0:T(8,128)(2,1)}, u32[]{:S(2)}, u32[]{:S(2)}) collective-permute-start(bf16[352,512]{1,0:T(8,128)(2,1)} %get-tuple-element.737), channel_id=1, source_target_pairs={{0,8},{8,0},{16,24},{24,16},{1,9},{9,1},{17,25},{25,17},{2,10},{10... | collective-permute-start | bytes 1081352 | tf_op jit(solution)/shard_map/ppermute | solution.py:326
  594.9 48.0 %collective-permute-start.65 = (bf16[352,1024]{1,0:T(8,128)(2,1)}, bf16[352,1024]{1,0:T(8,128)(2,1)}, u32[]{:S(2)}, u32[]{:S(2)}) collective-permute-start(bf16[352,1024]{1,0:T(8,128)(2,1)} %get-tuple-element.701), channel_id=1, source_target_pairs={{0,4},{1,5},{2,6},{3,7},{4,0},{5,1},{6,2},{7,3},{8,12},{9,13},{10,... | collective-permute-start | bytes 2162696 | tf_op jit(solution)/shard_map/ppermute | solution.py:340
  605.2 50.7 %all-to-all-start.2 = ((bf16[8,256,320]{1,2,0:T(8,128)(2,1)}), bf16[8,256,320]{1,2,0:T(8,128)(2,1)S(1)}, u32[]{:S(2)}, u32[]{:S(2)}) async-start(bf16[8,256,320]{1,2,0:T(8,128)(2,1)} %copy.27), calls=%async_computation.2 | async-start | bytes 2621440 | tf_op jit(solution)/shard_map/all_to_all | solution.py:879
  (150 other events, 2366.4 us)

commit v4 on v3

--- a/solution.py
+++ b/solution.py
@@ -10,15 +10,38 @@
 VD = 128
 LANES = 128
 VMEM = 60 * 1024 * 1024
+LITTLE = pl.CostEstimate(flops=1, bytes_accessed=1, transcendentals=0)
 epsilon = 1e-05
 NT = (((1,), (1,)), ((), ()))
 TN = (((0,), (0,)), ((), ()))
 
 
-def head_lanes(block, rows, head, offset):
-    lane = lax.broadcasted_iota(jnp.int32, (rows, LANES), 1)
-    low = offset + head * FD
-    return jnp.where((lane >= low) & (lane < low + FD), block, 0.0)
+def column_of(row):
+    count = row.shape[1]
+    same = lax.broadcasted_iota(jnp.int32, (count, count), 0) == lax.broadcasted_iota(
+        jnp.int32, (count, count), 1
+    )
+    return jnp.sum(jnp.where(same, row, 0.0), axis=1, keepdims=True)
+
+
+def padded(block):
+    rows, columns = block.shape
+    return jnp.concatenate([block, jnp.zeros((rows, -columns % LANES), block.dtype)], axis=1)
+
+
+def lanes_from(block, low, count):
+    width = block.shape[1]
+    moved = (block if low == 0 else pltpu.roll(block, width - low, 1))[:, :LANES]
+    if count == LANES:
+        return moved
+    lane = lax.broadcasted_iota(jnp.int32, moved.shape, 1)
+    return jnp.where(lane < count, moved, 0.0)
+
+
+def head_parts(block, head):
+    low = head * (2 * FD + VD)
+    query = lanes_from(block, low, FD) * 0.25
+    return query, lanes_from(block, low + FD, FD), lanes_from(block, low + 2 * FD, VD)
 
 
 def segment_start(ends_ref, positions):
@@ -50,21 +73,23 @@
         for copy in copies:
             copy.wait()
 
-    keep = keep_ref[own, :]
+    keep = column_of(keep_ref[:, own])
     normed = normed_s[own, :]
     normed_ref[...] = normed
-    projected = jnp.dot(normed, weight_ref[...], preferred_element_type=jnp.float32).astype(jnp.bfloat16)
+    projected = lax.dot_general(
+        normed, weight_ref[...], NT, preferred_element_type=jnp.float32
+    ).astype(jnp.bfloat16)
     projected_ref[...] = projected
-    packed = projected[:, heads * VD :].astype(jnp.float32)
-    key_s[own, :] = pltpu.roll(packed, LANES - heads * FD, 1).astype(jnp.bfloat16)
+    block = padded(projected.astype(jnp.float32))
     lane = lax.broadcasted_iota(jnp.int32, (rows, LANES), 1)
     ones = jnp.where(lane < 2, keep, 0.0).astype(jnp.bfloat16)
+    queries = []
     for head in range(heads):
-        value_s[head, own, :VD] = (
-            projected[:, head * VD : (head + 1) * VD].astype(jnp.float32) * keep
-        ).astype(jnp.bfloat16)
+        query, key, value = head_parts(block, head)
+        queries.append(query.astype(jnp.bfloat16))
+        key_s[head, own, :] = key.astype(jnp.bfloat16)
+        value_s[head, own, :VD] = (value * keep).astype(jnp.bfloat16)
         value_s[head, own, VD:] = ones
-    queries = [(head_lanes(packed, rows, head, 0) * 0.25).astype(jnp.bfloat16) for head in range(heads)]
     row = step * rows + lax.broadcasted_iota(jnp.int32, (rows, 1), 0)
     start = segment_start(ends_ref, row)
     column = lax.broadcasted_iota(jnp.int32, (rows, rows), 1)
@@ -74,10 +99,11 @@
         allowed = column >= start - block * rows
         if diagonal:
             allowed &= column <= lax.broadcasted_iota(jnp.int32, (rows, rows), 0)
-        keys = key_s[at, :]
         added = []
         for head in range(heads):
-            inner = lax.dot_general(queries[head], keys, NT, preferred_element_type=jnp.float32)
+            inner = lax.dot_general(
+                queries[head], key_s[head, at, :], NT, preferred_element_type=jnp.float32
+            )
             weights = jnp.where(allowed, (inner * 0.5 + 1.0) * inner + 1.0, 0.0).astype(jnp.bfloat16)
             added.append(
                 totals[head]
@@ -99,10 +125,10 @@
 
 
 def attend(pieces, places, weight, keep, ends, heads):
-    size, depth = pieces[0].shape[0], weight.shape[0]
+    size, depth = pieces[0].shape[0], weight.shape[1]
     total = size * len(pieces)
     rows = min(512, total)
-    width = weight.shape[1]
+    width = weight.shape[0]
     pairs = total * (total + rows) // 2 * heads
     blocked = lambda columns: pl.BlockSpec((rows, columns), lambda i, e, a: (i, 0))
     return pl.pallas_call(
@@ -112,15 +138,15 @@
             grid=(total // rows,),
             in_specs=[pl.BlockSpec(memory_space=pl.ANY)] * len(pieces)
             + [
-                pl.BlockSpec((depth, width), lambda i, e, a: (0, 0)),
-                pl.BlockSpec((total, 1), lambda i, e, a: (0, 0)),
+                pl.BlockSpec((width, depth), lambda i, e, a: (0, 0)),
+                pl.BlockSpec((1, total), lambda i, e, a: (0, 0)),
             ],
             out_specs=[
                 blocked(width), blocked(depth), blocked(heads * VD), blocked(LANES), blocked(heads * VD)
             ],
             scratch_shapes=[
                 pltpu.VMEM((total, depth), jnp.bfloat16),
-                pltpu.VMEM((total, LANES), jnp.bfloat16),
+                pltpu.VMEM((heads, total, LANES), jnp.bfloat16),
                 pltpu.VMEM((heads, total, 2 * VD), jnp.bfloat16),
                 pltpu.SemaphoreType.DMA((len(pieces),)),
             ],
@@ -135,9 +161,7 @@
         compiler_params=pltpu.CompilerParams(
             dimension_semantics=("arbitrary",), vmem_limit_bytes=VMEM
         ),
-        cost_estimate=pl.CostEstimate(
-            flops=pairs * 1024 + 2 * total * depth * width, bytes_accessed=28 << 20, transcendentals=0
-        ),
+        cost_estimate=LITTLE,
     )(ends, places, *pieces, weight, keep)
 
 
@@ -155,16 +179,16 @@
 
         def fill(block, nothing):
             at = pl.ds(pl.multiple_of(block * rows, rows), rows)
-            keep = keep_ref[at, :]
-            packed = projected_ref[at, heads * VD :].astype(jnp.float32)
-            rolled = pltpu.roll(packed, LANES - heads * FD, 1)
+            keep = column_of(keep_ref[:, at])
+            wide_block = padded(projected_ref[at, :].astype(jnp.float32))
             ones = jnp.where(lane < 2, keep, 0.0).astype(jnp.bfloat16)
             inverses = inv_ref[at, :]
             for head in range(heads):
                 columns = slice(head * VD, (head + 1) * VD)
-                key_s[head, at, :] = head_lanes(rolled, rows, head, 0).astype(jnp.bfloat16)
-                query_s[head, at, :] = (head_lanes(packed, rows, head, 0) * 0.25).astype(jnp.bfloat16)
-                value_s[head, at, :VD] = (projected_ref[at, columns].astype(jnp.float32) * keep).astype(jnp.bfloat16)
+                query, key, value = head_parts(wide_block, head)
+                key_s[head, at, :] = key.astype(jnp.bfloat16)
+                query_s[head, at, :] = query.astype(jnp.bfloat16)
+                value_s[head, at, :VD] = (value * keep).astype(jnp.bfloat16)
                 value_s[head, at, VD:] = ones
                 inverse = inverses[:, head : head + 1]
                 grad = grad_ref[at, columns].astype(jnp.float32)
@@ -187,8 +211,8 @@
         allowed = row >= segment_start(ends_ref, column) - step * rows
         if diagonal:
             allowed &= row <= lax.broadcasted_iota(jnp.int32, (rows, rows), 1)
-        dkey, dvalues = totals
-        added = []
+        dkeys, dvalues = totals
+        added, turned = [], []
         for head in range(heads):
             query = query_s[head, at, :]
             error = error_s[head, at, :]
@@ -201,77 +225,59 @@
             added.append(
                 dvalues[head] + jnp.dot(weights, error[:, :VD], preferred_element_type=jnp.float32)
             )
-            dkey = dkey + jnp.dot(dinner, query, preferred_element_type=jnp.float32)
-            dquery_s[at, :] += lax.dot_general(dinner, keys, TN, preferred_element_type=jnp.float32)
-        return dkey, tuple(added)
+            turned.append(dkeys[head] + jnp.dot(dinner, query, preferred_element_type=jnp.float32))
+            dquery_s[head, at, :] += lax.dot_general(dinner, keys, TN, preferred_element_type=jnp.float32)
+        return tuple(turned), tuple(added)
 
     totals = (
-        jnp.zeros((rows, LANES), jnp.float32),
+        tuple(jnp.zeros((rows, LANES), jnp.float32) for _ in range(heads)),
         tuple(jnp.zeros((rows, VD), jnp.float32) for _ in range(heads)),
     )
     totals = tile(step, totals, True)
-    dkey, dvalues = lax.fori_loop(step + 1, blocks, lambda block, held: tile(block, held, False), totals)
-    keep = keep_ref[own, :]
+    dkeys, dvalues = lax.fori_loop(step + 1, blocks, lambda block, held: tile(block, held, False), totals)
+    keep = column_of(keep_ref[:, own])
+    width = out_ref.shape[2]
+    total = jnp.zeros((rows, width + -width % LANES), jnp.float32)
+    blank = jnp.zeros((rows, total.shape[1] - LANES), jnp.float32)
+
+    def put(block, low):
+        spread = jnp.concatenate([block, blank], axis=1)
+        return spread if low == 0 else pltpu.roll(spread, low, 1)
+
     for head in range(heads):
-        out_ref[:, head * VD : (head + 1) * VD] = (dvalues[head] * keep).astype(jnp.bfloat16)
-    packed = (dquery_s[own, :] * 0.25 + pltpu.roll(dkey, heads * FD, 1)).astype(jnp.bfloat16)
-    out_ref[:, heads * VD :] = packed[:, : 2 * heads * FD]
-
-
-def attend_back(projected, keep, ends, y, inverses, grad, heads):
+        low = head * (2 * FD + VD)
+        total += put(dquery_s[head, own, :] * 0.25, low)
+        total += put(dkeys[head], low + FD)
+        total += put(dvalues[head] * keep, low + 2 * FD)
+    out_ref[...] = total[:, :width].astype(jnp.bfloat16).reshape(out_ref.shape)
+
+
+def attend_back(projected, keep, ends, y, inverses, grad, heads, each):
     total = projected.shape[0]
     rows = min(512, total)
     width = projected.shape[1]
-    pairs = total * (total + rows) // 2 * heads
-    packed = heads * (2 * FD + VD)
     whole = lambda columns: pl.BlockSpec((total, columns), lambda i, e: (0, 0))
     return pl.pallas_call(
         functools.partial(attend_back_kernel, heads, rows),
         grid_spec=pltpu.PrefetchScalarGridSpec(
             num_scalar_prefetch=1,
             grid=(total // rows,),
-            in_specs=[whole(width), whole(1), whole(heads * VD), whole(LANES), whole(heads * VD)],
-            out_specs=pl.BlockSpec((rows, packed), lambda i, e: (i, 0)),
+            in_specs=[whole(width), pl.BlockSpec((1, total), lambda i, e: (0, 0)), whole(heads * VD), whole(LANES), whole(heads * VD)],
+            out_specs=pl.BlockSpec((rows // each, each, width), lambda i, e: (i, 0, 0)),
             scratch_shapes=[
                 pltpu.VMEM((heads, total, LANES), jnp.bfloat16),
                 pltpu.VMEM((heads, total, LANES), jnp.bfloat16),
                 pltpu.VMEM((heads, total, 2 * VD), jnp.bfloat16),
                 pltpu.VMEM((heads, total, 2 * VD), jnp.bfloat16),
-                pltpu.VMEM((total, LANES), jnp.float32),
+                pltpu.VMEM((heads, total, LANES), jnp.float32),
             ],
         ),
-        out_shape=jax.ShapeDtypeStruct((total, packed), jnp.bfloat16),
+        out_shape=jax.ShapeDtypeStruct((total // each, each, width), jnp.bfloat16),
         compiler_params=pltpu.CompilerParams(
             dimension_semantics=("arbitrary",), vmem_limit_bytes=VMEM
         ),
-        cost_estimate=pl.CostEstimate(flops=pairs * 2560, bytes_accessed=12 << 20, transcendentals=0),
+        cost_estimate=LITTLE,
     )(ends, projected, keep, y, inverses, grad)
-
-
-def pack_columns(weight, heads):
-    depth = weight.shape[0]
-    per_head = weight.reshape(depth, heads, 2 * FD + VD)
-    return jnp.concatenate(
-        [
-            per_head[:, :, 2 * FD :].reshape(depth, heads * VD),
-            per_head[:, :, :FD].reshape(depth, heads * FD),
-            per_head[:, :, FD : 2 * FD].reshape(depth, heads * FD),
-        ],
-        axis=1,
-    )
-
-
-def unpack_columns(packed, heads):
-    depth = packed.shape[0]
-    wide, narrow = heads * VD, heads * FD
-    return jnp.concatenate(
-        [
-            packed[:, wide : wide + narrow].reshape(depth, heads, FD),
-            packed[:, wide + narrow : wide + 2 * narrow].reshape(depth, heads, FD),
-            packed[:, :wide].reshape(depth, heads, VD),
-        ],
-        axis=2,
-    ).reshape(depth, heads * (2 * FD + VD))
 
 
 def inv_root_mean(values):
@@ -328,6 +334,11 @@
     def over_y(self, values, shift):
         return lax.ppermute(
             values, "dp", [(i, ((i // 2 + shift) % self.ny) * 2 + i % 2) for i in range(self.dp)]
+        )
+
+    def over_dp(self, values, shift):
+        return lax.ppermute(
+            values, "dp", [(i, ((i // 2 + shift) % self.ny) * 2 + (i + 1) % 2) for i in range(self.dp)]
         )
 
     def over_core(self, values):
@@ -459,9 +470,9 @@
 
     def fill(self, places_ref, refs, scratch, sems):
         copies = []
-        for core in range(2):
-            for piece, (s, t, first, count) in enumerate(self.layout):
-                column = pl.multiple_of(places_ref[2 * self.nz + 2 * s + t], self.size)
+        for piece, (s, t, first, count) in enumerate(self.layout):
+            column = pl.multiple_of(places_ref[2 * self.nz + 2 * s + t], self.size)
+            for core in range(2):
                 for slot in range(count):
                     row = pl.multiple_of(places_ref[core * self.nz + first + slot], self.rows)
                     copies.append(
@@ -484,14 +495,27 @@
     return jnp.concatenate([blocks_ref[i] for i in range(blocks_ref.shape[0])], axis=1)
 
 
+def by_columns(whole, places_ref, copies, weight_s, blocks, total_ref):
+    each = len(copies) // len(whole.layout)
+    for piece, (s, t, _, _) in enumerate(whole.layout):
+        for copy in copies[piece * each : (piece + 1) * each]:
+            copy.wait()
+        at = pl.ds(pl.multiple_of(places_ref[2 * whole.nz + 2 * s + t], whole.size), whole.size)
+        total, low = 0.0, 0
+        for block in blocks:
+            total += jnp.dot(
+                block, weight_s[low : low + block.shape[1], at], preferred_element_type=jnp.float32
+            )
+            low += block.shape[1]
+        total_ref[:, at] = total
+
+
 def mix_kernel(whole, places_ref, *refs):
     count = len(whole.pieces)
     attended_ref, tokens_ref, gain_ref, middle_ref, normed_ref, weight_s, sems = refs[count:]
-    for copy in whole.fill(places_ref, refs[:count], weight_s, sems):
-        copy.wait()
-    middle = jnp.dot(
-        side_by_side(attended_ref), weight_s[...], preferred_element_type=jnp.float32
-    ) + wide(tokens_ref[...])
+    copies = whole.fill(places_ref, refs[:count], weight_s, sems)
+    by_columns(whole, places_ref, copies, weight_s, [side_by_side(attended_ref)], middle_ref)
+    middle = middle_ref[...] + wide(tokens_ref[...])
     middle_ref[...] = middle
     normed_ref[...] = (middle * inv_root_mean(middle) * gain_ref[...]).astype(jnp.bfloat16)
 
@@ -512,7 +536,7 @@
         ),
         out_shape=[jax.ShapeDtypeStruct(shape, kind) for shape, kind in outs],
         compiler_params=pltpu.CompilerParams(vmem_limit_bytes=VMEM),
-        cost_estimate=pl.CostEstimate(flops=flops, bytes_accessed=16 << 20, transcendentals=0),
+        cost_estimate=LITTLE,
     )(whole.places, *whole.pieces, *args)
 
 
@@ -571,16 +595,10 @@
 def last_kernel(whole, places_ref, *refs):
     count = len(whole.pieces)
     proj_ref, tokens_ref, dmiddle_ref, gain_ref, grad_ref, weight_s, sems = refs[count:]
-    for copy in whole.fill(places_ref, refs[:count], weight_s, sems):
-        copy.wait()
-    width = proj_ref.shape[2]
-    dnormed = jnp.zeros(grad_ref.shape, jnp.float32)
-    for head in range(proj_ref.shape[0]):
-        dnormed += jnp.dot(
-            proj_ref[head],
-            weight_s[head * width : (head + 1) * width, :],
-            preferred_element_type=jnp.float32,
-        )
+    copies = whole.fill(places_ref, refs[:count], weight_s, sems)
+    blocks = [proj_ref[head] for head in range(proj_ref.shape[0])]
+    by_columns(whole, places_ref, copies, weight_s, blocks, grad_ref)
+    dnormed = grad_ref[...]
     tokens = wide(tokens_ref[...])
     inv_one = inv_root_mean(tokens)
     scaled = tokens * inv_one
@@ -632,123 +650,187 @@
         return copies
 
 
-def gate_kernel(units, places_ref, *refs):
-    pieces, refs = refs[: len(units.pieces)], refs[len(units.pieces) :]
-    blocks, (gate_ref, up_ref, normed_ref, weight_s, sems, in_sems) = refs[:2], refs[2:]
-    rows = blocks[0].shape[0]
-    copies = [
-        pltpu.make_async_copy(blocks[i], normed_ref.at[pl.ds(i * rows, rows)], in_sems.at[i])
-        for i in range(2)
-    ]
-    for copy in copies:
-        copy.start()
-    weights = units.fill(places_ref, pieces, weight_s, sems)
-    each = len(weights) // units.matrices
-    for copy in copies + weights[:each]:
-        copy.wait()
-    normed = normed_ref[...]
-    gate_ref[...] = lax.dot_general(normed, weight_s[0], NT, preferred_element_type=jnp.float32)
-    for copy in weights[each:]:
-        copy.wait()
-    up_ref[...] = lax.dot_general(normed, weight_s[1], NT, preferred_element_type=jnp.float32)
-
-
-def with_units(kernel, units, blocks, values, outs, flops, transcendentals):
-    in_vmem, anywhere = pl.BlockSpec(memory_space=pltpu.VMEM), pl.BlockSpec(memory_space=pl.ANY)
+def with_units(kernel, units, blocks, outs, scratch, flops, transcendentals):
+    anywhere = pl.BlockSpec(memory_space=pl.ANY)
     copies = sum(count for _, count, _, _ in units.layout)
     return pl.pallas_call(
         functools.partial(kernel, units),
         grid_spec=pltpu.PrefetchScalarGridSpec(
             num_scalar_prefetch=1,
             grid=(),
-            in_specs=[anywhere] * (len(units.pieces) + len(blocks)) + [in_vmem] * len(values),
-            out_specs=[in_vmem] * len(outs),
+            in_specs=[anywhere] * (len(units.pieces) + len(blocks)),
+            out_specs=[anywhere] * len(outs),
             scratch_shapes=[
                 pltpu.VMEM(units.shape, jnp.bfloat16),
                 pltpu.SemaphoreType.DMA((copies,)),
-                pltpu.SemaphoreType.DMA((len(blocks),)),
-            ],
+            ]
+            + scratch,
         ),
         out_shape=[jax.ShapeDtypeStruct(shape, kind) for shape, kind in outs],
         compiler_params=pltpu.CompilerParams(vmem_limit_bytes=VMEM),
-        cost_estimate=pl.CostEstimate(
-            flops=flops, bytes_accessed=20 << 20, transcendentals=transcendentals
-        ),
-    )(units.places, *units.pieces, *blocks, *values)
-
-
-def gate_up(pair, units):
-    rows, depth = pair[0].shape
-    out = ((2 * rows, units.shape[1]), jnp.float32)
-    return with_units(
-        gate_kernel,
-        units,
-        pair,
-        (),
-        (out, out, ((2 * rows, depth), jnp.bfloat16)),
-        8 * rows * depth * units.shape[1],
-        0,
-    )
-
-
-def down_kernel(units, places_ref, *refs):
-    pieces, refs = refs[: len(units.pieces)], refs[len(units.pieces) :]
-    grads, (gate_ref, up_ref) = refs[:2], refs[2:4]
-    hidden_ref, dgate_ref, dup_ref, grad_ref = refs[4:8]
-    dnormed, branches = refs[8:10], refs[10:12]
-    weight_s, sems, in_sems = refs[12:]
-    rows = grads[0].shape[0]
-    both = [slice(0, rows), slice(rows, 2 * rows)]
-    copies = [
-        pltpu.make_async_copy(grads[i], grad_ref.at[both[i]], in_sems.at[i]) for i in range(2)
-    ]
+        cost_estimate=LITTLE,
+    )(units.places, *units.pieces, *blocks)
+
+
+def started(copies):
     for copy in copies:
         copy.start()
+    return copies
+
+
+def awaited(copies):
+    for copy in copies:
+        copy.wait()
+
+
+def gate_kernel(count, units, places_ref, *refs):
+    pieces, refs = refs[: len(units.pieces)], refs[len(units.pieces) :]
+    blocks, (gate_ref, up_ref, normed_ref) = refs[: 2 * count], refs[2 * count : 2 * count + 3]
+    weight_s, sems, normed_s, gate_s, up_s, in_sems, out_sems = refs[2 * count + 3 :]
+    rows = blocks[0].shape[0]
+    arrivals = [
+        pltpu.make_async_copy(
+            blocks[i], normed_s.at[i // 2, pl.ds(i % 2 * rows, rows)], in_sems.at[i]
+        )
+        for i in range(2 * count)
+    ]
+    started(arrivals[:2])
     weights = units.fill(places_ref, pieces, weight_s, sems)
+    started(arrivals[2:])
     each = len(weights) // units.matrices
-    gate, up = gate_ref[...], up_ref[...]
-    sigmoid = jax.nn.sigmoid(gate)
-    silu = gate * sigmoid
-    hidden = (silu * up).astype(jnp.bfloat16)
-    hidden_ref[...] = hidden
+    sent = []
+    for chunk in range(count):
+        awaited(arrivals[2 * chunk : 2 * chunk + 2])
+        sent += started(
+            [pltpu.make_async_copy(normed_s.at[chunk], normed_ref.at[chunk], out_sems.at[3 * chunk])]
+        )
+        normed = normed_s[chunk]
+        awaited(weights[:each] if chunk == 0 else [])
+        gate_s[chunk] = lax.dot_general(normed, weight_s[0], NT, preferred_element_type=jnp.float32)
+        sent += started(
+            [pltpu.make_async_copy(gate_s.at[chunk], gate_ref.at[chunk], out_sems.at[3 * chunk + 1])]
+        )
+        awaited(weights[each:] if chunk == 0 else [])
+        up_s[chunk] = lax.dot_general(normed, weight_s[1], NT, preferred_element_type=jnp.float32)
+        sent += started(
+            [pltpu.make_async_copy(up_s.at[chunk], up_ref.at[chunk], out_sems.at[3 * chunk + 2])]
+        )
+    awaited(sent)
+
+
+def gate_up(pairs, units):
+    count = len(pairs)
+    rows, depth = pairs[0][0].shape
+    unit, full = (count, 2 * rows, units.shape[1]), (count, 2 * rows, depth)
+    return with_units(
+        functools.partial(gate_kernel, count),
+        units,
+        [block for pair in pairs for block in pair],
+        ((unit, jnp.float32), (unit, jnp.float32), (full, jnp.bfloat16)),
+        [
+            pltpu.VMEM(full, jnp.bfloat16),
+            pltpu.VMEM(unit, jnp.float32),
+            pltpu.VMEM(unit, jnp.float32),
+            pltpu.SemaphoreType.DMA((2 * count,)),
+            pltpu.SemaphoreType.DMA((3 * count,)),
+        ],
+        8 * count * rows * depth * units.shape[1],
+        0,
+    )
+
+
+def down_kernel(places, units, places_ref, *refs):
+    count = len(places)
+    pieces, refs = refs[: len(units.pieces)], refs[len(units.pieces) :]
+    blocks, refs = refs[: 4 * count], refs[4 * count :]
+    unit_refs, grad_ref, refs = refs[:3], refs[3], refs[4:]
+    dnormed, branches = refs[: 2 * count], refs[2 * count : 4 * count]
+    weight_s, sems, pre_s, grad_s, unit_s, back_s, branch_s, in_sems, out_sems = refs[4 * count :]
+    rows = blocks[0].shape[0]
+    both = [pl.ds(0, rows), pl.ds(rows, rows)]
+    arrivals = []
+    for chunk, place in enumerate(places):
+        one, two, gate, up = blocks[4 * chunk : 4 * chunk + 4]
+        for i, (source, target) in enumerate(
+            (
+                (gate.at[place], pre_s.at[chunk, 0]),
+                (up.at[place], pre_s.at[chunk, 1]),
+                (one, grad_s.at[chunk, both[0]]),
+                (two, grad_s.at[chunk, both[1]]),
+            )
+        ):
+            arrivals.append(pltpu.make_async_copy(source, target, in_sems.at[4 * chunk + i]))
+    started(arrivals[:4])
+    weights = units.fill(places_ref, pieces, weight_s, sems)
+    started(arrivals[4:])
+    each = len(weights) // units.matrices
     dot = functools.partial(jnp.dot, preferred_element_type=jnp.float32)
-    for copy in copies + weights[:each]:
-        copy.wait()
-    dhidden = lax.dot_general(grad_ref[...], weight_s[0], NT, preferred_element_type=jnp.float32)
-    branch = dot(hidden, weight_s[0]).astype(jnp.bfloat16)
-    dgate = (dhidden * up * sigmoid * (1.0 + gate * (1.0 - sigmoid))).astype(jnp.bfloat16)
-    dup = (dhidden * silu).astype(jnp.bfloat16)
-    dgate_ref[...] = dgate
-    dup_ref[...] = dup
-    for copy in weights[each:]:
-        copy.wait()
-    back = (dot(dgate, weight_s[1]) + dot(dup, weight_s[2])).astype(jnp.bfloat16)
-    for i in range(2):
-        branches[i][...] = branch[both[i]]
-        dnormed[i][...] = back[both[i]]
-
-
-def down(grads, gate, up, units):
-    rows, depth = grads[0].shape
-    unit = (gate.shape, jnp.bfloat16)
+    sent = []
+
+    def send(source, target):
+        sent.append(pltpu.make_async_copy(source, target, out_sems.at[len(sent)]))
+        sent[-1].start()
+
+    for chunk in range(count):
+        awaited(arrivals[4 * chunk : 4 * chunk + 2])
+        gate, up = pre_s[chunk, 0], pre_s[chunk, 1]
+        sigmoid = jax.nn.sigmoid(gate)
+        silu = gate * sigmoid
+        hidden = (silu * up).astype(jnp.bfloat16)
+        unit_s[chunk, 0] = hidden
+        send(unit_s.at[chunk, 0], unit_refs[0].at[chunk])
+        awaited(arrivals[4 * chunk + 2 : 4 * chunk + 4])
+        send(grad_s.at[chunk], grad_ref.at[chunk])
+        awaited(weights[:each] if chunk == 0 else [])
+        dhidden = lax.dot_general(grad_s[chunk], weight_s[0], NT, preferred_element_type=jnp.float32)
+        dgate = (dhidden * up * sigmoid * (1.0 + gate * (1.0 - sigmoid))).astype(jnp.bfloat16)
+        dup = (dhidden * silu).astype(jnp.bfloat16)
+        unit_s[chunk, 1] = dgate
+        unit_s[chunk, 2] = dup
+        send(unit_s.at[chunk, 1], unit_refs[1].at[chunk])
+        send(unit_s.at[chunk, 2], unit_refs[2].at[chunk])
+        awaited(weights[each:] if chunk == 0 else [])
+        back_s[chunk] = (dot(dgate, weight_s[1]) + dot(dup, weight_s[2])).astype(jnp.bfloat16)
+        for i in range(2):
+            send(back_s.at[chunk, both[i]], dnormed[2 * chunk + i])
+        branch_s[chunk] = dot(hidden, weight_s[0]).astype(jnp.bfloat16)
+        for i in range(2):
+            send(branch_s.at[chunk, both[i]], branches[2 * chunk + i])
+    awaited(sent)
+
+
+def down(given, units):
+    count = len(given)
+    rows, depth = given[0][0].shape
+    unit, full = (count, 2 * rows, units.shape[1]), (count, 2 * rows, depth)
     part = ((rows, depth), jnp.bfloat16)
     outs = with_units(
-        down_kernel,
+        functools.partial(down_kernel, [chunk[4] for chunk in given]),
         units,
-        grads,
-        (gate, up),
-        (unit, unit, unit, ((2 * rows, depth), jnp.bfloat16), part, part, part, part),
-        16 * rows * depth * units.shape[1],
-        2 * rows * units.shape[1],
-    )
-    return outs[:4], outs[4:6], outs[6:]
-
-
-def unit_grad_kernel(count, ny, nzh, places_ref, *refs):
-    lefts, rights = refs[:count], refs[count : 2 * count]
-    mine_ref, sent_ref, total_s = refs[2 * count :]
-    for i in range(count):
-        added = lax.dot_general(lefts[i][...], rights[i][...], TN, preferred_element_type=jnp.float32)
+        [block for chunk in given for block in chunk[:4]],
+        ((unit, jnp.bfloat16),) * 3 + ((full, jnp.bfloat16),) + (part,) * (4 * count),
+        [
+            pltpu.VMEM((count, 2, 2 * rows, units.shape[1]), jnp.float32),
+            pltpu.VMEM(full, jnp.bfloat16),
+            pltpu.VMEM((count, 3, 2 * rows, units.shape[1]), jnp.bfloat16),
+            pltpu.VMEM(full, jnp.bfloat16),
+            pltpu.VMEM(full, jnp.bfloat16),
+            pltpu.SemaphoreType.DMA((4 * count,)),
+            pltpu.SemaphoreType.DMA((8 * count,)),
+        ],
+        16 * count * rows * depth * units.shape[1],
+        2 * count * rows * units.shape[1],
+    )
+    halves = lambda parts: [parts[2 * i : 2 * i + 2] for i in range(count)]
+    return outs[:4], halves(outs[4 : 4 + 2 * count]), halves(outs[4 + 2 * count :])
+
+
+def unit_grad_kernel(order, ny, nzh, places_ref, *refs):
+    arrays, (mine_ref, sent_ref, total_s) = refs[:-3], refs[-3:]
+    for i, (left, at, right, to) in enumerate(order):
+        added = lax.dot_general(
+            arrays[left][at], arrays[right][to], TN, preferred_element_type=jnp.float32
+        )
         if i == 0:
             total_s[...] = added
         else:
@@ -768,20 +850,29 @@
 
 def unit_grad(wires, lefts, rights):
     ny, nzh = wires.ny, wires.nzh
-    units, depth = lefts[0].shape[1], rights[0].shape[1]
+    arrays = []
+
+    def index(array):
+        for i, other in enumerate(arrays):
+            if other is array:
+                return i
+        arrays.append(array)
+        return len(arrays) - 1
+
+    order = [(index(left), at, index(right), to) for (left, at), (right, to) in zip(lefts, rights)]
+    units, depth = lefts[0][0].shape[2], rights[0][0].shape[2]
+    tokens = len(lefts) * lefts[0][0].shape[1]
     rows, columns = units // nzh, depth // ny
     places = jnp.stack(
-        [((wires.y + s) % ny) * columns for s in range(ny)]
-        + [s * rows for s in range(nzh)]
+        [((wires.y + s) % ny) * columns for s in range(ny)] + [s * rows for s in range(nzh)]
     ).astype(jnp.int32)
     in_vmem = pl.BlockSpec(memory_space=pltpu.VMEM)
-    tokens = sum(left.shape[0] for left in lefts)
     return pl.pallas_call(
-        functools.partial(unit_grad_kernel, len(lefts), ny, nzh),
+        functools.partial(unit_grad_kernel, order, ny, nzh),
         grid_spec=pltpu.PrefetchScalarGridSpec(
             num_scalar_prefetch=1,
             grid=(),
-            in_specs=[in_vmem] * (2 * len(lefts)),
+            in_specs=[in_vmem] * len(arrays),
             out_specs=[in_vmem] * 2,
             scratch_shapes=[pltpu.VMEM((units, depth), jnp.float32)],
         ),
@@ -790,57 +881,97 @@
             jax.ShapeDtypeStruct((ny - 1, nzh, rows, columns), jnp.bfloat16),
         ],
         compiler_params=pltpu.CompilerParams(vmem_limit_bytes=VMEM),
-        cost_estimate=pl.CostEstimate(
-            flops=2 * tokens * depth * units, bytes_accessed=14 << 20, transcendentals=0
-        ),
-    )(places, *lefts, *rights)
-
-
-def out_grad_kernel(nz, ny, places_ref, left_ref, right_ref, mine_ref, sent_ref):
+        cost_estimate=LITTLE,
+    )(places, *arrays)
+
+
+def out_grad_kernel(nz, ny, places_ref, mine_ref, other_ref, grad_ref, other_grad_ref, *refs):
+    outs, (left_s, right_s) = refs[: 2 * ny], refs[2 * ny :]
     step = pl.program_id(0)
-    width = mine_ref.shape[4]
-    for core, out_ref in ((0, mine_ref), (1, sent_ref)):
-        left = left_ref[places_ref[core * nz + step]]
-        total = lax.dot_general(left, right_ref[...], TN, preferred_element_type=jnp.float32)
-        for x in range(2):
-            for y in range(ny):
-                out_ref[x, y, 0] = total[:, (x * ny + y) * width : (x * ny + y + 1) * width].astype(
-                    jnp.bfloat16
-                )
-
-
-def out_grad_parts(wires, attended, d_mixed):
-    heads, tokens, rows = attended.shape
+    tokens, width = grad_ref.shape[0], outs[0].shape[2]
+
+    @pl.when(step == 0)
+    def _():
+        right_s[:tokens] = grad_ref[...]
+        right_s[tokens:] = other_grad_ref[...]
+
+    left_s[:tokens] = mine_ref[places_ref[step]]
+    left_s[tokens:] = other_ref[places_ref[step] // 2]
+    left = left_s[...]
+    for i, out_ref in enumerate(outs):
+        column = pl.multiple_of(places_ref[nz + i], width)
+        out_ref[0] = lax.dot_general(
+            left, right_s[:, pl.ds(column, width)], TN, preferred_element_type=jnp.float32
+        ).astype(jnp.bfloat16)
+
+
+def out_grad_parts(wires, mine, other, d_mixed, other_d_mixed):
+    heads, tokens, rows = mine.shape
     depth = d_mixed.shape[1]
     nz, ny, width = wires.nz, wires.ny, depth // wires.dp
     places = jnp.stack(
-        [((wires.z - s) % nz) * 2 + (wires.c ^ r) for r in range(2) for s in range(nz)]
+        [z * 2 + wires.c for z in range(nz)]
+        + [(((wires.y + s) % ny) * 2 + (wires.x ^ t)) * width for t in range(2) for s in range(ny)]
     ).astype(jnp.int32)
-    columns = [((wires.y + s) % ny) * 2 + (wires.x ^ t) for t in range(2) for s in range(ny)]
-    ordered = jnp.concatenate(
-        [lax.dynamic_slice_in_dim(d_mixed, column * width, width, 1) for column in columns], axis=1
-    )
-    out = jax.ShapeDtypeStruct((2, ny, nz, rows, width), jnp.bfloat16)
-    block = pl.BlockSpec((2, ny, 1, rows, width), lambda i, p: (0, 0, i, 0, 0))
-    return pl.pallas_call(
+    full = lambda *shape: pl.BlockSpec(shape, lambda i, p: (0,) * len(shape))
+    outs = pl.pallas_call(
         functools.partial(out_grad_kernel, nz, ny),
         grid_spec=pltpu.PrefetchScalarGridSpec(
             num_scalar_prefetch=1,
             grid=(nz,),
             in_specs=[
-                pl.BlockSpec((heads, tokens, rows), lambda i, p: (0, 0, 0)),
-                pl.BlockSpec((tokens, depth), lambda i, p: (0, 0)),
+                full(heads, tokens, rows),
+                full(nz, tokens, rows),
+                full(tokens, depth),
+                full(tokens, depth),
             ],
-            out_specs=[block, block],
+            out_specs=[pl.BlockSpec((1, rows, width), lambda i, p: (i, 0, 0))] * (2 * ny),
+            scratch_shapes=[
+                pltpu.VMEM((2 * tokens, rows), jnp.bfloat16),
+                pltpu.VMEM((2 * tokens, depth), jnp.bfloat16),
+            ],
         ),
-        out_shape=[out, out],
+        out_shape=[jax.ShapeDtypeStruct((nz, rows, width), jnp.bfloat16)] * (2 * ny),
         compiler_params=pltpu.CompilerParams(
             dimension_semantics=("arbitrary",), vmem_limit_bytes=VMEM
         ),
-        cost_estimate=pl.CostEstimate(
-            flops=2 * tokens * depth * heads * rows, bytes_accessed=10 << 20, transcendentals=0
+        cost_estimate=LITTLE,
+    )(places, mine, other, d_mixed, other_d_mixed)
+    return outs[:ny], outs[ny:]
+
+
+def in_grad_kernel(normed_ref, grad_ref, weight_ref, gain_ref, out_ref, part_ref):
+    blocks, rows, width = grad_ref.shape
+    grad = grad_ref[...].reshape(blocks * rows, width)
+    total = lax.dot_general(grad, normed_ref[...], TN, preferred_element_type=jnp.float32)
+    out_ref[...] = total.astype(jnp.bfloat16)
+    part_ref[...] = jnp.sum(total * wide(weight_ref[...]), axis=0, keepdims=True) / gain_ref[...]
+
+
+def in_grad_parts(normed, grad, weight, gain):
+    tokens, depth = normed.shape
+    width = grad.shape[2]
+    size = min(512, depth)
+    block = lambda rows: pl.BlockSpec((rows, size), lambda i: (0, i))
+    return pl.pallas_call(
+        in_grad_kernel,
+        grid=(depth // size,),
+        in_specs=[
+            block(tokens),
+            pl.BlockSpec(grad.shape, lambda i: (0, 0, 0)),
+            block(width),
+            block(1),
+        ],
+        out_specs=[block(width), block(1)],
+        out_shape=[
+            jax.ShapeDtypeStruct((width, depth), jnp.bfloat16),
+            jax.ShapeDtypeStruct((1, depth), jnp.float32),
+        ],
+        compiler_params=pltpu.CompilerParams(
+            dimension_semantics=("arbitrary",), vmem_limit_bytes=VMEM
         ),
-    )(places, attended, ordered)
+        cost_estimate=LITTLE,
+    )(normed, grad, weight, gain)
 
 
 def tie(*values):
@@ -865,7 +996,6 @@
     heads_here = in_weight.shape[1] // (2 * FD + VD)
     rows, depth = tokens.shape
     group_rows = rows * wires.head
-    half = rows // 2
     out_rows = heads_here * VD
     size = depth // wires.dp
     tokens_wide = wide(tokens)
@@ -881,11 +1011,10 @@
     def add(*values):
         return low(sum(wide(value) for value in values))
 
-    in_packed = pack_columns(in_weight, heads_here)
-    packed_width = in_packed.shape[1]
-    in_padded = jnp.pad(in_packed, ((0, 0), (0, heads_here * VD + LANES - packed_width)))
-    in_part = wires.quarter(in_packed.T)
-    keep_column = keep_mask.astype(jnp.float32)[:, None]
+    packed_width = in_weight.shape[1]
+    in_turned = in_weight.T
+    in_part = wires.quarter(in_turned)
+    keep_row = keep_mask.astype(jnp.float32)[None]
     ends = jnp.cumsum(seq_lengths[0])
     stacked = jnp.stack([gate_weight.T, up_weight.T, down_weight])
     unit_own = pick(stacked, wires.x, 2, 1)
@@ -933,7 +1062,7 @@
     out_line = shares(pieces[::2])
     out_x, out_y = wires.over_x(out_line), [wires.over_y(out_line, s) for s in across_y]
     projected, normed, attended_wide, inverses, attended = attend(
-        pieces, places, in_padded, keep_column, ends, heads_here
+        pieces, places, in_turned, keep_row, ends, heads_here
     )
     attended, out_x, out_y, by_zh_g, unit_pair, out_grad = tie(
         attended, out_x, out_y, by_zh_g, unit_pair, out_grad
@@ -944,8 +1073,8 @@
     by_zh_gy = on_y(by_zh_g)
     out_line_swap = shares(pieces[1::2])
     out_x_swap, out_y_swap = wires.over_core(out_x), [wires.over_core(piece) for piece in out_y]
-    attended_here, out_across, grad_z, out_x_swap, out_y_swap, unit_pair, by_zh_gy = tie(
-        attended_here, out_across, grad_z, out_x_swap, out_y_swap, unit_pair, by_zh_gy
+    attended_here, out_across, grad_z, out_x_swap, out_y_swap, unit_pair, by_zh_gy, out_line_swap = tie(
+        attended_here, out_across, grad_z, out_x_swap, out_y_swap, unit_pair, by_zh_gy, out_line_swap
     )
     out_across_swap = [wires.over_core(piece) for piece in out_across]
 
@@ -960,7 +1089,9 @@
     out_whole = Whole(wires, out_pieces, wires.whole_places(chips, out_rows, size), out_rows, size)
     middle, normed_two = mix(attended_here, out_whole, tokens, ffn_gain[None])
 
-    normed_two, unit_pair, grad_x, grad_z, out_grad = tie(normed_two, unit_pair, grad_x, grad_z, out_grad)
+    normed_two, unit_pair, grad_x, grad_z, out_grad = tie(
+        normed_two, unit_pair, grad_x, grad_z, out_grad
+    )
     two_x, two_z = wires.over_x(normed_two), wires.over_zl(normed_two)
     by_zh_u = [wires.over_zh(unit_pair[1:2], s) for s in range(1, wires.nzh)]
     by_y_d = [wires.over_y(unit_pair[2:], s) for s in across_y]
@@ -968,21 +1099,13 @@
     two_x, two_z, by_zh_u, two_swap, by_y_d, unit_pair = tie(
         two_x, two_z, by_zh_u, two_swap, by_y_d, unit_pair
     )
-    two_corner = (wires.over_zl(two_x[:half]), wires.over_x(two_z[half:]))
+    two_corner = wires.over_x(two_z)
     by_zh_uy = on_y(by_zh_u)
+    by_zh_d = [wires.over_zh(unit_pair[2:], s) for s in range(1, wires.nzh)]
     two_swaps = [two_swap] + [wires.over_core(piece) for piece in (two_x, two_z)]
-    two_corner, by_zh_uy, two_swaps, two_x, two_z, unit_pair = tie(
-        two_corner, by_zh_uy, two_swaps, two_x, two_z, unit_pair
-    )
-    two_corner = jnp.concatenate(two_corner, axis=0)
-
-    def spots(matrix, place, by_y, piece, on):
-        units = [(unit_pair[matrix : matrix + 1], place, 1, 0, 0)]
-        units += [(by_y[s - 1], place, 1, 0, s) for s in across_y]
-        for zh in range(1, wires.nzh):
-            units.append((piece[zh - 1], place, 1, zh, 0))
-            units += [(on[zh - 1][s - 1], place, 1, zh, s) for s in across_y]
-        return units
+    two_corner, by_zh_uy, two_swaps, two_x, two_z, grad_z, attended_here, by_zh_d = tie(
+        two_corner, by_zh_uy, two_swaps, two_x, two_z, grad_z, attended_here, by_zh_d
+    )
 
     spot = unit_pair.shape[1], unit_pair.shape[2]
     gu_pair = unit_pair[:2]
@@ -993,18 +1116,19 @@
             gates += [(on[zh - 1][s - 1], place, 1, zh, s) for s in across_y]
     units = Units(wires, gates, 2, *spot)
 
-    by_zh_d = [wires.over_zh(unit_pair[2:], s) for s in range(1, wires.nzh)]
     grad_corner = wires.over_x(grad_z)
     two_corner_swap = wires.over_core(two_corner)
-    first = [gate_up(pair, units) for pair in zip([normed_two, two_x, two_z], two_swaps)]
-    first, by_zh_d, grad_corner, two_corner, two_corner_swap, grad_z = tie(
-        first, by_zh_d, grad_corner, two_corner, two_corner_swap, grad_z
-    )
+    for_other = pick(attended_here.reshape(wires.nz, 2, rows, out_rows), 1 - wires.c, 2, 1)[:, 0]
+    attended_other = wires.over_core(for_other)
     by_zh_dy = on_y(by_zh_d)
-    grad_all = [out_grad, grad_x, grad_z, grad_corner]
-    grad_pairs = [(grad, wires.over_core(grad)) for grad in grad_all]
-    first.append(gate_up((two_corner, two_corner_swap), units))
-    first, by_zh_dy, grad_pairs = tie(first, by_zh_dy, grad_pairs)
+    first = gate_up(list(zip([normed_two, two_x, two_z], two_swaps)), units)
+    first, grad_corner, two_corner, two_corner_swap, grad_z, attended_other, by_zh_dy = tie(
+        first, grad_corner, two_corner, two_corner_swap, grad_z, attended_other, by_zh_dy
+    )
+    grad_swaps = [wires.over_core(grad) for grad in (out_grad, grad_x, grad_z, grad_corner)]
+    second = gate_up([(two_corner, two_corner_swap)], units)
+    second, grad_swaps = tie(second, grad_swaps)
+    grad_pairs = list(zip([out_grad, grad_x, grad_z, grad_corner], grad_swaps))
     downs = [(unit_pair[2:], 0, 1, 0, 0)] + [(by_y_d[s - 1], 0, 1, 0, s) for s in across_y]
     for zh in range(1, wires.nzh):
         downs.append((by_zh_d[zh - 1], 0, 1, zh, 0))
@@ -1013,147 +1137,172 @@
         wires, downs + [(array, at + 1, count, zh, s) for array, at, count, zh, s in gates], 3, *spot
     )
 
-    def feed(place, *after):
-        given, grads, *_ = tie(first[place], grad_pairs[place], *after)
-        gate, up, normed = given
-        outs, dnormed, branches = down(grads, gate, up, units)
-        return (*outs[:3], normed, outs[3]), dnormed, branches
-
     in_part, grad_corner = tie(flying["in_part"], grad_corner)
     in_line = [in_part] + [wires.over_z(in_part, s) for s in range(1, wires.nz)]
-    unit_c, dnormed_c, branch_c = feed(3)
-    swap_c = wires.over_core(dnormed_c[1])
-    unit_o, dnormed_o, branch_o = feed(0, unit_c)
-    unit_o, swap_c, in_line = tie(unit_o, swap_c, in_line)
+    outs_co, (dnormed_c, dnormed_o), (branch_c, branch_o) = down(
+        [(*grad_pairs[3], second[0], second[1], 0), (*grad_pairs[0], first[0], first[1], 0)], units
+    )
+    outs_co, in_line, dnormed_c, dnormed_o = tie(outs_co, in_line, dnormed_c, dnormed_o)
+    swap_c, swap_o = wires.over_core(dnormed_c[1]), wires.over_core(dnormed_o[1])
+    swap_c, swap_o, outs_co, in_line = tie(swap_c, swap_o, outs_co, in_line)
     sum_c = add(dnormed_c[0], swap_c)
-    to_z, to_x = wires.over_x(sum_c[:half]), wires.over_zl(sum_c[half:])
+    to_z = wires.over_x(sum_c)
     in_line = jnp.stack(in_line)
     in_y = [wires.over_y(in_line, s) for s in across_y]
-    swap_o = wires.over_core(dnormed_o[1])
-    unit_x, dnormed_x, branch_x = feed(1, unit_o, sum_c, in_line)
-    unit_x, to_x, to_z, swap_o = tie(unit_x, to_x, to_z, swap_o)
-    swap_x = wires.over_core(dnormed_x[1])
-    in_x = wires.over_x(in_line)
-    unit_z, dnormed_z, branch_z = feed(2, unit_x)
-    swap_z = wires.over_core(dnormed_z[1])
-    unit_z, swap_x, swap_z, in_x, in_y = tie(unit_z, swap_x, swap_z, in_x, in_y)
-    sum_x = jnp.concatenate(
-        [add(dnormed_x[0][:half], swap_x[:half]), add(dnormed_x[0][half:], swap_x[half:], to_x)], axis=0
-    )
+    grad_x_pair, grad_z_pair, *_ = tie(grad_pairs[1], grad_pairs[2], sum_c, outs_co)
+    outs_xz, (dnormed_x, dnormed_z), (branch_x, branch_z) = down(
+        [(*grad_x_pair, first[0], first[1], 1), (*grad_z_pair, first[0], first[1], 2)], units
+    )
+    dnormed_x, dnormed_z, to_z, in_y = tie(dnormed_x, dnormed_z, to_z, in_y)
+    swap_x, swap_z = wires.over_core(dnormed_x[1]), wires.over_core(dnormed_z[1])
+    swap_x, swap_z, to_z = tie(swap_x, swap_z, to_z)
+    sum_x = add(dnormed_x[0], swap_x)
     final_x = wires.over_x(sum_x)
-    sum_z = jnp.concatenate(
-        [add(dnormed_z[0][:half], swap_z[:half], to_z), add(dnormed_z[0][half:], swap_z[half:])], axis=0
-    )
+    sum_z = add(dnormed_z[0], swap_z, to_z)
     final_z = wires.over_zl(sum_z)
     sum_o = add(dnormed_o[0], swap_o)
-    in_across = [wires.over_y(in_x, s) for s in across_y]
-
-    every = [unit_o, unit_x, unit_z, unit_c]
+
+    every = (outs_co, outs_xz, first[2], second[2])
 
     def grad_of(every, unit, token):
-        return unit_grad(wires, [outs[unit] for outs in every], [outs[token] for outs in every])
+        co, xz, normed_oxz, normed_c = every
+        lefts = [(co[unit], 0), (co[unit], 1), (xz[unit], 0), (xz[unit], 1)]
+        if token:
+            rights = [(co[3], 0), (co[3], 1), (xz[3], 0), (xz[3], 1)]
+        else:
+            rights = [(normed_c, 0), (normed_oxz, 0), (normed_oxz, 1), (normed_oxz, 2)]
+        return unit_grad(wires, lefts, rights)
 
     def grad_y(mine, sent):
         return mine, [wires.over_y(sent[s - 1], s) for s in across_y]
 
-    def grad_zh(mine, sent):
-        total = add(mine, *sent)
-        return total[0], [wires.over_zh(total[s], -s) for s in range(1, wires.nzh)]
-
-    def grad_x_swap(mine, sent):
-        total = add(mine, *sent)
-        return pick(total, wires.x, 2, 1), wires.over_x(pick(total, 1 - wires.x, 2, 1))
-
     def grad_last(mine, sent):
         return wide(in_order([mine, sent], wires.x, 0))
 
     every, sum_x, sum_z = tie(every, sum_x, sum_z)
-    gate_mine, gate_sent = grad_of(every, 1, 3)
-    in_swaps = [wires.over_core(piece) for piece in (in_line, in_x, *in_y)]
-    final_x, final_z, gate_mine, gate_sent, in_swaps, in_across = tie(
-        final_x, final_z, gate_mine, gate_sent, in_swaps, in_across
+    gate_mine, gate_sent = grad_of(every, 1, False)
+    in_swaps = [wires.over_core(piece) for piece in (in_line, *in_y)]
+    final_x, final_z, gate_mine, gate_sent, in_swaps, sum_o, in_line = tie(
+        final_x, final_z, gate_mine, gate_sent, in_swaps, sum_o, in_line
     )
     gate_back = grad_y(gate_mine, gate_sent)
     d_middle, d_mixed, ffn_gain_part, d_attended = unmix(
         (sum_o, final_x, final_z), middle, out_grad, ffn_gain[None], out_whole, wires.head
     )
-    every, d_attended, d_mixed, branches = tie(
-        every, d_attended, d_mixed, (branch_o, branch_x, branch_z, branch_c)
+    every, d_attended, d_mixed, branches, in_line, in_y = tie(
+        every, d_attended, d_mixed, (branch_o, branch_x, branch_z, branch_c), in_line, in_y
     )
     d_attended = swap(d_attended).reshape(group_rows, out_rows)
-    out_mine, out_sent = out_grad_parts(wires, attended_here, d_mixed)
-    up_parts = grad_of(every, 2, 3)
-    down_parts = grad_of(every, 0, 4)
-    out_sent = wires.over_core(out_sent)
+    other_d_mixed = wires.over_core(d_mixed)
+    in_x = wires.over_x(in_line)
+    swap_c, swap_x, swap_z = (wires.over_core(branches[i][1]) for i in (3, 1, 2))
+    up_parts = grad_of(every, 2, False)
+    out_own, out_sent = out_grad_parts(wires, attended_here, attended_other, d_mixed, other_d_mixed)
+    down_parts = grad_of(every, 0, True)
+    d_attended, out_own, out_sent, up_parts, down_parts, gate_back, in_x, swap_c, swap_x, swap_z = tie(
+        d_attended, out_own, out_sent, up_parts, down_parts, gate_back, in_x, swap_c, swap_x, swap_z
+    )
+
+    def total_of(mine, sent):
+        return [add(mine[s], *[piece[s] for piece in sent]) for s in range(wires.nzh)]
+
+    def on_zh(totals):
+        return totals[0], [wires.over_zh(totals[s], -s) for s in range(1, wires.nzh)]
+
+    sum_c = add(branches[3][0], swap_c)
+    gate_totals = total_of(*gate_back)
+    gate_totals, d_attended, sum_c, out_sent, up_parts = tie(
+        gate_totals, d_attended, sum_c, out_sent, up_parts
+    )
+    up_back = grad_y(*up_parts)
+    gate_back = on_zh(gate_totals)
+    out_first = [wires.over_x(out_sent[s]) for s in across_y]
+    to_x = wires.over_zl(sum_c)
+    d_projected = attend_back(
+        projected, keep_row, ends, attended_wide, inverses, d_attended, heads_here, rows
+    )
+    d_projected, gate_back, up_back, to_x, out_first = tie(d_projected, gate_back, up_back, to_x, out_first)
+    d_projected, down_parts, in_y, out_own, out_first, in_x = tie(
+        d_projected, down_parts, in_y, out_own, out_first, in_x
+    )
+    d_here = swap(d_projected)
+    down_back = grad_y(*down_parts)
+    in_across = [wires.over_x(piece) for piece in in_y]
+    up_totals = total_of(*up_back)
+    in_back, attn_gain_part = in_grad_parts(normed, d_projected, in_turned, attn_gain[None])
+    d_here, in_back, attn_gain_part, down_back, up_totals, in_across = tie(
+        d_here, in_back, attn_gain_part, down_back, up_totals, in_across
+    )
     in_across_swap = [wires.over_core(piece) for piece in in_across]
-    d_attended, out_mine, out_sent, up_parts, down_parts, gate_back, in_across_swap = tie(
-        d_attended, out_mine, out_sent, up_parts, down_parts, gate_back, in_across_swap
-    )
-    up_back = grad_y(*up_parts)
-    gate_back = grad_zh(*gate_back)
-    out_total = add(out_mine, out_sent)
-    out_sent = wires.over_x(out_total[1])
-    d_attended, out_total = tie(d_attended, out_total)
-    d_projected = attend_back(
-        projected, keep_column, ends, attended_wide, inverses, d_attended, heads_here
-    )
-    swaps = [wires.over_core(branch[1]) for branch in branches]
-    d_projected, gate_back, up_back, branches, swaps = tie(
-        d_projected, gate_back, up_back, branches, swaps
-    )
-    d_here = swap(d_projected).reshape(wires.head, rows, packed_width)
-    up_back = grad_zh(*up_back)
-    down_back = grad_y(*down_parts)
-    gate_back = grad_x_swap(*gate_back)
-    sums = [add(branch[0], swap_) for branch, swap_ in zip(branches, swaps)]
-    in_back = lax.dot_general(normed, d_projected, TN, preferred_element_type=jnp.float32)
-    attn_gain_part = jnp.sum(in_back * wide(in_packed), axis=1) / attn_gain
-    in_back = low(in_back)
-    gains = jnp.stack([attn_gain_part, ffn_gain_part[0]])
-    d_here, up_back, in_back, down_back, out_sent, sums, gate_back, gains = tie(
-        d_here, up_back, in_back, down_back, out_sent, sums, gate_back, gains
-    )
+    in_x_swap = wires.over_core(in_x)
+    down_totals = total_of(*down_back)
+    out_total = [add(out_own[s], out_first[s - 1]) for s in across_y]
+    down_totals, up_totals, out_total, out_own, branches, in_across, in_across_swap, in_x_swap, gains, d_here = tie(
+        down_totals,
+        up_totals,
+        out_total,
+        out_own,
+        branches,
+        in_across,
+        in_across_swap,
+        in_x_swap,
+        jnp.concatenate([attn_gain_part, ffn_gain_part], axis=0),
+        d_here,
+    )
+    cut = packed_width // 2
     in_pieces = in_layout(in_line, in_x, in_y, in_across)
-    in_pieces += in_layout(in_swaps[0], in_swaps[1], in_swaps[2:], in_across_swap)
+    in_pieces += in_layout(in_swaps[0], in_x_swap, in_swaps[1:], in_across_swap)
     in_chips = [(wires.z - s) % wires.nz for s in range(wires.nz)]
     in_whole = Whole(
         wires, in_pieces, wires.whole_places(in_chips, packed_width, size), packed_width, size
     )
-    down_back = grad_zh(*down_back)
-    up_back = grad_x_swap(*up_back)
-    to_z, to_x = wires.over_x(sums[3][:half]), wires.over_zl(sums[3][half:])
-    out_total = add(out_total[0], out_sent)
-    out_y = [wires.over_y(out_total[s], s) for s in across_y]
+    up_back = on_zh(up_totals)
+    out_last = wires.over_x(out_sent[0])
+    out_y = [wires.over_y(total, s) for total, s in zip(out_total, across_y)]
+    final_z = wires.over_zl(add(branches[2][0], swap_z))
     in_grad = last(d_here, in_whole, tokens, d_middle, attn_gain[None])
+    in_grad, up_back, down_totals, out_last, out_y, final_z, in_back, gains, branches, swap_x, to_x = tie(
+        in_grad, up_back, down_totals, out_last, out_y, final_z, in_back, gains, branches, swap_x, to_x
+    )
+    down_back = on_zh(down_totals)
+    final_x = wires.over_x(add(branches[1][0], swap_x, to_x))
+    in_x, in_y = wires.over_x(in_back[:cut]), [wires.over_y(in_back[cut:], s) for s in across_y]
+    swap_o = wires.over_core(branches[0][1])
+    out_total = add(out_own[0], out_last, *out_y)
+    firsts = [add(mine, *sent) for mine, sent in (gate_back, up_back)]
     gains = gains + wires.over_core(gains)
-    in_grad, out_y, down_back, to_x, to_z, up_back, in_back, gains, sums = tie(
-        in_grad, out_y, down_back, to_x, to_z, up_back, in_back, gains, sums
-    )
-    cut = depth // 2
-    out_parts = add(out_total[0], *out_y)
-    out_turns = [wires.over_z(out_parts[s], -s) for s in range(1, wires.nz)]
-    in_halves = (wires.sum_x(in_back[:cut]), wires.sum_y(in_back[cut:]))
-    out_parts, out_turns, in_halves, by_x, by_z = tie(
-        out_parts, out_turns, in_halves, (sums[1], to_x), (sums[2], to_z)
-    )
-    out_part = add(out_parts[0], *out_turns)
-    by_x = jnp.concatenate([by_x[0][:half], add(by_x[0][half:], by_x[1])], axis=0)
-    by_z = jnp.concatenate([add(by_z[0][:half], by_z[1]), by_z[0][half:]], axis=0)
-    final_x, final_z = wires.over_x(by_x), wires.over_zl(by_z)
+    down_back, final_x, in_x, in_y, swap_o, out_total, firsts, gains = tie(
+        down_back, final_x, in_x, in_y, swap_o, out_total, firsts, gains
+    )
+    in_halves = (add(in_back[:cut], in_x), add(in_back[cut:], *in_y))
+    out_turns = lax.all_to_all(
+        out_total,
+        "head",
+        split_axis=0,
+        concat_axis=0,
+        tiled=True,
+        axis_index_groups=[[z * 2 + c for z in range(wires.nz)] for c in range(2)],
+    )
+    others = wires.over_x(jnp.stack([pick(total, 1 - wires.x, 2, 1) for total in firsts]))
     in_halves = (wires.sum_y(in_halves[0]), wires.sum_x(in_halves[1]))
+    output = low(middle + wide(branches[0][0]) + wide(swap_o) + wide(final_x) + wide(final_z))
     gains = gains + wires.over_zl(gains)
-    final_x, final_z, in_halves, out_part, gains, down_back = tie(
-        final_x, final_z, in_halves, out_part, gains, down_back
-    )
-    down_back = grad_x_swap(*down_back)
+    down_total = add(down_back[0], *down_back[1])
+    out_turns, others, in_halves, gains, output, down_total = tie(
+        out_turns, others, in_halves, gains, output, down_total
+    )
+    out_part = add(*[out_turns[z] for z in range(wires.nz)])
     out_x = wires.over_x(out_part)
     out_by_y = [wires.over_y(out_part, s) for s in across_y]
+    others = [others[0], others[1], wires.over_x(pick(down_total, 1 - wires.x, 2, 1))]
+    totals = [*firsts, down_total]
     gains = gains + sum(wires.over_zh(gains, s) for s in range(1, wires.nzh))
-    out_x, out_by_y, gains, down_back = tie(out_x, out_by_y, gains, down_back)
+    out_x, out_by_y, gains, others = tie(out_x, out_by_y, gains, others)
     out_by_yx = [wires.over_y(out_x, s) for s in across_y]
-    gains = gains + wires.over_x(gains)
-    out_by_yx, gains = tie(out_by_yx, gains)
-    gains = gains + sum(wires.over_y(gains, s) for s in across_y)
+    gains_x = wires.over_x(gains)
+    gains = gains + gains_x + sum(
+        wires.over_y(gains, s) + wires.over_dp(gains, s) for s in across_y
+    )
     out_weight_grad = wide(
         in_order(
             [
@@ -1164,11 +1313,11 @@
             1,
         )
     )
-    output = low(middle + wide(sums[0]) + wide(final_x) + wide(final_z))
-    gate_grad = grad_last(*gate_back).T
-    up_grad = grad_last(*up_back).T
-    down_grad = grad_last(*down_back)
-    in_weight_grad = unpack_columns(wide(jnp.concatenate(in_halves, axis=0)), heads_here)
+    gate_grad, up_grad, down_grad = (
+        grad_last(pick(total, wires.x, 2, 1), others[i]) for i, total in enumerate(totals)
+    )
+    gate_grad, up_grad = gate_grad.T, up_grad.T
+    in_weight_grad = wide(jnp.concatenate(in_halves, axis=0)).T
     return (
         output,
         in_grad,

time: 797 us -> 743 us (0.932)
  Pallas kernels: 231 us -> 213 us
  local copies, waits for them, and re-layouts: 42.2 us -> 27.2 us
  other arithmetic: 67.6 us -> 57.1 us
  starting transfers between devices: 112 us -> 104 us
    ppermute x7, waiting for transfers between devices: 46.5 us -> 84.7 us  [over_zh(): lax.ppermute(values, 'head', [(i, (i // 4 + shift) % self.nzh * 4 + i % 4...]
    pallas_call x8 -> x4, Pallas kernels: 98.6 us -> 73.4 us  [with_units(): pl.pallas_call(functools.partial(kernel, units), grid_spec=pltpu.Prefetch...]
    ppermute x6 -> x3, waiting for transfers between devices: 20.3 us -> 0.01 us  [over_z(): lax.ppermute(values, 'head', [(i, (i // 2 + shift) % self.nz * 2 + i % 2)...]
    ppermute x20, waiting for transfers between devices: 121 us -> 107 us  [over_x(): return lax.ppermute(values, 'dp', [(i, i ^ 1) for i in range(self.dp)])]
    all_to_all x3, waiting for transfers between devices: 12.9 us -> 0.01 us  [swap(): lax.all_to_all(values, 'head', split_axis=0, concat_axis=0, tiled=True)]
    ppermute x29 -> x30, waiting for transfers between devices: 4.29 us -> 16.9 us  [over_core(): return lax.ppermute(values, 'head', [(i, i ^ 1) for i in range(self.head)])]
    ppermute x8 -> x6, starting transfers between devices: 22 us -> 10.6 us  [over_zl(): return lax.ppermute(values, 'head', [(i, i ^ 2) for i in range(self.head)])]
    pallas_call x3 -> x4, Pallas kernels: 39.2 us -> 46.5 us  [the longest x3 38.8 us: unit_grad(): pl.pallas_call(functools.partial(unit_grad_kernel, order, ny, nzh), grid_...]
  transfers between devices with their start and end apart: 95 -> 92, of which waited for: 40 -> 35; matrix products, arithmetic and copies ran while one was open for 13% -> 8% of each run, Pallas kernels for 24% -> 27%
where the time goes in v4:
time: 743 us; the launch traced here: 731 us
  waiting for transfers between devices  328 us (44%)
  Pallas kernels  213 us (29%)
  starting transfers between devices  104 us (14%)
  other arithmetic  57.1 us (8%)
  local copies, waits for them, and re-layouts  27.2 us (4%)
    ppermute x20, waiting for transfers between devices, over_x(): return lax.ppermute(values, 'dp', [(i, i ^ 1) for i in range(self.dp)])  107 us
    ppermute x7, waiting for transfers between devices, over_zh(): lax.ppermute(values, 'head', [(i, (i // 4 + shift) % self.nzh * 4 + i % 4...  84.7 us
    pallas_call x4, Pallas kernels, with_units(): pl.pallas_call(functools.partial(kernel, units), grid_spec=pltpu.Prefetch...  73.4 us
    ppermute x16, waiting for transfers between devices, over_y(): lax.ppermute(values, 'dp', [(i, (i // 2 + shift) % self.ny * 2 + i % 2) f...  44.7 us
    pallas_call x3, Pallas kernels, unit_grad(): pl.pallas_call(functools.partial(unit_grad_kernel, order, ny, nzh), grid_...  38.8 us
    ppermute x6, waiting for transfers between devices, over_zl(): return lax.ppermute(values, 'head', [(i, i ^ 2) for i in range(self.head)])  37 us
    convert_element_type x20, other arithmetic, low(): return values.astype(jnp.bfloat16)  35 us
    pallas_call x1, Pallas kernels, attend_back(): pl.pallas_call(functools.partial(attend_back_kernel, heads, rows), grid_s...  32.1 us
  transfers between devices with their start and end apart: 92, of which 35 were waited for; matrix products, arithmetic and copies ran while one was open for 8% of the time, Pallas kernels for 27%

profile of v4, /device:TPU:0, one launch (start us, length us, event | category | flops | bytes accessed | tf_op | source)
XLA Modules:
  0.0 731.4 jit_solution(13270838653209642484)
XLA Ops:
  16.5 22.2 %collective-permute-done.2 = bf16[3,352,512]{2,1,0:T(8,128)(2,1)S(1)} collective-permute-done((bf16[3,352,512]{2,1,0:T(8,128)(2,1)S(1)}, bf16[3,352,512]{2,1,0:T(8,128)(2,1)S(1)}, u32[]{:S(2)}, u32[]{:S(2)}) %collective-permute-start.2) | collective-permute-done | bytes 1081376 | tf_op jit(solution)/shard_map/ppermute | solution.py:332
  46.1 21.3 %collective-permute-done.7.refs_10_ = bf16[256,2048]{1,0:T(8,128)(2,1)} collective-permute-done((bf16[256,2048]{1,0:T(8,128)(2,1)}, bf16[256,2048]{1,0:T(8,128)(2,1)}, u32[]{:S(2)}, u32[]{:S(2)}) %collective-permute-start.7) | collective-permute-done | bytes 1048608 | tf_op jit(solution)/shard_map/ppermute | solution.py:332
  82.0 28.6 %collective-permute-done.9 = bf16[256,2560]{1,0:T(8,128)(2,1)S(1)} collective-permute-done((bf16[256,2560]{1,0:T(8,128)(2,1)S(1)}, bf16[256,2560]{1,0:T(8,128)(2,1)S(1)}, u32[]{:S(2)}, u32[]{:S(2)}) %collective-permute-start.9) | collective-permute-done | bytes 1310752 | tf_op jit(solution)/shard_map/ppermute | solution.py:375
  122.0 23.0 %shard_map.178 = (bf16[2048,320]{1,0:T(8,128)(2,1)}, bf16[2048,2048]{1,0:T(8,128)(2,1)}, f32[2048,256]{1,0:T(8,128)}, f32[2048,128]{1,0:T(8,128)}, bf16[2048,256]{1,0:T(8,128)(2,1)}) custom-call(s32[3]{0:T(128)} %bitcast.133, s32[8]{0:T(128)} %stack.229.at_ref, bf16[256,2560]{1,0:T(8,128)(2,1)} %copy-done.9, ...), custom_call_target="tpu_custom_call" | custom-call | flops 1 | bytes 1 | tf_op jit(solution)/shard_map/pallas_call | solution.py:134
  167.1 13.4 %collective-permute-done.19.refs_3_.refs_7_ = bf16[1,352,1024]{2,1,0:T(8,128)(2,1)S(1)} collective-permute-done((bf16[1,352,1024]{2,1,0:T(8,128)(2,1)}, bf16[1,352,1024]{2,1,0:T(8,128)(2,1)S(1)}, u32[]{:S(2)}, u32[]{:S(2)}) %collective-permute-start.19) | collective-permute-done | bytes 720928 | tf_op jit(solution)/shard_map/ppermute | solution.py:335
  180.5 19.8 %collective-permute-done.16.refs_14_ = bf16[256,2048]{1,0:T(8,128)(2,1)S(1)} collective-permute-done((bf16[256,2048]{1,0:T(8,128)(2,1)}, bf16[256,2048]{1,0:T(8,128)(2,1)S(1)}, u32[]{:S(2)}, u32[]{:S(2)}) %collective-permute-start.16) | collective-permute-done | bytes 1048608 | tf_op jit(solution)/shard_map/ppermute | solution.py:348
  219.8 14.1 %collective-permute-done.25.refs_1_ = bf16[1,352,1024]{2,1,0:T(8,128)(2,1)} collective-permute-done((bf16[1,352,1024]{2,1,0:T(8,128)(2,1)S(1)}, bf16[1,352,1024]{2,1,0:T(8,128)(2,1)}, u32[]{:S(2)}, u32[]{:S(2)}) %collective-permute-start.25) | collective-permute-done | bytes 720928 | tf_op jit(solution)/shard_map/ppermute | solution.py:335
  233.9 19.9 %collective-permute-done.23.refs_4_.refs_8_ = bf16[1,352,1024]{2,1,0:T(8,128)(2,1)} collective-permute-done((bf16[1,352,1024]{2,1,0:T(8,128)(2,1)S(1)}, bf16[1,352,1024]{2,1,0:T(8,128)(2,1)}, u32[]{:S(2)}, u32[]{:S(2)}) %collective-permute-start.23) | collective-permute-done | bytes 720928 | tf_op jit(solution)/shard_map/ppermute | solution.py:351
  260.7 31.7 %collective-permute-done.30.refs_2_ = bf16[1,352,1024]{2,1,0:T(8,128)(2,1)} collective-permute-done((bf16[1,352,1024]{2,1,0:T(8,128)(2,1)}, bf16[1,352,1024]{2,1,0:T(8,128)(2,1)}, u32[]{:S(2)}, u32[]{:S(2)}) %collective-permute-start.30) | collective-permute-done | bytes 720928 | tf_op jit(solution)/shard_map/ppermute | solution.py:351
  300.2 16.7 %shard_map.180 = (f32[3,512,704]{2,1,0:T(8,128)}, f32[3,512,704]{2,1,0:T(8,128)}, bf16[3,512,2048]{2,1,0:T(8,128)(2,1)}) custom-call(s32[2]{0:T(128)} %pad_add_fusion.places_ref, bf16[2,352,1024]{2,1,0:T(8,128)(2,1)} %slice.164.refs_0_.refs_4_, bf16[2,352,1024]{2,1,0:T(8,128)(2,1)} %copy-done.2, bf16[1,352,1024]{2,1,0:T(8,128)(2,1)} %copy-done.6, ...), custom_call_target="tpu_custom_call" | custom-call | flops 1 | bytes 1 | tf_op jit(solution)/shard_map/pallas_call | solution.py:656
  321.4 9.8 %shard_map.181 = (f32[1,512,704]{2,1,0:T(8,128)}, f32[1,512,704]{2,1,0:T(8,128)}, bf16[1,512,2048]{2,1,0:T(8,128)(2,1)}) custom-call(s32[2]{0:T(128)} %pad_add_fusion.places_ref, bf16[2,352,1024]{2,1,0:T(8,128)(2,1)} %slice.164.refs_0_.refs_4_, bf16[2,352,1024]{2,1,0:T(8,128)(2,1)} %copy-done.2, bf16[1,352,1024]{2,1,0:T(8,128)(2,1)} %copy-done.6, ...), custom_call_target="tpu_custom_call" | custom-call | flops 1 | bytes 1 | tf_op jit(solution)/shard_map/pallas_call | solution.py:656
  331.2 23.3 %shard_map.182 = (bf16[2,512,704]{2,1,0:T(8,128)(2,1)}, bf16[2,512,704]{2,1,0:T(8,128)(2,1)}, bf16[2,512,704]{2,1,0:T(8,128)(2,1)}, bf16[2,512,2048]{2,1,0:T(8,1...) custom-call(s32[2]{0:T(128)} %pad_add_fusion.places_ref, ...), custom_call_target="tpu_custom_call" | custom-call | flops 1 | bytes 1 | tf_op jit(solution)/shard_map/pallas_call | solution.py:656
  363.8 23.6 %shard_map.183 = (bf16[2,512,704]{2,1,0:T(8,128)(2,1)}, bf16[2,512,704]{2,1,0:T(8,128)(2,1)}, bf16[2,512,704]{2,1,0:T(8,128)(2,1)}, bf16[2,512,2048]{2,1,0:T(8,1...) custom-call(s32[2]{0:T(128)} %pad_add_fusion.places_ref, ...), custom_call_target="tpu_custom_call" | custom-call | flops 1 | bytes 1 | tf_op jit(solution)/shard_map/pallas_call | solution.py:656
  409.5 13.0 %shard_map.184 = (bf16[2,352,1024]{2,1,0:T(8,128)(2,1)}, bf16[1,2,352,1024]{3,2,1,0:T(8,128)(2,1)}) custom-call(s32[4]{0:T(128)} %pad_add_fusion.1.places_ref, bf16[2,512,704]{2,1,0:T(8,128)(2,1)} %get-tuple-element.450.refs_0_, bf16[1,512,2048]{2,1,0:T(8,128)(2,1)} %get-tuple-element.491.refs_1_, bf16[3,512,2048]{2,1,0:T(8,128)(2,1)} %get-tuple-element.492.refs_2_, ...), custom_call_target="tpu_custom_call" | custom-call | flops 1 | bytes 1 | tf_op jit(solution)/shard_map/pallas_call | solution.py:870
  431.3 10.4 %shard_map.185 = (f32[256,2048]{1,0:T(8,128)}, bf16[256,2048]{1,0:T(8,128)(2,1)}, f32[1,2048]{1,0:T(1,128)}, bf16[8,256,256]{2,1,0:T(8,128)(2,1)}) custom-call(s32[12]{0:T(128)} %stack.219.places_ref, bf16[4,256,512]{2,1,0:T(8,128)(2,1)} %pad_maximum_fusion.4.refs_0_, bf16[4,256,512]{2,1,0:T(8,128)(2,1)} %collective-permute-done.12.refs_1_, ...), custom_call_target="tpu_custom_call" | custom-call | flops 1 | bytes 1 | tf_op jit(solution)/shard_map/pallas_call | solution.py:525
  449.5 12.8 %shard_map.187 = (bf16[2,352,1024]{2,1,0:T(8,128)(2,1)}, bf16[1,2,352,1024]{3,2,1,0:T(8,128)(2,1)}) custom-call(s32[4]{0:T(128)} %pad_add_fusion.1.places_ref, bf16[2,512,704]{2,1,0:T(8,128)(2,1)} %get-tuple-element.490.refs_0_, bf16[1,512,2048]{2,1,0:T(8,128)(2,1)} %get-tuple-element.491.refs_1_, bf16[3,512,2048]{2,1,0:T(8,128)(2,1)} %get-tuple-element.492.refs_2_, ...), custom_call_target="tpu_custom_call" | custom-call | flops 1 | bytes 1 | tf_op jit(solution)/shard_map/pallas_call | solution.py:870
  462.3 12.9 %shard_map.188 = (bf16[2,352,1024]{2,1,0:T(8,128)(2,1)}, bf16[1,2,352,1024]{3,2,1,0:T(8,128)(2,1)}) custom-call(s32[4]{0:T(128)} %pad_add_fusion.1.places_ref, bf16[2,512,704]{2,1,0:T(8,128)(2,1)} %get-tuple-element.496.refs_0_, bf16[2,512,2048]{2,1,0:T(8,128)(2,1)} %get-tuple-element.497.refs_1_, bf16[2,512,704]{2,1,0:T(8,128)(2,1)} %get-tuple-element.498.refs_2_, ...), custom_call_target="tpu_custom_call" | custom-call | flops 1 | bytes 1 | tf_op jit(solution)/shard_map/pallas_call | solution.py:870
  493.4 32.1 %shard_map.189.grad_ref = bf16[8,256,320]{2,1,0:T(8,128)(2,1)} custom-call(s32[3]{0:T(128)} %bitcast.134, bf16[2048,320]{1,0:T(8,128)(2,1)} %get-tuple-element.480.projected_ref, f32[1,2048]{1,0:T(1,128)} %bitcast.128, f32[2048,256]{1,0:T(8,128)} %get-tuple-element.481.y_ref, f32[2048,128]{1,0:T(8,128)} %get-tuple-element.482.inv_ref, ...), custom_call_target="tpu_custom_call" | custom-call | flops 1 | bytes 1 | tf_op jit(solution)/shard_map/pallas_call | solution.py:260
  550.4 19.4 %collective-permute-done.63.refs_3_ = bf16[4,320,512]{2,1,0:T(8,128)(2,1)} collective-permute-done((bf16[4,320,512]{2,1,0:T(8,128)(2,1)}, bf16[4,320,512]{2,1,0:T(8,128)(2,1)}, u32[]{:S(2)}, u32[]{:S(2)}) %collective-permute-start.63) | collective-permute-done | bytes 1310752 | tf_op jit(solution)/shard_map/ppermute | solution.py:332
  587.0 12.2 %shard_map.191 = f32[256,2048]{1,0:T(8,128)} custom-call(s32[12]{0:T(128)} %stack.207.places_ref, bf16[4,320,512]{2,1,0:T(8,128)(2,1)} %copy-done.13, bf16[4,320,512]{2,1,0:T(8,128)(2,1)} %collective-permute-done.54.refs_1_, bf16[4,320,512]{2,1,0:T(8,128)(2,1)} %collective-permute-done.45.refs_2_, bf16[4,320,512]{2,1,0:T(8,128)(2,1)} %collective-permute-done.63.refs_3_, ...), custom_call_target="tpu_custom_call" | custom-call | flops 1 | bytes 1 | tf_op jit(solution)/shard_map/pallas_call | solution.py:525
  599.3 21.5 %collective-permute-done.66 = bf16[352,1024]{1,0:T(8,128)(2,1)} collective-permute-done((bf16[352,1024]{1,0:T(8,128)(2,1)}, bf16[352,1024]{1,0:T(8,128)(2,1)}, u32[]{:S(2)}, u32[]{:S(2)}) %collective-permute-start.66) | collective-permute-done | bytes 720928 | tf_op jit(solution)/shard_map/ppermute | solution.py:351
  634.1 11.2 %collective-permute-done.73 = bf16[160,2048]{1,0:T(8,128)(2,1)S(1)} collective-permute-done((bf16[160,2048]{1,0:T(8,128)(2,1)S(1)}, bf16[160,2048]{1,0:T(8,128)(2,1)S(1)}, u32[]{:S(2)}, u32[]{:S(2)}) %collective-permute-start.73) | collective-permute-done | bytes 655392 | tf_op jit(solution)/shard_map/ppermute | solution.py:335
  645.3 20.4 %collective-permute-done.72 = bf16[160,2048]{1,0:T(8,128)(2,1)S(1)} collective-permute-done((bf16[160,2048]{1,0:T(8,128)(2,1)S(1)}, bf16[160,2048]{1,0:T(8,128)(2,1)S(1)}, u32[]{:S(2)}, u32[]{:S(2)}) %collective-permute-start.72) | collective-permute-done | bytes 655392 | tf_op jit(solution)/shard_map/ppermute | solution.py:332
  693.1 11.1 %collective-permute-done.76 = bf16[2,352,512]{2,1,0:T(8,128)(2,1)} collective-permute-done((bf16[2,352,512]{2,1,0:T(8,128)(2,1)S(1)}, bf16[2,352,512]{2,1,0:T(8,128)(2,1)}, u32[]{:S(2)}, u32[]{:S(2)}) %collective-permute-start.76) | collective-permute-done | bytes 720928 | tf_op jit(solution)/shard_map/ppermute | solution.py:332
  (383 shorter events, 284.8 us)
Async XLA Ops:
  154.3 48.4 %all-to-all-start = ((bf16[8,256,256]{2,1,0:T(8,128)(2,1)}), bf16[8,256,256]{2,1,0:T(8,128)(2,1)S(1)}, u32[]{:S(2)}, u32[]{:S(2)}) async-start(bf16[8,256,256]{2,1,0:T(8,128)(2,1)} %bitcast.119), calls=%async_computation | async-start | bytes 2097152 | tf_op jit(solution)/shard_map/all_to_all | solution.py:1009
  158.0 42.3 %collective-permute-start.18 = (bf16[4,256,512]{2,1,0:T(8,128)(2,1)}, bf16[4,256,512]{2,1,0:T(8,128)(2,1)S(1)}, u32[]{:S(2)}, u32[]{:S(2)}) collective-permute-start(bf16[4,256,512]{2,1,0:T(8,128)(2,1)} %collective-permute-done.13.refs_2_), channel_id=1, source_target_pairs={{0,1},{1,0},{2,3},{3,2},{4,5},{5,4},{6,7},{7,6},{8,9},{9,8},{10,11... | collective-permute-start | bytes 3145736 | tf_op jit(solution)/shard_map/ppermute | solution.py:345
  158.5 44.2 %collective-permute-start.15 = (bf16[4,256,512]{2,1,0:T(8,128)(2,1)}, bf16[4,256,512]{2,1,0:T(8,128)(2,1)}, u32[]{:S(2)}, u32[]{:S(2)}) collective-permute-start(bf16[4,256,512]{2,1,0:T(8,128)(2,1)} %collective-permute-done.13.refs_2_), channel_id=1, source_target_pairs={{0,8},{8,0},{16,24},{24,16},{1,9},{9,1},{17,25},{25,17},{2,10},{10... | collective-permute-start | bytes 3145736 | tf_op jit(solution)/shard_map/ppermute | solution.py:332
  159.0 41.3 %collective-permute-start.16 = (bf16[256,2048]{1,0:T(8,128)(2,1)}, bf16[256,2048]{1,0:T(8,128)(2,1)S(1)}, u32[]{:S(2)}, u32[]{:S(2)}) collective-permute-start(bf16[256,2048]{1,0:T(8,128)(2,1)} %refs_12_), channel_id=1, source_target_pairs={{0,2},{1,3},{2,0},{3,1},{4,6},{5,7},{6,4},{7,5},{8,10},{9,11},{10,... | collective-permute-start | bytes 3145736 | tf_op jit(solution)/shard_map/ppermute | solution.py:348
  160.7 39.6 %collective-permute-start.17 = (bf16[4,256,512]{2,1,0:T(8,128)(2,1)}, bf16[4,256,512]{2,1,0:T(8,128)(2,1)S(1)}, u32[]{:S(2)}, u32[]{:S(2)}) collective-permute-start(bf16[4,256,512]{2,1,0:T(8,128)(2,1)} %collective-permute-done.12.refs_1_), channel_id=1, source_target_pairs={{0,1},{1,0},{2,3},{3,2},{4,5},{5,4},{6,7},{7,6},{8,9},{9,8},{10,11... | collective-permute-start | bytes 3145736 | tf_op jit(solution)/shard_map/ppermute | solution.py:345
  214.6 39.3 %collective-permute-start.24 = (bf16[256,2048]{1,0:T(8,128)(2,1)}, bf16[256,2048]{1,0:T(8,128)(2,1)}, u32[]{:S(2)}, u32[]{:S(2)}) collective-permute-start(bf16[256,2048]{1,0:T(8,128)(2,1)} %get-tuple-element.355.refs_6_), channel_id=1, source_target_pairs={{0,1},{1,0},{2,3},{3,2},{4,5},{5,4},{6,7},{7,6},{8,9},{9,8},{10,11... | collective-permute-start | bytes 3145736 | tf_op jit(solution)/shard_map/ppermute | solution.py:345
  214.8 41.2 %collective-permute-start.22 = (bf16[256,2048]{1,0:T(8,128)(2,1)}, bf16[256,2048]{1,0:T(8,128)(2,1)}, u32[]{:S(2)}, u32[]{:S(2)}) collective-permute-start(bf16[256,2048]{1,0:T(8,128)(2,1)} %get-tuple-element.355.refs_6_), channel_id=1, source_target_pairs={{0,2},{1,3},{2,0},{3,1},{4,6},{5,7},{6,4},{7,5},{8,10},{9,11},{10,... | collective-permute-start | bytes 3145736 | tf_op jit(solution)/shard_map/ppermute | solution.py:348
  215.2 40.8 %collective-permute-start.21 = (bf16[256,2048]{1,0:T(8,128)(2,1)}, bf16[256,2048]{1,0:T(8,128)(2,1)}, u32[]{:S(2)}, u32[]{:S(2)}) collective-permute-start(bf16[256,2048]{1,0:T(8,128)(2,1)} %get-tuple-element.355.refs_6_), channel_id=1, source_target_pairs={{0,8},{8,0},{16,24},{24,16},{1,9},{9,1},{17,25},{25,17},{2,10},{10... | collective-permute-start | bytes 3145736 | tf_op jit(solution)/shard_map/ppermute | solution.py:332
  317.5 37.0 %collective-permute-start.41 = (bf16[320,512]{1,0:T(8,128)(2,1)S(1)}, bf16[320,512]{1,0:T(8,128)(2,1)S(1)}, u32[]{:S(2)}, u32[]{:S(2)}) collective-permute-start(bf16[320,512]{1,0:T(8,128)(2,1)S(1)} %copy-done.29), channel_id=1, source_target_pairs={{0,6},{1,7},{2,0},{3,1},{4,2},{5,3},{6,4},{7,5},{8,14},{9,15},{10,... | collective-permute-start | bytes 983048 | tf_op jit(solution)/shard_map/ppermute | solution.py:356
  441.9 40.1 %all-to-all-start.1 = ((bf16[8,256,256]{2,1,0:T(8,128)(2,1)}), bf16[8,256,256]{2,1,0:T(8,128)(2,1)S(1)}, u32[]{:S(2)}, u32[]{:S(2)}) async-start(bf16[8,256,256]{2,1,0:T(8,128)(2,1)} %get-tuple-element.483), calls=%async_computation.1 | async-start | bytes 2097152 | tf_op jit(solution)/shard_map/all_to_all | solution.py:1009
  487.9 41.6 %collective-permute-start.59 = (bf16[2,352,1024]{2,1,0:T(8,128)(2,1)}, bf16[2,352,1024]{2,1,0:T(8,128)(2,1)}, u32[]{:S(2)}, u32[]{:S(2)}) collective-permute-start(bf16[2,352,1024]{2,1,0:T(8,128)(2,1)} %bitcast.59), channel_id=1, source_target_pairs={{0,16},{8,24},{16,0},{24,8},{1,17},{9,25},{17,1},{25,9},{2,18},{10... | collective-permute-start | bytes 4325384 | tf_op jit(solution)/shard_map/ppermute | solution.py:335
  488.6 40.9 %collective-permute-start.60 = (bf16[256,2048]{1,0:T(8,128)(2,1)S(1)}, bf16[256,2048]{1,0:T(8,128)(2,1)S(1)}, u32[]{:S(2)}, u32[]{:S(2)}) collective-permute-start(bf16[256,2048]{1,0:T(8,128)(2,1)S(1)} %add_convert_fusion.5), channel_id=1, source_target_pairs={{0,2},{1,3},{2,0},{3,1},{4,6},{5,7},{6,4},{7,5},{8,10},{9,11},{10,... | collective-permute-start | bytes 3145736 | tf_op jit(solution)/shard_map/ppermute | solution.py:348
  490.4 39.0 %collective-permute-start.61 = (bf16[4,256,512]{2,1,0:T(8,128)(2,1)}, bf16[4,256,512]{2,1,0:T(8,128)(2,1)}, u32[]{:S(2)}, u32[]{:S(2)}) collective-permute-start(bf16[4,256,512]{2,1,0:T(8,128)(2,1)} %get-tuple-element.522), channel_id=1, source_target_pairs={{0,8},{8,0},{16,24},{24,16},{1,9},{9,1},{17,25},{25,17},{2,10},{10... | collective-permute-start | bytes 3145736 | tf_op jit(solution)/shard_map/ppermute | solution.py:332
  491.0 37.8 %collective-permute-start.58 = (bf16[352,1024]{1,0:T(8,128)(2,1)}, bf16[352,1024]{1,0:T(8,128)(2,1)S(1)}, u32[]{:S(2)}, u32[]{:S(2)}) collective-permute-start(bf16[352,1024]{1,0:T(8,128)(2,1)} %get-tuple-element.518), channel_id=1, source_target_pairs={{0,4},{1,5},{2,6},{3,7},{4,0},{5,1},{6,2},{7,3},{8,12},{9,13},{10,... | collective-permute-start | bytes 2162696 | tf_op jit(solution)/shard_map/ppermute | solution.py:351
  532.4 39.2 %all-to-all-start.2 = ((bf16[8,256,320]{1,2,0:T(8,128)(2,1)}), bf16[8,256,320]{1,2,0:T(8,128)(2,1)S(1)}, u32[]{:S(2)}, u32[]{:S(2)}) async-start(bf16[8,256,320]{1,2,0:T(8,128)(2,1)} %copy.24), calls=%async_computation.2 | async-start | bytes 2621440 | tf_op jit(solution)/shard_map/all_to_all | solution.py:1009
  539.1 38.9 %collective-permute-start.65 = (bf16[4,320,512]{2,1,0:T(8,128)(2,1)}, bf16[4,320,512]{2,1,0:T(8,128)(2,1)}, u32[]{:S(2)}, u32[]{:S(2)}) collective-permute-start(bf16[4,320,512]{2,1,0:T(8,128)(2,1)} %collective-permute-done.54.refs_1_), channel_id=1, source_target_pairs={{0,1},{1,0},{2,3},{3,2},{4,5},{5,4},{6,7},{7,6},{8,9},{9,8},{10,11... | collective-permute-start | bytes 3932168 | tf_op jit(solution)/shard_map/ppermute | solution.py:345
  578.0 42.7 %collective-permute-start.68 = (bf16[4,256,512]{2,1,0:T(8,128)(2,1)}, bf16[4,256,512]{2,1,0:T(8,128)(2,1)}, u32[]{:S(2)}, u32[]{:S(2)}) collective-permute-start(bf16[4,256,512]{2,1,0:T(8,128)(2,1)} %add_convert_fusion.4), channel_id=1, source_target_pairs={{0,16},{8,24},{16,0},{24,8},{1,17},{9,25},{17,1},{25,9},{2,18},{10... | collective-permute-start | bytes 3145736 | tf_op jit(solution)/shard_map/ppermute | solution.py:335
  580.8 40.6 %collective-permute-start.69 = (bf16[256,2048]{1,0:T(8,128)(2,1)}, bf16[256,2048]{1,0:T(8,128)(2,1)S(1)}, u32[]{:S(2)}, u32[]{:S(2)}) collective-permute-start(bf16[256,2048]{1,0:T(8,128)(2,1)} %add_convert_fusion.3), channel_id=1, source_target_pairs={{0,2},{1,3},{2,0},{3,1},{4,6},{5,7},{6,4},{7,5},{8,10},{9,11},{10,... | collective-permute-start | bytes 3145736 | tf_op jit(solution)/shard_map/ppermute | solution.py:348
  582.5 38.2 %collective-permute-start.66 = (bf16[352,1024]{1,0:T(8,128)(2,1)}, bf16[352,1024]{1,0:T(8,128)(2,1)}, u32[]{:S(2)}, u32[]{:S(2)}) collective-permute-start(bf16[352,1024]{1,0:T(8,128)(2,1)} %get-tuple-element.564), channel_id=1, source_target_pairs={{0,4},{1,5},{2,6},{3,7},{4,0},{5,1},{6,2},{7,3},{8,12},{9,13},{10,... | collective-permute-start | bytes 2162696 | tf_op jit(solution)/shard_map/ppermute | solution.py:351
  621.4 44.3 %collective-permute-start.70 = (bf16[352,1024]{1,0:T(8,128)(2,1)}, bf16[352,1024]{1,0:T(8,128)(2,1)S(1)}, u32[]{:S(2)}, u32[]{:S(2)}) collective-permute-start(bf16[352,1024]{1,0:T(8,128)(2,1)} %get-tuple-element.579), channel_id=1, source_target_pairs={{0,4},{1,5},{2,6},{3,7},{4,0},{5,1},{6,2},{7,3},{8,12},{9,13},{10,... | collective-permute-start | bytes 2162696 | tf_op jit(solution)/shard_map/ppermute | solution.py:351
  626.3 39.4 %collective-permute-start.71 = (bf16[256,2048]{1,0:T(8,128)(2,1)S(1)}, bf16[256,2048]{1,0:T(8,128)(2,1)}, u32[]{:S(2)}, u32[]{:S(2)}) collective-permute-start(bf16[256,2048]{1,0:T(8,128)(2,1)S(1)} %add_convert_fusion.2), channel_id=1, source_target_pairs={{0,8},{8,0},{16,24},{24,16},{1,9},{9,1},{17,25},{25,17},{2,10},{10... | collective-permute-start | bytes 3145736 | tf_op jit(solution)/shard_map/ppermute | solution.py:332
  627.9 38.7 %collective-permute-start.74 = (bf16[256,2048]{1,0:T(8,128)(2,1)S(1)}, bf16[256,2048]{1,0:T(8,128)(2,1)}, u32[]{:S(2)}, u32[]{:S(2)}) collective-permute-start(bf16[256,2048]{1,0:T(8,128)(2,1)S(1)} %copy-done.62), channel_id=1, source_target_pairs={{0,1},{1,0},{2,3},{3,2},{4,5},{5,4},{6,7},{7,6},{8,9},{9,8},{10,11... | collective-permute-start | bytes 3145736 | tf_op jit(solution)/shard_map/ppermute | solution.py:345
  628.8 36.9 %collective-permute-start.72 = (bf16[160,2048]{1,0:T(8,128)(2,1)S(1)}, bf16[160,2048]{1,0:T(8,128)(2,1)S(1)}, u32[]{:S(2)}, u32[]{:S(2)}) collective-permute-start(bf16[160,2048]{1,0:T(8,128)(2,1)S(1)} %get-tuple-element.637), channel_id=1, source_target_pairs={{0,8},{8,0},{16,24},{24,16},{1,9},{9,1},{17,25},{25,17},{2,10},{10... | collective-permute-start | bytes 1966088 | tf_op jit(solution)/shard_map/ppermute | solution.py:332
  666.8 37.4 %all-to-all-start.3 = ((bf16[4,256,512]{2,1,0:T(8,128)(2,1)}), bf16[4,256,512]{2,1,0:T(8,128)(2,1)S(1)}, u32[]{:S(2)}, u32[]{:S(2)}) async-start(bf16[4,256,512]{2,1,0:T(8,128)(2,1)} %add_convert_fusion.1), calls=%async_computation.3 | async-start | bytes 2097152 | tf_op jit(solution)/shard_map/all_to_all | solution.py:1278
  (132 other events, 2190.3 us)

commit v5 on v4

--- a/solution.py
+++ b/solution.py
@@ -352,6 +352,18 @@
             values, "head", [(i, ((i // 4 + shift) % self.nzh) * 4 + i % 4) for i in range(self.head)]
         )
 
+    def over_zh_half(self, values, shift, parity):
+        pairs = [
+            (i, ((i // 4 + shift) % self.nzh) * 4 + i % 4)
+            for i in range(self.head)
+            if (i // 4 + i // 2 % 2) % 2 == parity
+        ]
+        return lax.ppermute(values, "head", pairs)
+
+    def from_halves(self, first, second, shift):
+        even = (self.zh - shift + self.z) % 2 == 0
+        return jnp.where(even, first, second)
+
     def over_z(self, values, shift):
         return lax.ppermute(
             values, "head", [(i, ((i // 2 + shift) % self.nz) * 2 + i % 2) for i in range(self.head)]
@@ -685,54 +697,65 @@
 
 def gate_kernel(count, units, places_ref, *refs):
     pieces, refs = refs[: len(units.pieces)], refs[len(units.pieces) :]
-    blocks, (gate_ref, up_ref, normed_ref) = refs[: 2 * count], refs[2 * count : 2 * count + 3]
-    weight_s, sems, normed_s, gate_s, up_s, in_sems, out_sems = refs[2 * count + 3 :]
+    blocks, (unit_ref, normed_ref) = refs[: 2 * count], refs[2 * count : 2 * count + 2]
+    weight_s, sems, normed_s, unit_s, in_sems, out_sems = refs[2 * count + 2 :]
     rows = blocks[0].shape[0]
-    arrivals = [
-        pltpu.make_async_copy(
-            blocks[i], normed_s.at[i // 2, pl.ds(i % 2 * rows, rows)], in_sems.at[i]
+
+    def arrive(chunk):
+        started(
+            [
+                pltpu.make_async_copy(
+                    blocks[2 * chunk + i], normed_s.at[chunk, pl.ds(i * rows, rows)], in_sems.at[chunk]
+                )
+                for i in range(2)
+            ]
         )
-        for i in range(2 * count)
-    ]
-    started(arrivals[:2])
+
+    arrive(0)
     weights = units.fill(places_ref, pieces, weight_s, sems)
-    started(arrivals[2:])
+    for chunk in range(1, count):
+        arrive(chunk)
     each = len(weights) // units.matrices
-    sent = []
+
+    def sent(chunk, which):
+        source, target = ((normed_s, normed_ref), (unit_s, unit_ref))[which]
+        return pltpu.make_async_copy(source.at[chunk], target.at[chunk], out_sems.at[which, chunk])
+
+    def work(chunk, nothing):
+        pltpu.make_async_copy(normed_ref.at[chunk], normed_s.at[chunk], in_sems.at[chunk]).wait()
+        sent(chunk, 0).start()
+        pl.when(chunk == 0)(lambda: awaited(weights[:each]))
+        normed = normed_s[chunk]
+        gate = lax.dot_general(normed, weight_s[0], NT, preferred_element_type=jnp.float32)
+        pl.when(chunk == 0)(lambda: awaited(weights[each:]))
+        up = lax.dot_general(normed, weight_s[1], NT, preferred_element_type=jnp.float32)
+        sigmoid = jax.nn.sigmoid(gate)
+        silu = gate * sigmoid
+        unit_s[chunk, 0] = (silu * up).astype(jnp.bfloat16)
+        unit_s[chunk, 1] = (up * sigmoid * (1.0 + gate * (1.0 - sigmoid))).astype(jnp.bfloat16)
+        unit_s[chunk, 2] = silu.astype(jnp.bfloat16)
+        sent(chunk, 1).start()
+        return nothing
+
+    lax.fori_loop(0, count, work, 0)
     for chunk in range(count):
-        awaited(arrivals[2 * chunk : 2 * chunk + 2])
-        sent += started(
-            [pltpu.make_async_copy(normed_s.at[chunk], normed_ref.at[chunk], out_sems.at[3 * chunk])]
-        )
-        normed = normed_s[chunk]
-        awaited(weights[:each] if chunk == 0 else [])
-        gate_s[chunk] = lax.dot_general(normed, weight_s[0], NT, preferred_element_type=jnp.float32)
-        sent += started(
-            [pltpu.make_async_copy(gate_s.at[chunk], gate_ref.at[chunk], out_sems.at[3 * chunk + 1])]
-        )
-        awaited(weights[each:] if chunk == 0 else [])
-        up_s[chunk] = lax.dot_general(normed, weight_s[1], NT, preferred_element_type=jnp.float32)
-        sent += started(
-            [pltpu.make_async_copy(up_s.at[chunk], up_ref.at[chunk], out_sems.at[3 * chunk + 2])]
-        )
-    awaited(sent)
+        awaited([sent(chunk, 0), sent(chunk, 1)])
 
 
 def gate_up(pairs, units):
     count = len(pairs)
     rows, depth = pairs[0][0].shape
-    unit, full = (count, 2 * rows, units.shape[1]), (count, 2 * rows, depth)
+    unit, full = (count, 3, 2 * rows, units.shape[1]), (count, 2 * rows, depth)
     return with_units(
         functools.partial(gate_kernel, count),
         units,
         [block for pair in pairs for block in pair],
-        ((unit, jnp.float32), (unit, jnp.float32), (full, jnp.bfloat16)),
+        ((unit, jnp.bfloat16), (full, jnp.bfloat16)),
         [
             pltpu.VMEM(full, jnp.bfloat16),
-            pltpu.VMEM(unit, jnp.float32),
-            pltpu.VMEM(unit, jnp.float32),
-            pltpu.SemaphoreType.DMA((2 * count,)),
-            pltpu.SemaphoreType.DMA((3 * count,)),
+            pltpu.VMEM(unit, jnp.bfloat16),
+            pltpu.SemaphoreType.DMA((count,)),
+            pltpu.SemaphoreType.DMA((2, count)),
         ],
         8 * count * rows * depth * units.shape[1],
         0,
@@ -742,110 +765,123 @@
 def down_kernel(places, units, places_ref, *refs):
     count = len(places)
     pieces, refs = refs[: len(units.pieces)], refs[len(units.pieces) :]
-    blocks, refs = refs[: 4 * count], refs[4 * count :]
-    unit_refs, grad_ref, refs = refs[:3], refs[3], refs[4:]
+    blocks, refs = refs[: 3 * count], refs[3 * count :]
+    unit_ref, grad_ref, refs = refs[0], refs[1], refs[2:]
     dnormed, branches = refs[: 2 * count], refs[2 * count : 4 * count]
-    weight_s, sems, pre_s, grad_s, unit_s, back_s, branch_s, in_sems, out_sems = refs[4 * count :]
+    weight_s, sems, given_s, grad_s, unit_s, back_s, branch_s, in_sems, out_sems = refs[4 * count :]
     rows = blocks[0].shape[0]
     both = [pl.ds(0, rows), pl.ds(rows, rows)]
-    arrivals = []
-    for chunk, place in enumerate(places):
-        one, two, gate, up = blocks[4 * chunk : 4 * chunk + 4]
-        for i, (source, target) in enumerate(
-            (
-                (gate.at[place], pre_s.at[chunk, 0]),
-                (up.at[place], pre_s.at[chunk, 1]),
-                (one, grad_s.at[chunk, both[0]]),
-                (two, grad_s.at[chunk, both[1]]),
-            )
-        ):
-            arrivals.append(pltpu.make_async_copy(source, target, in_sems.at[4 * chunk + i]))
-    started(arrivals[:4])
+
+    def arrive(chunk):
+        one, two, given = blocks[3 * chunk : 3 * chunk + 3]
+        started(
+            [
+                pltpu.make_async_copy(one, grad_s.at[chunk, both[0]], in_sems.at[0, chunk]),
+                pltpu.make_async_copy(two, grad_s.at[chunk, both[1]], in_sems.at[0, chunk]),
+                pltpu.make_async_copy(given.at[places[chunk]], given_s.at[chunk], in_sems.at[1, chunk]),
+            ]
+        )
+
+    arrive(0)
     weights = units.fill(places_ref, pieces, weight_s, sems)
-    started(arrivals[4:])
+    for chunk in range(1, count):
+        arrive(chunk)
     each = len(weights) // units.matrices
     dot = functools.partial(jnp.dot, preferred_element_type=jnp.float32)
-    sent = []
-
-    def send(source, target):
-        sent.append(pltpu.make_async_copy(source, target, out_sems.at[len(sent)]))
-        sent[-1].start()
-
+
+    def sent(chunk, which):
+        source, target = ((grad_s, grad_ref), (unit_s, unit_ref))[which]
+        return pltpu.make_async_copy(source.at[chunk], target.at[chunk], out_sems.at[which, chunk])
+
+    def halves_sent(chunk, source, targets, place):
+        return [
+            pltpu.make_async_copy(
+                source.at[chunk, both[i]], targets[2 * chunk + i], out_sems.at[place + i, chunk]
+            )
+            for i in range(2)
+        ]
+
+    def work(chunk, nothing):
+        pltpu.make_async_copy(grad_ref.at[chunk], grad_s.at[chunk], in_sems.at[0, chunk]).wait()
+        sent(chunk, 0).start()
+        pl.when(chunk == 0)(lambda: awaited(weights[:each]))
+        dhidden = lax.dot_general(grad_s[chunk], weight_s[0], NT, preferred_element_type=jnp.float32)
+        pltpu.make_async_copy(given_s.at[chunk], given_s.at[chunk], in_sems.at[1, chunk]).wait()
+        dgate = (dhidden * wide(given_s[chunk, 1])).astype(jnp.bfloat16)
+        dup = (dhidden * wide(given_s[chunk, 2])).astype(jnp.bfloat16)
+        unit_s[chunk, 0] = dgate
+        unit_s[chunk, 1] = dup
+        sent(chunk, 1).start()
+        branch_s[chunk] = dot(given_s[chunk, 0], weight_s[0]).astype(jnp.bfloat16)
+        for k in range(count):
+            pl.when(chunk == k)(lambda k=k: started(halves_sent(k, branch_s, branches, 2)) and None)
+        pl.when(chunk == 0)(lambda: awaited(weights[each:]))
+        back_s[chunk] = (dot(dgate, weight_s[1]) + dot(dup, weight_s[2])).astype(jnp.bfloat16)
+        for k in range(count):
+            pl.when(chunk == k)(lambda k=k: started(halves_sent(k, back_s, dnormed, 4)) and None)
+        return nothing
+
+    lax.fori_loop(0, count, work, 0)
     for chunk in range(count):
-        awaited(arrivals[4 * chunk : 4 * chunk + 2])
-        gate, up = pre_s[chunk, 0], pre_s[chunk, 1]
-        sigmoid = jax.nn.sigmoid(gate)
-        silu = gate * sigmoid
-        hidden = (silu * up).astype(jnp.bfloat16)
-        unit_s[chunk, 0] = hidden
-        send(unit_s.at[chunk, 0], unit_refs[0].at[chunk])
-        awaited(arrivals[4 * chunk + 2 : 4 * chunk + 4])
-        send(grad_s.at[chunk], grad_ref.at[chunk])
-        awaited(weights[:each] if chunk == 0 else [])
-        dhidden = lax.dot_general(grad_s[chunk], weight_s[0], NT, preferred_element_type=jnp.float32)
-        dgate = (dhidden * up * sigmoid * (1.0 + gate * (1.0 - sigmoid))).astype(jnp.bfloat16)
-        dup = (dhidden * silu).astype(jnp.bfloat16)
-        unit_s[chunk, 1] = dgate
-        unit_s[chunk, 2] = dup
-        send(unit_s.at[chunk, 1], unit_refs[1].at[chunk])
-        send(unit_s.at[chunk, 2], unit_refs[2].at[chunk])
-        awaited(weights[each:] if chunk == 0 else [])
-        back_s[chunk] = (dot(dgate, weight_s[1]) + dot(dup, weight_s[2])).astype(jnp.bfloat16)
-        for i in range(2):
-            send(back_s.at[chunk, both[i]], dnormed[2 * chunk + i])
-        branch_s[chunk] = dot(hidden, weight_s[0]).astype(jnp.bfloat16)
-        for i in range(2):
-            send(branch_s.at[chunk, both[i]], branches[2 * chunk + i])
-    awaited(sent)
+        awaited([sent(chunk, 0), sent(chunk, 1)])
+        awaited(halves_sent(chunk, branch_s, branches, 2))
+        awaited(halves_sent(chunk, back_s, dnormed, 4))
 
 
 def down(given, units):
     count = len(given)
     rows, depth = given[0][0].shape
-    unit, full = (count, 2 * rows, units.shape[1]), (count, 2 * rows, depth)
+    size = units.shape[1]
+    full = (count, 2 * rows, depth)
     part = ((rows, depth), jnp.bfloat16)
     outs = with_units(
-        functools.partial(down_kernel, [chunk[4] for chunk in given]),
+        functools.partial(down_kernel, [chunk[3] for chunk in given]),
         units,
-        [block for chunk in given for block in chunk[:4]],
-        ((unit, jnp.bfloat16),) * 3 + ((full, jnp.bfloat16),) + (part,) * (4 * count),
+        [block for chunk in given for block in chunk[:3]],
+        (((count, 2, 2 * rows, size), jnp.bfloat16), (full, jnp.bfloat16)) + (part,) * (4 * count),
         [
-            pltpu.VMEM((count, 2, 2 * rows, units.shape[1]), jnp.float32),
+            pltpu.VMEM((count, 3, 2 * rows, size), jnp.bfloat16),
             pltpu.VMEM(full, jnp.bfloat16),
-            pltpu.VMEM((count, 3, 2 * rows, units.shape[1]), jnp.bfloat16),
+            pltpu.VMEM((count, 2, 2 * rows, size), jnp.bfloat16),
             pltpu.VMEM(full, jnp.bfloat16),
             pltpu.VMEM(full, jnp.bfloat16),
-            pltpu.SemaphoreType.DMA((4 * count,)),
-            pltpu.SemaphoreType.DMA((8 * count,)),
+            pltpu.SemaphoreType.DMA((2, count)),
+            pltpu.SemaphoreType.DMA((6, count)),
         ],
-        16 * count * rows * depth * units.shape[1],
-        2 * count * rows * units.shape[1],
+        16 * count * rows * depth * size,
+        0,
     )
     halves = lambda parts: [parts[2 * i : 2 * i + 2] for i in range(count)]
-    return outs[:4], halves(outs[4 : 4 + 2 * count]), halves(outs[4 + 2 * count :])
+    return outs[:2], halves(outs[2 : 2 + 2 * count]), halves(outs[2 + 2 * count :])
 
 
 def unit_grad_kernel(order, ny, nzh, places_ref, *refs):
-    arrays, (mine_ref, sent_ref, total_s) = refs[:-3], refs[-3:]
+    count = len(order)
+    scratch = refs[-4:]
+    arrays, outs = refs[: -4 - ny * nzh], refs[-4 - ny * nzh : -4]
+    left_s, right_s, total_s, sems = scratch
     for i, (left, at, right, to) in enumerate(order):
-        added = lax.dot_general(
-            arrays[left][at], arrays[right][to], TN, preferred_element_type=jnp.float32
+        started(
+            [
+                pltpu.make_async_copy(arrays[left].at[at], left_s.at[i], sems.at[0, i]),
+                pltpu.make_async_copy(arrays[right].at[to], right_s.at[i], sems.at[1, i]),
+            ]
         )
-        if i == 0:
-            total_s[...] = added
-        else:
-            total_s[...] += added
-    units, columns = mine_ref.shape[1:]
+    total_s[...] = jnp.zeros_like(total_s)
+
+    def work(i, nothing):
+        pltpu.make_async_copy(left_s.at[i], left_s.at[i], sems.at[0, i]).wait()
+        pltpu.make_async_copy(right_s.at[i], right_s.at[i], sems.at[1, i]).wait()
+        total_s[...] += lax.dot_general(left_s[i], right_s[i], TN, preferred_element_type=jnp.float32)
+        return nothing
+
+    lax.fori_loop(0, count, work, 0)
+    units, columns = outs[0].shape
     for y in range(ny):
         for zh in range(nzh):
-            block = total_s[
-                pl.ds(pl.multiple_of(places_ref[ny + zh], units), units),
-                pl.ds(pl.multiple_of(places_ref[y], columns), columns),
+            outs[y * nzh + zh][...] = total_s[
+                pl.ds(zh * units, units), pl.ds(pl.multiple_of(places_ref[y], columns), columns)
             ].astype(jnp.bfloat16)
-            if y == 0:
-                mine_ref[zh] = block
-            else:
-                sent_ref[y - 1, zh] = block
 
 
 def unit_grad(wires, lefts, rights):
@@ -860,29 +896,30 @@
         return len(arrays) - 1
 
     order = [(index(left), at, index(right), to) for (left, at), (right, to) in zip(lefts, rights)]
-    units, depth = lefts[0][0].shape[2], rights[0][0].shape[2]
-    tokens = len(lefts) * lefts[0][0].shape[1]
+    tokens, units = lefts[0][0].shape[-2:]
+    depth = rights[0][0].shape[-1]
     rows, columns = units // nzh, depth // ny
-    places = jnp.stack(
-        [((wires.y + s) % ny) * columns for s in range(ny)] + [s * rows for s in range(nzh)]
-    ).astype(jnp.int32)
+    places = jnp.stack([((wires.y + s) % ny) * columns for s in range(ny)]).astype(jnp.int32)
     in_vmem = pl.BlockSpec(memory_space=pltpu.VMEM)
-    return pl.pallas_call(
+    outs = pl.pallas_call(
         functools.partial(unit_grad_kernel, order, ny, nzh),
         grid_spec=pltpu.PrefetchScalarGridSpec(
             num_scalar_prefetch=1,
             grid=(),
-            in_specs=[in_vmem] * len(arrays),
-            out_specs=[in_vmem] * 2,
-            scratch_shapes=[pltpu.VMEM((units, depth), jnp.float32)],
+            in_specs=[pl.BlockSpec(memory_space=pl.ANY)] * len(arrays),
+            out_specs=[in_vmem] * (ny * nzh),
+            scratch_shapes=[
+                pltpu.VMEM((len(order), tokens, units), jnp.bfloat16),
+                pltpu.VMEM((len(order), tokens, depth), jnp.bfloat16),
+                pltpu.VMEM((units, depth), jnp.float32),
+                pltpu.SemaphoreType.DMA((2, len(order))),
+            ],
         ),
-        out_shape=[
-            jax.ShapeDtypeStruct((nzh, rows, columns), jnp.bfloat16),
-            jax.ShapeDtypeStruct((ny - 1, nzh, rows, columns), jnp.bfloat16),
-        ],
+        out_shape=[jax.ShapeDtypeStruct((rows, columns), jnp.bfloat16)] * (ny * nzh),
         compiler_params=pltpu.CompilerParams(vmem_limit_bytes=VMEM),
         cost_estimate=LITTLE,
     )(places, *arrays)
+    return [outs[zh::nzh] for zh in range(nzh)]
 
 
 def out_grad_kernel(nz, ny, places_ref, mine_ref, other_ref, grad_ref, other_grad_ref, *refs):
@@ -1008,6 +1045,9 @@
     def swap(values):
         return lax.all_to_all(values, "head", split_axis=0, concat_axis=0, tiled=True)
 
+    turned = dict(split_axis=0, concat_axis=0, tiled=True)
+    same_core = [[z * 2 + c for z in range(wires.nz)] for c in range(2)]
+
     def add(*values):
         return low(sum(wide(value) for value in values))
 
@@ -1038,8 +1078,9 @@
             )
         elif step == wires.nz - 1:
             by_y = [wires.over_y(flying["pair"][:2], s) for s in across_y]
-            values, flying["by_y"], flying["pair"], flying["grad_x"] = tie(
-                values, by_y, flying["pair"], flying["grad_x"]
+            halves = [wires.over_zh_half(flying["pair"][:2], s, 0) for s in range(1, wires.nzh)]
+            values, flying["by_y"], flying["pair"], flying["grad_x"], flying["halves"] = tie(
+                values, by_y, flying["pair"], flying["grad_x"], halves
             )
         else:
             (values,) = tie(values)
@@ -1058,23 +1099,23 @@
     def shares(blocks):
         return jnp.stack([piece[:, depth:].reshape(out_rows, size) for piece in blocks])
 
-    by_zh_g = [wires.over_zh(unit_pair[:1], s) for s in range(1, wires.nzh)]
+    halves = [wires.over_zh_half(unit_pair[:2], s, 1) for s in range(1, wires.nzh)]
     out_line = shares(pieces[::2])
     out_x, out_y = wires.over_x(out_line), [wires.over_y(out_line, s) for s in across_y]
     projected, normed, attended_wide, inverses, attended = attend(
         pieces, places, in_turned, keep_row, ends, heads_here
     )
-    attended, out_x, out_y, by_zh_g, unit_pair, out_grad = tie(
-        attended, out_x, out_y, by_zh_g, unit_pair, out_grad
-    )
+    attended, out_x, out_y, halves, unit_pair = tie(attended, out_x, out_y, halves, unit_pair)
     attended_here = swap(attended).reshape(wires.head, rows, out_rows)
-    grad_z = wires.over_zl(out_grad)
     out_across = [wires.over_x(piece) for piece in out_y]
-    by_zh_gy = on_y(by_zh_g)
+    by_zh_gu = [
+        wires.from_halves(flying["halves"][s - 1], halves[s - 1], s) for s in range(1, wires.nzh)
+    ]
+    by_zh_guy = on_y(by_zh_gu)
     out_line_swap = shares(pieces[1::2])
     out_x_swap, out_y_swap = wires.over_core(out_x), [wires.over_core(piece) for piece in out_y]
-    attended_here, out_across, grad_z, out_x_swap, out_y_swap, unit_pair, by_zh_gy, out_line_swap = tie(
-        attended_here, out_across, grad_z, out_x_swap, out_y_swap, unit_pair, by_zh_gy, out_line_swap
+    attended_here, out_across, out_x_swap, out_y_swap, unit_pair, by_zh_gu, by_zh_guy, out_line_swap = tie(
+        attended_here, out_across, out_x_swap, out_y_swap, unit_pair, by_zh_gu, by_zh_guy, out_line_swap
     )
     out_across_swap = [wires.over_core(piece) for piece in out_across]
 
@@ -1089,45 +1130,44 @@
     out_whole = Whole(wires, out_pieces, wires.whole_places(chips, out_rows, size), out_rows, size)
     middle, normed_two = mix(attended_here, out_whole, tokens, ffn_gain[None])
 
-    normed_two, unit_pair, grad_x, grad_z, out_grad = tie(
-        normed_two, unit_pair, grad_x, grad_z, out_grad
-    )
+    normed_two, unit_pair, grad_x, out_grad = tie(normed_two, unit_pair, grad_x, out_grad)
     two_x, two_z = wires.over_x(normed_two), wires.over_zl(normed_two)
-    by_zh_u = [wires.over_zh(unit_pair[1:2], s) for s in range(1, wires.nzh)]
+    by_zh_d = [wires.over_zh(unit_pair[2:], s) for s in range(1, wires.nzh)]
     by_y_d = [wires.over_y(unit_pair[2:], s) for s in across_y]
     two_swap = wires.over_core(normed_two)
-    two_x, two_z, by_zh_u, two_swap, by_y_d, unit_pair = tie(
-        two_x, two_z, by_zh_u, two_swap, by_y_d, unit_pair
+    two_x, two_z, by_zh_d, two_swap, by_y_d, unit_pair, out_grad = tie(
+        two_x, two_z, by_zh_d, two_swap, by_y_d, unit_pair, out_grad
     )
     two_corner = wires.over_x(two_z)
-    by_zh_uy = on_y(by_zh_u)
-    by_zh_d = [wires.over_zh(unit_pair[2:], s) for s in range(1, wires.nzh)]
+    by_zh_dy = on_y(by_zh_d)
+    grad_z = wires.over_zl(out_grad)
     two_swaps = [two_swap] + [wires.over_core(piece) for piece in (two_x, two_z)]
-    two_corner, by_zh_uy, two_swaps, two_x, two_z, grad_z, attended_here, by_zh_d = tie(
-        two_corner, by_zh_uy, two_swaps, two_x, two_z, grad_z, attended_here, by_zh_d
+    two_corner, by_zh_dy, two_swaps, two_x, two_z, grad_z, attended_here = tie(
+        two_corner, by_zh_dy, two_swaps, two_x, two_z, grad_z, attended_here
     )
 
     spot = unit_pair.shape[1], unit_pair.shape[2]
-    gu_pair = unit_pair[:2]
-    gates = [(gu_pair, 0, 2, 0, 0)] + [(flying["by_y"][s - 1], 0, 2, 0, s) for s in across_y]
+    gates = [(unit_pair[:2], 0, 2, 0, 0)] + [(flying["by_y"][s - 1], 0, 2, 0, s) for s in across_y]
     for zh in range(1, wires.nzh):
-        for place, piece, on in ((0, by_zh_g, by_zh_gy), (1, by_zh_u, by_zh_uy)):
-            gates.append((piece[zh - 1], place, 1, zh, 0))
-            gates += [(on[zh - 1][s - 1], place, 1, zh, s) for s in across_y]
+        gates.append((by_zh_gu[zh - 1], 0, 2, zh, 0))
+        gates += [(by_zh_guy[zh - 1][s - 1], 0, 2, zh, s) for s in across_y]
     units = Units(wires, gates, 2, *spot)
 
+    in_line = lax.all_to_all(
+        jnp.concatenate([flying["in_part"]] * wires.nz, axis=0), "head", axis_index_groups=same_core, **turned
+    ).reshape(wires.nz, packed_width, size)
     grad_corner = wires.over_x(grad_z)
     two_corner_swap = wires.over_core(two_corner)
     for_other = pick(attended_here.reshape(wires.nz, 2, rows, out_rows), 1 - wires.c, 2, 1)[:, 0]
     attended_other = wires.over_core(for_other)
-    by_zh_dy = on_y(by_zh_d)
+    grad_swaps = [wires.over_core(grad) for grad in (out_grad, grad_x)]
     first = gate_up(list(zip([normed_two, two_x, two_z], two_swaps)), units)
-    first, grad_corner, two_corner, two_corner_swap, grad_z, attended_other, by_zh_dy = tie(
-        first, grad_corner, two_corner, two_corner_swap, grad_z, attended_other, by_zh_dy
-    )
-    grad_swaps = [wires.over_core(grad) for grad in (out_grad, grad_x, grad_z, grad_corner)]
+    first, grad_corner, two_corner, two_corner_swap, grad_z, attended_other, grad_swaps = tie(
+        first, grad_corner, two_corner, two_corner_swap, grad_z, attended_other, grad_swaps
+    )
+    grad_swaps += [wires.over_core(grad) for grad in (grad_z, grad_corner)]
     second = gate_up([(two_corner, two_corner_swap)], units)
-    second, grad_swaps = tie(second, grad_swaps)
+    second, grad_swaps, in_line = tie(second, grad_swaps, in_line)
     grad_pairs = list(zip([out_grad, grad_x, grad_z, grad_corner], grad_swaps))
     downs = [(unit_pair[2:], 0, 1, 0, 0)] + [(by_y_d[s - 1], 0, 1, 0, s) for s in across_y]
     for zh in range(1, wires.nzh):
@@ -1137,23 +1177,28 @@
         wires, downs + [(array, at + 1, count, zh, s) for array, at, count, zh, s in gates], 3, *spot
     )
 
-    in_part, grad_corner = tie(flying["in_part"], grad_corner)
-    in_line = [in_part] + [wires.over_z(in_part, s) for s in range(1, wires.nz)]
+    in_x, in_y = wires.over_x(in_line), [wires.over_y(in_line, s) for s in across_y]
+    in_line_swap = wires.over_core(in_line)
     outs_co, (dnormed_c, dnormed_o), (branch_c, branch_o) = down(
-        [(*grad_pairs[3], second[0], second[1], 0), (*grad_pairs[0], first[0], first[1], 0)], units
-    )
-    outs_co, in_line, dnormed_c, dnormed_o = tie(outs_co, in_line, dnormed_c, dnormed_o)
+        [(*grad_pairs[3], second[0], 0), (*grad_pairs[0], first[0], 0)], units
+    )
+    outs_co, in_x, in_y, dnormed_c, dnormed_o, branch_c, in_line_swap = tie(
+        outs_co, in_x, in_y, dnormed_c, dnormed_o, branch_c, in_line_swap
+    )
     swap_c, swap_o = wires.over_core(dnormed_c[1]), wires.over_core(dnormed_o[1])
-    swap_c, swap_o, outs_co, in_line = tie(swap_c, swap_o, outs_co, in_line)
-    sum_c = add(dnormed_c[0], swap_c)
-    to_z = wires.over_x(sum_c)
-    in_line = jnp.stack(in_line)
-    in_y = [wires.over_y(in_line, s) for s in across_y]
-    grad_x_pair, grad_z_pair, *_ = tie(grad_pairs[1], grad_pairs[2], sum_c, outs_co)
+    swap_b = wires.over_core(branch_c[1])
+    swap_c, swap_o, swap_b, outs_co, in_x = tie(swap_c, swap_o, swap_b, outs_co, in_x)
+    sum_c, sum_b = add(dnormed_c[0], swap_c), add(branch_c[0], swap_b)
+    to_z, to_x = wires.over_x(sum_c), wires.over_zl(sum_b)
+    in_across = [wires.over_y(in_x, s) for s in across_y]
+    in_swaps = [wires.over_core(piece) for piece in (in_x, *in_y)]
+    grad_x_pair, grad_z_pair, *_ = tie(grad_pairs[1], grad_pairs[2], sum_c, sum_b, outs_co)
     outs_xz, (dnormed_x, dnormed_z), (branch_x, branch_z) = down(
-        [(*grad_x_pair, first[0], first[1], 1), (*grad_z_pair, first[0], first[1], 2)], units
-    )
-    dnormed_x, dnormed_z, to_z, in_y = tie(dnormed_x, dnormed_z, to_z, in_y)
+        [(*grad_x_pair, first[0], 1), (*grad_z_pair, first[0], 2)], units
+    )
+    outs_xz, dnormed_x, dnormed_z, branch_x, branch_z, to_z, to_x, in_across, in_swaps = tie(
+        outs_xz, dnormed_x, dnormed_z, branch_x, branch_z, to_z, to_x, in_across, in_swaps
+    )
     swap_x, swap_z = wires.over_core(dnormed_x[1]), wires.over_core(dnormed_z[1])
     swap_x, swap_z, to_z = tie(swap_x, swap_z, to_z)
     sum_x = add(dnormed_x[0], swap_x)
@@ -1162,142 +1207,123 @@
     final_z = wires.over_zl(sum_z)
     sum_o = add(dnormed_o[0], swap_o)
 
-    every = (outs_co, outs_xz, first[2], second[2])
-
-    def grad_of(every, unit, token):
-        co, xz, normed_oxz, normed_c = every
-        lefts = [(co[unit], 0), (co[unit], 1), (xz[unit], 0), (xz[unit], 1)]
-        if token:
-            rights = [(co[3], 0), (co[3], 1), (xz[3], 0), (xz[3], 1)]
+    every = (outs_co, outs_xz, first, second)
+
+    def grad_of(every, unit):
+        (units_co, grad_co), (units_xz, grad_xz), (made, normed_oxz), (made_c, normed_c) = every
+        if unit == 0:
+            lefts = [(made_c, (0, 0)), (made, (0, 0)), (made, (1, 0)), (made, (2, 0))]
+            rights = [(grad_co, 0), (grad_co, 1), (grad_xz, 0), (grad_xz, 1)]
         else:
+            lefts = [(array, (i, unit - 1)) for array in (units_co, units_xz) for i in range(2)]
             rights = [(normed_c, 0), (normed_oxz, 0), (normed_oxz, 1), (normed_oxz, 2)]
         return unit_grad(wires, lefts, rights)
 
-    def grad_y(mine, sent):
-        return mine, [wires.over_y(sent[s - 1], s) for s in across_y]
+    def on_y_steps(blocks):
+        return [wires.over_y(blocks[s], s) for s in across_y]
+
+    def on_zh(totals):
+        return [wires.over_zh(total, -s) for s, total in enumerate(totals, 1)]
+
+    def totals_of(parts, sent):
+        return [add(part[0], *more) for part, more in zip(parts, sent)]
 
     def grad_last(mine, sent):
         return wide(in_order([mine, sent], wires.x, 0))
 
-    every, sum_x, sum_z = tie(every, sum_x, sum_z)
-    gate_mine, gate_sent = grad_of(every, 1, False)
-    in_swaps = [wires.over_core(piece) for piece in (in_line, *in_y)]
-    final_x, final_z, gate_mine, gate_sent, in_swaps, sum_o, in_line = tie(
-        final_x, final_z, gate_mine, gate_sent, in_swaps, sum_o, in_line
-    )
-    gate_back = grad_y(gate_mine, gate_sent)
+    every, sum_x, sum_z, branch_x, branch_z = tie(every, sum_x, sum_z, branch_x, branch_z)
+    swap_x, swap_z = wires.over_core(branch_x[1]), wires.over_core(branch_z[1])
+    in_across_swap = [wires.over_core(piece) for piece in in_across]
+    gate_parts = grad_of(every, 1)
+    sum_x, sum_z = add(branch_x[0], swap_x, to_x), add(branch_z[0], swap_z)
+    final_x, final_z, gate_parts, sum_o, sum_x, sum_z, in_across_swap = tie(
+        final_x, final_z, gate_parts, sum_o, sum_x, sum_z, in_across_swap
+    )
+    gate_sent = [on_y_steps(part) for part in gate_parts[1:]]
     d_middle, d_mixed, ffn_gain_part, d_attended = unmix(
         (sum_o, final_x, final_z), middle, out_grad, ffn_gain[None], out_whole, wires.head
     )
-    every, d_attended, d_mixed, branches, in_line, in_y = tie(
-        every, d_attended, d_mixed, (branch_o, branch_x, branch_z, branch_c), in_line, in_y
+    every, d_attended, d_mixed, gate_parts, gate_sent, sum_x, sum_z = tie(
+        every, d_attended, d_mixed, gate_parts, gate_sent, sum_x, sum_z
     )
     d_attended = swap(d_attended).reshape(group_rows, out_rows)
+    final_x, final_z = wires.over_x(sum_x), wires.over_zl(sum_z)
+    gate_back = on_zh(totals_of(gate_parts[1:], gate_sent))
+    gate_sent = on_y_steps(gate_parts[0])
     other_d_mixed = wires.over_core(d_mixed)
-    in_x = wires.over_x(in_line)
-    swap_c, swap_x, swap_z = (wires.over_core(branches[i][1]) for i in (3, 1, 2))
-    up_parts = grad_of(every, 2, False)
+    up_parts = grad_of(every, 2)
+    up_sent = [on_y_steps(part) for part in up_parts[1:]]
     out_own, out_sent = out_grad_parts(wires, attended_here, attended_other, d_mixed, other_d_mixed)
-    down_parts = grad_of(every, 0, True)
-    d_attended, out_own, out_sent, up_parts, down_parts, gate_back, in_x, swap_c, swap_x, swap_z = tie(
-        d_attended, out_own, out_sent, up_parts, down_parts, gate_back, in_x, swap_c, swap_x, swap_z
-    )
-
-    def total_of(mine, sent):
-        return [add(mine[s], *[piece[s] for piece in sent]) for s in range(wires.nzh)]
-
-    def on_zh(totals):
-        return totals[0], [wires.over_zh(totals[s], -s) for s in range(1, wires.nzh)]
-
-    sum_c = add(branches[3][0], swap_c)
-    gate_totals = total_of(*gate_back)
-    gate_totals, d_attended, sum_c, out_sent, up_parts = tie(
-        gate_totals, d_attended, sum_c, out_sent, up_parts
-    )
-    up_back = grad_y(*up_parts)
-    gate_back = on_zh(gate_totals)
+    down_parts = grad_of(every, 0)
+    d_attended, final_x, final_z, gate_back, gate_sent, up_parts, up_sent, out_own, out_sent, down_parts = tie(
+        d_attended, final_x, final_z, gate_back, gate_sent, up_parts, up_sent, out_own, out_sent, down_parts
+    )
+    up_totals = totals_of(up_parts[1:], up_sent)
+    up_totals, d_attended, out_sent, up_parts, down_parts = tie(
+        up_totals, d_attended, out_sent, up_parts, down_parts
+    )
+    up_back = on_zh(up_totals)
+    up_sent = on_y_steps(up_parts[0])
+    down_sent = [on_y_steps(part) for part in down_parts[1:]]
     out_first = [wires.over_x(out_sent[s]) for s in across_y]
-    to_x = wires.over_zl(sum_c)
     d_projected = attend_back(
         projected, keep_row, ends, attended_wide, inverses, d_attended, heads_here, rows
     )
-    d_projected, gate_back, up_back, to_x, out_first = tie(d_projected, gate_back, up_back, to_x, out_first)
-    d_projected, down_parts, in_y, out_own, out_first, in_x = tie(
-        d_projected, down_parts, in_y, out_own, out_first, in_x
+    d_projected, up_back, up_sent, down_sent, out_first = tie(
+        d_projected, up_back, up_sent, down_sent, out_first
+    )
+    down_totals = totals_of(down_parts[1:], down_sent)
+    out_total = [add(out_own[s], out_first[s - 1]) for s in across_y]
+    down_totals, out_total, d_projected, down_parts, in_line, in_x, in_y, in_across = tie(
+        down_totals, out_total, d_projected, down_parts, in_line, in_x, in_y, in_across
     )
     d_here = swap(d_projected)
-    down_back = grad_y(*down_parts)
-    in_across = [wires.over_x(piece) for piece in in_y]
-    up_totals = total_of(*up_back)
+    down_sent = on_y_steps(down_parts[0])
+    out_last = wires.over_x(out_sent[0])
+    swap_o = wires.over_core(branch_o[1])
+    out_y = [wires.over_y(total, s) for total, s in zip(out_total, across_y)]
     in_back, attn_gain_part = in_grad_parts(normed, d_projected, in_turned, attn_gain[None])
-    d_here, in_back, attn_gain_part, down_back, up_totals, in_across = tie(
-        d_here, in_back, attn_gain_part, down_back, up_totals, in_across
-    )
-    in_across_swap = [wires.over_core(piece) for piece in in_across]
-    in_x_swap = wires.over_core(in_x)
-    down_totals = total_of(*down_back)
-    out_total = [add(out_own[s], out_first[s - 1]) for s in across_y]
-    down_totals, up_totals, out_total, out_own, branches, in_across, in_across_swap, in_x_swap, gains, d_here = tie(
-        down_totals,
-        up_totals,
-        out_total,
-        out_own,
-        branches,
-        in_across,
-        in_across_swap,
-        in_x_swap,
-        jnp.concatenate([attn_gain_part, ffn_gain_part], axis=0),
-        d_here,
+    firsts = [
+        add(parts[0][0], *sent, *back)
+        for parts, sent, back in ((gate_parts, gate_sent, gate_back), (up_parts, up_sent, up_back))
+    ]
+    d_here, in_back, attn_gain_part, down_sent, out_last, out_y, firsts, down_totals, swap_o = tie(
+        d_here, in_back, attn_gain_part, down_sent, out_last, out_y, firsts, down_totals, swap_o
     )
     cut = packed_width // 2
+    gains = jnp.concatenate([attn_gain_part, ffn_gain_part], axis=0)
     in_pieces = in_layout(in_line, in_x, in_y, in_across)
-    in_pieces += in_layout(in_swaps[0], in_x_swap, in_swaps[1:], in_across_swap)
-    in_chips = [(wires.z - s) % wires.nz for s in range(wires.nz)]
+    in_pieces += in_layout(in_line_swap, in_swaps[0], in_swaps[1:], in_across_swap)
     in_whole = Whole(
-        wires, in_pieces, wires.whole_places(in_chips, packed_width, size), packed_width, size
-    )
-    up_back = on_zh(up_totals)
-    out_last = wires.over_x(out_sent[0])
-    out_y = [wires.over_y(total, s) for total, s in zip(out_total, across_y)]
-    final_z = wires.over_zl(add(branches[2][0], swap_z))
+        wires, in_pieces, wires.whole_places(range(wires.nz), packed_width, size), packed_width, size
+    )
+    down_back = on_zh(down_totals)
+    out_total = add(out_own[0], out_last, *out_y)
+    in_x, in_y = wires.over_x(in_back[:cut]), [wires.over_y(in_back[cut:], s) for s in across_y]
+    others = wires.over_x(jnp.stack([pick(total, 1 - wires.x, 2, 1) for total in firsts]))
     in_grad = last(d_here, in_whole, tokens, d_middle, attn_gain[None])
-    in_grad, up_back, down_totals, out_last, out_y, final_z, in_back, gains, branches, swap_x, to_x = tie(
-        in_grad, up_back, down_totals, out_last, out_y, final_z, in_back, gains, branches, swap_x, to_x
-    )
-    down_back = on_zh(down_totals)
-    final_x = wires.over_x(add(branches[1][0], swap_x, to_x))
-    in_x, in_y = wires.over_x(in_back[:cut]), [wires.over_y(in_back[cut:], s) for s in across_y]
-    swap_o = wires.over_core(branches[0][1])
-    out_total = add(out_own[0], out_last, *out_y)
-    firsts = [add(mine, *sent) for mine, sent in (gate_back, up_back)]
+    in_grad, out_total, in_x, in_y, others, down_sent, down_back = tie(
+        in_grad, out_total, in_x, in_y, others, down_sent, down_back
+    )
+    out_turns = lax.all_to_all(out_total, "head", axis_index_groups=same_core, **turned)
+    in_halves = (wires.sum_y(add(in_back[:cut], in_x)), wires.sum_x(add(in_back[cut:], *in_y)))
+    totals = [*firsts, add(down_parts[0][0], *down_sent, *down_back)]
+    others = [others[0], others[1], wires.over_x(pick(totals[2], 1 - wires.x, 2, 1))]
     gains = gains + wires.over_core(gains)
-    down_back, final_x, in_x, in_y, swap_o, out_total, firsts, gains = tie(
-        down_back, final_x, in_x, in_y, swap_o, out_total, firsts, gains
-    )
-    in_halves = (add(in_back[:cut], in_x), add(in_back[cut:], *in_y))
-    out_turns = lax.all_to_all(
-        out_total,
-        "head",
-        split_axis=0,
-        concat_axis=0,
-        tiled=True,
-        axis_index_groups=[[z * 2 + c for z in range(wires.nz)] for c in range(2)],
-    )
-    others = wires.over_x(jnp.stack([pick(total, 1 - wires.x, 2, 1) for total in firsts]))
-    in_halves = (wires.sum_y(in_halves[0]), wires.sum_x(in_halves[1]))
-    output = low(middle + wide(branches[0][0]) + wide(swap_o) + wide(final_x) + wide(final_z))
-    gains = gains + wires.over_zl(gains)
-    down_total = add(down_back[0], *down_back[1])
-    out_turns, others, in_halves, gains, output, down_total = tie(
-        out_turns, others, in_halves, gains, output, down_total
-    )
+    out_turns, gains, others, in_halves, totals = tie(out_turns, gains, others, in_halves, totals)
     out_part = add(*[out_turns[z] for z in range(wires.nz)])
     out_x = wires.over_x(out_part)
     out_by_y = [wires.over_y(out_part, s) for s in across_y]
-    others = [others[0], others[1], wires.over_x(pick(down_total, 1 - wires.x, 2, 1))]
-    totals = [*firsts, down_total]
+    output = low(middle + wide(branch_o[0]) + wide(swap_o) + wide(final_x) + wide(final_z))
+    gains = gains + wires.over_zl(gains)
     gains = gains + sum(wires.over_zh(gains, s) for s in range(1, wires.nzh))
-    out_x, out_by_y, gains, others = tie(out_x, out_by_y, gains, others)
+    gate_grad, up_grad, down_grad = (
+        grad_last(pick(total, wires.x, 2, 1), other) for total, other in zip(totals, others)
+    )
+    gate_grad, up_grad = gate_grad.T, up_grad.T
+    out_x, out_by_y, gains, output, gate_grad, up_grad, down_grad = tie(
+        out_x, out_by_y, gains, output, gate_grad, up_grad, down_grad
+    )
     out_by_yx = [wires.over_y(out_x, s) for s in across_y]
     gains_x = wires.over_x(gains)
     gains = gains + gains_x + sum(
@@ -1313,10 +1339,6 @@
             1,
         )
     )
-    gate_grad, up_grad, down_grad = (
-        grad_last(pick(total, wires.x, 2, 1), others[i]) for i, total in enumerate(totals)
-    )
-    gate_grad, up_grad = gate_grad.T, up_grad.T
     in_weight_grad = wide(jnp.concatenate(in_halves, axis=0)).T
     return (
         output,

time: 743 us -> 709 us (0.954)
  waiting for transfers between devices: 328 us -> 287 us
  other arithmetic: 57.1 us -> 70.4 us
    ppermute x7 -> x5, waiting for transfers between devices: 84.7 us -> 58.7 us  [over_zh(): lax.ppermute(values, 'head', [(i, (i // 4 + shift) % self.nzh * 4 + i % 4...]
    ppermute x6, waiting for transfers between devices: 37 us -> 11.4 us  [over_zl(): return lax.ppermute(values, 'head', [(i, i ^ 2) for i in range(self.head)])]
    convert_element_type x20, other arithmetic: 35 us -> 46.1 us  [low(): return values.astype(jnp.bfloat16)]
    ppermute x20 -> x19, waiting for transfers between devices: 107 us -> 97.4 us  [over_x(): return lax.ppermute(values, 'dp', [(i, i ^ 1) for i in range(self.dp)])]
    all_to_all x1 -> x2, waiting for transfers between devices: 0.01 us -> 9.12 us  [the longest x1 9.11 us: per_device(): lax.all_to_all(out_total, 'head', axis_index_groups=same_core, **turned)]
    ppermute x16 -> x19, waiting for transfers between devices: 44.7 us -> 48.9 us  [over_y(): lax.ppermute(values, 'dp', [(i, (i // 2 + shift) % self.ny * 2 + i % 2) f...]
    ppermute x16 -> x19, starting transfers between devices: 18.1 us -> 16.6 us  [over_y(): lax.ppermute(values, 'dp', [(i, (i // 2 + shift) % self.ny * 2 + i % 2) f...]
    ppermute x20 -> x19, starting transfers between devices: 22.2 us -> 23.3 us  [over_x(): return lax.ppermute(values, 'dp', [(i, i ^ 1) for i in range(self.dp)])]
  transfers between devices with their start and end apart: 92 -> 92, of which waited for: 35 -> 40; matrix products, arithmetic and copies ran while one was open for 8% -> 9% of each run, Pallas kernels for 27% -> 28%
where the time goes in v5:
time: 709 us; the launch traced here: 701 us
  waiting for transfers between devices  287 us (40%)
  Pallas kernels  208 us (29%)
  starting transfers between devices  108 us (15%)
  other arithmetic  70.4 us (10%)
  local copies, waits for them, and re-layouts  26.2 us (4%)
    ppermute x19, waiting for transfers between devices, over_x(): return lax.ppermute(values, 'dp', [(i, i ^ 1) for i in range(self.dp)])  97.4 us
    pallas_call x4, Pallas kernels, with_units(): pl.pallas_call(functools.partial(kernel, units), grid_spec=pltpu.Prefetch...  72.6 us
    ppermute x5, waiting for transfers between devices, over_zh(): lax.ppermute(values, 'head', [(i, (i // 4 + shift) % self.nzh * 4 + i % 4...  58.7 us
    ppermute x19, waiting for transfers between devices, over_y(): lax.ppermute(values, 'dp', [(i, (i // 2 + shift) % self.ny * 2 + i % 2) f...  48.9 us
    convert_element_type x20, other arithmetic, low(): return values.astype(jnp.bfloat16)  46.1 us
    pallas_call x3, Pallas kernels, unit_grad(): pl.pallas_call(functools.partial(unit_grad_kernel, order, ny, nzh), grid_...  34 us
    pallas_call x1, Pallas kernels, attend_back(): pl.pallas_call(functools.partial(attend_back_kernel, heads, rows), grid_s...  31.9 us
    pallas_call x3, Pallas kernels, with_whole(): pl.pallas_call(functools.partial(kernel, whole), grid_spec=pltpu.Prefetch...  31.7 us
  transfers between devices with their start and end apart: 92, of which 40 were waited for; matrix products, arithmetic and copies ran while one was open for 9% of the time, Pallas kernels for 28%

profile of v5, /device:TPU:0, one launch (start us, length us, event | category | flops | bytes accessed | tf_op | source)
XLA Modules:
  0.0 701.2 jit_solution(16934729311791769551)
XLA Ops:
  15.5 23.0 %collective-permute-done.2 = bf16[3,352,512]{2,1,0:T(8,128)(2,1)S(1)} collective-permute-done((bf16[3,352,512]{2,1,0:T(8,128)(2,1)S(1)}, bf16[3,352,512]{2,1,0:T(8,128)(2,1)S(1)}, u32[]{:S(2)}, u32[]{:S(2)}) %collective-permute-start.2) | collective-permute-done | bytes 1081376 | tf_op jit(solution)/shard_map/ppermute | solution.py:332
  46.6 20.8 %collective-permute-done.7.refs_8_ = bf16[256,2048]{1,0:T(8,128)(2,1)} collective-permute-done((bf16[256,2048]{1,0:T(8,128)(2,1)}, bf16[256,2048]{1,0:T(8,128)(2,1)}, u32[]{:S(2)}, u32[]{:S(2)}) %collective-permute-start.7) | collective-permute-done | bytes 1048608 | tf_op jit(solution)/shard_map/ppermute | solution.py:332
  67.5 7.9 %collective-permute-done.6 = bf16[256,2560]{1,0:T(8,128)(2,1)} collective-permute-done((bf16[256,2560]{1,0:T(8,128)(2,1)}, bf16[256,2560]{1,0:T(8,128)(2,1)}, u32[]{:S(2)}, u32[]{:S(2)}) %collective-permute-start.6) | collective-permute-done | bytes 1310752 | tf_op jit(solution)/shard_map/ppermute | solution.py:378
  83.7 28.1 %collective-permute-done.9 = bf16[256,2560]{1,0:T(8,128)(2,1)S(1)} collective-permute-done((bf16[256,2560]{1,0:T(8,128)(2,1)S(1)}, bf16[256,2560]{1,0:T(8,128)(2,1)S(1)}, u32[]{:S(2)}, u32[]{:S(2)}) %collective-permute-start.9) | collective-permute-done | bytes 1310752 | tf_op jit(solution)/shard_map/ppermute | solution.py:387
  123.8 23.0 %shard_map.178 = (bf16[2048,320]{1,0:T(8,128)(2,1)}, bf16[2048,2048]{1,0:T(8,128)(2,1)}, f32[2048,256]{1,0:T(8,128)}, f32[2048,128]{1,0:T(8,128)}, bf16[2048,256]{1,0:T(8,128)(2,1)}) custom-call(s32[3]{0:T(128)} %bitcast.113, s32[8]{0:T(128)} %stack.214.at_ref, bf16[256,2560]{1,0:T(8,128)(2,1)} %copy-done.14, ...), custom_call_target="tpu_custom_call" | custom-call | flops 1 | bytes 1 | tf_op jit(solution)/shard_map/pallas_call | solution.py:134
  166.8 20.1 %collective-permute-done.16.refs_3_ = bf16[4,256,512]{2,1,0:T(8,128)(2,1)} collective-permute-done((bf16[4,256,512]{2,1,0:T(8,128)(2,1)S(1)}, bf16[4,256,512]{2,1,0:T(8,128)(2,1)}, u32[]{:S(2)}, u32[]{:S(2)}) %collective-permute-start.16) | collective-permute-done | bytes 1048608 | tf_op jit(solution)/shard_map/ppermute | solution.py:332
  199.0 9.0 %shard_map.179 = (f32[256,2048]{1,0:T(8,128)}, bf16[256,2048]{1,0:T(8,128)(2,1)}) custom-call(s32[12]{0:T(128)} %stack.204.places_ref, bf16[4,256,512]{2,1,0:T(8,128)(2,1)} %copy-done.10, bf16[4,256,512]{2,1,0:T(8,128)(2,1)} %copy-done.19, bf16[4,256,512]{2,1,0:T(8,128)(2,1)} %copy-done.20, bf16[4,256,512]{2,1,0:T(8,128)(2,1)} %collective-permute-done.16.refs_3_, ...), custom_call_target="tpu_custom_call" | custom-call | flops 1 | bytes 1 | tf_op jit(solution)/shard_map/pallas_call | solution.py:537
  214.2 35.1 %collective-permute-done.23.refs_2_ = bf16[1,352,1024]{2,1,0:T(8,128)(2,1)S(1)} collective-permute-done((bf16[1,352,1024]{2,1,0:T(8,128)(2,1)S(1)}, bf16[1,352,1024]{2,1,0:T(8,128)(2,1)S(1)}, u32[]{:S(2)}, u32[]{:S(2)}) %collective-permute-start.23) | collective-permute-done | bytes 720928 | tf_op jit(solution)/shard_map/ppermute | solution.py:351
  254.4 17.3 %collective-permute-done.27.refs_3_ = bf16[1,352,1024]{2,1,0:T(8,128)(2,1)S(1)} collective-permute-done((bf16[1,352,1024]{2,1,0:T(8,128)(2,1)S(1)}, bf16[1,352,1024]{2,1,0:T(8,128)(2,1)S(1)}, u32[]{:S(2)}, u32[]{:S(2)}) %collective-permute-start.27) | collective-permute-done | bytes 720928 | tf_op jit(solution)/shard_map/ppermute | solution.py:335
  288.5 19.0 %shard_map.180 = (bf16[3,3,512,704]{3,2,1,0:T(8,128)(2,1)}, bf16[3,512,2048]{2,1,0:T(8,128)(2,1)}) custom-call(s32[2]{0:T(128)} %get-tuple-element.602.places_ref, bf16[2,352,1024]{2,1,0:T(8,128)(2,1)} %slice.137.refs_0_.refs_4_, bf16[2,352,1024]{2,1,0:T(8,128)(2,1)} %copy-done.5, bf16[2,352,1024]{2,1,0:T(8,128)(2,1)} %copy-done.2, ...), custom_call_target="tpu_custom_call" | custom-call | flops 1 | bytes 1 | tf_op jit(solution)/shard_map/pallas_call | solution.py:668
  308.9 10.0 %shard_map.181 = (bf16[1,3,512,704]{3,2,1,0:T(8,128)(2,1)}, bf16[1,512,2048]{2,1,0:T(8,128)(2,1)}) custom-call(s32[2]{0:T(128)} %get-tuple-element.602.places_ref, bf16[2,352,1024]{2,1,0:T(8,128)(2,1)} %slice.137.refs_0_.refs_4_, bf16[2,352,1024]{2,1,0:T(8,128)(2,1)} %copy-done.5, bf16[2,352,1024]{2,1,0:T(8,128)(2,1)} %copy-done.2, ...), custom_call_target="tpu_custom_call" | custom-call | flops 1 | bytes 1 | tf_op jit(solution)/shard_map/pallas_call | solution.py:668
  320.9 21.7 %shard_map.182 = (bf16[2,2,512,704]{3,2,1,0:T(8,128)(2,1)}, bf16[2,512,2048]{2,1,0:T(8,128)(2,1)}, bf16[256,2048]{1,0:T(8,128)(2,1)}, bf16[256,2048]{1,0:T(8,128...) custom-call(s32[2]{0:T(128)} %get-tuple-element.602.places_ref, ...), custom_call_target="tpu_custom_call" | custom-call | flops 1 | bytes 1 | tf_op jit(solution)/shard_map/pallas_call | solution.py:668
  363.2 21.8 %shard_map.183 = (bf16[2,2,512,704]{3,2,1,0:T(8,128)(2,1)}, bf16[2,512,2048]{2,1,0:T(8,128)(2,1)}, bf16[256,2048]{1,0:T(8,128)(2,1)}, bf16[256,2048]{1,0:T(8,128...) custom-call(s32[2]{0:T(128)} %get-tuple-element.602.places_ref, ...), custom_call_target="tpu_custom_call" | custom-call | flops 1 | bytes 1 | tf_op jit(solution)/shard_map/pallas_call | solution.py:668
  402.6 11.5 %shard_map.184 = (bf16[352,1024]{1,0:T(8,128)(2,1)}, bf16[352,1024]{1,0:T(8,128)(2,1)}, bf16[352,1024]{1,0:T(8,128)(2,1)}, bf16[352,1024]{1,0:T(8,128)(2,1)}) custom-call(s32[2]{0:T(128)} %get-tuple-element.603.places_ref, bf16[2,2,512,704]{3,2,1,0:T(8,128)(2,1)} %get-tuple-element.463.refs_0_, bf16[1,512,2048]{2,1,0:T(8,128)(2,1)} %get-tuple-element.464.refs_1_, ...), custom_call_target="tpu_custom_call" | custom-call | flops 1 | bytes 1 | tf_op jit(solution)/shard_map/pallas_call | solution.py:904
  427.0 10.5 %shard_map.185 = (f32[256,2048]{1,0:T(8,128)}, bf16[256,2048]{1,0:T(8,128)(2,1)}, f32[1,2048]{1,0:T(1,128)}, bf16[8,256,256]{2,1,0:T(8,128)(2,1)}) custom-call(s32[12]{0:T(128)} %stack.204.places_ref, bf16[4,256,512]{2,1,0:T(8,128)(2,1)} %copy-done.10, bf16[4,256,512]{2,1,0:T(8,128)(2,1)} %copy-done.19, bf16[4,256,512]{2,1,0:T(8,128)(2,1)} %copy-done.20, ...), custom_call_target="tpu_custom_call" | custom-call | flops 1 | bytes 1 | tf_op jit(solution)/shard_map/pallas_call | solution.py:537
  452.9 11.2 %shard_map.186 = (bf16[352,1024]{1,0:T(8,128)(2,1)}, bf16[352,1024]{1,0:T(8,128)(2,1)}, bf16[352,1024]{1,0:T(8,128)(2,1)}, bf16[352,1024]{1,0:T(8,128)(2,1)}) custom-call(s32[2]{0:T(128)} %get-tuple-element.603.places_ref, bf16[2,2,512,704]{3,2,1,0:T(8,128)(2,1)} %get-tuple-element.463.refs_0_, bf16[1,512,2048]{2,1,0:T(8,128)(2,1)} %get-tuple-element.464.refs_1_, ...), custom_call_target="tpu_custom_call" | custom-call | flops 1 | bytes 1 | tf_op jit(solution)/shard_map/pallas_call | solution.py:904
  471.6 11.3 %shard_map.188 = (bf16[352,1024]{1,0:T(8,128)(2,1)}, bf16[352,1024]{1,0:T(8,128)(2,1)}, bf16[352,1024]{1,0:T(8,128)(2,1)}, bf16[352,1024]{1,0:T(8,128)(2,1)}) custom-call(s32[2]{0:T(128)} %get-tuple-element.603.places_ref, bf16[1,3,512,704]{3,2,1,0:T(8,128)(2,1)} %get-tuple-element.477.refs_10_.refs_0_, bf16[2,512,2048]{2,1,0:T(8,128)(2,1)} %get-tuple-element.478.refs_1_, ...), custom_call_target="tpu_custom_call" | custom-call | flops 1 | bytes 1 | tf_op jit(solution)/shard_map/pallas_call | solution.py:904
  489.5 15.6 %collective-permute-done.59 = bf16[352,1024]{1,0:T(8,128)(2,1)} collective-permute-done((bf16[352,1024]{1,0:T(8,128)(2,1)}, bf16[352,1024]{1,0:T(8,128)(2,1)}, u32[]{:S(2)}, u32[]{:S(2)}) %collective-permute-start.59) | collective-permute-done | bytes 720928 | tf_op jit(solution)/shard_map/ppermute | solution.py:351
  515.6 31.9 %shard_map.189.grad_ref = bf16[8,256,320]{2,1,0:T(8,128)(2,1)} custom-call(s32[3]{0:T(128)} %bitcast.114, bf16[2048,320]{1,0:T(8,128)(2,1)} %get-tuple-element.497.projected_ref, f32[1,2048]{1,0:T(1,128)} %bitcast.108, f32[2048,256]{1,0:T(8,128)} %get-tuple-element.498.y_ref, f32[2048,128]{1,0:T(8,128)} %get-tuple-element.499.inv_ref, ...), custom_call_target="tpu_custom_call" | custom-call | flops 1 | bytes 1 | tf_op jit(solution)/shard_map/pallas_call | solution.py:260
  564.7 7.7 %shard_map.190 = (bf16[320,2048]{1,0:T(8,128)(2,1)}, f32[1,2048]{1,0:T(1,128)}) custom-call(bf16[2048,2048]{1,0:T(8,128)(2,1)} %get-tuple-element.520.normed_ref, bf16[8,256,320]{2,1,0:T(8,128)(2,1)} %shard_map.189.grad_ref, bf16[320,2048]{1,0:T(8,128)(2,1)} %bitcast.98, f32[1,2048]{1,0:T(1,128)} %bitcast.105), custom_call_target="tpu_custom_call" | custom-call | flops 1 | bytes 1 | tf_op jit(solution)/shard_map/pallas_call | solution.py:993
  574.4 10.8 %collective-permute-done.68 = bf16[4,256,512]{2,1,0:T(8,128)(2,1)} collective-permute-done((bf16[4,256,512]{2,1,0:T(8,128)(2,1)}, bf16[4,256,512]{2,1,0:T(8,128)(2,1)}, u32[]{:S(2)}, u32[]{:S(2)}) %collective-permute-start.68) | collective-permute-done | bytes 1048608 | tf_op jit(solution)/shard_map/ppermute | solution.py:332
  585.1 15.7 %collective-permute-done.67 = bf16[352,1024]{1,0:T(8,128)(2,1)} collective-permute-done((bf16[352,1024]{1,0:T(8,128)(2,1)}, bf16[352,1024]{1,0:T(8,128)(2,1)}, u32[]{:S(2)}, u32[]{:S(2)}) %collective-permute-start.67) | collective-permute-done | bytes 720928 | tf_op jit(solution)/shard_map/ppermute | solution.py:335
  617.1 12.2 %shard_map.191 = f32[256,2048]{1,0:T(8,128)} custom-call(s32[12]{0:T(128)} %stack.192.places_ref, bf16[4,320,512]{2,1,0:T(8,128)(2,1)} %all-to-all-done.1.refs_0_, bf16[4,320,512]{2,1,0:T(8,128)(2,1)} %collective-permute-done.38.refs_1_, bf16[4,320,512]{2,1,0:T(8,128)(2,1)} %collective-permute-done.39.refs_2_, bf16[4,320,512]{2,1,0:T(8,128)(2,1)} %copy-done.36, ...), custom_call_target="tpu_custom_call" | custom-call | flops 1 | bytes 1 | tf_op jit(solution)/shard_map/pallas_call | solution.py:537
  666.1 9.1 %all-to-all-done.4 = bf16[4,256,512]{2,1,0:T(8,128)(2,1)S(1)} async-done(((bf16[4,256,512]{2,1,0:T(8,128)(2,1)}), bf16[4,256,512]{2,1,0:T(8,128)(2,1)S(1)}, u32[]{:S(2)}, u32[]{:S(2)}) %all-to-all-start.4) | async-done | bytes 1048608 | tf_op jit(solution)/shard_map/all_to_all | solution.py:1308
  (388 shorter events, 294.7 us)
Async XLA Ops:
  2.9 35.6 %collective-permute-start = (bf16[256,2560]{1,0:T(8,128)(2,1)S(1)}, bf16[256,2560]{1,0:T(8,128)(2,1)}, u32[]{:S(2)}, u32[]{:S(2)}) collective-permute-start(bf16[256,2560]{1,0:T(8,128)(2,1)S(1)} %pad_maximum_fusion.2.refs_0_), channel_id=1, source_target_pairs={{0,2},{1,3},{2,4},{3,5},{4,6},{5,7},{8,10},{9,11},{10,12},{11,13},... | collective-permute-start | bytes 3932168 | tf_op jit(solution)/shard_map/ppermute | solution.py:373
  75.4 36.4 %collective-permute-start.10 = (bf16[2,352,1024]{2,1,0:T(8,128)(2,1)S(1)}, bf16[2,352,1024]{2,1,0:T(8,128)(2,1)S(1)}, u32[]{:S(2)}, u32[]{:S(2)}) collective-permute-start(bf16[2,352,1024]{2,1,0:T(8,128)(2,1)S(1)} %slice.125), channel_id=1, source_target_pairs={{0,16},{8,24},{16,0},{24,8},{1,17},{9,25},{17,1},{25,9},{2,18},{10... | collective-permute-start | bytes 4325384 | tf_op jit(solution)/shard_map/ppermute | solution.py:335
  77.0 34.8 %collective-permute-start.11 = (bf16[2,352,1024]{2,1,0:T(8,128)(2,1)S(1)}, bf16[2,352,1024]{2,1,0:T(8,128)(2,1)S(1)}, u32[]{:S(2)}, u32[]{:S(2)}) collective-permute-start(bf16[2,352,1024]{2,1,0:T(8,128)(2,1)S(1)} %slice.125), channel_id=1, source_target_pairs={{0,4},{1,5},{6,2},{7,3},{8,12},{9,13},{14,10},{15,11},{16,20},{17,... | collective-permute-start | bytes 4325384 | tf_op jit(solution)/shard_map/ppermute | solution.py:361
  117.2 36.7 %collective-permute-start.15 = (bf16[2,352,1024]{2,1,0:T(8,128)(2,1)}, bf16[2,352,1024]{2,1,0:T(8,128)(2,1)}, u32[]{:S(2)}, u32[]{:S(2)}) collective-permute-start(bf16[2,352,1024]{2,1,0:T(8,128)(2,1)} %slice.130), channel_id=1, source_target_pairs={{2,6},{3,7},{4,0},{5,1},{10,14},{11,15},{12,8},{13,9},{18,22},{19,... | collective-permute-start | bytes 4325384 | tf_op jit(solution)/shard_map/ppermute | solution.py:361
  153.9 41.2 %all-to-all-start = ((bf16[8,256,256]{2,1,0:T(8,128)(2,1)}), bf16[8,256,256]{2,1,0:T(8,128)(2,1)S(1)}, u32[]{:S(2)}, u32[]{:S(2)}) async-start(bf16[8,256,256]{2,1,0:T(8,128)(2,1)} %bitcast.101), calls=%async_computation | async-start | bytes 2097152 | tf_op jit(solution)/shard_map/all_to_all | solution.py:1046
  161.0 34.2 %collective-permute-start.19 = (bf16[2,352,1024]{2,1,0:T(8,128)(2,1)S(1)}, bf16[2,352,1024]{2,1,0:T(8,128)(2,1)}, u32[]{:S(2)}, u32[]{:S(2)}) collective-permute-start(bf16[2,352,1024]{2,1,0:T(8,128)(2,1)S(1)} %broadcast_select_fusion.refs_2_.refs_6_), channel_id=1, source_target_pairs={{0,16},{8,24},{16,0},{24,8},{1,17},{9,25},{17,1},{25,9},{2,18},{10... | collective-permute-start | bytes 4325384 | tf_op jit(solution)/shard_map/ppermute | solution.py:335
  208.0 41.3 %collective-permute-start.21 = (bf16[256,2048]{1,0:T(8,128)(2,1)}, bf16[256,2048]{1,0:T(8,128)(2,1)S(1)}, u32[]{:S(2)}, u32[]{:S(2)}) collective-permute-start(bf16[256,2048]{1,0:T(8,128)(2,1)} %get-tuple-element.332.refs_4_), channel_id=1, source_target_pairs={{0,8},{8,0},{16,24},{24,16},{1,9},{9,1},{17,25},{25,17},{2,10},{10... | collective-permute-start | bytes 3145736 | tf_op jit(solution)/shard_map/ppermute | solution.py:332
  209.6 40.6 %collective-permute-start.22 = (bf16[256,2048]{1,0:T(8,128)(2,1)}, bf16[256,2048]{1,0:T(8,128)(2,1)S(1)}, u32[]{:S(2)}, u32[]{:S(2)}) collective-permute-start(bf16[256,2048]{1,0:T(8,128)(2,1)} %get-tuple-element.332.refs_4_), channel_id=1, source_target_pairs={{0,2},{1,3},{2,0},{3,1},{4,6},{5,7},{6,4},{7,5},{8,10},{9,11},{10,... | collective-permute-start | bytes 3145736 | tf_op jit(solution)/shard_map/ppermute | solution.py:348
  211.2 38.9 %collective-permute-start.24 = (bf16[256,2048]{1,0:T(8,128)(2,1)}, bf16[256,2048]{1,0:T(8,128)(2,1)S(1)}, u32[]{:S(2)}, u32[]{:S(2)}) collective-permute-start(bf16[256,2048]{1,0:T(8,128)(2,1)} %get-tuple-element.332.refs_4_), channel_id=1, source_target_pairs={{0,1},{1,0},{2,3},{3,2},{4,5},{5,4},{6,7},{7,6},{8,9},{9,8},{10,11... | collective-permute-start | bytes 3145736 | tf_op jit(solution)/shard_map/ppermute | solution.py:345
  211.3 38.0 %collective-permute-start.23 = (bf16[1,352,1024]{2,1,0:T(8,128)(2,1)S(1)}, bf16[1,352,1024]{2,1,0:T(8,128)(2,1)S(1)}, u32[]{:S(2)}, u32[]{:S(2)}) collective-permute-start(bf16[1,352,1024]{2,1,0:T(8,128)(2,1)S(1)} %slice.135), channel_id=1, source_target_pairs={{0,4},{1,5},{2,6},{3,7},{4,0},{5,1},{6,2},{7,3},{8,12},{9,13},{10,... | collective-permute-start | bytes 2162696 | tf_op jit(solution)/shard_map/ppermute | solution.py:351
  213.7 35.6 %collective-permute-start.25 = (bf16[1,352,1024]{2,1,0:T(8,128)(2,1)S(1)}, bf16[1,352,1024]{2,1,0:T(8,128)(2,1)S(1)}, u32[]{:S(2)}, u32[]{:S(2)}) collective-permute-start(bf16[1,352,1024]{2,1,0:T(8,128)(2,1)S(1)} %slice.135), channel_id=1, source_target_pairs={{0,16},{8,24},{16,0},{24,8},{1,17},{9,25},{17,1},{25,9},{2,18},{10... | collective-permute-start | bytes 2162696 | tf_op jit(solution)/shard_map/ppermute | solution.py:335
  271.7 35.8 %collective-permute-start.35 = (bf16[256,2048]{1,0:T(8,128)(2,1)}, bf16[256,2048]{1,0:T(8,128)(2,1)}, u32[]{:S(2)}, u32[]{:S(2)}) collective-permute-start(bf16[256,2048]{1,0:T(8,128)(2,1)} %collective-permute-done.7.refs_8_), channel_id=1, source_target_pairs={{0,1},{1,0},{2,3},{3,2},{4,5},{5,4},{6,7},{7,6},{8,9},{9,8},{10,11... | collective-permute-start | bytes 3145736 | tf_op jit(solution)/shard_map/ppermute | solution.py:345
  280.2 38.7 %all-to-all-start.1 = ((bf16[4,320,512]{2,1,0:T(8,128)(2,1)}), bf16[4,320,512]{2,1,0:T(8,128)(2,1)}, u32[]{:S(2)}, u32[]{:S(2)}) async-start(bf16[4,320,512]{2,1,0:T(8,128)(2,1)} %bitcast.99), calls=%async_computation.1 | async-start | bytes 2621440 | tf_op jit(solution)/shard_map/all_to_all | solution.py:1156
  350.8 34.2 %collective-permute-start.48 = (bf16[4,320,512]{2,1,0:T(8,128)(2,1)}, bf16[4,320,512]{2,1,0:T(8,128)(2,1)S(1)}, u32[]{:S(2)}, u32[]{:S(2)}) collective-permute-start(bf16[4,320,512]{2,1,0:T(8,128)(2,1)} %collective-permute-done.39.refs_2_), channel_id=1, source_target_pairs={{0,1},{1,0},{2,3},{3,2},{4,5},{5,4},{6,7},{7,6},{8,9},{9,8},{10,11... | collective-permute-start | bytes 3932168 | tf_op jit(solution)/shard_map/ppermute | solution.py:345
  444.9 62.1 %all-to-all-start.2 = ((bf16[8,256,256]{2,1,0:T(8,128)(2,1)}), bf16[8,256,256]{2,1,0:T(8,128)(2,1)S(1)}, u32[]{:S(2)}, u32[]{:S(2)}) async-start(bf16[8,256,256]{2,1,0:T(8,128)(2,1)} %get-tuple-element.457), calls=%async_computation.2 | async-start | bytes 2097152 | tf_op jit(solution)/shard_map/all_to_all | solution.py:1046
  449.7 55.4 %collective-permute-start.57 = (bf16[256,2048]{1,0:T(8,128)(2,1)}, bf16[256,2048]{1,0:T(8,128)(2,1)S(1)}, u32[]{:S(2)}, u32[]{:S(2)}) collective-permute-start(bf16[256,2048]{1,0:T(8,128)(2,1)} %add_convert_fusion.4), channel_id=1, source_target_pairs={{0,8},{8,0},{16,24},{24,16},{1,9},{9,1},{17,25},{25,17},{2,10},{10... | collective-permute-start | bytes 3145736 | tf_op jit(solution)/shard_map/ppermute | solution.py:332
  451.2 55.9 %collective-permute-start.58 = (bf16[256,2048]{1,0:T(8,128)(2,1)}, bf16[256,2048]{1,0:T(8,128)(2,1)S(1)}, u32[]{:S(2)}, u32[]{:S(2)}) collective-permute-start(bf16[256,2048]{1,0:T(8,128)(2,1)} %add_convert_fusion.3), channel_id=1, source_target_pairs={{0,2},{1,3},{2,0},{3,1},{4,6},{5,7},{6,4},{7,5},{8,10},{9,11},{10,... | collective-permute-start | bytes 3145736 | tf_op jit(solution)/shard_map/ppermute | solution.py:348
  467.5 37.6 %collective-permute-start.59 = (bf16[352,1024]{1,0:T(8,128)(2,1)}, bf16[352,1024]{1,0:T(8,128)(2,1)}, u32[]{:S(2)}, u32[]{:S(2)}) collective-permute-start(bf16[352,1024]{1,0:T(8,128)(2,1)} %add_convert_fusion.15), channel_id=1, source_target_pairs={{0,4},{1,5},{2,6},{3,7},{4,0},{5,1},{6,2},{7,3},{8,12},{9,13},{10,... | collective-permute-start | bytes 2162696 | tf_op jit(solution)/shard_map/ppermute | solution.py:351
  469.9 35.2 %collective-permute-start.60 = (bf16[352,1024]{1,0:T(8,128)(2,1)}, bf16[352,1024]{1,0:T(8,128)(2,1)}, u32[]{:S(2)}, u32[]{:S(2)}) collective-permute-start(bf16[352,1024]{1,0:T(8,128)(2,1)} %get-tuple-element.462), channel_id=1, source_target_pairs={{0,16},{8,24},{16,0},{24,8},{1,17},{9,25},{17,1},{25,9},{2,18},{10... | collective-permute-start | bytes 2162696 | tf_op jit(solution)/shard_map/ppermute | solution.py:335
  510.3 37.2 %collective-permute-start.66 = (bf16[4,256,512]{2,1,0:T(8,128)(2,1)}, bf16[4,256,512]{2,1,0:T(8,128)(2,1)}, u32[]{:S(2)}, u32[]{:S(2)}) collective-permute-start(bf16[4,256,512]{2,1,0:T(8,128)(2,1)} %get-tuple-element.504), channel_id=1, source_target_pairs={{0,8},{8,0},{16,24},{24,16},{1,9},{9,1},{17,25},{25,17},{2,10},{10... | collective-permute-start | bytes 3145736 | tf_op jit(solution)/shard_map/ppermute | solution.py:332
  511.8 35.7 %collective-permute-start.63 = (bf16[352,1024]{1,0:T(8,128)(2,1)}, bf16[352,1024]{1,0:T(8,128)(2,1)}, u32[]{:S(2)}, u32[]{:S(2)}) collective-permute-start(bf16[352,1024]{1,0:T(8,128)(2,1)} %add_convert_fusion.14), channel_id=1, source_target_pairs={{0,4},{1,5},{2,6},{3,7},{4,0},{5,1},{6,2},{7,3},{8,12},{9,13},{10,... | collective-permute-start | bytes 2162696 | tf_op jit(solution)/shard_map/ppermute | solution.py:351
  554.4 46.5 %all-to-all-start.3 = ((bf16[8,256,320]{1,2,0:T(8,128)(2,1)}), bf16[8,256,320]{1,2,0:T(8,128)(2,1)S(1)}, u32[]{:S(2)}, u32[]{:S(2)}) async-start(bf16[8,256,320]{1,2,0:T(8,128)(2,1)} %copy.24), calls=%async_computation.3 | async-start | bytes 2621440 | tf_op jit(solution)/shard_map/all_to_all | solution.py:1046
  560.3 40.6 %collective-permute-start.69 = (bf16[4,256,512]{2,1,0:T(8,128)(2,1)}, bf16[4,256,512]{2,1,0:T(8,128)(2,1)}, u32[]{:S(2)}, u32[]{:S(2)}) collective-permute-start(bf16[4,256,512]{2,1,0:T(8,128)(2,1)} %add_convert_fusion.2), channel_id=1, source_target_pairs={{0,16},{8,24},{16,0},{24,8},{1,17},{9,25},{17,1},{25,9},{2,18},{10... | collective-permute-start | bytes 3145736 | tf_op jit(solution)/shard_map/ppermute | solution.py:335
  561.2 39.6 %collective-permute-start.67 = (bf16[352,1024]{1,0:T(8,128)(2,1)}, bf16[352,1024]{1,0:T(8,128)(2,1)}, u32[]{:S(2)}, u32[]{:S(2)}) collective-permute-start(bf16[352,1024]{1,0:T(8,128)(2,1)} %get-tuple-element.523), channel_id=1, source_target_pairs={{0,16},{8,24},{16,0},{24,8},{1,17},{9,25},{17,1},{25,9},{2,18},{10... | collective-permute-start | bytes 2162696 | tf_op jit(solution)/shard_map/ppermute | solution.py:335
  (136 other events, 2217.9 us)

commit v6 on v5

--- a/solution.py
+++ b/solution.py
@@ -564,12 +564,12 @@
 
 def unmix_kernel(whole, places_ref, *refs):
     count = len(whole.pieces)
-    a_ref, b_ref, c_ref, middle_ref, grad_ref, gain_ref = refs[count : count + 6]
-    dmiddle_ref, dmixed_ref, part_ref, out_ref, weight_s, sems = refs[count + 6 :]
+    parts, (middle_ref, grad_ref, gain_ref) = refs[count : count + 4], refs[count + 4 : count + 7]
+    dmiddle_ref, dmixed_ref, part_ref, out_ref, weight_s, sems = refs[count + 7 :]
     copies = whole.fill(places_ref, refs[:count], weight_s, sems)
     middle = middle_ref[...]
     inv_two = inv_root_mean(middle)
-    dnormed = wide(a_ref[...]) + wide(b_ref[...]) + wide(c_ref[...])
+    dnormed = sum(wide(part[...]) for part in parts)
     scaled = middle * inv_two
     error = dnormed * gain_ref[...]
     dmiddle = wide(grad_ref[...]) + inv_two * (
@@ -1105,7 +1105,7 @@
     projected, normed, attended_wide, inverses, attended = attend(
         pieces, places, in_turned, keep_row, ends, heads_here
     )
-    attended, out_x, out_y, halves, unit_pair = tie(attended, out_x, out_y, halves, unit_pair)
+    attended, out_x, out_y, unit_pair = tie(attended, out_x, out_y, unit_pair)
     attended_here = swap(attended).reshape(wires.head, rows, out_rows)
     out_across = [wires.over_x(piece) for piece in out_y]
     by_zh_gu = [
@@ -1114,8 +1114,8 @@
     by_zh_guy = on_y(by_zh_gu)
     out_line_swap = shares(pieces[1::2])
     out_x_swap, out_y_swap = wires.over_core(out_x), [wires.over_core(piece) for piece in out_y]
-    attended_here, out_across, out_x_swap, out_y_swap, unit_pair, by_zh_gu, by_zh_guy, out_line_swap = tie(
-        attended_here, out_across, out_x_swap, out_y_swap, unit_pair, by_zh_gu, by_zh_guy, out_line_swap
+    attended_here, out_across, out_x_swap, out_y_swap, unit_pair, by_zh_gu, out_line_swap = tie(
+        attended_here, out_across, out_x_swap, out_y_swap, unit_pair, by_zh_gu, out_line_swap
     )
     out_across_swap = [wires.over_core(piece) for piece in out_across]
 
@@ -1135,8 +1135,8 @@
     by_zh_d = [wires.over_zh(unit_pair[2:], s) for s in range(1, wires.nzh)]
     by_y_d = [wires.over_y(unit_pair[2:], s) for s in across_y]
     two_swap = wires.over_core(normed_two)
-    two_x, two_z, by_zh_d, two_swap, by_y_d, unit_pair, out_grad = tie(
-        two_x, two_z, by_zh_d, two_swap, by_y_d, unit_pair, out_grad
+    two_x, two_z, by_zh_d, two_swap, by_y_d, unit_pair, out_grad, by_zh_guy = tie(
+        two_x, two_z, by_zh_d, two_swap, by_y_d, unit_pair, out_grad, by_zh_guy
     )
     two_corner = wires.over_x(two_z)
     by_zh_dy = on_y(by_zh_d)
@@ -1200,12 +1200,10 @@
         outs_xz, dnormed_x, dnormed_z, branch_x, branch_z, to_z, to_x, in_across, in_swaps
     )
     swap_x, swap_z = wires.over_core(dnormed_x[1]), wires.over_core(dnormed_z[1])
-    swap_x, swap_z, to_z = tie(swap_x, swap_z, to_z)
     sum_x = add(dnormed_x[0], swap_x)
     final_x = wires.over_x(sum_x)
     sum_z = add(dnormed_z[0], swap_z, to_z)
     final_z = wires.over_zl(sum_z)
-    sum_o = add(dnormed_o[0], swap_o)
 
     every = (outs_co, outs_xz, first, second)
 
@@ -1236,15 +1234,15 @@
     in_across_swap = [wires.over_core(piece) for piece in in_across]
     gate_parts = grad_of(every, 1)
     sum_x, sum_z = add(branch_x[0], swap_x, to_x), add(branch_z[0], swap_z)
-    final_x, final_z, gate_parts, sum_o, sum_x, sum_z, in_across_swap = tie(
-        final_x, final_z, gate_parts, sum_o, sum_x, sum_z, in_across_swap
+    final_x, final_z, gate_parts, sum_x, sum_z, in_across_swap = tie(
+        final_x, final_z, gate_parts, sum_x, sum_z, in_across_swap
     )
     gate_sent = [on_y_steps(part) for part in gate_parts[1:]]
     d_middle, d_mixed, ffn_gain_part, d_attended = unmix(
-        (sum_o, final_x, final_z), middle, out_grad, ffn_gain[None], out_whole, wires.head
-    )
-    every, d_attended, d_mixed, gate_parts, gate_sent, sum_x, sum_z = tie(
-        every, d_attended, d_mixed, gate_parts, gate_sent, sum_x, sum_z
+        (dnormed_o[0], swap_o, final_x, final_z), middle, out_grad, ffn_gain[None], out_whole, wires.head
+    )
+    every, d_attended, d_mixed, gate_parts, sum_x, sum_z = tie(
+        every, d_attended, d_mixed, gate_parts, sum_x, sum_z
     )
     d_attended = swap(d_attended).reshape(group_rows, out_rows)
     final_x, final_z = wires.over_x(sum_x), wires.over_zl(sum_z)
@@ -1259,9 +1257,6 @@
         d_attended, final_x, final_z, gate_back, gate_sent, up_parts, up_sent, out_own, out_sent, down_parts
     )
     up_totals = totals_of(up_parts[1:], up_sent)
-    up_totals, d_attended, out_sent, up_parts, down_parts = tie(
-        up_totals, d_attended, out_sent, up_parts, down_parts
-    )
     up_back = on_zh(up_totals)
     up_sent = on_y_steps(up_parts[0])
     down_sent = [on_y_steps(part) for part in down_parts[1:]]
@@ -1272,23 +1267,19 @@
     d_projected, up_back, up_sent, down_sent, out_first = tie(
         d_projected, up_back, up_sent, down_sent, out_first
     )
+    d_here = swap(d_projected)
     down_totals = totals_of(down_parts[1:], down_sent)
     out_total = [add(out_own[s], out_first[s - 1]) for s in across_y]
-    down_totals, out_total, d_projected, down_parts, in_line, in_x, in_y, in_across = tie(
-        down_totals, out_total, d_projected, down_parts, in_line, in_x, in_y, in_across
-    )
-    d_here = swap(d_projected)
     down_sent = on_y_steps(down_parts[0])
     out_last = wires.over_x(out_sent[0])
     swap_o = wires.over_core(branch_o[1])
-    out_y = [wires.over_y(total, s) for total, s in zip(out_total, across_y)]
     in_back, attn_gain_part = in_grad_parts(normed, d_projected, in_turned, attn_gain[None])
     firsts = [
         add(parts[0][0], *sent, *back)
         for parts, sent, back in ((gate_parts, gate_sent, gate_back), (up_parts, up_sent, up_back))
     ]
-    d_here, in_back, attn_gain_part, down_sent, out_last, out_y, firsts, down_totals, swap_o = tie(
-        d_here, in_back, attn_gain_part, down_sent, out_last, out_y, firsts, down_totals, swap_o
+    d_here, in_back, attn_gain_part, down_sent, out_last, out_total, firsts, down_totals, swap_o = tie(
+        d_here, in_back, attn_gain_part, down_sent, out_last, out_total, firsts, down_totals, swap_o
     )
     cut = packed_width // 2
     gains = jnp.concatenate([attn_gain_part, ffn_gain_part], axis=0)
@@ -1298,13 +1289,14 @@
         wires, in_pieces, wires.whole_places(range(wires.nz), packed_width, size), packed_width, size
     )
     down_back = on_zh(down_totals)
-    out_total = add(out_own[0], out_last, *out_y)
+    out_y = [wires.over_y(total, s) for total, s in zip(out_total, across_y)]
     in_x, in_y = wires.over_x(in_back[:cut]), [wires.over_y(in_back[cut:], s) for s in across_y]
     others = wires.over_x(jnp.stack([pick(total, 1 - wires.x, 2, 1) for total in firsts]))
     in_grad = last(d_here, in_whole, tokens, d_middle, attn_gain[None])
-    in_grad, out_total, in_x, in_y, others, down_sent, down_back = tie(
-        in_grad, out_total, in_x, in_y, others, down_sent, down_back
-    )
+    in_grad, out_y, in_x, in_y, others, down_sent, down_back, gains = tie(
+        in_grad, out_y, in_x, in_y, others, down_sent, down_back, gains
+    )
+    out_total = add(out_own[0], out_last, *out_y)
     out_turns = lax.all_to_all(out_total, "head", axis_index_groups=same_core, **turned)
     in_halves = (wires.sum_y(add(in_back[:cut], in_x)), wires.sum_x(add(in_back[cut:], *in_y)))
     totals = [*firsts, add(down_parts[0][0], *down_sent, *down_back)]

time: 709 us -> 671 us (0.946)
  waiting for transfers between devices: 287 us -> 254 us
    ppermute x5, waiting for transfers between devices: 58.7 us -> 34.3 us  [over_zh(): lax.ppermute(values, 'head', [(i, (i // 4 + shift) % self.nzh * 4 + i % 4...]
    ppermute x19, waiting for transfers between devices: 48.9 us -> 38.9 us  [over_y(): lax.ppermute(values, 'dp', [(i, (i // 2 + shift) % self.ny * 2 + i % 2) f...]
    ppermute x6, waiting for transfers between devices: 11.4 us -> 21.2 us  [over_zl(): return lax.ppermute(values, 'head', [(i, i ^ 2) for i in range(self.head)])]
    convert_element_type x20 -> x19, other arithmetic: 46.1 us -> 44.4 us  [low(): return values.astype(jnp.bfloat16)]
  transfers between devices with their start and end apart: 92 -> 92, of which waited for: 40 -> 39; matrix products, arithmetic and copies ran while one was open for 9% -> 11% of each run, Pallas kernels for 28% -> 30%
where the time goes in v6:
time: 671 us; the launch traced here: 663 us
  waiting for transfers between devices  254 us (38%)
  Pallas kernels  207 us (31%)
  starting transfers between devices  107 us (16%)
  other arithmetic  68.5 us (10%)
  local copies, waits for them, and re-layouts  24.3 us (4%)
    ppermute x19, waiting for transfers between devices, over_x(): return lax.ppermute(values, 'dp', [(i, i ^ 1) for i in range(self.dp)])  91.5 us
    pallas_call x4, Pallas kernels, with_units(): pl.pallas_call(functools.partial(kernel, units), grid_spec=pltpu.Prefetch...  72.5 us
    convert_element_type x19, other arithmetic, low(): return values.astype(jnp.bfloat16)  44.4 us
    ppermute x19, waiting for transfers between devices, over_y(): lax.ppermute(values, 'dp', [(i, (i // 2 + shift) % self.ny * 2 + i % 2) f...  38.9 us
    ppermute x5, waiting for transfers between devices, over_zh(): lax.ppermute(values, 'head', [(i, (i // 4 + shift) % self.nzh * 4 + i % 4...  34.3 us
    pallas_call x3, Pallas kernels, unit_grad(): pl.pallas_call(functools.partial(unit_grad_kernel, order, ny, nzh), grid_...  33.9 us
    pallas_call x3, Pallas kernels, with_whole(): pl.pallas_call(functools.partial(kernel, whole), grid_spec=pltpu.Prefetch...  31.9 us
    pallas_call x1, Pallas kernels, attend_back(): pl.pallas_call(functools.partial(attend_back_kernel, heads, rows), grid_s...  31.7 us
  transfers between devices with their start and end apart: 92, of which 39 were waited for; matrix products, arithmetic and copies ran while one was open for 11% of the time, Pallas kernels for 30%

profile of v6, /device:TPU:0, one launch (start us, length us, event | category | flops | bytes accessed | tf_op | source)
XLA Modules:
  0.0 663.1 jit_solution(15540897751043721803)
XLA Ops:
  15.5 23.0 %collective-permute-done.2 = bf16[3,352,512]{2,1,0:T(8,128)(2,1)S(1)} collective-permute-done((bf16[3,352,512]{2,1,0:T(8,128)(2,1)S(1)}, bf16[3,352,512]{2,1,0:T(8,128)(2,1)S(1)}, u32[]{:S(2)}, u32[]{:S(2)}) %collective-permute-start.2) | collective-permute-done | bytes 1081376 | tf_op jit(solution)/shard_map/ppermute | solution.py:332
  46.6 20.8 %collective-permute-done.7.refs_8_ = bf16[256,2048]{1,0:T(8,128)(2,1)} collective-permute-done((bf16[256,2048]{1,0:T(8,128)(2,1)}, bf16[256,2048]{1,0:T(8,128)(2,1)}, u32[]{:S(2)}, u32[]{:S(2)}) %collective-permute-start.7) | collective-permute-done | bytes 1048608 | tf_op jit(solution)/shard_map/ppermute | solution.py:332
  67.5 7.9 %collective-permute-done.6 = bf16[256,2560]{1,0:T(8,128)(2,1)} collective-permute-done((bf16[256,2560]{1,0:T(8,128)(2,1)}, bf16[256,2560]{1,0:T(8,128)(2,1)}, u32[]{:S(2)}, u32[]{:S(2)}) %collective-permute-start.6) | collective-permute-done | bytes 1310752 | tf_op jit(solution)/shard_map/ppermute | solution.py:378
  83.7 28.1 %collective-permute-done.9 = bf16[256,2560]{1,0:T(8,128)(2,1)S(1)} collective-permute-done((bf16[256,2560]{1,0:T(8,128)(2,1)S(1)}, bf16[256,2560]{1,0:T(8,128)(2,1)S(1)}, u32[]{:S(2)}, u32[]{:S(2)}) %collective-permute-start.9) | collective-permute-done | bytes 1310752 | tf_op jit(solution)/shard_map/ppermute | solution.py:387
  122.8 23.1 %shard_map.178 = (bf16[2048,320]{1,0:T(8,128)(2,1)}, bf16[2048,2048]{1,0:T(8,128)(2,1)}, f32[2048,256]{1,0:T(8,128)}, f32[2048,128]{1,0:T(8,128)}, bf16[2048,256]{1,0:T(8,128)(2,1)}) custom-call(s32[3]{0:T(128)} %bitcast.113, s32[8]{0:T(128)} %stack.205.at_ref, bf16[256,2560]{1,0:T(8,128)(2,1)} %copy-done.15, ...), custom_call_target="tpu_custom_call" | custom-call | flops 1 | bytes 1 | tf_op jit(solution)/shard_map/pallas_call | solution.py:134
  161.1 18.5 %collective-permute-done.15.refs_3_ = bf16[4,256,512]{2,1,0:T(8,128)(2,1)} collective-permute-done((bf16[4,256,512]{2,1,0:T(8,128)(2,1)}, bf16[4,256,512]{2,1,0:T(8,128)(2,1)}, u32[]{:S(2)}, u32[]{:S(2)}) %collective-permute-start.15) | collective-permute-done | bytes 1048608 | tf_op jit(solution)/shard_map/ppermute | solution.py:332
  184.0 8.8 %shard_map.179 = (f32[256,2048]{1,0:T(8,128)}, bf16[256,2048]{1,0:T(8,128)(2,1)}) custom-call(s32[12]{0:T(128)} %stack.195.places_ref, bf16[4,256,512]{2,1,0:T(8,128)(2,1)} %copy-done.9, bf16[4,256,512]{2,1,0:T(8,128)(2,1)} %copy-done.19, bf16[4,256,512]{2,1,0:T(8,128)(2,1)} %collective-permute-done.14.refs_2_, ...), custom_call_target="tpu_custom_call" | custom-call | flops 1 | bytes 1 | tf_op jit(solution)/shard_map/pallas_call | solution.py:537
  199.7 33.0 %collective-permute-done.22.refs_2_ = bf16[1,352,1024]{2,1,0:T(8,128)(2,1)S(1)} collective-permute-done((bf16[1,352,1024]{2,1,0:T(8,128)(2,1)S(1)}, bf16[1,352,1024]{2,1,0:T(8,128)(2,1)S(1)}, u32[]{:S(2)}, u32[]{:S(2)}) %collective-permute-start.22) | collective-permute-done | bytes 720928 | tf_op jit(solution)/shard_map/ppermute | solution.py:351
  239.7 16.2 %collective-permute-done.27.refs_3_ = bf16[1,352,1024]{2,1,0:T(8,128)(2,1)S(1)} collective-permute-done((bf16[1,352,1024]{2,1,0:T(8,128)(2,1)S(1)}, bf16[1,352,1024]{2,1,0:T(8,128)(2,1)S(1)}, u32[]{:S(2)}, u32[]{:S(2)}) %collective-permute-start.27) | collective-permute-done | bytes 720928 | tf_op jit(solution)/shard_map/ppermute | solution.py:335
  271.8 19.0 %shard_map.180 = (bf16[3,3,512,704]{3,2,1,0:T(8,128)(2,1)}, bf16[3,512,2048]{2,1,0:T(8,128)(2,1)}) custom-call(s32[2]{0:T(128)} %get-tuple-element.554.places_ref, bf16[2,352,1024]{2,1,0:T(8,128)(2,1)} %slice.137.refs_0_.refs_4_, bf16[2,352,1024]{2,1,0:T(8,128)(2,1)} %copy-done.5, bf16[2,352,1024]{2,1,0:T(8,128)(2,1)} %copy-done.2, ...), custom_call_target="tpu_custom_call" | custom-call | flops 1 | bytes 1 | tf_op jit(solution)/shard_map/pallas_call | solution.py:668
  292.2 10.0 %shard_map.181 = (bf16[1,3,512,704]{3,2,1,0:T(8,128)(2,1)}, bf16[1,512,2048]{2,1,0:T(8,128)(2,1)}) custom-call(s32[2]{0:T(128)} %get-tuple-element.554.places_ref, bf16[2,352,1024]{2,1,0:T(8,128)(2,1)} %slice.137.refs_0_.refs_4_, bf16[2,352,1024]{2,1,0:T(8,128)(2,1)} %copy-done.5, bf16[2,352,1024]{2,1,0:T(8,128)(2,1)} %copy-done.2, ...), custom_call_target="tpu_custom_call" | custom-call | flops 1 | bytes 1 | tf_op jit(solution)/shard_map/pallas_call | solution.py:668
  306.3 21.8 %shard_map.182 = (bf16[2,2,512,704]{3,2,1,0:T(8,128)(2,1)}, bf16[2,512,2048]{2,1,0:T(8,128)(2,1)}, bf16[256,2048]{1,0:T(8,128)(2,1)}, bf16[256,2048]{1,0:T(8,128...) custom-call(s32[2]{0:T(128)} %get-tuple-element.554.places_ref, ...), custom_call_target="tpu_custom_call" | custom-call | flops 1 | bytes 1 | tf_op jit(solution)/shard_map/pallas_call | solution.py:668
  347.6 21.7 %shard_map.183 = (bf16[2,2,512,704]{3,2,1,0:T(8,128)(2,1)}, bf16[2,512,2048]{2,1,0:T(8,128)(2,1)}, bf16[256,2048]{1,0:T(8,128)(2,1)}, bf16[256,2048]{1,0:T(8,128...) custom-call(s32[2]{0:T(128)} %get-tuple-element.554.places_ref, ...), custom_call_target="tpu_custom_call" | custom-call | flops 1 | bytes 1 | tf_op jit(solution)/shard_map/pallas_call | solution.py:668
  383.0 11.5 %shard_map.184 = (bf16[352,1024]{1,0:T(8,128)(2,1)}, bf16[352,1024]{1,0:T(8,128)(2,1)}, bf16[352,1024]{1,0:T(8,128)(2,1)}, bf16[352,1024]{1,0:T(8,128)(2,1)}) custom-call(s32[2]{0:T(128)} %get-tuple-element.555.places_ref, bf16[2,2,512,704]{3,2,1,0:T(8,128)(2,1)} %get-tuple-element.433.refs_0_, bf16[1,512,2048]{2,1,0:T(8,128)(2,1)} %get-tuple-element.434.refs_1_, ...), custom_call_target="tpu_custom_call" | custom-call | flops 1 | bytes 1 | tf_op jit(solution)/shard_map/pallas_call | solution.py:904
  407.9 10.8 %shard_map.185 = (f32[256,2048]{1,0:T(8,128)}, bf16[256,2048]{1,0:T(8,128)(2,1)}, f32[1,2048]{1,0:T(1,128)}, bf16[8,256,256]{2,1,0:T(8,128)(2,1)}) custom-call(s32[12]{0:T(128)} %stack.195.places_ref, bf16[4,256,512]{2,1,0:T(8,128)(2,1)} %copy-done.9, bf16[4,256,512]{2,1,0:T(8,128)(2,1)} %copy-done.19, bf16[4,256,512]{2,1,0:T(8,128)(2,1)} %collective-permute-done.14.refs_2_, ...), custom_call_target="tpu_custom_call" | custom-call | flops 1 | bytes 1 | tf_op jit(solution)/shard_map/pallas_call | solution.py:537
  427.2 11.2 %shard_map.186 = (bf16[352,1024]{1,0:T(8,128)(2,1)}, bf16[352,1024]{1,0:T(8,128)(2,1)}, bf16[352,1024]{1,0:T(8,128)(2,1)}, bf16[352,1024]{1,0:T(8,128)(2,1)}) custom-call(s32[2]{0:T(128)} %get-tuple-element.555.places_ref, bf16[2,2,512,704]{3,2,1,0:T(8,128)(2,1)} %get-tuple-element.433.refs_0_, bf16[1,512,2048]{2,1,0:T(8,128)(2,1)} %get-tuple-element.434.refs_1_, ...), custom_call_target="tpu_custom_call" | custom-call | flops 1 | bytes 1 | tf_op jit(solution)/shard_map/pallas_call | solution.py:904
  449.9 11.1 %shard_map.188 = (bf16[352,1024]{1,0:T(8,128)(2,1)}, bf16[352,1024]{1,0:T(8,128)(2,1)}, bf16[352,1024]{1,0:T(8,128)(2,1)}, bf16[352,1024]{1,0:T(8,128)(2,1)}) custom-call(s32[2]{0:T(128)} %get-tuple-element.555.places_ref, bf16[1,3,512,704]{3,2,1,0:T(8,128)(2,1)} %get-tuple-element.447.refs_10_.refs_0_, bf16[2,512,2048]{2,1,0:T(8,128)(2,1)} %get-tuple-element.448.refs_1_, ...), custom_call_target="tpu_custom_call" | custom-call | flops 1 | bytes 1 | tf_op jit(solution)/shard_map/pallas_call | solution.py:904
  473.3 8.1 %collective-permute-done.57 = bf16[256,2048]{1,0:T(8,128)(2,1)S(1)} collective-permute-done((bf16[256,2048]{1,0:T(8,128)(2,1)}, bf16[256,2048]{1,0:T(8,128)(2,1)S(1)}, u32[]{:S(2)}, u32[]{:S(2)}) %collective-permute-start.57) | collective-permute-done | bytes 1048608 | tf_op jit(solution)/shard_map/ppermute | solution.py:348
  487.8 31.7 %shard_map.189.grad_ref = bf16[8,256,320]{2,1,0:T(8,128)(2,1)} custom-call(s32[3]{0:T(128)} %bitcast.114, bf16[2048,320]{1,0:T(8,128)(2,1)} %get-tuple-element.456.projected_ref, f32[1,2048]{1,0:T(1,128)} %bitcast.108, f32[2048,256]{1,0:T(8,128)} %get-tuple-element.457.y_ref, f32[2048,128]{1,0:T(8,128)} %get-tuple-element.458.inv_ref, ...), custom_call_target="tpu_custom_call" | custom-call | flops 1 | bytes 1 | tf_op jit(solution)/shard_map/pallas_call | solution.py:260
  534.8 7.7 %shard_map.190 = (bf16[320,2048]{1,0:T(8,128)(2,1)}, f32[1,2048]{1,0:T(1,128)}) custom-call(bf16[2048,2048]{1,0:T(8,128)(2,1)} %get-tuple-element.466.normed_ref, bf16[8,256,320]{2,1,0:T(8,128)(2,1)} %shard_map.189.grad_ref, bf16[320,2048]{1,0:T(8,128)(2,1)} %bitcast.98, f32[1,2048]{1,0:T(1,128)} %bitcast.105), custom_call_target="tpu_custom_call" | custom-call | flops 1 | bytes 1 | tf_op jit(solution)/shard_map/pallas_call | solution.py:993
  567.3 12.2 %shard_map.191 = f32[256,2048]{1,0:T(8,128)} custom-call(s32[12]{0:T(128)} %stack.228.places_ref, bf16[4,320,512]{2,1,0:T(8,128)(2,1)} %all-to-all-done.1.refs_0_, bf16[4,320,512]{2,1,0:T(8,128)(2,1)} %collective-permute-done.38.refs_1_, bf16[4,320,512]{2,1,0:T(8,128)(2,1)} %collective-permute-done.39.refs_2_, bf16[4,320,512]{2,1,0:T(8,128)(2,1)} %copy-done.34, ...), custom_call_target="tpu_custom_call" | custom-call | flops 1 | bytes 1 | tf_op jit(solution)/shard_map/pallas_call | solution.py:537
  583.7 8.8 %collective-permute-done.71 = bf16[160,2048]{1,0:T(8,128)(2,1)} collective-permute-done((bf16[160,2048]{1,0:T(8,128)(2,1)}, bf16[160,2048]{1,0:T(8,128)(2,1)}, u32[]{:S(2)}, u32[]{:S(2)}) %collective-permute-start.71) | collective-permute-done | bytes 655392 | tf_op jit(solution)/shard_map/ppermute | solution.py:332
  592.5 8.2 %collective-permute-done.72 = bf16[160,2048]{1,0:T(8,128)(2,1)} collective-permute-done((bf16[160,2048]{1,0:T(8,128)(2,1)}, bf16[160,2048]{1,0:T(8,128)(2,1)}, u32[]{:S(2)}, u32[]{:S(2)}) %collective-permute-start.72) | collective-permute-done | bytes 655392 | tf_op jit(solution)/shard_map/ppermute | solution.py:335
  627.3 9.1 %all-to-all-done.4 = bf16[4,256,512]{2,1,0:T(8,128)(2,1)S(1)} async-done(((bf16[4,256,512]{2,1,0:T(8,128)(2,1)}), bf16[4,256,512]{2,1,0:T(8,128)(2,1)S(1)}, u32[]{:S(2)}, u32[]{:S(2)}) %all-to-all-start.4) | async-done | bytes 1048608 | tf_op jit(solution)/shard_map/all_to_all | solution.py:1300
  (379 shorter events, 278.6 us)
Async XLA Ops:
  2.9 35.6 %collective-permute-start = (bf16[256,2560]{1,0:T(8,128)(2,1)S(1)}, bf16[256,2560]{1,0:T(8,128)(2,1)}, u32[]{:S(2)}, u32[]{:S(2)}) collective-permute-start(bf16[256,2560]{1,0:T(8,128)(2,1)S(1)} %pad_maximum_fusion.2.refs_0_), channel_id=1, source_target_pairs={{0,2},{1,3},{2,4},{3,5},{4,6},{5,7},{8,10},{9,11},{10,12},{11,13},... | collective-permute-start | bytes 3932168 | tf_op jit(solution)/shard_map/ppermute | solution.py:373
  75.4 36.4 %collective-permute-start.10 = (bf16[2,352,1024]{2,1,0:T(8,128)(2,1)S(1)}, bf16[2,352,1024]{2,1,0:T(8,128)(2,1)S(1)}, u32[]{:S(2)}, u32[]{:S(2)}) collective-permute-start(bf16[2,352,1024]{2,1,0:T(8,128)(2,1)S(1)} %slice.125), channel_id=1, source_target_pairs={{0,16},{8,24},{16,0},{24,8},{1,17},{9,25},{17,1},{25,9},{2,18},{10... | collective-permute-start | bytes 4325384 | tf_op jit(solution)/shard_map/ppermute | solution.py:335
  77.0 34.8 %collective-permute-start.11 = (bf16[2,352,1024]{2,1,0:T(8,128)(2,1)S(1)}, bf16[2,352,1024]{2,1,0:T(8,128)(2,1)S(1)}, u32[]{:S(2)}, u32[]{:S(2)}) collective-permute-start(bf16[2,352,1024]{2,1,0:T(8,128)(2,1)S(1)} %slice.125), channel_id=1, source_target_pairs={{0,4},{1,5},{6,2},{7,3},{8,12},{9,13},{14,10},{15,11},{16,20},{17,... | collective-permute-start | bytes 4325384 | tf_op jit(solution)/shard_map/ppermute | solution.py:361
  119.6 37.3 %collective-permute-start.18 = (bf16[2,352,1024]{2,1,0:T(8,128)(2,1)S(1)}, bf16[2,352,1024]{2,1,0:T(8,128)(2,1)}, u32[]{:S(2)}, u32[]{:S(2)}) collective-permute-start(bf16[2,352,1024]{2,1,0:T(8,128)(2,1)S(1)} %slice.130), channel_id=1, source_target_pairs={{2,6},{3,7},{4,0},{5,1},{10,14},{11,15},{12,8},{13,9},{18,22},{19,... | collective-permute-start | bytes 4325384 | tf_op jit(solution)/shard_map/ppermute | solution.py:361
  145.9 34.2 %all-to-all-start = ((bf16[8,256,256]{2,1,0:T(8,128)(2,1)}), bf16[8,256,256]{2,1,0:T(8,128)(2,1)S(1)}, u32[]{:S(2)}, u32[]{:S(2)}) async-start(bf16[8,256,256]{2,1,0:T(8,128)(2,1)} %bitcast.101), calls=%async_computation | async-start | bytes 2097152 | tf_op jit(solution)/shard_map/all_to_all | solution.py:1046
  158.4 39.8 %collective-permute-start.25 = (bf16[2,352,1024]{2,1,0:T(8,128)(2,1)S(1)}, bf16[2,352,1024]{2,1,0:T(8,128)(2,1)}, u32[]{:S(2)}, u32[]{:S(2)}) collective-permute-start(bf16[2,352,1024]{2,1,0:T(8,128)(2,1)S(1)} %broadcast_select_fusion.refs_2_.refs_6_), channel_id=1, source_target_pairs={{0,16},{8,24},{16,0},{24,8},{1,17},{9,25},{17,1},{25,9},{2,18},{10... | collective-permute-start | bytes 4325384 | tf_op jit(solution)/shard_map/ppermute | solution.py:335
  192.8 39.9 %collective-permute-start.20 = (bf16[256,2048]{1,0:T(8,128)(2,1)}, bf16[256,2048]{1,0:T(8,128)(2,1)S(1)}, u32[]{:S(2)}, u32[]{:S(2)}) collective-permute-start(bf16[256,2048]{1,0:T(8,128)(2,1)} %get-tuple-element.307.refs_4_), channel_id=1, source_target_pairs={{0,8},{8,0},{16,24},{24,16},{1,9},{9,1},{17,25},{25,17},{2,10},{10... | collective-permute-start | bytes 3145736 | tf_op jit(solution)/shard_map/ppermute | solution.py:332
  193.4 40.6 %collective-permute-start.21 = (bf16[256,2048]{1,0:T(8,128)(2,1)}, bf16[256,2048]{1,0:T(8,128)(2,1)S(1)}, u32[]{:S(2)}, u32[]{:S(2)}) collective-permute-start(bf16[256,2048]{1,0:T(8,128)(2,1)} %get-tuple-element.307.refs_4_), channel_id=1, source_target_pairs={{0,2},{1,3},{2,0},{3,1},{4,6},{5,7},{6,4},{7,5},{8,10},{9,11},{10,... | collective-permute-start | bytes 3145736 | tf_op jit(solution)/shard_map/ppermute | solution.py:348
  194.5 39.4 %collective-permute-start.23 = (bf16[256,2048]{1,0:T(8,128)(2,1)}, bf16[256,2048]{1,0:T(8,128)(2,1)S(1)}, u32[]{:S(2)}, u32[]{:S(2)}) collective-permute-start(bf16[256,2048]{1,0:T(8,128)(2,1)} %get-tuple-element.307.refs_4_), channel_id=1, source_target_pairs={{0,1},{1,0},{2,3},{3,2},{4,5},{5,4},{6,7},{7,6},{8,9},{9,8},{10,11... | collective-permute-start | bytes 3145736 | tf_op jit(solution)/shard_map/ppermute | solution.py:345
  195.7 36.9 %collective-permute-start.22 = (bf16[1,352,1024]{2,1,0:T(8,128)(2,1)S(1)}, bf16[1,352,1024]{2,1,0:T(8,128)(2,1)S(1)}, u32[]{:S(2)}, u32[]{:S(2)}) collective-permute-start(bf16[1,352,1024]{2,1,0:T(8,128)(2,1)S(1)} %slice.135), channel_id=1, source_target_pairs={{0,4},{1,5},{2,6},{3,7},{4,0},{5,1},{6,2},{7,3},{8,12},{9,13},{10,... | collective-permute-start | bytes 2162696 | tf_op jit(solution)/shard_map/ppermute | solution.py:351
  198.1 34.5 %collective-permute-start.24 = (bf16[1,352,1024]{2,1,0:T(8,128)(2,1)S(1)}, bf16[1,352,1024]{2,1,0:T(8,128)(2,1)S(1)}, u32[]{:S(2)}, u32[]{:S(2)}) collective-permute-start(bf16[1,352,1024]{2,1,0:T(8,128)(2,1)S(1)} %slice.135), channel_id=1, source_target_pairs={{0,16},{8,24},{16,0},{24,8},{1,17},{9,25},{17,1},{25,9},{2,18},{10... | collective-permute-start | bytes 2162696 | tf_op jit(solution)/shard_map/ppermute | solution.py:335
  255.9 34.9 %collective-permute-start.35 = (bf16[256,2048]{1,0:T(8,128)(2,1)}, bf16[256,2048]{1,0:T(8,128)(2,1)}, u32[]{:S(2)}, u32[]{:S(2)}) collective-permute-start(bf16[256,2048]{1,0:T(8,128)(2,1)} %collective-permute-done.7.refs_8_), channel_id=1, source_target_pairs={{0,1},{1,0},{2,3},{3,2},{4,5},{5,4},{6,7},{7,6},{8,9},{9,8},{10,11... | collective-permute-start | bytes 3145736 | tf_op jit(solution)/shard_map/ppermute | solution.py:345
  263.5 38.7 %all-to-all-start.1 = ((bf16[4,320,512]{2,1,0:T(8,128)(2,1)}), bf16[4,320,512]{2,1,0:T(8,128)(2,1)}, u32[]{:S(2)}, u32[]{:S(2)}) async-start(bf16[4,320,512]{2,1,0:T(8,128)(2,1)} %bitcast.99), calls=%async_computation.1 | async-start | bytes 2621440 | tf_op jit(solution)/shard_map/all_to_all | solution.py:1156
  418.7 62.6 %all-to-all-start.2 = ((bf16[8,256,256]{2,1,0:T(8,128)(2,1)}), bf16[8,256,256]{2,1,0:T(8,128)(2,1)S(1)}, u32[]{:S(2)}, u32[]{:S(2)}) async-start(bf16[8,256,256]{2,1,0:T(8,128)(2,1)} %get-tuple-element.428), calls=%async_computation.2 | async-start | bytes 2097152 | tf_op jit(solution)/shard_map/all_to_all | solution.py:1046
  425.0 48.3 %collective-permute-start.56 = (bf16[256,2048]{1,0:T(8,128)(2,1)}, bf16[256,2048]{1,0:T(8,128)(2,1)S(1)}, u32[]{:S(2)}, u32[]{:S(2)}) collective-permute-start(bf16[256,2048]{1,0:T(8,128)(2,1)} %add_convert_fusion.4), channel_id=1, source_target_pairs={{0,8},{8,0},{16,24},{24,16},{1,9},{9,1},{17,25},{25,17},{2,10},{10... | collective-permute-start | bytes 3145736 | tf_op jit(solution)/shard_map/ppermute | solution.py:332
  425.5 55.8 %collective-permute-start.57 = (bf16[256,2048]{1,0:T(8,128)(2,1)}, bf16[256,2048]{1,0:T(8,128)(2,1)S(1)}, u32[]{:S(2)}, u32[]{:S(2)}) collective-permute-start(bf16[256,2048]{1,0:T(8,128)(2,1)} %add_convert_fusion.3), channel_id=1, source_target_pairs={{0,2},{1,3},{2,0},{3,1},{4,6},{5,7},{6,4},{7,5},{8,10},{9,11},{10,... | collective-permute-start | bytes 3145736 | tf_op jit(solution)/shard_map/ppermute | solution.py:348
  446.7 34.6 %collective-permute-start.59 = (bf16[352,1024]{1,0:T(8,128)(2,1)}, bf16[352,1024]{1,0:T(8,128)(2,1)}, u32[]{:S(2)}, u32[]{:S(2)}) collective-permute-start(bf16[352,1024]{1,0:T(8,128)(2,1)} %add_convert_fusion.14), channel_id=1, source_target_pairs={{0,4},{1,5},{2,6},{3,7},{4,0},{5,1},{6,2},{7,3},{8,12},{9,13},{10,... | collective-permute-start | bytes 2162696 | tf_op jit(solution)/shard_map/ppermute | solution.py:351
  481.3 38.2 %collective-permute-start.66 = (bf16[4,256,512]{2,1,0:T(8,128)(2,1)}, bf16[4,256,512]{2,1,0:T(8,128)(2,1)}, u32[]{:S(2)}, u32[]{:S(2)}) collective-permute-start(bf16[4,256,512]{2,1,0:T(8,128)(2,1)} %get-tuple-element.464), channel_id=1, source_target_pairs={{0,8},{8,0},{16,24},{24,16},{1,9},{9,1},{17,25},{25,17},{2,10},{10... | collective-permute-start | bytes 3145736 | tf_op jit(solution)/shard_map/ppermute | solution.py:332
  484.6 35.0 %collective-permute-start.63 = (bf16[352,1024]{1,0:T(8,128)(2,1)}, bf16[352,1024]{1,0:T(8,128)(2,1)}, u32[]{:S(2)}, u32[]{:S(2)}) collective-permute-start(bf16[352,1024]{1,0:T(8,128)(2,1)} %add_convert_fusion.13), channel_id=1, source_target_pairs={{0,4},{1,5},{2,6},{3,7},{4,0},{5,1},{6,2},{7,3},{8,12},{9,13},{10,... | collective-permute-start | bytes 2162696 | tf_op jit(solution)/shard_map/ppermute | solution.py:351
  522.3 37.1 %all-to-all-start.3 = ((bf16[8,256,320]{1,2,0:T(8,128)(2,1)}), bf16[8,256,320]{1,2,0:T(8,128)(2,1)S(1)}, u32[]{:S(2)}, u32[]{:S(2)}) async-start(bf16[8,256,320]{1,2,0:T(8,128)(2,1)} %copy.24), calls=%async_computation.3 | async-start | bytes 2621440 | tf_op jit(solution)/shard_map/all_to_all | solution.py:1046
  560.4 40.3 %collective-permute-start.73 = (bf16[2,352,512]{2,1,0:T(8,128)(2,1)}, bf16[2,352,512]{2,1,0:T(8,128)(2,1)S(1)}, u32[]{:S(2)}, u32[]{:S(2)}) collective-permute-start(bf16[2,352,512]{2,1,0:T(8,128)(2,1)} %pad_maximum_fusion.6), channel_id=1, source_target_pairs={{0,8},{8,0},{16,24},{24,16},{1,9},{9,1},{17,25},{25,17},{2,10},{10... | collective-permute-start | bytes 2162696 | tf_op jit(solution)/shard_map/ppermute | solution.py:332
  561.9 39.6 %collective-permute-start.70 = (bf16[4,256,512]{2,1,0:T(8,128)(2,1)}, bf16[4,256,512]{2,1,0:T(8,128)(2,1)}, u32[]{:S(2)}, u32[]{:S(2)}) collective-permute-start(bf16[4,256,512]{2,1,0:T(8,128)(2,1)} %add_convert_fusion.2), channel_id=1, source_target_pairs={{0,16},{8,24},{16,0},{24,8},{1,17},{9,25},{17,1},{25,9},{2,18},{10... | collective-permute-start | bytes 3145736 | tf_op jit(solution)/shard_map/ppermute | solution.py:335
  564.7 36.0 %collective-permute-start.72 = (bf16[160,2048]{1,0:T(8,128)(2,1)}, bf16[160,2048]{1,0:T(8,128)(2,1)}, u32[]{:S(2)}, u32[]{:S(2)}) collective-permute-start(bf16[160,2048]{1,0:T(8,128)(2,1)} %get-tuple-element.536), channel_id=1, source_target_pairs={{0,16},{8,24},{16,0},{24,8},{1,17},{9,25},{17,1},{25,9},{2,18},{10... | collective-permute-start | bytes 1966088 | tf_op jit(solution)/shard_map/ppermute | solution.py:335
  565.7 35.0 %collective-permute-start.74 = (bf16[352,1024]{1,0:T(8,128)(2,1)}, bf16[352,1024]{1,0:T(8,128)(2,1)}, u32[]{:S(2)}, u32[]{:S(2)}) collective-permute-start(bf16[352,1024]{1,0:T(8,128)(2,1)} %add_convert_fusion.10), channel_id=1, source_target_pairs={{0,4},{1,5},{2,6},{3,7},{4,0},{5,1},{6,2},{7,3},{8,12},{9,13},{10,... | collective-permute-start | bytes 2162696 | tf_op jit(solution)/shard_map/ppermute | solution.py:351
  (132 other events, 2180.8 us)

commit v7 on v6

--- a/solution.py
+++ b/solution.py
@@ -1272,6 +1272,7 @@
     out_total = [add(out_own[s], out_first[s - 1]) for s in across_y]
     down_sent = on_y_steps(down_parts[0])
     out_last = wires.over_x(out_sent[0])
+    out_y = [wires.over_y(total, s) for total, s in zip(out_total, across_y)]
     swap_o = wires.over_core(branch_o[1])
     in_back, attn_gain_part = in_grad_parts(normed, d_projected, in_turned, attn_gain[None])
     firsts = [
@@ -1289,7 +1290,6 @@
         wires, in_pieces, wires.whole_places(range(wires.nz), packed_width, size), packed_width, size
     )
     down_back = on_zh(down_totals)
-    out_y = [wires.over_y(total, s) for total, s in zip(out_total, across_y)]
     in_x, in_y = wires.over_x(in_back[:cut]), [wires.over_y(in_back[cut:], s) for s in across_y]
     others = wires.over_x(jnp.stack([pick(total, 1 - wires.x, 2, 1) for total in firsts]))
     in_grad = last(d_here, in_whole, tokens, d_middle, attn_gain[None])

time: 671 us -> 668 us (level)
    ppermute x19, waiting for transfers between devices: 38.9 us -> 31.2 us  [over_y(): lax.ppermute(values, 'dp', [(i, (i // 2 + shift) % self.ny * 2 + i % 2) f...]
where the time goes in v7:
time: 668 us; the launch traced here: 661 us
  waiting for transfers between devices  253 us (38%)
  Pallas kernels  208 us (31%)
  starting transfers between devices  106 us (16%)
  other arithmetic  68 us (10%)
  local copies, waits for them, and re-layouts  24.4 us (4%)
    ppermute x19, waiting for transfers between devices, over_x(): return lax.ppermute(values, 'dp', [(i, i ^ 1) for i in range(self.dp)])  92.4 us
    pallas_call x4, Pallas kernels, with_units(): pl.pallas_call(functools.partial(kernel, units), grid_spec=pltpu.Prefetch...  72.5 us
    convert_element_type x19, other arithmetic, low(): return values.astype(jnp.bfloat16)  43.8 us
    ppermute x5, waiting for transfers between devices, over_zh(): lax.ppermute(values, 'head', [(i, (i // 4 + shift) % self.nzh * 4 + i % 4...  39.2 us
    pallas_call x3, Pallas kernels, unit_grad(): pl.pallas_call(functools.partial(unit_grad_kernel, order, ny, nzh), grid_...  34 us
    pallas_call x3, Pallas kernels, with_whole(): pl.pallas_call(functools.partial(kernel, whole), grid_spec=pltpu.Prefetch...  31.9 us
    pallas_call x1, Pallas kernels, attend_back(): pl.pallas_call(functools.partial(attend_back_kernel, heads, rows), grid_s...  31.7 us
    ppermute x19, waiting for transfers between devices, over_y(): lax.ppermute(values, 'dp', [(i, (i // 2 + shift) % self.ny * 2 + i % 2) f...  31.2 us
  transfers between devices with their start and end apart: 92, of which 39 were waited for; matrix products, arithmetic and copies ran while one was open for 11% of the time, Pallas kernels for 30%

profile of v7, /device:TPU:0, one launch (start us, length us, event | category | flops | bytes accessed | tf_op | source)
XLA Modules:
  0.0 660.7 jit_solution(18268109095866070999)
XLA Ops:
  15.5 23.0 %collective-permute-done.2 = bf16[3,352,512]{2,1,0:T(8,128)(2,1)S(1)} collective-permute-done((bf16[3,352,512]{2,1,0:T(8,128)(2,1)S(1)}, bf16[3,352,512]{2,1,0:T(8,128)(2,1)S(1)}, u32[]{:S(2)}, u32[]{:S(2)}) %collective-permute-start.2) | collective-permute-done | bytes 1081376 | tf_op jit(solution)/shard_map/ppermute | solution.py:332
  46.6 20.8 %collective-permute-done.7.refs_8_ = bf16[256,2048]{1,0:T(8,128)(2,1)} collective-permute-done((bf16[256,2048]{1,0:T(8,128)(2,1)}, bf16[256,2048]{1,0:T(8,128)(2,1)}, u32[]{:S(2)}, u32[]{:S(2)}) %collective-permute-start.7) | collective-permute-done | bytes 1048608 | tf_op jit(solution)/shard_map/ppermute | solution.py:332
  67.4 7.9 %collective-permute-done.6 = bf16[256,2560]{1,0:T(8,128)(2,1)} collective-permute-done((bf16[256,2560]{1,0:T(8,128)(2,1)}, bf16[256,2560]{1,0:T(8,128)(2,1)}, u32[]{:S(2)}, u32[]{:S(2)}) %collective-permute-start.6) | collective-permute-done | bytes 1310752 | tf_op jit(solution)/shard_map/ppermute | solution.py:378
  83.7 28.1 %collective-permute-done.9 = bf16[256,2560]{1,0:T(8,128)(2,1)S(1)} collective-permute-done((bf16[256,2560]{1,0:T(8,128)(2,1)S(1)}, bf16[256,2560]{1,0:T(8,128)(2,1)S(1)}, u32[]{:S(2)}, u32[]{:S(2)}) %collective-permute-start.9) | collective-permute-done | bytes 1310752 | tf_op jit(solution)/shard_map/ppermute | solution.py:387
  123.0 23.1 %shard_map.178 = (bf16[2048,320]{1,0:T(8,128)(2,1)}, bf16[2048,2048]{1,0:T(8,128)(2,1)}, f32[2048,256]{1,0:T(8,128)}, f32[2048,128]{1,0:T(8,128)}, bf16[2048,256]{1,0:T(8,128)(2,1)}) custom-call(s32[3]{0:T(128)} %bitcast.113, s32[8]{0:T(128)} %stack.205.at_ref, bf16[256,2560]{1,0:T(8,128)(2,1)} %copy-done.15, ...), custom_call_target="tpu_custom_call" | custom-call | flops 1 | bytes 1 | tf_op jit(solution)/shard_map/pallas_call | solution.py:134
  146.1 7.6 %all-to-all-start = ((bf16[8,256,256]{2,1,0:T(8,128)(2,1)}), bf16[8,256,256]{2,1,0:T(8,128)(2,1)S(1)}, u32[]{:S(2)}, u32[]{:S(2)}) async-start(bf16[8,256,256]{2,1,0:T(8,128)(2,1)} %bitcast.101), calls=%async_computation | async-start | bytes 2097152 | tf_op jit(solution)/shard_map/all_to_all | solution.py:1046
  161.2 18.5 %collective-permute-done.15.refs_3_ = bf16[4,256,512]{2,1,0:T(8,128)(2,1)} collective-permute-done((bf16[4,256,512]{2,1,0:T(8,128)(2,1)}, bf16[4,256,512]{2,1,0:T(8,128)(2,1)}, u32[]{:S(2)}, u32[]{:S(2)}) %collective-permute-start.15) | collective-permute-done | bytes 1048608 | tf_op jit(solution)/shard_map/ppermute | solution.py:332
  184.1 8.8 %shard_map.179 = (f32[256,2048]{1,0:T(8,128)}, bf16[256,2048]{1,0:T(8,128)(2,1)}) custom-call(s32[12]{0:T(128)} %stack.195.places_ref, bf16[4,256,512]{2,1,0:T(8,128)(2,1)} %copy-done.9, bf16[4,256,512]{2,1,0:T(8,128)(2,1)} %copy-done.19, bf16[4,256,512]{2,1,0:T(8,128)(2,1)} %collective-permute-done.14.refs_2_, ...), custom_call_target="tpu_custom_call" | custom-call | flops 1 | bytes 1 | tf_op jit(solution)/shard_map/pallas_call | solution.py:537
  199.8 33.0 %collective-permute-done.22.refs_2_ = bf16[1,352,1024]{2,1,0:T(8,128)(2,1)S(1)} collective-permute-done((bf16[1,352,1024]{2,1,0:T(8,128)(2,1)S(1)}, bf16[1,352,1024]{2,1,0:T(8,128)(2,1)S(1)}, u32[]{:S(2)}, u32[]{:S(2)}) %collective-permute-start.22) | collective-permute-done | bytes 720928 | tf_op jit(solution)/shard_map/ppermute | solution.py:351
  239.8 16.2 %collective-permute-done.27.refs_3_ = bf16[1,352,1024]{2,1,0:T(8,128)(2,1)S(1)} collective-permute-done((bf16[1,352,1024]{2,1,0:T(8,128)(2,1)S(1)}, bf16[1,352,1024]{2,1,0:T(8,128)(2,1)S(1)}, u32[]{:S(2)}, u32[]{:S(2)}) %collective-permute-start.27) | collective-permute-done | bytes 720928 | tf_op jit(solution)/shard_map/ppermute | solution.py:335
  272.0 19.0 %shard_map.180 = (bf16[3,3,512,704]{3,2,1,0:T(8,128)(2,1)}, bf16[3,512,2048]{2,1,0:T(8,128)(2,1)}) custom-call(s32[2]{0:T(128)} %get-tuple-element.552.places_ref, bf16[2,352,1024]{2,1,0:T(8,128)(2,1)} %slice.137.refs_0_.refs_4_, bf16[2,352,1024]{2,1,0:T(8,128)(2,1)} %copy-done.5, bf16[2,352,1024]{2,1,0:T(8,128)(2,1)} %copy-done.2, ...), custom_call_target="tpu_custom_call" | custom-call | flops 1 | bytes 1 | tf_op jit(solution)/shard_map/pallas_call | solution.py:668
  292.4 10.0 %shard_map.181 = (bf16[1,3,512,704]{3,2,1,0:T(8,128)(2,1)}, bf16[1,512,2048]{2,1,0:T(8,128)(2,1)}) custom-call(s32[2]{0:T(128)} %get-tuple-element.552.places_ref, bf16[2,352,1024]{2,1,0:T(8,128)(2,1)} %slice.137.refs_0_.refs_4_, bf16[2,352,1024]{2,1,0:T(8,128)(2,1)} %copy-done.5, bf16[2,352,1024]{2,1,0:T(8,128)(2,1)} %copy-done.2, ...), custom_call_target="tpu_custom_call" | custom-call | flops 1 | bytes 1 | tf_op jit(solution)/shard_map/pallas_call | solution.py:668
  306.5 21.8 %shard_map.182 = (bf16[2,2,512,704]{3,2,1,0:T(8,128)(2,1)}, bf16[2,512,2048]{2,1,0:T(8,128)(2,1)}, bf16[256,2048]{1,0:T(8,128)(2,1)}, bf16[256,2048]{1,0:T(8,128...) custom-call(s32[2]{0:T(128)} %get-tuple-element.552.places_ref, ...), custom_call_target="tpu_custom_call" | custom-call | flops 1 | bytes 1 | tf_op jit(solution)/shard_map/pallas_call | solution.py:668
  347.8 21.7 %shard_map.183 = (bf16[2,2,512,704]{3,2,1,0:T(8,128)(2,1)}, bf16[2,512,2048]{2,1,0:T(8,128)(2,1)}, bf16[256,2048]{1,0:T(8,128)(2,1)}, bf16[256,2048]{1,0:T(8,128...) custom-call(s32[2]{0:T(128)} %get-tuple-element.552.places_ref, ...), custom_call_target="tpu_custom_call" | custom-call | flops 1 | bytes 1 | tf_op jit(solution)/shard_map/pallas_call | solution.py:668
  383.2 11.6 %shard_map.184 = (bf16[352,1024]{1,0:T(8,128)(2,1)}, bf16[352,1024]{1,0:T(8,128)(2,1)}, bf16[352,1024]{1,0:T(8,128)(2,1)}, bf16[352,1024]{1,0:T(8,128)(2,1)}) custom-call(s32[2]{0:T(128)} %get-tuple-element.553.places_ref, bf16[2,2,512,704]{3,2,1,0:T(8,128)(2,1)} %get-tuple-element.432.refs_0_, bf16[1,512,2048]{2,1,0:T(8,128)(2,1)} %get-tuple-element.433.refs_1_, ...), custom_call_target="tpu_custom_call" | custom-call | flops 1 | bytes 1 | tf_op jit(solution)/shard_map/pallas_call | solution.py:904
  408.1 10.8 %shard_map.185 = (f32[256,2048]{1,0:T(8,128)}, bf16[256,2048]{1,0:T(8,128)(2,1)}, f32[1,2048]{1,0:T(1,128)}, bf16[8,256,256]{2,1,0:T(8,128)(2,1)}) custom-call(s32[12]{0:T(128)} %stack.195.places_ref, bf16[4,256,512]{2,1,0:T(8,128)(2,1)} %copy-done.9, bf16[4,256,512]{2,1,0:T(8,128)(2,1)} %copy-done.19, bf16[4,256,512]{2,1,0:T(8,128)(2,1)} %collective-permute-done.14.refs_2_, ...), custom_call_target="tpu_custom_call" | custom-call | flops 1 | bytes 1 | tf_op jit(solution)/shard_map/pallas_call | solution.py:537
  427.4 11.2 %shard_map.186 = (bf16[352,1024]{1,0:T(8,128)(2,1)}, bf16[352,1024]{1,0:T(8,128)(2,1)}, bf16[352,1024]{1,0:T(8,128)(2,1)}, bf16[352,1024]{1,0:T(8,128)(2,1)}) custom-call(s32[2]{0:T(128)} %get-tuple-element.553.places_ref, bf16[2,2,512,704]{3,2,1,0:T(8,128)(2,1)} %get-tuple-element.432.refs_0_, bf16[1,512,2048]{2,1,0:T(8,128)(2,1)} %get-tuple-element.433.refs_1_, ...), custom_call_target="tpu_custom_call" | custom-call | flops 1 | bytes 1 | tf_op jit(solution)/shard_map/pallas_call | solution.py:904
  450.2 11.2 %shard_map.188 = (bf16[352,1024]{1,0:T(8,128)(2,1)}, bf16[352,1024]{1,0:T(8,128)(2,1)}, bf16[352,1024]{1,0:T(8,128)(2,1)}, bf16[352,1024]{1,0:T(8,128)(2,1)}) custom-call(s32[2]{0:T(128)} %get-tuple-element.553.places_ref, bf16[1,3,512,704]{3,2,1,0:T(8,128)(2,1)} %get-tuple-element.446.refs_10_.refs_0_, bf16[2,512,2048]{2,1,0:T(8,128)(2,1)} %get-tuple-element.447.refs_1_, ...), custom_call_target="tpu_custom_call" | custom-call | flops 1 | bytes 1 | tf_op jit(solution)/shard_map/pallas_call | solution.py:904
  473.5 8.1 %collective-permute-done.57 = bf16[256,2048]{1,0:T(8,128)(2,1)S(1)} collective-permute-done((bf16[256,2048]{1,0:T(8,128)(2,1)}, bf16[256,2048]{1,0:T(8,128)(2,1)S(1)}, u32[]{:S(2)}, u32[]{:S(2)}) %collective-permute-start.57) | collective-permute-done | bytes 1048608 | tf_op jit(solution)/shard_map/ppermute | solution.py:348
  488.0 31.7 %shard_map.189.grad_ref = bf16[8,256,320]{2,1,0:T(8,128)(2,1)} custom-call(s32[3]{0:T(128)} %bitcast.114, bf16[2048,320]{1,0:T(8,128)(2,1)} %get-tuple-element.455.projected_ref, f32[1,2048]{1,0:T(1,128)} %bitcast.108, f32[2048,256]{1,0:T(8,128)} %get-tuple-element.456.y_ref, f32[2048,128]{1,0:T(8,128)} %get-tuple-element.457.inv_ref, ...), custom_call_target="tpu_custom_call" | custom-call | flops 1 | bytes 1 | tf_op jit(solution)/shard_map/pallas_call | solution.py:260
  536.3 7.8 %shard_map.190 = (bf16[320,2048]{1,0:T(8,128)(2,1)}, f32[1,2048]{1,0:T(1,128)}) custom-call(bf16[2048,2048]{1,0:T(8,128)(2,1)} %get-tuple-element.465.normed_ref, bf16[8,256,320]{2,1,0:T(8,128)(2,1)} %shard_map.189.grad_ref, bf16[320,2048]{1,0:T(8,128)(2,1)} %bitcast.98, f32[1,2048]{1,0:T(1,128)} %bitcast.105), custom_call_target="tpu_custom_call" | custom-call | flops 1 | bytes 1 | tf_op jit(solution)/shard_map/pallas_call | solution.py:993
  566.3 12.2 %shard_map.191 = f32[256,2048]{1,0:T(8,128)} custom-call(s32[12]{0:T(128)} %stack.228.places_ref, bf16[4,320,512]{2,1,0:T(8,128)(2,1)} %all-to-all-done.1.refs_0_, bf16[4,320,512]{2,1,0:T(8,128)(2,1)} %collective-permute-done.38.refs_1_, bf16[4,320,512]{2,1,0:T(8,128)(2,1)} %collective-permute-done.39.refs_2_, bf16[4,320,512]{2,1,0:T(8,128)(2,1)} %copy-done.34, ...), custom_call_target="tpu_custom_call" | custom-call | flops 1 | bytes 1 | tf_op jit(solution)/shard_map/pallas_call | solution.py:537
  582.7 10.0 %collective-permute-done.71 = bf16[160,2048]{1,0:T(8,128)(2,1)} collective-permute-done((bf16[160,2048]{1,0:T(8,128)(2,1)}, bf16[160,2048]{1,0:T(8,128)(2,1)}, u32[]{:S(2)}, u32[]{:S(2)}) %collective-permute-start.71) | collective-permute-done | bytes 655392 | tf_op jit(solution)/shard_map/ppermute | solution.py:332
  624.9 9.7 %all-to-all-done.4 = bf16[4,256,512]{2,1,0:T(8,128)(2,1)S(1)} async-done(((bf16[4,256,512]{2,1,0:T(8,128)(2,1)}), bf16[4,256,512]{2,1,0:T(8,128)(2,1)S(1)}, u32[]{:S(2)}, u32[]{:S(2)}) %all-to-all-start.4) | async-done | bytes 1048608 | tf_op jit(solution)/shard_map/all_to_all | solution.py:1300
  (377 shorter events, 274.8 us)
Async XLA Ops:
  2.9 35.6 %collective-permute-start = (bf16[256,2560]{1,0:T(8,128)(2,1)S(1)}, bf16[256,2560]{1,0:T(8,128)(2,1)}, u32[]{:S(2)}, u32[]{:S(2)}) collective-permute-start(bf16[256,2560]{1,0:T(8,128)(2,1)S(1)} %pad_maximum_fusion.2.refs_0_), channel_id=1, source_target_pairs={{0,2},{1,3},{2,4},{3,5},{4,6},{5,7},{8,10},{9,11},{10,12},{11,13},... | collective-permute-start | bytes 3932168 | tf_op jit(solution)/shard_map/ppermute | solution.py:373
  42.1 33.3 %collective-permute-start.6 = (bf16[256,2560]{1,0:T(8,128)(2,1)}, bf16[256,2560]{1,0:T(8,128)(2,1)}, u32[]{:S(2)}, u32[]{:S(2)}) collective-permute-start(bf16[256,2560]{1,0:T(8,128)(2,1)} %collective-permute-done.1), channel_id=1, source_target_pairs={{2,0},{3,1},{4,2},{5,3},{10,8},{11,9},{12,10},{13,11},{18,16},{19,... | collective-permute-start | bytes 3932168 | tf_op jit(solution)/shard_map/ppermute | solution.py:378
  75.4 36.4 %collective-permute-start.10 = (bf16[2,352,1024]{2,1,0:T(8,128)(2,1)S(1)}, bf16[2,352,1024]{2,1,0:T(8,128)(2,1)S(1)}, u32[]{:S(2)}, u32[]{:S(2)}) collective-permute-start(bf16[2,352,1024]{2,1,0:T(8,128)(2,1)S(1)} %slice.125), channel_id=1, source_target_pairs={{0,16},{8,24},{16,0},{24,8},{1,17},{9,25},{17,1},{25,9},{2,18},{10... | collective-permute-start | bytes 4325384 | tf_op jit(solution)/shard_map/ppermute | solution.py:335
  77.0 34.8 %collective-permute-start.11 = (bf16[2,352,1024]{2,1,0:T(8,128)(2,1)S(1)}, bf16[2,352,1024]{2,1,0:T(8,128)(2,1)S(1)}, u32[]{:S(2)}, u32[]{:S(2)}) collective-permute-start(bf16[2,352,1024]{2,1,0:T(8,128)(2,1)S(1)} %slice.125), channel_id=1, source_target_pairs={{0,4},{1,5},{6,2},{7,3},{8,12},{9,13},{14,10},{15,11},{16,20},{17,... | collective-permute-start | bytes 4325384 | tf_op jit(solution)/shard_map/ppermute | solution.py:361
  119.6 37.4 %collective-permute-start.18 = (bf16[2,352,1024]{2,1,0:T(8,128)(2,1)S(1)}, bf16[2,352,1024]{2,1,0:T(8,128)(2,1)}, u32[]{:S(2)}, u32[]{:S(2)}) collective-permute-start(bf16[2,352,1024]{2,1,0:T(8,128)(2,1)S(1)} %slice.130), channel_id=1, source_target_pairs={{2,6},{3,7},{4,0},{5,1},{10,14},{11,15},{12,8},{13,9},{18,22},{19,... | collective-permute-start | bytes 4325384 | tf_op jit(solution)/shard_map/ppermute | solution.py:361
  146.1 34.2 %all-to-all-start = ((bf16[8,256,256]{2,1,0:T(8,128)(2,1)}), bf16[8,256,256]{2,1,0:T(8,128)(2,1)S(1)}, u32[]{:S(2)}, u32[]{:S(2)}) async-start(bf16[8,256,256]{2,1,0:T(8,128)(2,1)} %bitcast.101), calls=%async_computation | async-start | bytes 2097152 | tf_op jit(solution)/shard_map/all_to_all | solution.py:1046
  158.5 39.8 %collective-permute-start.25 = (bf16[2,352,1024]{2,1,0:T(8,128)(2,1)S(1)}, bf16[2,352,1024]{2,1,0:T(8,128)(2,1)}, u32[]{:S(2)}, u32[]{:S(2)}) collective-permute-start(bf16[2,352,1024]{2,1,0:T(8,128)(2,1)S(1)} %broadcast_select_fusion.refs_2_.refs_6_), channel_id=1, source_target_pairs={{0,16},{8,24},{16,0},{24,8},{1,17},{9,25},{17,1},{25,9},{2,18},{10... | collective-permute-start | bytes 4325384 | tf_op jit(solution)/shard_map/ppermute | solution.py:335
  192.9 39.9 %collective-permute-start.20 = (bf16[256,2048]{1,0:T(8,128)(2,1)}, bf16[256,2048]{1,0:T(8,128)(2,1)S(1)}, u32[]{:S(2)}, u32[]{:S(2)}) collective-permute-start(bf16[256,2048]{1,0:T(8,128)(2,1)} %get-tuple-element.306.refs_4_), channel_id=1, source_target_pairs={{0,8},{8,0},{16,24},{24,16},{1,9},{9,1},{17,25},{25,17},{2,10},{10... | collective-permute-start | bytes 3145736 | tf_op jit(solution)/shard_map/ppermute | solution.py:332
  193.5 40.6 %collective-permute-start.21 = (bf16[256,2048]{1,0:T(8,128)(2,1)}, bf16[256,2048]{1,0:T(8,128)(2,1)S(1)}, u32[]{:S(2)}, u32[]{:S(2)}) collective-permute-start(bf16[256,2048]{1,0:T(8,128)(2,1)} %get-tuple-element.306.refs_4_), channel_id=1, source_target_pairs={{0,2},{1,3},{2,0},{3,1},{4,6},{5,7},{6,4},{7,5},{8,10},{9,11},{10,... | collective-permute-start | bytes 3145736 | tf_op jit(solution)/shard_map/ppermute | solution.py:348
  194.7 39.4 %collective-permute-start.23 = (bf16[256,2048]{1,0:T(8,128)(2,1)}, bf16[256,2048]{1,0:T(8,128)(2,1)S(1)}, u32[]{:S(2)}, u32[]{:S(2)}) collective-permute-start(bf16[256,2048]{1,0:T(8,128)(2,1)} %get-tuple-element.306.refs_4_), channel_id=1, source_target_pairs={{0,1},{1,0},{2,3},{3,2},{4,5},{5,4},{6,7},{7,6},{8,9},{9,8},{10,11... | collective-permute-start | bytes 3145736 | tf_op jit(solution)/shard_map/ppermute | solution.py:345
  195.9 36.9 %collective-permute-start.22 = (bf16[1,352,1024]{2,1,0:T(8,128)(2,1)S(1)}, bf16[1,352,1024]{2,1,0:T(8,128)(2,1)S(1)}, u32[]{:S(2)}, u32[]{:S(2)}) collective-permute-start(bf16[1,352,1024]{2,1,0:T(8,128)(2,1)S(1)} %slice.135), channel_id=1, source_target_pairs={{0,4},{1,5},{2,6},{3,7},{4,0},{5,1},{6,2},{7,3},{8,12},{9,13},{10,... | collective-permute-start | bytes 2162696 | tf_op jit(solution)/shard_map/ppermute | solution.py:351
  198.3 34.5 %collective-permute-start.24 = (bf16[1,352,1024]{2,1,0:T(8,128)(2,1)S(1)}, bf16[1,352,1024]{2,1,0:T(8,128)(2,1)S(1)}, u32[]{:S(2)}, u32[]{:S(2)}) collective-permute-start(bf16[1,352,1024]{2,1,0:T(8,128)(2,1)S(1)} %slice.135), channel_id=1, source_target_pairs={{0,16},{8,24},{16,0},{24,8},{1,17},{9,25},{17,1},{25,9},{2,18},{10... | collective-permute-start | bytes 2162696 | tf_op jit(solution)/shard_map/ppermute | solution.py:335
  256.1 35.0 %collective-permute-start.35 = (bf16[256,2048]{1,0:T(8,128)(2,1)}, bf16[256,2048]{1,0:T(8,128)(2,1)}, u32[]{:S(2)}, u32[]{:S(2)}) collective-permute-start(bf16[256,2048]{1,0:T(8,128)(2,1)} %collective-permute-done.7.refs_8_), channel_id=1, source_target_pairs={{0,1},{1,0},{2,3},{3,2},{4,5},{5,4},{6,7},{7,6},{8,9},{9,8},{10,11... | collective-permute-start | bytes 3145736 | tf_op jit(solution)/shard_map/ppermute | solution.py:345
  263.7 38.8 %all-to-all-start.1 = ((bf16[4,320,512]{2,1,0:T(8,128)(2,1)}), bf16[4,320,512]{2,1,0:T(8,128)(2,1)}, u32[]{:S(2)}, u32[]{:S(2)}) async-start(bf16[4,320,512]{2,1,0:T(8,128)(2,1)} %bitcast.99), calls=%async_computation.1 | async-start | bytes 2621440 | tf_op jit(solution)/shard_map/all_to_all | solution.py:1156
  335.4 34.2 %collective-permute-start.48 = (bf16[4,320,512]{2,1,0:T(8,128)(2,1)}, bf16[4,320,512]{2,1,0:T(8,128)(2,1)S(1)}, u32[]{:S(2)}, u32[]{:S(2)}) collective-permute-start(bf16[4,320,512]{2,1,0:T(8,128)(2,1)} %collective-permute-done.39.refs_2_), channel_id=1, source_target_pairs={{0,1},{1,0},{2,3},{3,2},{4,5},{5,4},{6,7},{7,6},{8,9},{9,8},{10,11... | collective-permute-start | bytes 3932168 | tf_op jit(solution)/shard_map/ppermute | solution.py:345
  419.0 62.6 %all-to-all-start.2 = ((bf16[8,256,256]{2,1,0:T(8,128)(2,1)}), bf16[8,256,256]{2,1,0:T(8,128)(2,1)S(1)}, u32[]{:S(2)}, u32[]{:S(2)}) async-start(bf16[8,256,256]{2,1,0:T(8,128)(2,1)} %get-tuple-element.427), calls=%async_computation.2 | async-start | bytes 2097152 | tf_op jit(solution)/shard_map/all_to_all | solution.py:1046
  425.2 48.3 %collective-permute-start.56 = (bf16[256,2048]{1,0:T(8,128)(2,1)}, bf16[256,2048]{1,0:T(8,128)(2,1)S(1)}, u32[]{:S(2)}, u32[]{:S(2)}) collective-permute-start(bf16[256,2048]{1,0:T(8,128)(2,1)} %add_convert_fusion.4), channel_id=1, source_target_pairs={{0,8},{8,0},{16,24},{24,16},{1,9},{9,1},{17,25},{25,17},{2,10},{10... | collective-permute-start | bytes 3145736 | tf_op jit(solution)/shard_map/ppermute | solution.py:332
  425.7 55.8 %collective-permute-start.57 = (bf16[256,2048]{1,0:T(8,128)(2,1)}, bf16[256,2048]{1,0:T(8,128)(2,1)S(1)}, u32[]{:S(2)}, u32[]{:S(2)}) collective-permute-start(bf16[256,2048]{1,0:T(8,128)(2,1)} %add_convert_fusion.3), channel_id=1, source_target_pairs={{0,2},{1,3},{2,0},{3,1},{4,6},{5,7},{6,4},{7,5},{8,10},{9,11},{10,... | collective-permute-start | bytes 3145736 | tf_op jit(solution)/shard_map/ppermute | solution.py:348
  447.0 34.6 %collective-permute-start.59 = (bf16[352,1024]{1,0:T(8,128)(2,1)}, bf16[352,1024]{1,0:T(8,128)(2,1)}, u32[]{:S(2)}, u32[]{:S(2)}) collective-permute-start(bf16[352,1024]{1,0:T(8,128)(2,1)} %add_convert_fusion.14), channel_id=1, source_target_pairs={{0,4},{1,5},{2,6},{3,7},{4,0},{5,1},{6,2},{7,3},{8,12},{9,13},{10,... | collective-permute-start | bytes 2162696 | tf_op jit(solution)/shard_map/ppermute | solution.py:351
  481.6 38.2 %collective-permute-start.66 = (bf16[4,256,512]{2,1,0:T(8,128)(2,1)}, bf16[4,256,512]{2,1,0:T(8,128)(2,1)}, u32[]{:S(2)}, u32[]{:S(2)}) collective-permute-start(bf16[4,256,512]{2,1,0:T(8,128)(2,1)} %get-tuple-element.463), channel_id=1, source_target_pairs={{0,8},{8,0},{16,24},{24,16},{1,9},{9,1},{17,25},{25,17},{2,10},{10... | collective-permute-start | bytes 3145736 | tf_op jit(solution)/shard_map/ppermute | solution.py:332
  484.7 35.0 %collective-permute-start.63 = (bf16[352,1024]{1,0:T(8,128)(2,1)}, bf16[352,1024]{1,0:T(8,128)(2,1)}, u32[]{:S(2)}, u32[]{:S(2)}) collective-permute-start(bf16[352,1024]{1,0:T(8,128)(2,1)} %add_convert_fusion.13), channel_id=1, source_target_pairs={{0,4},{1,5},{2,6},{3,7},{4,0},{5,1},{6,2},{7,3},{8,12},{9,13},{10,... | collective-permute-start | bytes 2162696 | tf_op jit(solution)/shard_map/ppermute | solution.py:351
  486.0 33.8 %collective-permute-start.64 = (bf16[352,1024]{1,0:T(8,128)(2,1)}, bf16[352,1024]{1,0:T(8,128)(2,1)}, u32[]{:S(2)}, u32[]{:S(2)}) collective-permute-start(bf16[352,1024]{1,0:T(8,128)(2,1)} %get-tuple-element.461), channel_id=1, source_target_pairs={{0,16},{8,24},{16,0},{24,8},{1,17},{9,25},{17,1},{25,9},{2,18},{10... | collective-permute-start | bytes 2162696 | tf_op jit(solution)/shard_map/ppermute | solution.py:335
  522.5 37.1 %all-to-all-start.3 = ((bf16[8,256,320]{1,2,0:T(8,128)(2,1)}), bf16[8,256,320]{1,2,0:T(8,128)(2,1)S(1)}, u32[]{:S(2)}, u32[]{:S(2)}) async-start(bf16[8,256,320]{1,2,0:T(8,128)(2,1)} %copy.24), calls=%async_computation.3 | async-start | bytes 2621440 | tf_op jit(solution)/shard_map/all_to_all | solution.py:1046
  535.3 47.4 %collective-permute-start.70 = (bf16[4,256,512]{2,1,0:T(8,128)(2,1)}, bf16[4,256,512]{2,1,0:T(8,128)(2,1)}, u32[]{:S(2)}, u32[]{:S(2)}) collective-permute-start(bf16[4,256,512]{2,1,0:T(8,128)(2,1)} %add_convert_fusion.2), channel_id=1, source_target_pairs={{0,16},{8,24},{16,0},{24,8},{1,17},{9,25},{17,1},{25,9},{2,18},{10... | collective-permute-start | bytes 3145736 | tf_op jit(solution)/shard_map/ppermute | solution.py:335
  (131 other events, 2171.6 us)

commit v8 on v7

--- a/solution.py
+++ b/solution.py
@@ -121,6 +121,7 @@
         y_ref[:, head * VD : (head + 1) * VD] = y
         att_ref[:, head * VD : (head + 1) * VD] = y.astype(jnp.bfloat16)
         inverses = jnp.where(lane == head, inverse, inverses)
+    inverses = jnp.where(lane == heads, keep, inverses)
     inv_ref[...] = inverses
 
 
@@ -166,7 +167,7 @@
 
 
 def attend_back_kernel(
-    heads, rows, ends_ref, projected_ref, keep_ref, y_ref, inv_ref, grad_ref, out_ref,
+    heads, rows, ends_ref, projected_ref, y_ref, inv_ref, grad_ref, out_ref,
     key_s, query_s, value_s, error_s, dquery_s,
 ):
     step = pl.program_id(0)
@@ -179,7 +180,7 @@
 
         def fill(block, nothing):
             at = pl.ds(pl.multiple_of(block * rows, rows), rows)
-            keep = column_of(keep_ref[:, at])
+            keep = inv_ref[at, heads : heads + 1]
             wide_block = padded(projected_ref[at, :].astype(jnp.float32))
             ones = jnp.where(lane < 2, keep, 0.0).astype(jnp.bfloat16)
             inverses = inv_ref[at, :]
@@ -235,7 +236,7 @@
     )
     totals = tile(step, totals, True)
     dkeys, dvalues = lax.fori_loop(step + 1, blocks, lambda block, held: tile(block, held, False), totals)
-    keep = column_of(keep_ref[:, own])
+    keep = inv_ref[own, heads : heads + 1]
     width = out_ref.shape[2]
     total = jnp.zeros((rows, width + -width % LANES), jnp.float32)
     blank = jnp.zeros((rows, total.shape[1] - LANES), jnp.float32)
@@ -252,7 +253,7 @@
     out_ref[...] = total[:, :width].astype(jnp.bfloat16).reshape(out_ref.shape)
 
 
-def attend_back(projected, keep, ends, y, inverses, grad, heads, each):
+def attend_back(projected, ends, y, inverses, grad, heads, each):
     total = projected.shape[0]
     rows = min(512, total)
     width = projected.shape[1]
@@ -262,7 +263,7 @@
         grid_spec=pltpu.PrefetchScalarGridSpec(
             num_scalar_prefetch=1,
             grid=(total // rows,),
-            in_specs=[whole(width), pl.BlockSpec((1, total), lambda i, e: (0, 0)), whole(heads * VD), whole(LANES), whole(heads * VD)],
+            in_specs=[whole(width), whole(heads * VD), whole(LANES), whole(heads * VD)],
             out_specs=pl.BlockSpec((rows // each, each, width), lambda i, e: (i, 0, 0)),
             scratch_shapes=[
                 pltpu.VMEM((heads, total, LANES), jnp.bfloat16),
@@ -277,7 +278,7 @@
             dimension_semantics=("arbitrary",), vmem_limit_bytes=VMEM
         ),
         cost_estimate=LITTLE,
-    )(ends, projected, keep, y, inverses, grad)
+    )(ends, projected, y, inverses, grad)
 
 
 def inv_root_mean(values):
@@ -582,10 +583,12 @@
     for copy in copies:
         copy.wait()
     width = out_ref.shape[2]
-    for head in range(out_ref.shape[0]):
-        out_ref[head] = lax.dot_general(
-            dmixed, weight_s[head * width : (head + 1) * width, :], NT, preferred_element_type=jnp.float32
+    for head in range(0, out_ref.shape[0], 2):
+        pair = lax.dot_general(
+            dmixed, weight_s[head * width : (head + 2) * width, :], NT, preferred_element_type=jnp.float32
         ).astype(jnp.bfloat16)
+        out_ref[head] = pair[:, :width]
+        out_ref[head + 1] = pair[:, width:]
 
 
 def unmix(parts, middle, grad, gain, whole, heads):
@@ -1262,7 +1265,7 @@
     down_sent = [on_y_steps(part) for part in down_parts[1:]]
     out_first = [wires.over_x(out_sent[s]) for s in across_y]
     d_projected = attend_back(
-        projected, keep_row, ends, attended_wide, inverses, d_attended, heads_here, rows
+        projected, ends, attended_wide, inverses, d_attended, heads_here, rows
     )
     d_projected, up_back, up_sent, down_sent, out_first = tie(
         d_projected, up_back, up_sent, down_sent, out_first

time: 668 us -> 669 us (level)
  no operation moved by 1% of the time
where the time goes in v8:
time: 669 us; the launch traced here: 662 us
  waiting for transfers between devices  252 us (38%)
  Pallas kernels  209 us (31%)
  starting transfers between devices  106 us (16%)
  other arithmetic  67.9 us (10%)
  local copies, waits for them, and re-layouts  24.4 us (4%)
    ppermute x19, waiting for transfers between devices, over_x(): return lax.ppermute(values, 'dp', [(i, i ^ 1) for i in range(self.dp)])  92.4 us
    pallas_call x4, Pallas kernels, with_units(): pl.pallas_call(functools.partial(kernel, units), grid_spec=pltpu.Prefetch...  72.5 us
    convert_element_type x19, other arithmetic, low(): return values.astype(jnp.bfloat16)  43.8 us
    ppermute x5, waiting for transfers between devices, over_zh(): lax.ppermute(values, 'head', [(i, (i // 4 + shift) % self.nzh * 4 + i % 4...  39.2 us
    pallas_call x3, Pallas kernels, unit_grad(): pl.pallas_call(functools.partial(unit_grad_kernel, order, ny, nzh), grid_...  34.1 us
    pallas_call x1, Pallas kernels, attend_back(): pl.pallas_call(functools.partial(attend_back_kernel, heads, rows), grid_s...  32.8 us
    pallas_call x3, Pallas kernels, with_whole(): pl.pallas_call(functools.partial(kernel, whole), grid_spec=pltpu.Prefetch...  31.9 us
    ppermute x19, waiting for transfers between devices, over_y(): lax.ppermute(values, 'dp', [(i, (i // 2 + shift) % self.ny * 2 + i % 2) f...  31.1 us
  transfers between devices with their start and end apart: 92, of which 39 were waited for; matrix products, arithmetic and copies ran while one was open for 11% of the time, Pallas kernels for 30%

profile of v8, /device:TPU:0, one launch (start us, length us, event | category | flops | bytes accessed | tf_op | source)
XLA Modules:
  0.0 661.6 jit_solution(9739702155153338566)
XLA Ops:
  15.5 23.0 %collective-permute-done.2 = bf16[3,352,512]{2,1,0:T(8,128)(2,1)S(1)} collective-permute-done((bf16[3,352,512]{2,1,0:T(8,128)(2,1)S(1)}, bf16[3,352,512]{2,1,0:T(8,128)(2,1)S(1)}, u32[]{:S(2)}, u32[]{:S(2)}) %collective-permute-start.2) | collective-permute-done | bytes 1081376 | tf_op jit(solution)/shard_map/ppermute | solution.py:333
  46.6 20.8 %collective-permute-done.7.refs_8_ = bf16[256,2048]{1,0:T(8,128)(2,1)} collective-permute-done((bf16[256,2048]{1,0:T(8,128)(2,1)}, bf16[256,2048]{1,0:T(8,128)(2,1)}, u32[]{:S(2)}, u32[]{:S(2)}) %collective-permute-start.7) | collective-permute-done | bytes 1048608 | tf_op jit(solution)/shard_map/ppermute | solution.py:333
  67.4 7.9 %collective-permute-done.6 = bf16[256,2560]{1,0:T(8,128)(2,1)} collective-permute-done((bf16[256,2560]{1,0:T(8,128)(2,1)}, bf16[256,2560]{1,0:T(8,128)(2,1)}, u32[]{:S(2)}, u32[]{:S(2)}) %collective-permute-start.6) | collective-permute-done | bytes 1310752 | tf_op jit(solution)/shard_map/ppermute | solution.py:379
  83.7 28.1 %collective-permute-done.9 = bf16[256,2560]{1,0:T(8,128)(2,1)S(1)} collective-permute-done((bf16[256,2560]{1,0:T(8,128)(2,1)S(1)}, bf16[256,2560]{1,0:T(8,128)(2,1)S(1)}, u32[]{:S(2)}, u32[]{:S(2)}) %collective-permute-start.9) | collective-permute-done | bytes 1310752 | tf_op jit(solution)/shard_map/ppermute | solution.py:388
  123.0 23.1 %shard_map.178 = (bf16[2048,320]{1,0:T(8,128)(2,1)}, bf16[2048,2048]{1,0:T(8,128)(2,1)}, f32[2048,256]{1,0:T(8,128)}, f32[2048,128]{1,0:T(8,128)}, bf16[2048,256]{1,0:T(8,128)(2,1)}) custom-call(s32[3]{0:T(128)} %bitcast.112, s32[8]{0:T(128)} %stack.205.at_ref, bf16[256,2560]{1,0:T(8,128)(2,1)} %copy-done.15, ...), custom_call_target="tpu_custom_call" | custom-call | flops 1 | bytes 1 | tf_op jit(solution)/shard_map/pallas_call | solution.py:135
  146.1 7.6 %all-to-all-start = ((bf16[8,256,256]{2,1,0:T(8,128)(2,1)}), bf16[8,256,256]{2,1,0:T(8,128)(2,1)S(1)}, u32[]{:S(2)}, u32[]{:S(2)}) async-start(bf16[8,256,256]{2,1,0:T(8,128)(2,1)} %bitcast.101), calls=%async_computation | async-start | bytes 2097152 | tf_op jit(solution)/shard_map/all_to_all | solution.py:1049
  161.2 18.5 %collective-permute-done.15.refs_3_ = bf16[4,256,512]{2,1,0:T(8,128)(2,1)} collective-permute-done((bf16[4,256,512]{2,1,0:T(8,128)(2,1)}, bf16[4,256,512]{2,1,0:T(8,128)(2,1)}, u32[]{:S(2)}, u32[]{:S(2)}) %collective-permute-start.15) | collective-permute-done | bytes 1048608 | tf_op jit(solution)/shard_map/ppermute | solution.py:333
  184.1 8.8 %shard_map.179 = (f32[256,2048]{1,0:T(8,128)}, bf16[256,2048]{1,0:T(8,128)(2,1)}) custom-call(s32[12]{0:T(128)} %stack.195.places_ref, bf16[4,256,512]{2,1,0:T(8,128)(2,1)} %copy-done.9, bf16[4,256,512]{2,1,0:T(8,128)(2,1)} %copy-done.19, bf16[4,256,512]{2,1,0:T(8,128)(2,1)} %collective-permute-done.14.refs_2_, ...), custom_call_target="tpu_custom_call" | custom-call | flops 1 | bytes 1 | tf_op jit(solution)/shard_map/pallas_call | solution.py:538
  199.8 33.0 %collective-permute-done.22.refs_2_ = bf16[1,352,1024]{2,1,0:T(8,128)(2,1)S(1)} collective-permute-done((bf16[1,352,1024]{2,1,0:T(8,128)(2,1)S(1)}, bf16[1,352,1024]{2,1,0:T(8,128)(2,1)S(1)}, u32[]{:S(2)}, u32[]{:S(2)}) %collective-permute-start.22) | collective-permute-done | bytes 720928 | tf_op jit(solution)/shard_map/ppermute | solution.py:352
  239.8 16.2 %collective-permute-done.27.refs_3_ = bf16[1,352,1024]{2,1,0:T(8,128)(2,1)S(1)} collective-permute-done((bf16[1,352,1024]{2,1,0:T(8,128)(2,1)S(1)}, bf16[1,352,1024]{2,1,0:T(8,128)(2,1)S(1)}, u32[]{:S(2)}, u32[]{:S(2)}) %collective-permute-start.27) | collective-permute-done | bytes 720928 | tf_op jit(solution)/shard_map/ppermute | solution.py:336
  272.0 19.0 %shard_map.180 = (bf16[3,3,512,704]{3,2,1,0:T(8,128)(2,1)}, bf16[3,512,2048]{2,1,0:T(8,128)(2,1)}) custom-call(s32[2]{0:T(128)} %get-tuple-element.552.places_ref, bf16[2,352,1024]{2,1,0:T(8,128)(2,1)} %slice.137.refs_0_.refs_4_, bf16[2,352,1024]{2,1,0:T(8,128)(2,1)} %copy-done.5, bf16[2,352,1024]{2,1,0:T(8,128)(2,1)} %copy-done.2, ...), custom_call_target="tpu_custom_call" | custom-call | flops 1 | bytes 1 | tf_op jit(solution)/shard_map/pallas_call | solution.py:671
  292.4 10.0 %shard_map.181 = (bf16[1,3,512,704]{3,2,1,0:T(8,128)(2,1)}, bf16[1,512,2048]{2,1,0:T(8,128)(2,1)}) custom-call(s32[2]{0:T(128)} %get-tuple-element.552.places_ref, bf16[2,352,1024]{2,1,0:T(8,128)(2,1)} %slice.137.refs_0_.refs_4_, bf16[2,352,1024]{2,1,0:T(8,128)(2,1)} %copy-done.5, bf16[2,352,1024]{2,1,0:T(8,128)(2,1)} %copy-done.2, ...), custom_call_target="tpu_custom_call" | custom-call | flops 1 | bytes 1 | tf_op jit(solution)/shard_map/pallas_call | solution.py:671
  306.4 21.8 %shard_map.182 = (bf16[2,2,512,704]{3,2,1,0:T(8,128)(2,1)}, bf16[2,512,2048]{2,1,0:T(8,128)(2,1)}, bf16[256,2048]{1,0:T(8,128)(2,1)}, bf16[256,2048]{1,0:T(8,128...) custom-call(s32[2]{0:T(128)} %get-tuple-element.552.places_ref, ...), custom_call_target="tpu_custom_call" | custom-call | flops 1 | bytes 1 | tf_op jit(solution)/shard_map/pallas_call | solution.py:671
  347.8 21.7 %shard_map.183 = (bf16[2,2,512,704]{3,2,1,0:T(8,128)(2,1)}, bf16[2,512,2048]{2,1,0:T(8,128)(2,1)}, bf16[256,2048]{1,0:T(8,128)(2,1)}, bf16[256,2048]{1,0:T(8,128...) custom-call(s32[2]{0:T(128)} %get-tuple-element.552.places_ref, ...), custom_call_target="tpu_custom_call" | custom-call | flops 1 | bytes 1 | tf_op jit(solution)/shard_map/pallas_call | solution.py:671
  383.1 11.7 %shard_map.184 = (bf16[352,1024]{1,0:T(8,128)(2,1)}, bf16[352,1024]{1,0:T(8,128)(2,1)}, bf16[352,1024]{1,0:T(8,128)(2,1)}, bf16[352,1024]{1,0:T(8,128)(2,1)}) custom-call(s32[2]{0:T(128)} %get-tuple-element.553.places_ref, bf16[2,2,512,704]{3,2,1,0:T(8,128)(2,1)} %get-tuple-element.432.refs_0_, bf16[1,512,2048]{2,1,0:T(8,128)(2,1)} %get-tuple-element.433.refs_1_, ...), custom_call_target="tpu_custom_call" | custom-call | flops 1 | bytes 1 | tf_op jit(solution)/shard_map/pallas_call | solution.py:907
  408.1 10.8 %shard_map.185 = (f32[256,2048]{1,0:T(8,128)}, bf16[256,2048]{1,0:T(8,128)(2,1)}, f32[1,2048]{1,0:T(1,128)}, bf16[8,256,256]{2,1,0:T(8,128)(2,1)}) custom-call(s32[12]{0:T(128)} %stack.195.places_ref, bf16[4,256,512]{2,1,0:T(8,128)(2,1)} %copy-done.9, bf16[4,256,512]{2,1,0:T(8,128)(2,1)} %copy-done.19, bf16[4,256,512]{2,1,0:T(8,128)(2,1)} %collective-permute-done.14.refs_2_, ...), custom_call_target="tpu_custom_call" | custom-call | flops 1 | bytes 1 | tf_op jit(solution)/shard_map/pallas_call | solution.py:538
  427.4 11.2 %shard_map.186 = (bf16[352,1024]{1,0:T(8,128)(2,1)}, bf16[352,1024]{1,0:T(8,128)(2,1)}, bf16[352,1024]{1,0:T(8,128)(2,1)}, bf16[352,1024]{1,0:T(8,128)(2,1)}) custom-call(s32[2]{0:T(128)} %get-tuple-element.553.places_ref, bf16[2,2,512,704]{3,2,1,0:T(8,128)(2,1)} %get-tuple-element.432.refs_0_, bf16[1,512,2048]{2,1,0:T(8,128)(2,1)} %get-tuple-element.433.refs_1_, ...), custom_call_target="tpu_custom_call" | custom-call | flops 1 | bytes 1 | tf_op jit(solution)/shard_map/pallas_call | solution.py:907
  450.1 11.2 %shard_map.188 = (bf16[352,1024]{1,0:T(8,128)(2,1)}, bf16[352,1024]{1,0:T(8,128)(2,1)}, bf16[352,1024]{1,0:T(8,128)(2,1)}, bf16[352,1024]{1,0:T(8,128)(2,1)}) custom-call(s32[2]{0:T(128)} %get-tuple-element.553.places_ref, bf16[1,3,512,704]{3,2,1,0:T(8,128)(2,1)} %get-tuple-element.446.refs_10_.refs_0_, bf16[2,512,2048]{2,1,0:T(8,128)(2,1)} %get-tuple-element.447.refs_1_, ...), custom_call_target="tpu_custom_call" | custom-call | flops 1 | bytes 1 | tf_op jit(solution)/shard_map/pallas_call | solution.py:907
  473.5 8.1 %collective-permute-done.57 = bf16[256,2048]{1,0:T(8,128)(2,1)S(1)} collective-permute-done((bf16[256,2048]{1,0:T(8,128)(2,1)}, bf16[256,2048]{1,0:T(8,128)(2,1)S(1)}, u32[]{:S(2)}, u32[]{:S(2)}) %collective-permute-start.57) | collective-permute-done | bytes 1048608 | tf_op jit(solution)/shard_map/ppermute | solution.py:349
  487.9 32.8 %shard_map.189.grad_ref = bf16[8,256,320]{2,1,0:T(8,128)(2,1)} custom-call(s32[3]{0:T(128)} %bitcast.113, bf16[2048,320]{1,0:T(8,128)(2,1)} %get-tuple-element.455.projected_ref, f32[2048,256]{1,0:T(8,128)} %get-tuple-element.456.y_ref, f32[2048,128]{1,0:T(8,128)} %get-tuple-element.457.inv_ref, bf16[2048,256]{1,0:T(8,128)(2,1)} %bitcast.100), custom_call_target="tpu_custom_call" | custom-call | flops 1 | bytes 1 | tf_op jit(solution)/shard_map/pallas_call | solution.py:261
  537.3 7.8 %shard_map.190 = (bf16[320,2048]{1,0:T(8,128)(2,1)}, f32[1,2048]{1,0:T(1,128)}) custom-call(bf16[2048,2048]{1,0:T(8,128)(2,1)} %get-tuple-element.465.normed_ref, bf16[8,256,320]{2,1,0:T(8,128)(2,1)} %shard_map.189.grad_ref, bf16[320,2048]{1,0:T(8,128)(2,1)} %bitcast.98, f32[1,2048]{1,0:T(1,128)} %bitcast.105), custom_call_target="tpu_custom_call" | custom-call | flops 1 | bytes 1 | tf_op jit(solution)/shard_map/pallas_call | solution.py:996
  567.3 12.2 %shard_map.191 = f32[256,2048]{1,0:T(8,128)} custom-call(s32[12]{0:T(128)} %stack.228.places_ref, bf16[4,320,512]{2,1,0:T(8,128)(2,1)} %all-to-all-done.1.refs_0_, bf16[4,320,512]{2,1,0:T(8,128)(2,1)} %collective-permute-done.38.refs_1_, bf16[4,320,512]{2,1,0:T(8,128)(2,1)} %collective-permute-done.39.refs_2_, bf16[4,320,512]{2,1,0:T(8,128)(2,1)} %copy-done.34, ...), custom_call_target="tpu_custom_call" | custom-call | flops 1 | bytes 1 | tf_op jit(solution)/shard_map/pallas_call | solution.py:538
  583.7 10.0 %collective-permute-done.71 = bf16[160,2048]{1,0:T(8,128)(2,1)} collective-permute-done((bf16[160,2048]{1,0:T(8,128)(2,1)}, bf16[160,2048]{1,0:T(8,128)(2,1)}, u32[]{:S(2)}, u32[]{:S(2)}) %collective-permute-start.71) | collective-permute-done | bytes 655392 | tf_op jit(solution)/shard_map/ppermute | solution.py:333
  625.8 9.7 %all-to-all-done.4 = bf16[4,256,512]{2,1,0:T(8,128)(2,1)S(1)} async-done(((bf16[4,256,512]{2,1,0:T(8,128)(2,1)}), bf16[4,256,512]{2,1,0:T(8,128)(2,1)S(1)}, u32[]{:S(2)}, u32[]{:S(2)}) %all-to-all-start.4) | async-done | bytes 1048608 | tf_op jit(solution)/shard_map/all_to_all | solution.py:1303
  (377 shorter events, 274.7 us)
Async XLA Ops:
  2.9 35.6 %collective-permute-start = (bf16[256,2560]{1,0:T(8,128)(2,1)S(1)}, bf16[256,2560]{1,0:T(8,128)(2,1)}, u32[]{:S(2)}, u32[]{:S(2)}) collective-permute-start(bf16[256,2560]{1,0:T(8,128)(2,1)S(1)} %pad_maximum_fusion.2.refs_0_), channel_id=1, source_target_pairs={{0,2},{1,3},{2,4},{3,5},{4,6},{5,7},{8,10},{9,11},{10,12},{11,13},... | collective-permute-start | bytes 3932168 | tf_op jit(solution)/shard_map/ppermute | solution.py:374
  75.4 36.4 %collective-permute-start.10 = (bf16[2,352,1024]{2,1,0:T(8,128)(2,1)S(1)}, bf16[2,352,1024]{2,1,0:T(8,128)(2,1)S(1)}, u32[]{:S(2)}, u32[]{:S(2)}) collective-permute-start(bf16[2,352,1024]{2,1,0:T(8,128)(2,1)S(1)} %slice.125), channel_id=1, source_target_pairs={{0,16},{8,24},{16,0},{24,8},{1,17},{9,25},{17,1},{25,9},{2,18},{10... | collective-permute-start | bytes 4325384 | tf_op jit(solution)/shard_map/ppermute | solution.py:336
  77.0 34.8 %collective-permute-start.11 = (bf16[2,352,1024]{2,1,0:T(8,128)(2,1)S(1)}, bf16[2,352,1024]{2,1,0:T(8,128)(2,1)S(1)}, u32[]{:S(2)}, u32[]{:S(2)}) collective-permute-start(bf16[2,352,1024]{2,1,0:T(8,128)(2,1)S(1)} %slice.125), channel_id=1, source_target_pairs={{0,4},{1,5},{6,2},{7,3},{8,12},{9,13},{14,10},{15,11},{16,20},{17,... | collective-permute-start | bytes 4325384 | tf_op jit(solution)/shard_map/ppermute | solution.py:362
  119.6 37.4 %collective-permute-start.18 = (bf16[2,352,1024]{2,1,0:T(8,128)(2,1)S(1)}, bf16[2,352,1024]{2,1,0:T(8,128)(2,1)}, u32[]{:S(2)}, u32[]{:S(2)}) collective-permute-start(bf16[2,352,1024]{2,1,0:T(8,128)(2,1)S(1)} %slice.130), channel_id=1, source_target_pairs={{2,6},{3,7},{4,0},{5,1},{10,14},{11,15},{12,8},{13,9},{18,22},{19,... | collective-permute-start | bytes 4325384 | tf_op jit(solution)/shard_map/ppermute | solution.py:362
  146.1 34.2 %all-to-all-start = ((bf16[8,256,256]{2,1,0:T(8,128)(2,1)}), bf16[8,256,256]{2,1,0:T(8,128)(2,1)S(1)}, u32[]{:S(2)}, u32[]{:S(2)}) async-start(bf16[8,256,256]{2,1,0:T(8,128)(2,1)} %bitcast.101), calls=%async_computation | async-start | bytes 2097152 | tf_op jit(solution)/shard_map/all_to_all | solution.py:1049
  158.5 39.8 %collective-permute-start.25 = (bf16[2,352,1024]{2,1,0:T(8,128)(2,1)S(1)}, bf16[2,352,1024]{2,1,0:T(8,128)(2,1)}, u32[]{:S(2)}, u32[]{:S(2)}) collective-permute-start(bf16[2,352,1024]{2,1,0:T(8,128)(2,1)S(1)} %broadcast_select_fusion.refs_2_.refs_6_), channel_id=1, source_target_pairs={{0,16},{8,24},{16,0},{24,8},{1,17},{9,25},{17,1},{25,9},{2,18},{10... | collective-permute-start | bytes 4325384 | tf_op jit(solution)/shard_map/ppermute | solution.py:336
  192.9 39.9 %collective-permute-start.20 = (bf16[256,2048]{1,0:T(8,128)(2,1)}, bf16[256,2048]{1,0:T(8,128)(2,1)S(1)}, u32[]{:S(2)}, u32[]{:S(2)}) collective-permute-start(bf16[256,2048]{1,0:T(8,128)(2,1)} %get-tuple-element.306.refs_4_), channel_id=1, source_target_pairs={{0,8},{8,0},{16,24},{24,16},{1,9},{9,1},{17,25},{25,17},{2,10},{10... | collective-permute-start | bytes 3145736 | tf_op jit(solution)/shard_map/ppermute | solution.py:333
  193.5 40.6 %collective-permute-start.21 = (bf16[256,2048]{1,0:T(8,128)(2,1)}, bf16[256,2048]{1,0:T(8,128)(2,1)S(1)}, u32[]{:S(2)}, u32[]{:S(2)}) collective-permute-start(bf16[256,2048]{1,0:T(8,128)(2,1)} %get-tuple-element.306.refs_4_), channel_id=1, source_target_pairs={{0,2},{1,3},{2,0},{3,1},{4,6},{5,7},{6,4},{7,5},{8,10},{9,11},{10,... | collective-permute-start | bytes 3145736 | tf_op jit(solution)/shard_map/ppermute | solution.py:349
  194.7 39.4 %collective-permute-start.23 = (bf16[256,2048]{1,0:T(8,128)(2,1)}, bf16[256,2048]{1,0:T(8,128)(2,1)S(1)}, u32[]{:S(2)}, u32[]{:S(2)}) collective-permute-start(bf16[256,2048]{1,0:T(8,128)(2,1)} %get-tuple-element.306.refs_4_), channel_id=1, source_target_pairs={{0,1},{1,0},{2,3},{3,2},{4,5},{5,4},{6,7},{7,6},{8,9},{9,8},{10,11... | collective-permute-start | bytes 3145736 | tf_op jit(solution)/shard_map/ppermute | solution.py:346
  195.9 36.9 %collective-permute-start.22 = (bf16[1,352,1024]{2,1,0:T(8,128)(2,1)S(1)}, bf16[1,352,1024]{2,1,0:T(8,128)(2,1)S(1)}, u32[]{:S(2)}, u32[]{:S(2)}) collective-permute-start(bf16[1,352,1024]{2,1,0:T(8,128)(2,1)S(1)} %slice.135), channel_id=1, source_target_pairs={{0,4},{1,5},{2,6},{3,7},{4,0},{5,1},{6,2},{7,3},{8,12},{9,13},{10,... | collective-permute-start | bytes 2162696 | tf_op jit(solution)/shard_map/ppermute | solution.py:352
  198.3 34.5 %collective-permute-start.24 = (bf16[1,352,1024]{2,1,0:T(8,128)(2,1)S(1)}, bf16[1,352,1024]{2,1,0:T(8,128)(2,1)S(1)}, u32[]{:S(2)}, u32[]{:S(2)}) collective-permute-start(bf16[1,352,1024]{2,1,0:T(8,128)(2,1)S(1)} %slice.135), channel_id=1, source_target_pairs={{0,16},{8,24},{16,0},{24,8},{1,17},{9,25},{17,1},{25,9},{2,18},{10... | collective-permute-start | bytes 2162696 | tf_op jit(solution)/shard_map/ppermute | solution.py:336
  256.1 35.0 %collective-permute-start.35 = (bf16[256,2048]{1,0:T(8,128)(2,1)}, bf16[256,2048]{1,0:T(8,128)(2,1)}, u32[]{:S(2)}, u32[]{:S(2)}) collective-permute-start(bf16[256,2048]{1,0:T(8,128)(2,1)} %collective-permute-done.7.refs_8_), channel_id=1, source_target_pairs={{0,1},{1,0},{2,3},{3,2},{4,5},{5,4},{6,7},{7,6},{8,9},{9,8},{10,11... | collective-permute-start | bytes 3145736 | tf_op jit(solution)/shard_map/ppermute | solution.py:346
  263.7 38.7 %all-to-all-start.1 = ((bf16[4,320,512]{2,1,0:T(8,128)(2,1)}), bf16[4,320,512]{2,1,0:T(8,128)(2,1)}, u32[]{:S(2)}, u32[]{:S(2)}) async-start(bf16[4,320,512]{2,1,0:T(8,128)(2,1)} %bitcast.99), calls=%async_computation.1 | async-start | bytes 2621440 | tf_op jit(solution)/shard_map/all_to_all | solution.py:1159
  335.3 34.2 %collective-permute-start.48 = (bf16[4,320,512]{2,1,0:T(8,128)(2,1)}, bf16[4,320,512]{2,1,0:T(8,128)(2,1)S(1)}, u32[]{:S(2)}, u32[]{:S(2)}) collective-permute-start(bf16[4,320,512]{2,1,0:T(8,128)(2,1)} %collective-permute-done.39.refs_2_), channel_id=1, source_target_pairs={{0,1},{1,0},{2,3},{3,2},{4,5},{5,4},{6,7},{7,6},{8,9},{9,8},{10,11... | collective-permute-start | bytes 3932168 | tf_op jit(solution)/shard_map/ppermute | solution.py:346
  418.9 62.6 %all-to-all-start.2 = ((bf16[8,256,256]{2,1,0:T(8,128)(2,1)}), bf16[8,256,256]{2,1,0:T(8,128)(2,1)S(1)}, u32[]{:S(2)}, u32[]{:S(2)}) async-start(bf16[8,256,256]{2,1,0:T(8,128)(2,1)} %get-tuple-element.427), calls=%async_computation.2 | async-start | bytes 2097152 | tf_op jit(solution)/shard_map/all_to_all | solution.py:1049
  425.2 48.3 %collective-permute-start.56 = (bf16[256,2048]{1,0:T(8,128)(2,1)}, bf16[256,2048]{1,0:T(8,128)(2,1)S(1)}, u32[]{:S(2)}, u32[]{:S(2)}) collective-permute-start(bf16[256,2048]{1,0:T(8,128)(2,1)} %add_convert_fusion.4), channel_id=1, source_target_pairs={{0,8},{8,0},{16,24},{24,16},{1,9},{9,1},{17,25},{25,17},{2,10},{10... | collective-permute-start | bytes 3145736 | tf_op jit(solution)/shard_map/ppermute | solution.py:333
  425.7 55.8 %collective-permute-start.57 = (bf16[256,2048]{1,0:T(8,128)(2,1)}, bf16[256,2048]{1,0:T(8,128)(2,1)S(1)}, u32[]{:S(2)}, u32[]{:S(2)}) collective-permute-start(bf16[256,2048]{1,0:T(8,128)(2,1)} %add_convert_fusion.3), channel_id=1, source_target_pairs={{0,2},{1,3},{2,0},{3,1},{4,6},{5,7},{6,4},{7,5},{8,10},{9,11},{10,... | collective-permute-start | bytes 3145736 | tf_op jit(solution)/shard_map/ppermute | solution.py:349
  446.9 34.6 %collective-permute-start.59 = (bf16[352,1024]{1,0:T(8,128)(2,1)}, bf16[352,1024]{1,0:T(8,128)(2,1)}, u32[]{:S(2)}, u32[]{:S(2)}) collective-permute-start(bf16[352,1024]{1,0:T(8,128)(2,1)} %add_convert_fusion.14), channel_id=1, source_target_pairs={{0,4},{1,5},{2,6},{3,7},{4,0},{5,1},{6,2},{7,3},{8,12},{9,13},{10,... | collective-permute-start | bytes 2162696 | tf_op jit(solution)/shard_map/ppermute | solution.py:352
  481.5 39.2 %collective-permute-start.66 = (bf16[4,256,512]{2,1,0:T(8,128)(2,1)}, bf16[4,256,512]{2,1,0:T(8,128)(2,1)}, u32[]{:S(2)}, u32[]{:S(2)}) collective-permute-start(bf16[4,256,512]{2,1,0:T(8,128)(2,1)} %get-tuple-element.463), channel_id=1, source_target_pairs={{0,8},{8,0},{16,24},{24,16},{1,9},{9,1},{17,25},{25,17},{2,10},{10... | collective-permute-start | bytes 3145736 | tf_op jit(solution)/shard_map/ppermute | solution.py:333
  484.7 36.1 %collective-permute-start.63 = (bf16[352,1024]{1,0:T(8,128)(2,1)}, bf16[352,1024]{1,0:T(8,128)(2,1)}, u32[]{:S(2)}, u32[]{:S(2)}) collective-permute-start(bf16[352,1024]{1,0:T(8,128)(2,1)} %add_convert_fusion.13), channel_id=1, source_target_pairs={{0,4},{1,5},{2,6},{3,7},{4,0},{5,1},{6,2},{7,3},{8,12},{9,13},{10,... | collective-permute-start | bytes 2162696 | tf_op jit(solution)/shard_map/ppermute | solution.py:352
  485.9 34.8 %collective-permute-start.64 = (bf16[352,1024]{1,0:T(8,128)(2,1)}, bf16[352,1024]{1,0:T(8,128)(2,1)}, u32[]{:S(2)}, u32[]{:S(2)}) collective-permute-start(bf16[352,1024]{1,0:T(8,128)(2,1)} %get-tuple-element.461), channel_id=1, source_target_pairs={{0,16},{8,24},{16,0},{24,8},{1,17},{9,25},{17,1},{25,9},{2,18},{10... | collective-permute-start | bytes 2162696 | tf_op jit(solution)/shard_map/ppermute | solution.py:336
  486.9 33.8 %collective-permute-start.65 = (bf16[352,1024]{1,0:T(8,128)(2,1)}, bf16[352,1024]{1,0:T(8,128)(2,1)}, u32[]{:S(2)}, u32[]{:S(2)}) collective-permute-start(bf16[352,1024]{1,0:T(8,128)(2,1)} %get-tuple-element.462), channel_id=1, source_target_pairs={{0,16},{8,24},{16,0},{24,8},{1,17},{9,25},{17,1},{25,9},{2,18},{10... | collective-permute-start | bytes 2162696 | tf_op jit(solution)/shard_map/ppermute | solution.py:336
  523.5 37.1 %all-to-all-start.3 = ((bf16[8,256,320]{1,2,0:T(8,128)(2,1)}), bf16[8,256,320]{1,2,0:T(8,128)(2,1)S(1)}, u32[]{:S(2)}, u32[]{:S(2)}) async-start(bf16[8,256,320]{1,2,0:T(8,128)(2,1)} %copy.24), calls=%async_computation.3 | async-start | bytes 2621440 | tf_op jit(solution)/shard_map/all_to_all | solution.py:1049
  536.3 47.4 %collective-permute-start.70 = (bf16[4,256,512]{2,1,0:T(8,128)(2,1)}, bf16[4,256,512]{2,1,0:T(8,128)(2,1)}, u32[]{:S(2)}, u32[]{:S(2)}) collective-permute-start(bf16[4,256,512]{2,1,0:T(8,128)(2,1)} %add_convert_fusion.2), channel_id=1, source_target_pairs={{0,16},{8,24},{16,0},{24,8},{1,17},{9,25},{17,1},{25,9},{2,18},{10... | collective-permute-start | bytes 3145736 | tf_op jit(solution)/shard_map/ppermute | solution.py:336
  (131 other events, 2174.4 us)
